TPU v7x, 32 devices: a whole 2x2x4 slice. The times are simulated.
32 devices in a mesh: replica: 8 (over z, x), shard: 4 (over y, core).
Axes of the slice: x: 2, y: 2, z: 4, core: 2. Of those that a mesh axis runs over, the one named last changes fastest.
Arguments:
- tokens: bfloat16 [192, 160, 1024], P(('replica', 'shard')), may hold values from -6 to 6
- out_grad: bfloat16 [192, 160, 1024], P(('replica', 'shard')), may hold values from -6 to 6
- kept_count: int32 [192], P(('replica', 'shard')), may hold values from 0 to 96
- attn_w: float32 [1024, 4096], P('shard')
- mlp_w: float32 [1024, 8192], P('shard')
- vectors: float32 [1024, 12], P('shard'), as said below
- attn_m: float32 [1024, 4096], P('shard')
- mlp_m: float32 [1024, 8192], P('shard')
- small_m: float32 [1024, 12], P('shard')
- attn_v: float32 [1024, 4096], P('shard'), as said below
- mlp_v: float32 [1024, 8192], P('shard'), as said below
- small_v: float32 [1024, 12], P('shard'), as said below
Outputs:
- out_tokens: bfloat16 [192, 160, 1024], P(('replica', 'shard'))
- in_grad: bfloat16 [192, 160, 1024], P(('replica', 'shard'))
- attn_grad: float32 [1024, 4096], P('shard')
- attn_first: float32 [1024, 4096], P('shard')
- attn_second: float32 [1024, 4096], P('shard')
- attn_new: float32 [1024, 4096], P('shard')
- attn_low: bfloat16 [1024, 4096], P('shard')
- mlp_grad: float32 [1024, 8192], P('shard')
- mlp_first: float32 [1024, 8192], P('shard')
- mlp_second: float32 [1024, 8192], P('shard')
- mlp_new: float32 [1024, 8192], P('shard')
- mlp_low: bfloat16 [1024, 8192], P('shard')
- small_grad: float32 [1024, 12], P('shard')
- small_first: float32 [1024, 12], P('shard')
- small_second: float32 [1024, 12], P('shard')
- small_new: float32 [1024, 12], P('shard')
- small_low: bfloat16 [1024, 12], P('shard')
Inputs may be any that keep to these rules, and one draw needn't show every extreme that they name: Slot s of image i is a real token where s < 64 + kept_count[i]; later slots are padding. `vectors`: columns 0 and 5 are gains near one, the others biases. `attn_v`: Positive. `mlp_v`: Positive. `small_v`: Positive.
All inputs are finite; a program needn't handle non-finite values.
Results may differ from a plain program's by a relative error of at most 0.025.
Values may be sent and summed in bfloat16 or wider, within the bound.
No kernel may reach another device: no remote copies, remote signals or barrier semaphores. Data moves between devices by JAX's collectives and lax.ppermute only.
A program may use at most 320 MiB of HBM per device.

v0:
```python
import jax
import jax.numpy as jnp
from jax import lax
from jax.sharding import PartitionSpec as P

D = 1024
HEADS = 16
HEAD_DIM = 64
FF = 4096
BUF = 64
STEP = 10


EPS_NORM = 1e-06
MASKED = -1000000000.0
BETA_ONE = 0.9
BETA_TWO = 0.999
EPS_ADAM = 1e-08


def normalize(values):
    average = jnp.mean(values, axis=-1, keepdims=True)
    centred = values - average
    inverse = lax.rsqrt(jnp.mean(centred * centred, axis=-1, keepdims=True) + EPS_NORM)
    return (centred * inverse, inverse)


def norm_back(upstream, normed, inverse):
    first_term = jnp.mean(upstream, axis=-1, keepdims=True)
    second_term = normed * jnp.mean(upstream * normed, axis=-1, keepdims=True)
    return inverse * (upstream - first_term - second_term)


def gelu_exact(values):
    return jax.nn.gelu(values, approximate=False)


def row_contract(left, right):
    return lax.dot_general(
        left, right, (((0,), (0,)), ((), ())), preferred_element_type=jnp.float32
    )


def col_contract(left, right):
    return lax.dot_general(
        left, right, (((1,), (1,)), ((), ())), preferred_element_type=jnp.float32
    )


def adam_update(weight, first_mom, second_mom, gradient, rate, decay):
    first_new = BETA_ONE * first_mom + (1.0 - BETA_ONE) * gradient
    second_new = BETA_TWO * second_mom + (1.0 - BETA_TWO) * gradient * gradient
    first_hat = first_new / (1.0 - BETA_ONE**STEP)
    second_hat = second_new / (1.0 - BETA_TWO**STEP)
    weight_new = weight - rate * (first_hat / (jnp.sqrt(second_hat) + EPS_ADAM) + decay * weight)
    return (gradient, first_new, second_new, weight_new, weight_new.astype(jnp.bfloat16))


def on_device(
    tokens,
    out_grad,
    kept_count,
    attn_w,
    mlp_w,
    vectors,
    attn_m,
    mlp_m,
    small_m,
    attn_v,
    mlp_v,
    small_v,
):
    images = tokens.shape[0]
    slot_count = tokens.shape[1]
    total_rows = images * slot_count
    score_scale = HEAD_DIM ** (-0.5)
    attn_full, mlp_full, small_full = (
        lax.all_gather(attn_w.astype(jnp.bfloat16), "shard", axis=0, tiled=True),
        lax.all_gather(mlp_w.astype(jnp.bfloat16), "shard", axis=0, tiled=True),
        lax.all_gather(vectors.astype(jnp.bfloat16), "shard", axis=0, tiled=True),
    )
    positions = jnp.arange(slot_count, dtype=jnp.int32)
    valid_mask = (positions[None, :] < (BUF + kept_count)[:, None]).astype(jnp.float32)
    key_shift = jnp.where(valid_mask > 0.5, 0.0, MASKED)[:, None, None, :]
    valid_rows = valid_mask.reshape(total_rows, 1)
    small_vals = small_full.astype(jnp.float32)
    gain_one, shift_one = (small_vals[:, 0], small_vals[:, 1])
    query_bias, value_bias, out_bias = (small_vals[:, 2], small_vals[:, 3], small_vals[:, 4])
    gain_two, shift_two, down_bias = (small_vals[:, 5], small_vals[:, 6], small_vals[:, 7])
    up_bias = small_vals[:, 8:12].T.reshape(FF)
    inputs = tokens.astype(jnp.float32).reshape(total_rows, D)
    normed_one, inverse_one = normalize(inputs)
    hidden_one = (normed_one * gain_one + shift_one).astype(jnp.bfloat16)
    qkv_bias = jnp.concatenate([query_bias, jnp.zeros_like(query_bias), value_bias])
    projected = (
        jnp.dot(hidden_one, attn_full[:, : 3 * D], preferred_element_type=jnp.float32) + qkv_bias
    )
    projected = projected.astype(jnp.bfloat16).reshape(images, slot_count, 3, HEADS, HEAD_DIM)
    queries, key_rows, values = (projected[:, :, 0], projected[:, :, 1], projected[:, :, 2])
    scores = (
        jnp.einsum("ishd,ithd->ihst", queries, key_rows, preferred_element_type=jnp.float32)
        * score_scale
        + key_shift
    )
    top_score = jnp.max(scores, axis=-1, keepdims=True)
    exp_scores = jnp.exp(scores - top_score)
    row_totals = jnp.sum(exp_scores, axis=-1, keepdims=True)
    attn_probs = exp_scores / row_totals
    log_total = top_score + jnp.log(row_totals)
    attn_mixed = jnp.einsum(
        "ihst,ithd->ishd",
        attn_probs.astype(jnp.bfloat16),
        values,
        preferred_element_type=jnp.float32,
    )
    attn_mixed = attn_mixed.astype(jnp.bfloat16).reshape(total_rows, D)
    branch = (
        jnp.dot(attn_mixed, attn_full[:, 3 * D :], preferred_element_type=jnp.float32) + out_bias
    )
    middle = inputs + branch
    normed_two, inverse_two = normalize(middle)
    hidden_two = (normed_two * gain_two + shift_two).astype(jnp.bfloat16)
    pre_act = jnp.dot(hidden_two, mlp_full[:, :FF], preferred_element_type=jnp.float32) + up_bias
    activated, gelu_pull = jax.vjp(gelu_exact, pre_act)
    act_low = activated.astype(jnp.bfloat16)
    down_out = col_contract(act_low, mlp_full[:, FF:]) + down_bias
    result = ((middle + down_out) * valid_rows).astype(jnp.bfloat16).reshape(images, slot_count, D)
    attn_back, mlp_back, small_back = (
        lax.all_gather(attn_w.astype(jnp.bfloat16), "shard", axis=0, tiled=True),
        lax.all_gather(mlp_w.astype(jnp.bfloat16), "shard", axis=0, tiled=True),
        lax.all_gather(vectors.astype(jnp.bfloat16), "shard", axis=0, tiled=True),
    )
    gain_back_one = small_back[:, 0].astype(jnp.float32)
    gain_back_two = small_back[:, 5].astype(jnp.float32)
    grad_rows = out_grad.astype(jnp.float32).reshape(total_rows, D) * valid_rows
    down_grad = grad_rows.astype(jnp.bfloat16)
    grad_down_w = row_contract(down_grad, act_low)
    grad_down_b = jnp.sum(down_grad, axis=0, dtype=jnp.float32)
    act_grad = jnp.dot(down_grad, mlp_back[:, FF:], preferred_element_type=jnp.float32)
    (pre_grad,) = gelu_pull(act_grad)
    pre_low = pre_grad.astype(jnp.bfloat16)
    grad_up_w = row_contract(hidden_two, pre_low)
    grad_up_b = jnp.sum(pre_low, axis=0, dtype=jnp.float32)
    two_grad = col_contract(pre_low, mlp_back[:, :FF])
    grad_gain_two = jnp.sum(two_grad * normed_two, axis=0)
    grad_shift_two = jnp.sum(two_grad, axis=0)
    middle_grad = norm_back(two_grad * gain_back_two, normed_two, inverse_two) + grad_rows
    mlp_grad = jnp.concatenate([grad_up_w, grad_down_w], axis=1)
    branch_grad = middle_grad.astype(jnp.bfloat16)
    grad_out_w = row_contract(attn_mixed, branch_grad)
    grad_out_b = jnp.sum(branch_grad, axis=0, dtype=jnp.float32)
    mixed_grad = col_contract(branch_grad, attn_back[:, 3 * D :])
    mixed_grad = mixed_grad.astype(jnp.bfloat16).reshape(images, slot_count, HEADS, HEAD_DIM)
    scores_again = (
        jnp.einsum("ishd,ithd->ihst", queries, key_rows, preferred_element_type=jnp.float32)
        * score_scale
        + key_shift
    )
    probs_again = jnp.exp(scores_again - log_total)
    value_grad = jnp.einsum(
        "ihst,ishd->ithd",
        probs_again.astype(jnp.bfloat16),
        mixed_grad,
        preferred_element_type=jnp.float32,
    )
    prob_grad = jnp.einsum(
        "ishd,ithd->ihst", mixed_grad, values, preferred_element_type=jnp.float32
    )
    score_grad = probs_again * (
        prob_grad - jnp.sum(probs_again * prob_grad, axis=-1, keepdims=True)
    )
    score_low = score_grad.astype(jnp.bfloat16)
    query_grad = (
        jnp.einsum("ihst,ithd->ishd", score_low, key_rows, preferred_element_type=jnp.float32)
        * score_scale
    )
    key_grad = (
        jnp.einsum("ihst,ishd->ithd", score_low, queries, preferred_element_type=jnp.float32)
        * score_scale
    )
    proj_grad = (
        jnp.stack([query_grad, key_grad, value_grad], axis=2)
        .astype(jnp.bfloat16)
        .reshape(total_rows, 3 * D)
    )
    grad_qkv_w = row_contract(hidden_one, proj_grad)
    proj_sums = jnp.sum(proj_grad, axis=0, dtype=jnp.float32)
    one_grad = col_contract(proj_grad, attn_back[:, : 3 * D])
    grad_gain_one = jnp.sum(one_grad * normed_one, axis=0)
    grad_shift_one = jnp.sum(one_grad, axis=0)
    input_grad = norm_back(one_grad * gain_back_one, normed_one, inverse_one) + middle_grad
    in_grad = input_grad.astype(jnp.bfloat16).reshape(images, slot_count, D)
    attn_grad = jnp.concatenate([grad_qkv_w, grad_out_w], axis=1)
    column_grads = jnp.stack(
        [
            grad_gain_one,
            grad_shift_one,
            proj_sums[:D],
            proj_sums[2 * D :],
            grad_out_b,
            grad_gain_two,
            grad_shift_two,
            grad_down_b,
        ],
        axis=1,
    )
    small_grad = jnp.concatenate([column_grads, grad_up_b.reshape(4, D).T], axis=1)
    attn_part, mlp_part, small_part = (
        lax.psum_scatter(
            attn_grad.astype(jnp.bfloat16), "shard", scatter_dimension=0, tiled=True
        ).astype(jnp.float32),
        lax.psum_scatter(
            mlp_grad.astype(jnp.bfloat16), "shard", scatter_dimension=0, tiled=True
        ).astype(jnp.float32),
        lax.psum_scatter(
            small_grad.astype(jnp.bfloat16), "shard", scatter_dimension=0, tiled=True
        ).astype(jnp.float32),
    )
    attn_sum, mlp_sum, small_sum = (
        lax.psum(attn_part.astype(jnp.bfloat16), "replica").astype(jnp.float32),
        lax.psum(mlp_part.astype(jnp.bfloat16), "replica").astype(jnp.float32),
        lax.psum(small_part.astype(jnp.bfloat16), "replica").astype(jnp.float32),
    )
    image_total = images * lax.axis_size("replica") * lax.axis_size("shard")
    attn_out = adam_update(attn_w, attn_m, attn_v, attn_sum / image_total, 0.1, 0.05)
    mlp_out = adam_update(mlp_w, mlp_m, mlp_v, mlp_sum / image_total, 0.05, 0.05)
    small_out = adam_update(vectors, small_m, small_v, small_sum / image_total, 1.0, 0.0)
    return (
        result,
        in_grad,
        attn_out[0],
        attn_out[1],
        attn_out[2],
        attn_out[3],
        attn_out[4],
        mlp_out[0],
        mlp_out[1],
        mlp_out[2],
        mlp_out[3],
        mlp_out[4],
        small_out[0],
        small_out[1],
        small_out[2],
        small_out[3],
        small_out[4],
    )


def solution(mesh):
    in_specs = (
        P(("replica", "shard"), None, None),
        P(("replica", "shard"), None, None),
        P(("replica", "shard")),
        P("shard", None),
        P("shard", None),
        P("shard", None),
        P("shard", None),
        P("shard", None),
        P("shard", None),
        P("shard", None),
        P("shard", None),
        P("shard", None),
    )
    out_specs = (
        P(("replica", "shard"), None, None),
        P(("replica", "shard"), None, None),
        P("shard", None),
        P("shard", None),
        P("shard", None),
        P("shard", None),
        P("shard", None),
        P("shard", None),
        P("shard", None),
        P("shard", None),
        P("shard", None),
        P("shard", None),
        P("shard", None),
        P("shard", None),
        P("shard", None),
        P("shard", None),
        P("shard", None),
    )
    return jax.shard_map(
        on_device, mesh=mesh, in_specs=in_specs, out_specs=out_specs, check_vma=False
    )
```

profile of v0, /device:TPU:0, one launch (start us, length us, event | category | flops | bytes accessed | tf_op | source)
XLA Modules:
  0.0 872.8 jit_solution(16453652174582792887)
XLA Ops:
  7.2 3.8 convert_element_type.171
  11.1 6.1 convert_element_type.178
  17.3 0.3 convert_reduce_fusion
  17.8 0.7 multiply_reduce_fusion.6
  18.5 6.2 all_gather.12
  24.9 0.6 fusion.81
  25.6 0.6 slice_convert_fusion
  26.2 3.3 fusion.31
  29.5 2.1 add_convert_fusion.2
  31.6 40.6 %all-gather.3.cloned.1.call-done = bf16[1024,4096]{1,0:T(8,128)(2,1)} async-done(((bf16[256,4096]{1,0:T(8,128)(2,1)}), bf16[1024,4096]{1,0:T(8,128)(2,1)}) %all-gather.3.cloned.1.call-update) | async-done | bytes 8388624 | tf_op jit(solution)/shard_map/all_gather | solution.py:78
  72.2 11.2 %add_convert_fusion.1 = bf16[960,3072]{1,0:T(8,128)(2,1)} fusion(f32[3072]{0:T(1024)S(1)} %pad_maximum_fusion.2, bf16[1024,4096]{1,0:T(8,128)(2,1)} %all-gather.3.cloned.1.call-done, f32[1024]{0:T(1024)S(1)} %bitcast.108, f32[1024]{0:T(1024)S(1)} %bitcast.106, f32[960]{0:T(1024)S(1)} %rsqrt.21, f32[960]{0:T(1024)S(1)} %div.98, ...), kind=kOutput, calls=%fused_computation.30 | convolution fusion | flops 6051594240 | bytes 14183936 | tf_op jit(solution)/shard_map/dot_general | solution.py:96
  83.5 15.4 %reshape.232 = bf16[6,160,3,16,64]{4,3,2,1,0:T(8,128)(2,1)} reshape(bf16[960,3072]{1,0:T(8,128)(2,1)} %add_convert_fusion.1) | data formatting | bytes 11796480 | tf_op jit(solution)/shard_map/reshape | solution.py:98
  98.9 8.6 fusion.80
  107.5 6.8 copy.57
  114.3 5.5 copy.58
  119.8 7.5 copy.56
  127.4 11.0 %fusion.83 = (f32[6,16,160]{2,1,0:T(8,128)S(1)}, f32[6,16,160,160]{2,3,1,0:T(8,128)}) fusion(f32[6,160]{1,0:T(8,128)S(1)} %compare_select_fusion, bf16[6,160,1,16,64]{1,4,3,0,2:T(8,128)(2,1)S(1)} %copy.58, bf16[6,160,1,16,64]{1,4,3,0,2:T(8,128)(2,1)} %copy.57), kind=kOutput, calls=%fused_computation.139 | convolution fusion | flops 321930240 | bytes 13827840 | tf_op jit(solution)/shard_map/ishd,ithd->ihst/dot_general | solution.py:101
  138.4 9.8 %fusion.6 = f32[6,16,160]{2,1,0:T(8,128)S(1)} fusion(f32[6,16,160,160]{2,3,1,0:T(8,128)} %get-tuple-element.64, f32[6,16,160]{2,1,0:T(8,128)S(1)} %get-tuple-element.63), kind=kLoop, calls=%fused_computation.25 | loop fusion | flops 4899840 | bytes 9953280 | tf_op jit(solution)/shard_map/reduce_sum | solution.py:107
  148.2 10.3 %convert_bitcast_fusion = bf16[6,160,16,64]{1,3,2,0:T(8,128)(2,1)} fusion(f32[6,16,160,160]{2,3,1,0:T(8,128)} %get-tuple-element.64, f32[6,16,160]{2,1,0:T(8,128)S(1)} %fusion.6, f32[6,16,160]{2,1,0:T(8,128)S(1)} %get-tuple-element.63, bf16[6,160,1,16,64]{1,4,3,0,2:T(8,128)(2,1)S(1)} %copy-done.14), kind=kOutput, calls=%fused_computation.91 | convolution fusion | flops 322928640 | bytes 13885440 | tf_op jit(solution)/shard_map/ihst,ithd->ishd/dot_general | solution.py:110
  158.5 6.8 copy.43
  165.3 6.6 reshape.233
  171.9 4.5 fusion.84
  176.5 1.9 copy-done.9
  178.4 0.5 multiply_reduce_fusion.5
  178.9 0.7 log_add_fusion
  179.6 0.8 all-gather.5.cloned.1.call-done
  180.4 48.8 %multiply_convert_fusion.1 = (bf16[960,4096]{1,0:T(8,128)(2,1)}, f32[960,4096]{1,0:T(8,128)}, f32[960,4096]{1,0:T(8,128)}) fusion(f32[4096]{0:T(1024)S(1)} %bitcast.101, bf16[1024,8192]{1,0:T(8,128)(2,1)} %all-gather.5.cloned.1.call-done, f32[960,1024]{1,0:T(8,128)} %copy-done.9, f32[1024]{0:T(1024)S(1)} %bitcast.112, f32[1024]{0:T(1024)S(1)} %bitcast.110, ...), kind=kOutput, calls=%fused_computation.8 | convolution fusion | flops 8317501440 | bytes 51674624 | tf_op jit(solution)/shard_map/dot_general | solution.py:123
  229.2 22.8 %fusion.85 = (bf16[4096]{0:T(1024)(128)(2,1)}, bf16[960,4096]{1,0:T(8,128)(2,1)}) fusion(f32[960,4096]{1,0:T(8,128)} %get-tuple-element.47, bf16[960,1024]{1,0:T(8,128)(2,1)S(1)} %copy-done.21, bf16[1024,8192]{1,0:T(8,128)(2,1)} %all-gather.5.cloned.1.call-done, f32[960,4096]{1,0:T(8,128)} %get-tuple-element.67, f32[4096]{0:T(1024)S(1)} %bitcast.102), kind=kOutput, calls=%fused_computation.141 | convolution fusion | flops 8115974144 | bytes 49700864 | tf_op jit(solution)/shard_map/dot_general | solution.py:139
  252.0 15.5 %multiply_reduce_fusion.1 = (bf16[1024]{0:T(1024)(128)(2,1)}, f32[960]{0:T(1024)S(1)}, f32[960]{0:T(1024)S(1)}, bf16[1024]{0:T(1024)(128)(2,1)}, f32[960,1024]{1,0:T(8,128)S(1)}) fusion(f32[960,1024]{1,0:T(8,128)} %copy-done.9, f32[960]{0:T(1024)S(1)} %add_rsqrt_fusion.1, f32[960]{0:T(1024)S(1)} %broadcast_multiply_fusion.5, f32[1024]{0:T(1024)S(1)} %bitcast.97, ...), kind=kOutput, calls=%fused_computation.64 | convolution fusion | flops 8061906944 | bytes 24140800 | tf_op jit(solution)/shard_map/dot_general | solution.py:45
  267.5 1.8 convert_reduce_fusion.1
  269.3 1.9 copy-done.13
  271.2 3.8 fusion.60
  275.0 4.1 reshape.236
  279.2 5.4 copy.44
  284.7 13.2 %multiply_reduce_fusion = (f32[6,16,160]{2,1,0:T(8,128)S(1)}, f32[6,16,160,160]{2,3,1,0:T(8,128)}) fusion(f32[6,16,160,160]{2,3,1,0:T(8,128)} %get-tuple-element.64, f32[6,16,160]{2,1,0:T(8,128)S(1)} %copy-done.23, bf16[6,160,16,64]{1,3,2,0:T(8,128)(2,1)S(1)} %copy.44, bf16[6,160,1,16,64]{1,4,3,0,2:T(8,128)(2,1)} %copy.56), kind=kOutput, calls=%fused_computation.5 | convolution fusion | flops 321930240 | bytes 23715840 | tf_op jit(solution)/shard_map/ishd,ithd->ihst/dot_general | solution.py:166
  297.8 11.6 %multiply_convert_fusion = bf16[6,16,160,160]{2,3,1,0:T(8,128)(2,1)S(1)} fusion(f32[6,16,160,160]{2,3,1,0:T(8,128)} %get-tuple-element.70, f32[6,16,160,160]{2,3,1,0:T(8,128)} %get-tuple-element.64, f32[6,16,160]{2,1,0:T(8,128)S(1)} %get-tuple-element.69, f32[6,16,160]{2,1,0:T(8,128)S(1)} %copy-done.23), kind=kLoop, calls=%fused_computation.4 | loop fusion | flops 9830400 | bytes 24698880 | tf_op jit(solution)/shard_map/convert_element_type | solution.py:172
  309.4 2.9 multiply_bitcast_fusion.1
  312.3 4.3 multiply_bitcast_fusion
  316.6 9.0 %fusion.45 = bf16[6,160,1,16,64]{1,4,3,0,2:T(8,128)(2,1)S(1)} fusion(bf16[6,160,16,64]{1,3,2,0:T(8,128)(2,1)} %copy-done.6, f32[6,16,160,160]{2,3,1,0:T(8,128)} %get-tuple-element.64, f32[6,16,160]{2,1,0:T(8,128)S(1)} %copy-done.23), kind=kOutput, calls=%fused_computation.93 | convolution fusion | flops 319488000 | bytes 13824000 | tf_op jit(solution)/shard_map/ihst,ishd->ithd/dot_general | solution.py:160
  325.7 6.6 convolution_convert_fusion.3
  332.2 4.9 fusion.72
  337.1 18.0 %copy.49 = bf16[6,160,3,16,64]{4,3,2,1,0:T(8,128)(2,1)} copy(bf16[6,160,3,16,64]{1,4,3,0,2:T(8,128)(2,1)} %get-tuple-element.35) | data formatting | bytes 11796480 | tf_op jit(solution)/shard_map/convert_element_type | solution.py:183
  355.1 15.5 %convert_element_type.193 = bf16[960,3072]{1,0:T(8,128)(2,1)} reshape(bf16[6,160,3,16,64]{4,3,2,1,0:T(8,128)(2,1)} %copy.49) | data formatting | bytes 11796480 | tf_op jit(solution)/shard_map/convert_element_type | solution.py:183
  370.6 11.7 %convolution_convert_fusion.2 = bf16[1024,3072]{1,0:T(8,128)(2,1)} fusion(bf16[960,1024]{1,0:T(8,128)(2,1)} %bitcast.94, bf16[960,3072]{1,0:T(8,128)(2,1)} %convert_element_type.193), kind=kOutput, calls=%fused_computation.54 | convolution fusion | flops 6042943488 | bytes 14155776 | tf_op jit(solution)/shard_map/dot_general | solution.py:39
  382.4 7.0 pad_maximum_fusion.1
  389.5 1.5 copy-done.22
  390.9 11.4 %convolution_convert_fusion = bf16[1024,4096]{1,0:T(8,128)(2,1)S(1)} fusion(bf16[960,1024]{1,0:T(8,128)(2,1)S(1)} %copy-done.22, bf16[960,4096]{1,0:T(8,128)(2,1)} %get-tuple-element.46), kind=kOutput, calls=%fused_computation.39 | convolution fusion | flops 8057257984 | bytes 18219008 | tf_op jit(solution)/shard_map/dot_general | solution.py:39
  402.4 12.8 %convolution_convert_fusion.1 = bf16[1024,4096]{1,0:T(8,128)(2,1)S(1)} fusion(bf16[960,4096]{1,0:T(8,128)(2,1)} %get-tuple-element.73, f32[960,1024]{1,0:T(8,128)S(1)} %copy-done.11, f32[1024]{0:T(1024)S(1)} %bitcast.113, f32[1024]{0:T(1024)S(1)} %bitcast.111, f32[960]{0:T(1024)S(1)} %add_rsqrt_fusion.1, f32[960]{0:T(1024)S(1)} %broadcast_multiply_fusion.5), kind=kOutput, calls=%fused_computation.40 | convolution fusion | flops 8062173184 | bytes 20200960 | tf_op jit(solution)/shard_map/dot_general | solution.py:39
  415.3 6.7 pad_maximum_fusion
  422.1 0.6 copy-done.25
  422.7 2.0 fusion.52
  424.8 12.9 %multiply_reduce_fusion.2 = (bf16[1024]{0:T(1024)(128)(2,1)S(1)}, f32[960]{0:T(1024)S(1)}, f32[960]{0:T(1024)S(1)}, bf16[1024]{0:T(1024)(128)(2,1)S(1)}, f32[960,1024]{1,0:T(8,128)}) fusion(f32[960]{0:T(1024)S(1)} %copy-done.35, f32[960]{0:T(1024)S(1)} %copy-done.33, bf16[6,160,1024]{2,1,0:T(8,128)(2,1)S(1)} %copy-done.4, f32[1024]{0:T(1024)S(1)} %bitcast.99, ...), kind=kOutput, calls=%fused_computation.65 | convolution fusion | flops 6052573184 | bytes 20077568 | tf_op jit(solution)/shard_map/dot_general | solution.py:45
  437.7 0.1 stack.50
  438.0 1.3 concatenate.18
  439.3 22.0 %reduce-scatter.4.cloned.1.call-done = bf16[256,4096]{1,0:T(8,128)(2,1)} async-done(((bf16[1024,4096]{1,0:T(8,128)(2,1)}), bf16[256,4096]{1,0:T(8,128)(2,1)}) %reduce-scatter.4.cloned.1.call-update) | async-done | bytes 2097168 | tf_op jit(solution)/shard_map/reduce_scatter | solution.py:209
  461.3 128.8 %reduce-scatter.6.cloned.1.call-done = bf16[256,8192]{1,0:T(8,128)(2,1)} async-done(((bf16[1024,8192]{1,0:T(8,128)(2,1)}), bf16[256,8192]{1,0:T(8,128)(2,1)}) %reduce-scatter.6.cloned.1.call-update) | async-done | bytes 4194320 | tf_op jit(solution)/shard_map/reduce_scatter | solution.py:212
  590.1 5.1 add_convert_fusion.3
  595.3 14.0 %multiply_convert_fusion.3 = bf16[960,1024]{1,0:T(8,128)(2,1)} fusion(f32[960,1024]{1,0:T(8,128)S(1)} %copy-done.12, bf16[960,4096]{1,0:T(8,128)(2,1)} %get-tuple-element.46, bf16[1024,8192]{1,0:T(8,128)(2,1)} %all-gather.5.cloned.1.call-done, f32[960]{0:T(1024)S(1)} %copy-done.30, f32[1024]{0:T(1024)S(1)} %bitcast.109), kind=kOutput, calls=%fused_computation.71 | convolution fusion | flops 8056995840 | bytes 22159104 | tf_op jit(solution)/shard_map/dot_general | solution.py:45
  609.3 2.9 reduce-scatter.8.cloned.1.call-done
  612.3 22.3 %psum.23 = bf16[256,12]{0,1:T(8,128)(2,1)S(1)} all-reduce(bf16[256,12]{0,1:T(8,128)(2,1)} %reduce-scatter.8.cloned.1.call-done), channel_id=1, replica_groups=mesh['replica'=8,'shard'=4] {'replica'}, use_global_device_ids=true, to_apply=%region_24.25 | all-reduce | flops 3072 | bytes 12288 | tf_op jit(solution)/shard_map/psum | solution.py:222
  634.6 0.6 fusion.69
  635.2 194.9 %all-reduce.3.cloned.1.call-done = (bf16[256,4096]{1,0:T(8,128)(2,1)}, bf16[256,8192]{1,0:T(8,128)(2,1)}) async-done(((bf16[256,4096]{1,0:T(8,128)(2,1)}, bf16[256,8192]{1,0:T(8,128)(2,1)}), (bf16[256,4096]{1,0:T(8,128)(2,1)}, bf16[256,8192]{1,0:T(8,128)(2,1)})) %all-reduce.3.cloned.1.call-update) | async-done | bytes 6291472 | tf_op jit(solution)/shard_map/psum | solution.py:220
  830.1 25.8 %fusion.73 = (bf16[256,8192]{1,0:T(8,128)(2,1)}, f32[256,8192]{1,0:T(8,128)}, f32[256,8192]{1,0:T(8,128)}, f32[256,8192]{1,0:T(8,128)}, f32[256,8192]{1,0:T(8,128)}) fusion(f32[256,8192]{1,0:T(8,128)} %param.16, bf16[256,8192]{1,0:T(8,128)(2,1)} %get-tuple-element.26, f32[256,8192]{1,0:T(8,128)} %param.22, f32[256,8192]{1,0:T(8,128)} %param.19), kind=kLoop, calls=%fused_computation.134 | loop fusion | flops 37748736 | bytes 67108864 | tf_op jit(solution)/shard_map/convert_element_type | solution.py:56
  855.9 9.6 %fusion.76 = (bf16[256,4096]{1,0:T(8,128)(2,1)}, f32[256,4096]{1,0:T(8,128)}, f32[256,4096]{1,0:T(8,128)}, f32[256,4096]{1,0:T(8,128)}, f32[256,4096]{1,0:T(8,128)}) fusion(f32[256,4096]{1,0:T(8,128)S(1)} %copy-done.8, bf16[256,4096]{1,0:T(8,128)(2,1)S(1)} %copy-done.19, f32[256,4096]{1,0:T(8,128)S(1)} %copy-done.17, f32[256,4096]{1,0:T(8,128)S(1)} %copy-done.18), kind=kLoop, calls=%fused_computation.135 | loop fusion | flops 18874368 | bytes 33554432 | tf_op jit(solution)/shard_map/convert_element_type | solution.py:56
  (132 shorter events, 1.1 us)
Async XLA Ops:
  7.2 65.0 %all-gather.3.cloned.1.call-start = ((), (), s32[]{:S(2)}) async-start(), calls=%async_computation.3 | async-start | bytes 10485760 | tf_op jit(solution)/shard_map/all_gather | solution.py:78
  11.1 6.2 copy-start.26
  11.1 6.3 copy-start.2
  11.1 169.3 %all-gather.5.cloned.1.call-start = ((), (), s32[]{:S(2)}) async-start(), calls=%async_computation.4 | async-start | bytes 20971520 | tf_op jit(solution)/shard_map/all_gather | solution.py:79
  17.2 7.6 copy-start.47
  17.2 444.0 %reduce-scatter.4.cloned.1.call-start = ((), (), s32[]{:S(2)}) async-start(), calls=%async_computation.5 | async-start | bytes 10485760 | tf_op jit(solution)/shard_map/reduce_scatter | solution.py:209
  17.8 65.7 %copy-start.32 = (f32[960]{0:T(1024)}, f32[960]{0:T(1024)S(1)}, u32[]{:S(2)}) copy-start(f32[960]{0:T(1024)S(1)} %div.98) | copy-start | bytes 11524
  18.5 64.9 %copy-start.34 = (f32[960]{0:T(1024)}, f32[960]{0:T(1024)S(1)}, u32[]{:S(2)}) copy-start(f32[960]{0:T(1024)S(1)} %rsqrt.21) | copy-start | bytes 11524
  24.9 58.6 %copy-start.24 = (f32[6,160]{1,0:T(8,128)}, f32[6,160]{1,0:T(8,128)S(1)}, u32[]{:S(2)}) copy-start(f32[6,160]{1,0:T(8,128)S(1)} %fusion.66) | copy-start | bytes 11524
  24.9 58.5 %copy-start.28 = (f32[960]{0:T(1024)}, f32[960]{0:T(1024)S(1)}, u32[]{:S(2)}) copy-start(f32[960]{0:T(1024)S(1)} %reshape.239) | copy-start | bytes 11524
  25.6 154.8 %copy-start.41 = (f32[1024,1]{0,1:T(1,128)}, f32[1024,1]{0,1:T(1,128)S(1)}, u32[]{:S(2)}) copy-start(f32[1024,1]{0,1:T(1,128)S(1)} %get-tuple-element.54) | copy-start | bytes 12292
  25.6 154.8 %copy-start.43 = (f32[1024,1]{0,1:T(1,128)}, f32[1024,1]{0,1:T(1,128)S(1)}, u32[]{:S(2)}) copy-start(f32[1024,1]{0,1:T(1,128)S(1)} %get-tuple-element.55) | copy-start | bytes 12292
  119.8 18.6 %copy-start = (bf16[6,160,1,16,64]{1,4,3,0,2:T(8,128)(2,1)}, bf16[6,160,1,16,64]{1,4,3,0,2:T(8,128)(2,1)S(1)}, u32[]{:S(2)}) copy-start(bf16[6,160,1,16,64]{1,4,3,0,2:T(8,128)(2,1)S(1)} %copy.58) | copy-start | bytes 5898244
  138.4 9.8 %copy-start.14 = (bf16[6,160,1,16,64]{1,4,3,0,2:T(8,128)(2,1)S(1)}, bf16[6,160,1,16,64]{1,4,3,0,2:T(8,128)(2,1)}, u32[]{:S(2)}) copy-start(bf16[6,160,1,16,64]{1,4,3,0,2:T(8,128)(2,1)} %copy.56) | copy-start | bytes 5898244
  158.5 13.4 %copy-start.3 = (bf16[6,160,1024]{2,1,0:T(8,128)(2,1)S(1)}, bf16[6,160,1024]{2,1,0:T(8,128)(2,1)}, u32[]{:S(2)}) copy-start(bf16[6,160,1024]{2,1,0:T(8,128)(2,1)} %param.12) | copy-start | bytes 5898244
  176.5 1.9 copy-start.9
  180.4 48.8 %copy-start.21 = (bf16[960,1024]{1,0:T(8,128)(2,1)S(1)}, bf16[960,1024]{1,0:T(8,128)(2,1)}, u32[]{:S(2)}) copy-start(bf16[960,1024]{1,0:T(8,128)(2,1)} %fusion.31) | copy-start | bytes 5898244
  229.2 22.8 %copy-start.31 = (f32[1024,1]{0,1:T(1,128)S(1)}, f32[1024,1]{0,1:T(1,128)}, u32[]{:S(2)}) copy-start(f32[1024,1]{0,1:T(1,128)} %get-tuple-element.52) | copy-start | bytes 12292
  252.0 15.5 %copy-start.7 = (bf16[6,160,1024]{2,1,0:T(8,128)(2,1)S(1)}, bf16[6,160,1024]{2,1,0:T(8,128)(2,1)}, u32[]{:S(2)}) copy-start(bf16[6,160,1024]{2,1,0:T(8,128)(2,1)} %param.13) | copy-start | bytes 5898244
  252.0 15.5 %copy-start.10 = (f32[960,1024]{1,0:T(8,128)S(1)}, f32[960,1024]{1,0:T(8,128)}, u32[]{:S(2)}) copy-start(f32[960,1024]{1,0:T(8,128)} %copy-done.9) | copy-start | bytes 11796484
  252.0 15.5 %copy-start.29 = (f32[960]{0:T(1024)S(1)}, f32[960]{0:T(1024)}, u32[]{:S(2)}) copy-start(f32[960]{0:T(1024)} %copy-done.28) | copy-start | bytes 11524
  269.3 1.9 copy-start.13
  275.0 9.6 %copy-start.23 = (f32[6,16,160]{2,1,0:T(8,128)S(1)}, f32[6,16,160]{2,1,0:T(8,128)}, u32[]{:S(2)}) copy-start(f32[6,16,160]{2,1,0:T(8,128)} %log_add_fusion) | copy-start | bytes 184324
  284.7 13.2 %copy-start.6 = (bf16[6,160,16,64]{1,3,2,0:T(8,128)(2,1)}, bf16[6,160,16,64]{1,3,2,0:T(8,128)(2,1)S(1)}, u32[]{:S(2)}) copy-start(bf16[6,160,16,64]{1,3,2,0:T(8,128)(2,1)S(1)} %copy.44) | copy-start | bytes 5898244
  297.8 11.6 %copy-start.1 = (bf16[6,160,1,16,64]{1,4,3,0,2:T(8,128)(2,1)S(1)}, bf16[6,160,1,16,64]{1,4,3,0,2:T(8,128)(2,1)}, u32[]{:S(2)}) copy-start(bf16[6,160,1,16,64]{1,4,3,0,2:T(8,128)(2,1)} %copy-done) | copy-start | bytes 5898244
  309.4 2.9 copy-start.5
  325.6 6.6 copy-start.15
  325.7 6.6 copy-start.16
  370.6 11.7 %copy-start.20 = (bf16[1024,1024]{1,0:T(8,128)(2,1)S(1)}, bf16[1024,1024]{1,0:T(8,128)(2,1)}, u32[]{:S(2)}) copy-start(bf16[1024,1024]{1,0:T(8,128)(2,1)} %convolution_convert_fusion.3) | copy-start | bytes 6291460
  389.4 1.5 copy-start.22
  389.4 200.6 %reduce-scatter.6.cloned.1.call-start = ((), (), s32[]{:S(2)}) async-start(), calls=%async_computation.6 | async-start | bytes 20971520 | tf_op jit(solution)/shard_map/reduce_scatter | solution.py:212
  390.9 11.5 %copy-start.11 = (f32[960,1024]{1,0:T(8,128)S(1)}, f32[960,1024]{1,0:T(8,128)}, u32[]{:S(2)}) copy-start(f32[960,1024]{1,0:T(8,128)} %copy-done.9) | copy-start | bytes 11796484
  390.9 11.5 %copy-start.42 = (f32[1024,1]{0,1:T(1,128)S(1)}, f32[1024,1]{0,1:T(1,128)}, u32[]{:S(2)}) copy-start(f32[1024,1]{0,1:T(1,128)} %copy-done.41) | copy-start | bytes 12292
  390.9 11.5 %copy-start.44 = (f32[1024,1]{0,1:T(1,128)S(1)}, f32[1024,1]{0,1:T(1,128)}, u32[]{:S(2)}) copy-start(f32[1024,1]{0,1:T(1,128)} %copy-done.43) | copy-start | bytes 12292
  422.0 0.7 copy-start.25
  422.0 2.7 copy-start.4
  422.0 2.7 copy-start.33
  422.0 2.8 copy-start.35
  422.0 2.8 copy-start.36
  422.0 190.3 %reduce-scatter.8.cloned.1.call-start = ((), (), s32[]{:S(2)}) async-start(), calls=%async_computation.7 | async-start | bytes 40960 | tf_op jit(solution)/shard_map/reduce_scatter | solution.py:215
  424.7 13.2 %copy-start.46 = (bf16[1024]{0:T(1024)(128)(2,1)S(1)}, bf16[1024]{0:T(1024)(128)(2,1)}, u32[]{:S(2)}) copy-start(bf16[1024]{0:T(1024)(128)(2,1)} %get-tuple-element.17) | copy-start | bytes 6148
  424.7 13.2 %copy-start.45 = (bf16[1024]{0:T(1024)(128)(2,1)S(1)}, bf16[1024]{0:T(1024)(128)(2,1)}, u32[]{:S(2)}) copy-start(bf16[1024]{0:T(1024)(128)(2,1)} %get-tuple-element.23) | copy-start | bytes 6148
  424.8 13.2 %copy-start.39 = (bf16[4096]{0:T(1024)(128)(2,1)S(1)}, bf16[4096]{0:T(1024)(128)(2,1)}, u32[]{:S(2)}) copy-start(bf16[4096]{0:T(1024)(128)(2,1)} %get-tuple-element.72) | copy-start | bytes 24580
  439.3 390.8 %all-reduce.3.cloned.1.call-start = ((), (), s32[]{:S(2)}) async-start(), calls=%async_computation.8 | async-start | bytes 12582912 | tf_op jit(solution)/shard_map/psum | solution.py:220
  590.1 5.2 copy-start.12
  590.1 5.2 copy-start.30
  590.1 5.2 copy-start.40
  595.3 39.2 %copy-start.27 = (f32[256,12]{0,1:T(8,128)S(1)}, f32[256,12]{0,1:T(8,128)}, u32[]{:S(2)}) copy-start(f32[256,12]{0,1:T(8,128)} %param.17) | copy-start | bytes 36868
  595.3 39.2 %copy-start.37 = (f32[256,12]{0,1:T(8,128)S(1)}, f32[256,12]{0,1:T(8,128)}, u32[]{:S(2)}) copy-start(f32[256,12]{0,1:T(8,128)} %param.23) | copy-start | bytes 36868
  595.3 39.2 %copy-start.38 = (f32[256,12]{0,1:T(8,128)S(1)}, f32[256,12]{0,1:T(8,128)}, u32[]{:S(2)}) copy-start(f32[256,12]{0,1:T(8,128)} %param.20) | copy-start | bytes 36868
  830.1 25.8 %copy-start.8 = (f32[256,4096]{1,0:T(8,128)S(1)}, f32[256,4096]{1,0:T(8,128)}, u32[]{:S(2)}) copy-start(f32[256,4096]{1,0:T(8,128)} %param.15) | copy-start | bytes 12582916
  830.1 25.8 %copy-start.17 = (f32[256,4096]{1,0:T(8,128)S(1)}, f32[256,4096]{1,0:T(8,128)}, u32[]{:S(2)}) copy-start(f32[256,4096]{1,0:T(8,128)} %param.21) | copy-start | bytes 12582916
  830.1 25.8 %copy-start.18 = (f32[256,4096]{1,0:T(8,128)S(1)}, f32[256,4096]{1,0:T(8,128)}, u32[]{:S(2)}) copy-start(f32[256,4096]{1,0:T(8,128)} %param.18) | copy-start | bytes 12582916
  830.1 25.8 %copy-start.19 = (bf16[256,4096]{1,0:T(8,128)(2,1)S(1)}, bf16[256,4096]{1,0:T(8,128)(2,1)}, u32[]{:S(2)}) copy-start(bf16[256,4096]{1,0:T(8,128)(2,1)} %get-tuple-element.25) | copy-start | bytes 6291460
Sparse Core Ops, SparseCore 0:
  11.2 60.9 all-gather.2
  74.3 105.9 all-gather.4
  389.5 71.7 reduce-scatter.3
  463.9 126.1 reduce-scatter.5
  592.9 19.3 reduce-scatter.7
  616.6 213.4 all-reduce.2
where the time goes:
time: 882 us; the launch traced here: 873 us
  waiting for transfers between devices  390 us (44%)
  matrix products  227 us (26%)
  local copies, waits for them, and re-layouts  109 us (12%)
  other arithmetic  103 us (12%)
  blocking collectives  28.5 us (3%)
  between operations  15.2 us (2%)
    psum x1, waiting for transfers between devices, on_device(): lax.psum(attn_part.astype(jnp.bfloat16), 'replica').astype(jnp.float32)  195 us
    reduce_scatter x1, waiting for transfers between devices, on_device(): lax.psum_scatter(mlp_grad.astype(jnp.bfloat16), 'shard', scatter_dimensio...  129 us
    dot_general x1, matrix products, on_device(): jnp.dot(hidden_two, mlp_full[:, :FF], preferred_element_type=jnp.float32)  48.8 us
    dot_general x4, matrix products, col_contract(): lax.dot_general(left, right, (((1,), (1,)), ((), ())), preferred_element_...  46.2 us
    dot_general x4, matrix products, row_contract(): lax.dot_general(left, right, (((0,), (0,)), ((), ())), preferred_element_...  42.6 us
    all_gather x1, waiting for transfers between devices, on_device(): lax.all_gather(attn_w.astype(jnp.bfloat16), 'shard', axis=0, tiled=True)  40.6 us
    convert_element_type x3, other arithmetic, adam_update(): weight_new.astype(jnp.bfloat16)  36 us
    convert_element_type x2, local copies, waits for them, and re-layouts, on_device(): proj_grad = jnp.stack([query_grad, key_grad, value_grad], axis=2).astype(...  33.5 us
  transfers between devices with their start and end apart: 6, of which 6 were waited for; matrix products, arithmetic and copies ran while one was open for 21% of the time, Pallas kernels for 0%

commit v1 on v0

v1 whole, which is shorter than its diff:
```python
import jax
import jax.numpy as jnp
from jax import lax
from jax.experimental import pallas as pl
from jax.experimental.pallas import tpu as pltpu
from jax.sharding import PartitionSpec as P

D = 1024
HEADS = 16
HEAD_DIM = 64
FF = 4096
BUF = 64
STEP = 10
BLOCKS = 4
BLOCK = D // BLOCKS
PARTS = 4
PART = FF // PARTS
GROUP = 4
GROUP_W = GROUP * HEAD_DIM

EPS_NORM = 1e-06
MASKED = -1000000000.0
BETA_ONE = 0.9
BETA_TWO = 0.999
EPS_ADAM = 1e-08

BF16 = jnp.bfloat16
F32 = jnp.float32
MIB = 1 << 20


def normalize(values):
    average = jnp.mean(values, axis=-1, keepdims=True)
    centred = values - average
    inverse = lax.rsqrt(jnp.mean(centred * centred, axis=-1, keepdims=True) + EPS_NORM)
    return (centred * inverse, inverse)


def norm_back(upstream, normed, inverse):
    first_term = jnp.mean(upstream, axis=-1, keepdims=True)
    second_term = normed * jnp.mean(upstream * normed, axis=-1, keepdims=True)
    return inverse * (upstream - first_term - second_term)


def dot(left, right):
    return jnp.dot(left, right, preferred_element_type=F32)


def dot_nt(left, right):
    return lax.dot_general(left, right, (((1,), (1,)), ((), ())), preferred_element_type=F32)


def dot_tn(left, right):
    return lax.dot_general(left, right, (((0,), (0,)), ((), ())), preferred_element_type=F32)


def gelu_pair(values):
    size = jnp.abs(values)
    denominator = 1.0 + size * (0.3275911 * 0.7071067811865476)
    ratio = pl.reciprocal(denominator, approx=True)
    ratio = ratio * (2.0 - denominator * ratio)
    bell = jnp.exp(values * values * (-0.5))
    poly = 0.5 * 1.061405429 * ratio - 0.5 * 1.453152027
    poly = poly * ratio + 0.5 * 1.421413741
    poly = poly * ratio - 0.5 * 0.284496736
    poly = poly * ratio + 0.5 * 0.254829592
    tail = poly * ratio * bell
    below = jnp.where(values >= 0, 1.0 - tail, tail)
    return (values * below, below + values * bell * 0.3989422804014327)


def whole(array):
    rank = len(array.shape)
    return pl.BlockSpec(array.shape, lambda *_: (0,) * rank, pipeline_mode=pl.Buffered(1))


def params(limit):
    return pltpu.CompilerParams(vmem_limit_bytes=limit * MIB)


def cost(flops, nbytes):
    return pl.CostEstimate(flops=int(flops), bytes_accessed=int(nbytes), transcendentals=0)


def place(order_ref, target, pieces):
    for j, piece in enumerate(pieces):
        at = pl.multiple_of(order_ref[j] * BLOCK, BLOCK)
        target[pl.ds(at, BLOCK), :] = piece[...]


def heads_apart(values, scale=None):
    lane = lax.broadcasted_iota(jnp.int32, values.shape, 1) // HEAD_DIM
    if scale is not None:
        values = values * jnp.asarray(scale, values.dtype)
    zero = jnp.zeros_like(values)
    return jnp.concatenate([jnp.where(lane == h, values, zero) for h in range(GROUP)], axis=0)


def heads_together(values, slots):
    lane = lax.broadcasted_iota(jnp.int32, (slots, GROUP_W), 1) // HEAD_DIM
    out = values[:slots]
    for h in range(1, GROUP):
        out = jnp.where(lane == h, values[h * slots : (h + 1) * slots], out)
    return out


def probs_of(keys, queries_apart, shift):
    scores = dot_nt(keys, queries_apart) + shift
    scores = jnp.exp(scores - jnp.max(scores, axis=0, keepdims=True))
    return scores * (1.0 / jnp.sum(scores, axis=0, keepdims=True))


def key_shift(kept, slots):
    at = lax.broadcasted_iota(jnp.int32, (slots, 1), 0)
    return jnp.where(at < BUF + kept, 0.0, MASKED).astype(F32)


def attn_forward(order, kept, x, wqkv, wo, vec):
    images, slots, _ = x.shape
    rows = images * slots

    def body(order_ref, kept_ref, x_ref, *refs):
        wq_refs, wo_refs = refs[:BLOCKS], refs[BLOCKS : 2 * BLOCKS]
        vec_ref, h1_ref, qkv_ref, mixed_ref, middle_ref, h2_ref, wq_s, wo_s = refs[2 * BLOCKS :]
        image = pl.program_id(0)

        @pl.when(image == 0)
        def _():
            place(order_ref, wq_s, wq_refs)
            place(order_ref, wo_s, wo_refs)

        inputs = x_ref[0].astype(F32)
        normed, _ = normalize(inputs)
        hidden = (normed * vec_ref[0:1, :] + vec_ref[1:2, :]).astype(BF16)
        h1_ref[...] = hidden
        shift = key_shift(kept_ref[image], slots)
        for g in range(HEADS // GROUP):
            at = g * GROUP_W
            span = slice(at, at + GROUP_W)
            q = (dot(hidden, wq_s[:, span]) + vec_ref[2:3, span]).astype(BF16)
            k = dot(hidden, wq_s[:, D + at : D + at + GROUP_W]).astype(BF16)
            v = (
                dot(hidden, wq_s[:, 2 * D + at : 2 * D + at + GROUP_W]) + vec_ref[3:4, span]
            ).astype(BF16)
            qkv_ref[:, span] = q
            qkv_ref[:, D + at : D + at + GROUP_W] = k
            qkv_ref[:, 2 * D + at : 2 * D + at + GROUP_W] = v
            probs = probs_of(k, heads_apart(q, HEAD_DIM**-0.5), shift).astype(BF16)
            mixed_ref[:, span] = heads_together(dot_tn(probs, v), slots).astype(BF16)
        middle = inputs + dot(mixed_ref[...], wo_s[...]) + vec_ref[4:5, :]
        middle_ref[...] = middle
        normed, _ = normalize(middle)
        h2_ref[...] = (normed * vec_ref[5:6, :] + vec_ref[6:7, :]).astype(BF16)

    row = lambda width: pl.BlockSpec((slots, width), lambda i, *_: (i, 0))
    return pl.pallas_call(
        body,
        grid_spec=pltpu.PrefetchScalarGridSpec(
            num_scalar_prefetch=2,
            grid=(images,),
            in_specs=[pl.BlockSpec((1, slots, D), lambda i, *_: (i, 0, 0))]
            + [whole(w) for w in wqkv]
            + [whole(w) for w in wo]
            + [whole(vec)],
            out_specs=[row(D), row(3 * D), row(D), row(D), row(D)],
            scratch_shapes=[pltpu.VMEM((D, 3 * D), BF16), pltpu.VMEM((D, D), BF16)],
        ),
        out_shape=[
            jax.ShapeDtypeStruct((rows, D), BF16),
            jax.ShapeDtypeStruct((rows, 3 * D), BF16),
            jax.ShapeDtypeStruct((rows, D), BF16),
            jax.ShapeDtypeStruct((rows, D), F32),
            jax.ShapeDtypeStruct((rows, D), BF16),
        ],
        compiler_params=params(40),
        cost_estimate=cost(12 * rows * D * D, 30 * MIB),
        name="attn_forward",
    )(order, kept, x, *wqkv, *wo, vec)


def mlp_part(order, h2, h2t, dm, dmt, wup, wdn, bu, width=256):
    rows = h2.shape[0]
    steps = PART // width

    def body(order_ref, h2_ref, h2t_ref, dm_ref, dmt_ref, *refs):
        up_refs, dn_refs = refs[:BLOCKS], refs[BLOCKS : 2 * BLOCKS]
        bu_ref, act_ref, dpre_ref, ups, upk, dns, dnk, gbu_ref, up_s, dn_s = refs[2 * BLOCKS :]
        place(order_ref, up_s, up_refs)
        place(order_ref, dn_s, dn_refs)
        pre = dot(h2_ref[...], up_s[...]) + bu_ref[...]
        act, slope = gelu_pair(pre)
        act = act.astype(BF16)
        act_ref[...] = act
        dpre = (dot(dm_ref[...], dn_s[...]) * slope).astype(BF16)
        dpre_ref[...] = dpre
        gbu_ref[...] = jnp.sum(dpre.astype(F32), axis=0, keepdims=True)
        for left_ref, right, keep, send in ((dmt_ref, act, dnk, dns), (h2t_ref, dpre, upk, ups)):
            for j in range(BLOCKS):
                at = pl.multiple_of(order_ref[j] * BLOCK, BLOCK)
                grad = dot(left_ref[pl.ds(at, BLOCK), :rows], right).astype(BF16)
                (send if j % 2 else keep)[j // 2] = grad

    weight = pl.BlockSpec((BLOCK, width), lambda i, *_: (0, i))
    column = pl.BlockSpec((rows, width), lambda i, *_: (0, i))
    grads = pl.BlockSpec((2, BLOCK, width), lambda i, *_: (0, 0, i))
    one = pl.BlockSpec((1, width), lambda i, *_: (0, i))
    return pl.pallas_call(
        body,
        grid_spec=pltpu.PrefetchScalarGridSpec(
            num_scalar_prefetch=1,
            grid=(steps,),
            in_specs=[whole(a) for a in (h2, h2t, dm, dmt)] + [weight] * (2 * BLOCKS) + [one],
            out_specs=[column] * 2 + [grads] * 4 + [one],
            scratch_shapes=[pltpu.VMEM((D, width), BF16)] * 2,
        ),
        out_shape=[jax.ShapeDtypeStruct((rows, PART), BF16)] * 2
        + [jax.ShapeDtypeStruct((2, BLOCK, PART), BF16)] * 4
        + [jax.ShapeDtypeStruct((1, PART), F32)],
        compiler_params=params(30),
        cost_estimate=cost(8 * rows * D * PART, 12 * MIB),
        name="mlp_part",
    )(order, h2, h2t, dm, dmt, *wup, *wdn, bu)


def mlp_back(order, dpres, wups, middle, gy, vec):
    rows = middle.shape[0]

    def body(order_ref, *refs):
        dpre_refs, refs = refs[:PARTS], refs[PARTS:]
        up_refs, refs = refs[: PARTS * BLOCKS], refs[PARTS * BLOCKS :]
        middle_ref, gy_ref, vec_ref, dmid_ref, da_ref, sums_ref, acc = refs
        part = pl.program_id(0)
        for p in range(PARTS):

            @pl.when(part == p)
            def _():
                for j in range(BLOCKS):
                    at = pl.multiple_of(order_ref[j] * BLOCK, BLOCK)
                    term = dot_nt(dpre_refs[p][...], up_refs[p * BLOCKS + j][...])
                    if p == 0:
                        acc[:, pl.ds(at, BLOCK)] = term
                    else:
                        acc[:, pl.ds(at, BLOCK)] += term

        @pl.when(part == PARTS - 1)
        def _():
            gain, shift, bias = (jnp.zeros((1, D), F32) for _ in range(3))
            step = rows // 6
            for r in range(0, rows, step):
                span = slice(r, r + step)
                dh2 = acc[span, :]
                normed, inverse = normalize(middle_ref[span, :])
                gain += jnp.sum(dh2 * normed, axis=0, keepdims=True)
                shift += jnp.sum(dh2, axis=0, keepdims=True)
                dmid = norm_back(dh2 * vec_ref[5:6, :], normed, inverse) + gy_ref[span, :].astype(F32)
                dmid_ref[span, :] = dmid
                da = dmid.astype(BF16)
                da_ref[span, :] = da
                bias += jnp.sum(da.astype(F32), axis=0, keepdims=True)
            sums_ref[...] = jnp.concatenate([gain, shift, bias, jnp.zeros((5, D), F32)], axis=0)

    def once(array, p):
        return pl.BlockSpec(array.shape, lambda i, *_: (0, 0), pipeline_mode=pl.Buffered(1))

    flat = [w for part in wups for w in part]
    ins = [*dpres, *flat, middle, gy, vec]
    return pl.pallas_call(
        body,
        grid_spec=pltpu.PrefetchScalarGridSpec(
            num_scalar_prefetch=1,
            grid=(PARTS,),
            in_specs=[whole(a) for a in ins],
            out_specs=[
                pl.BlockSpec((rows, D), lambda i, *_: (0, 0)),
                pl.BlockSpec((rows, D), lambda i, *_: (0, 0)),
                pl.BlockSpec((8, D), lambda i, *_: (0, 0)),
            ],
            scratch_shapes=[pltpu.VMEM((rows, D), F32)],
        ),
        out_shape=[
            jax.ShapeDtypeStruct((rows, D), F32),
            jax.ShapeDtypeStruct((rows, D), BF16),
            jax.ShapeDtypeStruct((8, D), F32),
        ],
        compiler_params=params(50),
        cost_estimate=cost(2 * rows * D * FF, 30 * MIB),
        name="mlp_back",
    )(order, *ins)


def mlp_out(order, acts, wdns, middle, valid, vec):
    rows = middle.shape[0]

    def body(order_ref, *refs):
        act_refs, refs = refs[:PARTS], refs[PARTS:]
        dn_refs, refs = refs[: PARTS * BLOCKS], refs[PARTS * BLOCKS :]
        middle_ref, valid_ref, vec_ref, out_ref = refs
        for j in range(BLOCKS):

            @pl.when(pl.program_id(0) == j)
            def _():
                at = pl.multiple_of(order_ref[j] * BLOCK, BLOCK)
                total = middle_ref[:, pl.ds(at, BLOCK)] + vec_ref[7:8, pl.ds(at, BLOCK)]
                for p in range(PARTS):
                    total = total + dot_nt(act_refs[p][...], dn_refs[p * BLOCKS + j][...])
                out_ref[:, pl.ds(at, BLOCK)] = (total * valid_ref[...]).astype(BF16)

    flat = [w for part in wdns for w in part]
    ins = [*acts, *flat, middle, valid, vec]
    return pl.pallas_call(
        body,
        grid_spec=pltpu.PrefetchScalarGridSpec(
            num_scalar_prefetch=1,
            grid=(BLOCKS,),
            in_specs=[whole(a) for a in ins],
            out_specs=pl.BlockSpec((rows, D), lambda i, *_: (0, 0)),
        ),
        out_shape=jax.ShapeDtypeStruct((rows, D), BF16),
        compiler_params=params(50),
        cost_estimate=cost(2 * rows * D * FF, 24 * MIB),
        name="mlp_out",
    )(order, *ins)


def attn_back(order, kept, da, wo, qkv, slots):
    rows = da.shape[0]
    images = rows // slots

    def body(order_ref, kept_ref, da_ref, *refs):
        wo_refs, (qkv_ref, dqkv_ref, sums_ref, wo_s) = refs[:BLOCKS], refs[BLOCKS:]
        image = pl.program_id(0)

        @pl.when(image == 0)
        def _():
            place(order_ref, wo_s, wo_refs)
            sums_ref[...] = jnp.zeros_like(sums_ref)

        shift = key_shift(kept_ref[image], slots)
        da = da_ref[...]
        scale = HEAD_DIM**-0.5
        for g in range(HEADS // GROUP):
            at = g * GROUP_W
            spans = [slice(n * D + at, n * D + at + GROUP_W) for n in range(3)]
            q, k, v = (qkv_ref[:, span] for span in spans)
            dmix = dot_nt(da, wo_s[at : at + GROUP_W, :]).astype(BF16)
            apart = heads_apart(q, scale)
            probs = probs_of(k, apart, shift)
            dmix_apart = heads_apart(dmix)
            dv = dot(probs.astype(BF16), dmix_apart).astype(BF16)
            dprob = dot_nt(v, dmix_apart)
            product = probs * dprob
            dsc = (product - probs * jnp.sum(product, axis=0, keepdims=True)).astype(BF16)
            dk = dot(dsc, apart).astype(BF16)
            dq = (heads_together(dot_tn(dsc, k), slots) * scale).astype(BF16)
            for n, grad in enumerate((dq, dk, dv)):
                dqkv_ref[:, spans[n]] = grad
                if n != 1:
                    sums_ref[n : n + 1, at : at + GROUP_W] += jnp.sum(
                        grad.astype(F32), axis=0, keepdims=True
                    )

    row = lambda width: pl.BlockSpec((slots, width), lambda i, *_: (i, 0))
    return pl.pallas_call(
        body,
        grid_spec=pltpu.PrefetchScalarGridSpec(
            num_scalar_prefetch=2,
            grid=(images,),
            in_specs=[row(D)] + [whole(w) for w in wo] + [row(3 * D)],
            out_specs=[row(3 * D), pl.BlockSpec((8, D), lambda i, *_: (0, 0))],
            scratch_shapes=[pltpu.VMEM((D, D), BF16)],
        ),
        out_shape=[
            jax.ShapeDtypeStruct((rows, 3 * D), BF16),
            jax.ShapeDtypeStruct((8, D), F32),
        ],
        compiler_params=params(30),
        cost_estimate=cost(8 * rows * D * D, 18 * MIB),
        name="attn_back",
    )(order, kept, da, *wo, qkv)


def input_back(order, dqkv, wqkv, x, dmid, vec):
    images, slots, _ = x.shape
    rows = images * slots

    def body(order_ref, dqkv_ref, *refs):
        wq_refs = refs[:BLOCKS]
        x_ref, dmid_ref, vec_ref, out_ref, sums_ref, acc = refs[BLOCKS:]

        @pl.when(pl.program_id(0) == 0)
        def _():
            sums_ref[...] = jnp.zeros_like(sums_ref)

        grad = dqkv_ref[...]
        for j in range(BLOCKS):
            at = pl.multiple_of(order_ref[j] * BLOCK, BLOCK)
            acc[:, pl.ds(at, BLOCK)] = dot_nt(grad, wq_refs[j][...])
        dh1 = acc[...]
        normed, inverse = normalize(x_ref[0].astype(F32))
        sums_ref[0:1, :] += jnp.sum(dh1 * normed, axis=0, keepdims=True)
        sums_ref[1:2, :] += jnp.sum(dh1, axis=0, keepdims=True)
        total = norm_back(dh1 * vec_ref[0:1, :], normed, inverse) + dmid_ref[...]
        out_ref[0] = total.astype(BF16)

    row = lambda width: pl.BlockSpec((slots, width), lambda i, *_: (i, 0))
    image = pl.BlockSpec((1, slots, D), lambda i, *_: (i, 0, 0))
    return pl.pallas_call(
        body,
        grid_spec=pltpu.PrefetchScalarGridSpec(
            num_scalar_prefetch=1,
            grid=(images,),
            in_specs=[row(3 * D)] + [whole(w) for w in wqkv] + [image, row(D), whole(vec)],
            out_specs=[image, pl.BlockSpec((8, D), lambda i, *_: (0, 0))],
            scratch_shapes=[pltpu.VMEM((slots, D), F32)],
        ),
        out_shape=[
            jax.ShapeDtypeStruct((images, slots, D), BF16),
            jax.ShapeDtypeStruct((8, D), F32),
        ],
        compiler_params=params(30),
        cost_estimate=cost(6 * rows * D * D, 24 * MIB),
        name="input_back",
    )(order, dqkv, *wqkv, x, dmid, vec)


def weight_grad(order, left_t, right, width=512):
    rows, columns = right.shape

    def body(order_ref, left_ref, right_ref, send, keep):
        for j in range(BLOCKS):
            at = pl.multiple_of(order_ref[j] * BLOCK, BLOCK)
            grad = dot(left_ref[pl.ds(at, BLOCK), :rows], right_ref[...]).astype(BF16)
            (send if j % 2 else keep)[j // 2] = grad

    grads = pl.BlockSpec((2, BLOCK, width), lambda i, *_: (0, 0, i))
    return pl.pallas_call(
        body,
        grid_spec=pltpu.PrefetchScalarGridSpec(
            num_scalar_prefetch=1,
            grid=(columns // width,),
            in_specs=[whole(left_t), pl.BlockSpec((rows, width), lambda i, *_: (0, i))],
            out_specs=[grads] * 2,
        ),
        out_shape=[jax.ShapeDtypeStruct((2, BLOCK, columns), BF16)] * 2,
        compiler_params=params(30),
        cost_estimate=cost(2 * rows * D * columns, 12 * MIB),
        name="weight_grad",
    )(order, left_t, right)


def transposed(values):
    rows = values.shape[0]
    return jnp.pad(values.T, ((0, 0), (0, -rows % 256)))


def swap(values, axis, bit):
    size = lax.axis_size(axis)
    return lax.ppermute(values, axis, [(i, i ^ bit) for i in range(size)])


def my_bit(axis, bit):
    return (lax.axis_index(axis) & bit) != 0


def bits_of(size):
    return [1 << n for n in range(size.bit_length() - 1)]


class Distances:
    def __init__(self):
        self.shards = lax.axis_size("shard")
        self.replicas = lax.axis_size("replica")
        self.direct = self.shards == BLOCKS and self.replicas & (self.replicas - 1) == 0
        index = jnp.arange(BLOCKS, dtype=jnp.int32)
        self.order = index ^ lax.axis_index("shard") if self.direct else index

    def gather(self, own):
        if not self.direct:
            full = lax.all_gather(own, "shard", axis=0, tiled=True)
            return [full[j * BLOCK : (j + 1) * BLOCK] for j in range(BLOCKS)]
        far = swap(own, "shard", 2)
        return [own, swap(own, "shard", 1), far, swap(far, "shard", 1)]

    def reduce(self, send, keep, stages):
        if not self.direct:
            full = jnp.stack([keep[0], send[0], keep[1], send[1]]).reshape(D, -1)
            part = lax.psum_scatter(full, "shard", scatter_dimension=0, tiled=True)
            return lax.psum(part, "replica")
        now = keep.astype(F32) + swap(send, "shard", 1).astype(F32)
        now = now.astype(BF16)
        taken = []
        for axis, bit in stages:
            if axis == "shard":
                now = (now[:1].astype(F32) + swap(now[1:], axis, bit).astype(F32)).astype(BF16)
                continue
            half = now.shape[1] // 2
            up = my_bit(axis, bit).astype(jnp.int32)
            mine = lax.dynamic_slice_in_dim(now, up * half, half, 1)
            other = lax.dynamic_slice_in_dim(now, (1 - up) * half, half, 1)
            now = (mine.astype(F32) + swap(other, axis, bit).astype(F32)).astype(BF16)
            taken.append((axis, bit))
        now = now[0]
        for axis, bit in reversed(taken):
            other = swap(now, axis, bit)
            now = jnp.where(
                my_bit(axis, bit),
                jnp.concatenate([other, now], axis=0),
                jnp.concatenate([now, other], axis=0),
            )
        return now

    def total(self, values):
        if not self.direct:
            return lax.psum(values, ("replica", "shard"))
        for axis, size in (("shard", self.shards), ("replica", self.replicas)):
            for bit in bits_of(size):
                values = values + swap(values, axis, bit)
        return values

    def stages(self, first):
        far = [("shard", 2)]
        rest = [("replica", bit) for bit in bits_of(self.replicas)]
        return far + rest if first == "shard" else rest + far


def adam_update(weight, first_mom, second_mom, gradient, rate, decay):
    first_new = BETA_ONE * first_mom + (1.0 - BETA_ONE) * gradient
    second_new = BETA_TWO * second_mom + (1.0 - BETA_TWO) * gradient * gradient
    first_hat = first_new / (1.0 - BETA_ONE**STEP)
    second_hat = second_new / (1.0 - BETA_TWO**STEP)
    weight_new = weight - rate * (first_hat / (jnp.sqrt(second_hat) + EPS_ADAM) + decay * weight)
    return (gradient, first_new, second_new, weight_new, weight_new.astype(BF16))


def on_device(
    tokens,
    out_grad,
    kept_count,
    attn_w,
    mlp_w,
    vectors,
    attn_m,
    mlp_m,
    small_m,
    attn_v,
    mlp_v,
    small_v,
):
    images, slots, _ = tokens.shape
    rows = images * slots
    links = Distances()
    order = links.order
    owned = vectors.shape[0]

    small_low = jnp.pad(vectors.astype(BF16).T, ((0, 4), (0, 0)))
    if links.direct:
        pieces = links.gather(small_low)
        stacked = jnp.stack(pieces)[order]
        small_full = stacked.transpose(1, 0, 2).reshape(16, D)
    else:
        small_full = lax.all_gather(small_low, "shard", axis=1, tiled=True)
    vec = small_full.astype(F32)
    wqkv = links.gather(attn_w[:, : 3 * D].astype(BF16))
    wo = links.gather(attn_w[:, 3 * D :].astype(BF16))
    wups, wdns = [], []
    for p in range(PARTS):
        span = slice(p * PART, (p + 1) * PART)
        wups.append(links.gather(mlp_w[:, :FF][:, span].astype(BF16)))
        wdns.append(links.gather(mlp_w[:, FF:][:, span].astype(BF16)))

    h1, qkv, mixed, middle, h2 = attn_forward(order, kept_count, tokens, wqkv, wo, vec)

    at = jnp.arange(slots, dtype=jnp.int32)
    valid = (at[None, :] < (BUF + kept_count)[:, None]).reshape(rows, 1)
    gy = jnp.where(valid, out_grad.reshape(rows, D), jnp.zeros((), BF16))
    gyt = transposed(gy)
    h2t = transposed(h2)
    acts, dpres, ups, dns, gbus = [], [], [], [], []
    for p in range(PARTS):
        act, dpre, up_send, up_keep, dn_send, dn_keep, gbu = mlp_part(
            order, h2, h2t, gy, gyt, wups[p], wdns[p], vec[8 + p : 9 + p]
        )
        acts.append(act)
        dpres.append(dpre)
        dns.append(links.reduce(dn_send, dn_keep, links.stages("shard")))
        ups.append(links.reduce(up_send, up_keep, links.stages("replica")))
        gbus.append(gbu)
    dmid, da, two_sums = mlp_back(order, dpres, wups, middle, gy, vec)

    out_send, out_keep = weight_grad(order, transposed(mixed), da)
    g_out = links.reduce(out_send, out_keep, links.stages("replica"))
    dqkv, qkv_sums = attn_back(order, kept_count, da, wo, qkv, slots)
    qkv_send, qkv_keep = weight_grad(order, transposed(h1), dqkv)
    g_qkv = links.reduce(qkv_send, qkv_keep, links.stages("shard"))
    in_grad, one_sums = input_back(order, dqkv, wqkv, tokens, dmid, vec)
    result = mlp_out(order, acts, wdns, middle, valid.astype(F32), vec)
    result = result.reshape(images, slots, D)

    g_down = jnp.sum(gy, axis=0, dtype=F32, keepdims=True)
    small = jnp.concatenate(
        [
            one_sums[0:2],
            qkv_sums[0:1],
            qkv_sums[2:3],
            two_sums[2:3],
            two_sums[0:2],
            g_down,
            *gbus,
            jnp.zeros((4, D), F32),
        ],
        axis=0,
    )
    small = links.total(small)
    small = lax.dynamic_slice_in_dim(small, lax.axis_index("shard") * owned, owned, 1)[:12].T

    image_total = images * links.replicas * links.shards
    attn_sum = jnp.concatenate([g_qkv, g_out], axis=1).astype(F32)
    mlp_sum = jnp.concatenate([*ups, *dns], axis=1).astype(F32)
    attn_out = adam_update(attn_w, attn_m, attn_v, attn_sum / image_total, 0.1, 0.05)
    mlp_out_ = adam_update(mlp_w, mlp_m, mlp_v, mlp_sum / image_total, 0.05, 0.05)
    small_out = adam_update(vectors, small_m, small_v, small / image_total, 1.0, 0.0)
    return (result, in_grad, *attn_out, *mlp_out_, *small_out)


def solution(mesh):
    tokens = P(("replica", "shard"), None, None)
    owned = P("shard", None)
    in_specs = (tokens, tokens, P(("replica", "shard")), *[owned] * 9)
    out_specs = (tokens, tokens, *[owned] * 15)
    return jax.shard_map(
        on_device, mesh=mesh, in_specs=in_specs, out_specs=out_specs, check_vma=False
    )
```

time: 882 us -> 655 us (0.74)
  matrix products: 227 us -> 0 us
  Pallas kernels: 0 us -> 188 us
  waiting for transfers between devices: 390 us -> 221 us
  starting transfers between devices: 0.25 us -> 99.8 us
  other arithmetic: 103 us -> 58.5 us
  blocking collectives: 28.5 us -> 0 us
  local copies, waits for them, and re-layouts: 109 us -> 80.9 us
  between operations: 15.2 us -> 2.95 us
    dot_general x18 -> x0, matrix products: 227 us -> none  [the longest x1 48.8 us: on_device(): jnp.dot(hidden_two, mlp_full[:, :FF], preferred_element_type=jnp.float32)]
    ppermute x0 -> x118, waiting for transfers between devices: none -> 221 us  [swap(): return lax.ppermute(values, axis, [(i, i ^ bit) for i in range(size)])]
    psum x1 -> x0, waiting for transfers between devices: 195 us -> none  [on_device(): lax.psum(attn_part.astype(jnp.bfloat16), 'replica').astype(jnp.float32)]
    pallas_call x0 -> x11, Pallas kernels: none -> 188 us  [the longest x4 62.9 us: mlp_part(): pl.pallas_call(body, grid_spec=pltpu.PrefetchScalarGridSpec(num_scalar_pr...]
    reduce_scatter x3 -> x0, waiting for transfers between devices: 154 us -> none  [the longest x1 129 us: on_device(): lax.psum_scatter(mlp_grad.astype(jnp.bfloat16), 'shard', scatter_dimensio...]
    ppermute x0 -> x118, starting transfers between devices: none -> 99.8 us  [swap(): return lax.ppermute(values, axis, [(i, i ^ bit) for i in range(size)])]
    all_gather x2 -> x0, waiting for transfers between devices: 41.3 us -> none  [the longest x1 40.6 us: on_device(): lax.all_gather(attn_w.astype(jnp.bfloat16), 'shard', axis=0, tiled=True)]
    convert_element_type x4 -> x2, local copies, waits for them, and re-layouts: 40.4 us -> 0.36 us  [the longest x1 0.35 us: on_device(): result = mlp_out(order, acts, wdns, middle, valid.astype(F32), vec)]
  transfers between devices with their start and end apart: 6 -> 118, of which waited for: 6 -> 41; matrix products, arithmetic and copies ran while one was open for 21% -> 11% of each run, Pallas kernels for 0% -> 16%
where the time goes in v1:
time: 655 us; the launch traced here: 652 us
  waiting for transfers between devices  221 us (34%)
  Pallas kernels  188 us (29%)
  starting transfers between devices  99.8 us (15%)
  local copies, waits for them, and re-layouts  80.9 us (12%)
  other arithmetic  58.5 us (9%)
    ppermute x118, waiting for transfers between devices, swap(): return lax.ppermute(values, axis, [(i, i ^ bit) for i in range(size)])  221 us
    ppermute x118, starting transfers between devices, swap(): return lax.ppermute(values, axis, [(i, i ^ bit) for i in range(size)])  99.8 us
    pallas_call x4, Pallas kernels, mlp_part(): pl.pallas_call(body, grid_spec=pltpu.PrefetchScalarGridSpec(num_scalar_pr...  62.9 us
    unnamed x199, local copies, waits for them, and re-layouts  53.6 us
    convert_element_type x3, other arithmetic, adam_update(): weight_new.astype(BF16)  30.2 us
    pallas_call x1, Pallas kernels, attn_forward(): pl.pallas_call(body, grid_spec=pltpu.PrefetchScalarGridSpec(num_scalar_pr...  28.6 us
    pallas_call x1, Pallas kernels, attn_back(): pl.pallas_call(body, grid_spec=pltpu.PrefetchScalarGridSpec(num_scalar_pr...  24.5 us
    pallas_call x1, Pallas kernels, mlp_back(): pl.pallas_call(body, grid_spec=pltpu.PrefetchScalarGridSpec(num_scalar_pr...  23 us
  transfers between devices with their start and end apart: 118, of which 41 were waited for; matrix products, arithmetic and copies ran while one was open for 11% of the time, Pallas kernels for 16%

profile of v1, /device:TPU:0, one launch (start us, length us, event | category | flops | bytes accessed | tf_op | source)
XLA Modules:
  0.0 651.7 jit_solution(7265622699235498791)
XLA Ops:
  0.7 2.6 convert.16
  3.4 3.0 collective-permute-start.1
  10.1 2.0 fusion.35
  12.7 29.1 %collective-permute-done.1.refs_2_ = bf16[256,3072]{1,0:T(8,128)(2,1)} collective-permute-done((bf16[256,3072]{1,0:T(8,128)(2,1)S(1)}, bf16[256,3072]{1,0:T(8,128)(2,1)}, u32[]{:S(2)}, u32[]{:S(2)}) %collective-permute-start.1) | collective-permute-done | bytes 1572896 | tf_op jit(solution)/shard_map/ppermute | solution.py:458
  45.6 2.1 collective-permute-start.31
  47.6 5.6 collective-permute-done.4.refs_6_.refs_2_
  53.2 2.1 collective-permute-start.28
  55.8 2.7 copy.46
  58.5 3.3 pad.19.clone.dmt_ref
  64.5 2.1 collective-permute-start.25
  66.5 9.2 %collective-permute-done.28.refs_2_.refs_18_ = bf16[256,1024]{1,0:T(8,128)(2,1)} collective-permute-done((bf16[256,1024]{1,0:T(8,128)(2,1)}, bf16[256,1024]{1,0:T(8,128)(2,1)}, u32[]{:S(2)}, u32[]{:S(2)}) %collective-permute-start.28) | collective-permute-done | bytes 524320 | tf_op jit(solution)/shard_map/ppermute | solution.py:458
  77.0 2.0 gather_fusion
  81.0 5.1 collective-permute-done.25.refs_6_.refs_14_
  89.1 28.6 %attn_forward.1 = (bf16[960,1024]{1,0:T(8,128)(2,1)S(1)}, bf16[960,3072]{1,0:T(8,128)(2,1)}, bf16[960,1024]{1,0:T(8,128)(2,1)S(1)}, f32[960,1024]{1,0:T(8,128)}, bf16[960,1024]{1,0:T(8,128)(2,1)S(1)}) custom-call(s32[4]{0:T(128)S(1)} %copy-done.66, s32[6]{0:T(128)S(1)} %copy-done.64, bf16[6,160,1024]{2,1,0:T(8,128)(2,1)} %refs_4_.1, ...), custom_call_target="tpu_custom_call" | custom-call | flops 12079595520 | bytes 31457280 | tf_op jit(solution)/shard_map/attn_forward/pallas_call | solution.py:156
  121.5 3.9 copy.38
  125.4 2.0 pad.18.h2t_ref
  131.3 16.0 %mlp_part.7 = (bf16[960,1024]{1,0:T(8,128)(2,1)S(1)}, bf16[960,1024]{1,0:T(8,128)(2,1)S(1)}, bf16[2,256,1024]{2,1,0:T(8,128)(2,1)S(1)}, bf16[2,256,1024]{2,1,0:T...) custom-call(s32[4]{0:T(128)S(1)} %copy-done.67, ...), custom_call_target="tpu_custom_call" | custom-call | flops 8053063680 | bytes 12582912 | tf_op jit(solution)/shard_map/mlp_part/pallas_call | solution.py:207
  156.6 16.2 %mlp_part.6 = (bf16[960,1024]{1,0:T(8,128)(2,1)S(1)}, bf16[960,1024]{1,0:T(8,128)(2,1)S(1)}, bf16[2,256,1024]{2,1,0:T(8,128)(2,1)S(1)}, bf16[2,256,1024]{2,1,0:T...) custom-call(s32[4]{0:T(128)S(1)} %copy-done.67, ...), custom_call_target="tpu_custom_call" | custom-call | flops 8053063680 | bytes 12582912 | tf_op jit(solution)/shard_map/mlp_part/pallas_call | solution.py:207
  180.3 15.3 %mlp_part.5 = (bf16[960,1024]{1,0:T(8,128)(2,1)S(1)}, bf16[960,1024]{1,0:T(8,128)(2,1)S(1)}, bf16[2,256,1024]{2,1,0:T(8,128)(2,1)S(1)}, bf16[2,256,1024]{2,1,0:T...) custom-call(s32[4]{0:T(128)S(1)} %copy-done.67, ...), custom_call_target="tpu_custom_call" | custom-call | flops 8053063680 | bytes 12582912 | tf_op jit(solution)/shard_map/mlp_part/pallas_call | solution.py:207
  202.3 15.3 %mlp_part.4 = (bf16[960,1024]{1,0:T(8,128)(2,1)S(1)}, bf16[960,1024]{1,0:T(8,128)(2,1)S(1)}, bf16[2,256,1024]{2,1,0:T(8,128)(2,1)S(1)}, bf16[2,256,1024]{2,1,0:T...) custom-call(s32[4]{0:T(128)S(1)} %copy-done.67, ...), custom_call_target="tpu_custom_call" | custom-call | flops 8053063680 | bytes 12582912 | tf_op jit(solution)/shard_map/mlp_part/pallas_call | solution.py:207
  224.1 23.0 %mlp_back.1 = (f32[960,1024]{1,0:T(8,128)}, bf16[960,1024]{1,0:T(8,128)(2,1)}, f32[8,1024]{1,0:T(8,128)S(1)}) custom-call(s32[4]{0:T(128)S(1)} %copy-done.67, bf16[960,1024]{1,0:T(8,128)(2,1)} %copy-done.82, bf16[960,1024]{1,0:T(8,128)(2,1)} %copy-done.81, bf16[960,1024]{1,0:T(8,128)(2,1)} %copy-done.80, bf16[960,1024]{1,0:T(8,128)(2,1)} %copy-done.79, ...), custom_call_target="tpu_custom_call" | custom-call | flops 8053063680 | bytes 31457280 | tf_op jit(solution)/shard_map/mlp_back/pallas_call | solution.py:267
  248.7 2.7 copy-done.83
  251.3 24.5 %attn_back.1 = (bf16[960,3072]{1,0:T(8,128)(2,1)S(1)}, f32[8,1024]{1,0:T(8,128)S(1)}) custom-call(s32[4]{0:T(128)S(1)} %copy-done.67, s32[6]{0:T(128)S(1)} %copy-done.65, bf16[960,1024]{1,0:T(8,128)(2,1)S(1)} %copy-done.73, bf16[256,1024]{1,0:T(8,128)(2,1)} %slice.205.refs_4_.refs_0_, bf16[256,1024]{1,0:T(8,128)(2,1)} %collective-permute-done.3.refs_5_.refs_1_, ...), custom_call_target="tpu_custom_call" | custom-call | flops 8053063680 | bytes 18874368 | tf_op jit(solution)/shard_map/attn_back/pallas_call | solution.py:363
  275.8 2.6 copy-done.69
  278.4 2.7 copy-done.70
  281.1 19.4 %input_back.1 = (bf16[6,160,1024]{2,1,0:T(8,128)(2,1)}, f32[8,1024]{1,0:T(8,128)S(1)}) custom-call(s32[4]{0:T(128)S(1)} %copy-done.67, bf16[960,3072]{1,0:T(8,128)(2,1)S(1)} %copy-done.70, bf16[256,3072]{1,0:T(8,128)(2,1)S(1)} %slice.204.refs_0_, bf16[256,3072]{1,0:T(8,128)(2,1)} %collective-permute-done.refs_1_, ...), custom_call_target="tpu_custom_call" | custom-call | flops 6039797760 | bytes 25165824 | tf_op jit(solution)/shard_map/input_back/pallas_call | solution.py:407
  303.4 2.9 collective-permute-done.114
  313.4 17.2 %mlp_out.1 = bf16[960,1024]{1,0:T(8,128)(2,1)} custom-call(s32[4]{0:T(128)S(1)} %copy-done.68, bf16[960,1024]{1,0:T(8,128)(2,1)} %copy-done.78, bf16[960,1024]{1,0:T(8,128)(2,1)} %copy-done.77, bf16[960,1024]{1,0:T(8,128)(2,1)} %copy-done.76, bf16[960,1024]{1,0:T(8,128)(2,1)} %copy-done.75, bf16[256,1024]{1,0:T(8,128)(2,1)S(1)} %copy-done.27, ...), custom_call_target="tpu_custom_call" | custom-call | flops 8053063680 | bytes 25165824 | tf_op jit(solution)/shard_map/mlp_out/pallas_call | solution.py:310
  330.6 2.5 copy.44
  337.5 2.7 copy-done.71
  340.2 8.9 %weight_grad.2 = (bf16[2,256,3072]{2,1,0:T(8,128)(2,1)S(1)}, bf16[2,256,3072]{2,1,0:T(8,128)(2,1)S(1)}) custom-call(s32[4]{0:T(128)S(1)} %copy-done.68, bf16[1024,1024]{1,0:T(8,128)(2,1)S(1)} %pad.20.left_ref, bf16[960,3072]{1,0:T(8,128)(2,1)S(1)} %copy-done.71), custom_call_target="tpu_custom_call" | custom-call | flops 6039797760 | bytes 12582912 | tf_op jit(solution)/shard_map/weight_grad/pallas_call | solution.py:436
  350.8 3.9 copy.45
  354.7 2.0 pad.21.left_ref
  356.9 2.7 collective-permute-start.117
  359.5 3.8 weight_grad.3
  378.7 8.6 %collective-permute-done.74 = bf16[2,128,1024]{2,1,0:T(8,128)(2,1)S(1)} collective-permute-done((bf16[2,128,1024]{2,1,0:T(8,128)(2,1)S(1)}, bf16[2,128,1024]{2,1,0:T(8,128)(2,1)S(1)}, u32[]{:S(2)}, u32[]{:S(2)}) %collective-permute-start.74) | collective-permute-done | bytes 524320 | tf_op jit(solution)/shard_map/ppermute | solution.py:458
  388.1 10.5 %collective-permute-done.66 = bf16[2,128,1024]{2,1,0:T(8,128)(2,1)S(1)} collective-permute-done((bf16[2,128,1024]{2,1,0:T(8,128)(2,1)S(1)}, bf16[2,128,1024]{2,1,0:T(8,128)(2,1)S(1)}, u32[]{:S(2)}, u32[]{:S(2)}) %collective-permute-start.66) | collective-permute-done | bytes 524320 | tf_op jit(solution)/shard_map/ppermute | solution.py:458
  399.3 9.6 %collective-permute-done.58 = bf16[2,128,1024]{2,1,0:T(8,128)(2,1)S(1)} collective-permute-done((bf16[2,128,1024]{2,1,0:T(8,128)(2,1)S(1)}, bf16[2,128,1024]{2,1,0:T(8,128)(2,1)S(1)}, u32[]{:S(2)}, u32[]{:S(2)}) %collective-permute-start.58) | collective-permute-done | bytes 524320 | tf_op jit(solution)/shard_map/ppermute | solution.py:458
  413.0 10.8 %collective-permute-done.42 = bf16[2,128,1024]{2,1,0:T(8,128)(2,1)S(1)} collective-permute-done((bf16[2,128,1024]{2,1,0:T(8,128)(2,1)S(1)}, bf16[2,128,1024]{2,1,0:T(8,128)(2,1)S(1)}, u32[]{:S(2)}, u32[]{:S(2)}) %collective-permute-start.42) | collective-permute-done | bytes 524320 | tf_op jit(solution)/shard_map/ppermute | solution.py:458
  424.5 10.5 %collective-permute-done.50 = bf16[2,128,1024]{2,1,0:T(8,128)(2,1)S(1)} collective-permute-done((bf16[2,128,1024]{2,1,0:T(8,128)(2,1)S(1)}, bf16[2,128,1024]{2,1,0:T(8,128)(2,1)S(1)}, u32[]{:S(2)}, u32[]{:S(2)}) %collective-permute-start.50) | collective-permute-done | bytes 524320 | tf_op jit(solution)/shard_map/ppermute | solution.py:458
  436.5 4.1 collective-permute-done.107
  443.6 2.7 collective-permute-done.99
  446.7 3.2 collective-permute-done.59
  453.3 4.2 collective-permute-done.43
  457.6 9.1 %collective-permute-done.51 = bf16[2,64,1024]{2,1,0:T(8,128)(2,1)S(1)} collective-permute-done((bf16[2,64,1024]{2,1,0:T(8,128)(2,1)S(1)}, bf16[2,64,1024]{2,1,0:T(8,128)(2,1)S(1)}, u32[]{:S(2)}, u32[]{:S(2)}) %collective-permute-start.51) | collective-permute-done | bytes 262176 | tf_op jit(solution)/shard_map/ppermute | solution.py:458
  466.8 3.2 collective-permute-start.100
  472.2 7.4 %collective-permute-done.68 = bf16[2,32,1024]{2,1,0:T(8,128)(2,1)S(1)} collective-permute-done((bf16[2,32,1024]{2,1,0:T(8,128)(2,1)S(1)}, bf16[2,32,1024]{2,1,0:T(8,128)(2,1)S(1)}, u32[]{:S(2)}, u32[]{:S(2)}) %collective-permute-start.68) | collective-permute-done | bytes 131104 | tf_op jit(solution)/shard_map/ppermute | solution.py:458
  479.6 3.0 collective-permute-start.52
  483.5 5.5 collective-permute-done.44
  496.3 2.1 collective-permute-done.61
  499.4 4.1 collective-permute-done.45
  504.4 4.1 collective-permute-done.53
  528.9 4.6 collective-permute-done.34
  546.8 9.1 %collective-permute-done.35 = bf16[1,128,3072]{2,1,0:T(8,128)(2,1)S(1)} collective-permute-done((bf16[1,128,3072]{2,1,0:T(8,128)(2,1)S(1)}, bf16[1,128,3072]{2,1,0:T(8,128)(2,1)S(1)}, u32[]{:S(2)}, u32[]{:S(2)}) %collective-permute-start.35) | collective-permute-done | bytes 786464 | tf_op jit(solution)/shard_map/ppermute | solution.py:458
  561.5 4.6 collective-permute-done.36
  567.3 16.8 %collective-permute-done.56 = bf16[128,1024]{1,0:T(8,128)(2,1)S(1)} collective-permute-done((bf16[128,1024]{1,0:T(8,128)(2,1)S(1)}, bf16[128,1024]{1,0:T(8,128)(2,1)S(1)}, u32[]{:S(2)}, u32[]{:S(2)}) %collective-permute-start.56) | collective-permute-done | bytes 262176 | tf_op jit(solution)/shard_map/ppermute | solution.py:458
  585.0 7.7 %collective-permute-done.37 = bf16[1,32,3072]{2,1,0:T(8,128)(2,1)S(1)} collective-permute-done((bf16[1,32,3072]{2,1,0:T(8,128)(2,1)S(1)}, bf16[1,32,3072]{2,1,0:T(8,128)(2,1)S(1)}, u32[]{:S(2)}, u32[]{:S(2)}) %collective-permute-start.37) | collective-permute-done | bytes 196640 | tf_op jit(solution)/shard_map/ppermute | solution.py:458
  595.3 5.9 collective-permute-done.38
  601.2 2.0 collective-permute-start.88
  603.3 7.7 %collective-permute-done.88 = bf16[128,1024]{1,0:T(8,128)(2,1)S(1)} collective-permute-done((bf16[128,1024]{1,0:T(8,128)(2,1)S(1)}, bf16[128,1024]{1,0:T(8,128)(2,1)S(1)}, u32[]{:S(2)}, u32[]{:S(2)}) %collective-permute-start.88) | collective-permute-done | bytes 262176 | tf_op jit(solution)/shard_map/ppermute | solution.py:458
  613.2 5.5 collective-permute-done.39
  619.3 17.6 %fusion.29 = (bf16[256,8192]{1,0:T(8,128)(2,1)}, f32[256,8192]{1,0:T(8,128)}, f32[256,8192]{1,0:T(8,128)}, f32[256,8192]{1,0:T(8,128)}, f32[256,8192]{1,0:T(8,128)}) fusion(f32[256,8192]{1,0:T(8,128)S(1)} %bitcast.67, bf16[256,8192]{1,0:T(8,128)(2,1)S(1)} %fusion.13, f32[256,8192]{1,0:T(8,128)S(1)} %bitcast.72, f32[256,8192]{1,0:T(8,128)} %param.19), kind=kLoop, calls=%fused_computation.165 | loop fusion | flops 37748736 | bytes 67108864 | tf_op jit(solution)/shard_map/convert_element_type | solution.py:532
  637.1 2.0 maximum_select_fusion
  639.6 11.9 %fusion.32 = (bf16[256,4096]{1,0:T(8,128)(2,1)}, f32[256,4096]{1,0:T(8,128)}, f32[256,4096]{1,0:T(8,128)}, f32[256,4096]{1,0:T(8,128)}, f32[256,4096]{1,0:T(8,128)}) fusion(f32[256,4096]{1,0:T(8,128)S(1)} %copy-done.85, bf16[256,1024]{1,0:T(8,128)(2,1)S(1)} %maximum_select_fusion.2, bf16[256,3072]{1,0:T(8,128)(2,1)S(1)} %maximum_select_fusion, ...), kind=kLoop, calls=%fused_computation.166 | loop fusion | flops 22020096 | bytes 33554432 | tf_op jit(solution)/shard_map/convert_element_type | solution.py:532
  (545 shorter events, 161.5 us)
Async XLA Ops:
  3.4 38.4 %collective-permute-start.1 = (bf16[256,3072]{1,0:T(8,128)(2,1)S(1)}, bf16[256,3072]{1,0:T(8,128)(2,1)}, u32[]{:S(2)}, u32[]{:S(2)}) collective-permute-start(bf16[256,3072]{1,0:T(8,128)(2,1)S(1)} %slice.204.refs_0_), channel_id=1, source_target_pairs={{0,2},{1,3},{2,0},{3,1},{4,6},{5,7},{6,4},{7,5},{8,10},{9,11},{10,... | collective-permute-start | bytes 4718600 | tf_op jit(solution)/shard_map/ppermute | solution.py:458
  6.6 36.6 %collective-permute-start.7 = (bf16[16,256]{1,0:T(8,128)(2,1)S(1)}, bf16[16,256]{1,0:T(8,128)(2,1)}, u32[]{:S(2)}, u32[]{:S(2)}) collective-permute-start(bf16[16,256]{1,0:T(8,128)(2,1)S(1)} %get-tuple-element.137), channel_id=1, source_target_pairs={{0,2},{1,3},{2,0},{3,1},{4,6},{5,7},{6,4},{7,5},{8,10},{9,11},{10,... | collective-permute-start | bytes 24584 | tf_op jit(solution)/shard_map/ppermute | solution.py:458
  7.5 45.7 %collective-permute-start.4 = (bf16[256,1024]{1,0:T(8,128)(2,1)}, bf16[256,1024]{1,0:T(8,128)(2,1)}, u32[]{:S(2)}, u32[]{:S(2)}) collective-permute-start(bf16[256,1024]{1,0:T(8,128)(2,1)} %slice.205.refs_4_.refs_0_), channel_id=1, source_target_pairs={{0,2},{1,3},{2,0},{3,1},{4,6},{5,7},{6,4},{7,5},{8,10},{9,11},{10,... | collective-permute-start | bytes 1572872 | tf_op jit(solution)/shard_map/ppermute | solution.py:458
  9.5 43.7 %collective-permute-start.3 = (bf16[256,1024]{1,0:T(8,128)(2,1)}, bf16[256,1024]{1,0:T(8,128)(2,1)}, u32[]{:S(2)}, u32[]{:S(2)}) collective-permute-start(bf16[256,1024]{1,0:T(8,128)(2,1)} %slice.205.refs_4_.refs_0_), channel_id=1, source_target_pairs={{0,1},{1,0},{2,3},{3,2},{4,5},{5,4},{6,7},{7,6},{8,9},{9,8},{10,11... | collective-permute-start | bytes 1572872 | tf_op jit(solution)/shard_map/ppermute | solution.py:458
  12.2 75.7 %collective-permute-start = (bf16[256,3072]{1,0:T(8,128)(2,1)S(1)}, bf16[256,3072]{1,0:T(8,128)(2,1)}, u32[]{:S(2)}, u32[]{:S(2)}) collective-permute-start(bf16[256,3072]{1,0:T(8,128)(2,1)S(1)} %slice.204.refs_0_), channel_id=1, source_target_pairs={{0,1},{1,0},{2,3},{3,2},{4,5},{5,4},{6,7},{7,6},{8,9},{9,8},{10,11... | collective-permute-start | bytes 4718600 | tf_op jit(solution)/shard_map/ppermute | solution.py:458
  41.8 46.5 %collective-permute-start.2 = (bf16[256,3072]{1,0:T(8,128)(2,1)}, bf16[256,3072]{1,0:T(8,128)(2,1)}, u32[]{:S(2)}, u32[]{:S(2)}) collective-permute-start(bf16[256,3072]{1,0:T(8,128)(2,1)} %collective-permute-done.1.refs_2_), channel_id=1, source_target_pairs={{0,1},{1,0},{2,3},{3,2},{4,5},{5,4},{6,7},{7,6},{8,9},{9,8},{10,11... | collective-permute-start | bytes 4718600 | tf_op jit(solution)/shard_map/ppermute | solution.py:458
  45.6 18.9 %collective-permute-start.31 = (bf16[256,1024]{1,0:T(8,128)(2,1)}, bf16[256,1024]{1,0:T(8,128)(2,1)}, u32[]{:S(2)}, u32[]{:S(2)}) collective-permute-start(bf16[256,1024]{1,0:T(8,128)(2,1)} %get-tuple-element.120.refs_4_.refs_16_), channel_id=1, source_target_pairs={{0,2},{1,3},{2,0},{3,1},{4,6},{5,7},{6,4},{7,5},{8,10},{9,11},{10,... | collective-permute-start | bytes 1572872 | tf_op jit(solution)/shard_map/ppermute | solution.py:458
  53.2 22.5 %collective-permute-start.28 = (bf16[256,1024]{1,0:T(8,128)(2,1)}, bf16[256,1024]{1,0:T(8,128)(2,1)}, u32[]{:S(2)}, u32[]{:S(2)}) collective-permute-start(bf16[256,1024]{1,0:T(8,128)(2,1)} %get-tuple-element.121.refs_0_.refs_16_), channel_id=1, source_target_pairs={{0,2},{1,3},{2,0},{3,1},{4,6},{5,7},{6,4},{7,5},{8,10},{9,11},{10,... | collective-permute-start | bytes 1572872 | tf_op jit(solution)/shard_map/ppermute | solution.py:458
  64.5 16.0 %collective-permute-start.27 = (bf16[256,1024]{1,0:T(8,128)(2,1)}, bf16[256,1024]{1,0:T(8,128)(2,1)}, u32[]{:S(2)}, u32[]{:S(2)}) collective-permute-start(bf16[256,1024]{1,0:T(8,128)(2,1)} %get-tuple-element.121.refs_0_.refs_16_), channel_id=1, source_target_pairs={{0,1},{1,0},{2,3},{3,2},{4,5},{5,4},{6,7},{7,6},{8,9},{9,8},{10,11... | collective-permute-start | bytes 1572872 | tf_op jit(solution)/shard_map/ppermute | solution.py:458
  64.5 21.6 %collective-permute-start.25 = (bf16[256,1024]{1,0:T(8,128)(2,1)}, bf16[256,1024]{1,0:T(8,128)(2,1)}, u32[]{:S(2)}, u32[]{:S(2)}) collective-permute-start(bf16[256,1024]{1,0:T(8,128)(2,1)} %get-tuple-element.122.refs_4_.refs_12_), channel_id=1, source_target_pairs={{0,2},{1,3},{2,0},{3,1},{4,6},{5,7},{6,4},{7,5},{8,10},{9,11},{10,... | collective-permute-start | bytes 1572872 | tf_op jit(solution)/shard_map/ppermute | solution.py:458
  80.5 46.9 %collective-permute-start.24 = (bf16[256,1024]{1,0:T(8,128)(2,1)}, bf16[256,1024]{1,0:T(8,128)(2,1)}, u32[]{:S(2)}, u32[]{:S(2)}) collective-permute-start(bf16[256,1024]{1,0:T(8,128)(2,1)} %get-tuple-element.122.refs_4_.refs_12_), channel_id=1, source_target_pairs={{0,1},{1,0},{2,3},{3,2},{4,5},{5,4},{6,7},{7,6},{8,9},{9,8},{10,11... | collective-permute-start | bytes 1572872 | tf_op jit(solution)/shard_map/ppermute | solution.py:458
  86.1 41.7 %collective-permute-start.22 = (bf16[256,1024]{1,0:T(8,128)(2,1)}, bf16[256,1024]{1,0:T(8,128)(2,1)}, u32[]{:S(2)}, u32[]{:S(2)}) collective-permute-start(bf16[256,1024]{1,0:T(8,128)(2,1)} %get-tuple-element.123.refs_0_.refs_12_), channel_id=1, source_target_pairs={{0,2},{1,3},{2,0},{3,1},{4,6},{5,7},{6,4},{7,5},{8,10},{9,11},{10,... | collective-permute-start | bytes 1572872 | tf_op jit(solution)/shard_map/ppermute | solution.py:458
  87.8 40.2 %collective-permute-start.21 = (bf16[256,1024]{1,0:T(8,128)(2,1)}, bf16[256,1024]{1,0:T(8,128)(2,1)}, u32[]{:S(2)}, u32[]{:S(2)}) collective-permute-start(bf16[256,1024]{1,0:T(8,128)(2,1)} %get-tuple-element.123.refs_0_.refs_12_), channel_id=1, source_target_pairs={{0,1},{1,0},{2,3},{3,2},{4,5},{5,4},{6,7},{7,6},{8,9},{9,8},{10,11... | collective-permute-start | bytes 1572872 | tf_op jit(solution)/shard_map/ppermute | solution.py:458
  87.8 41.8 %collective-permute-start.32 = (bf16[256,1024]{1,0:T(8,128)(2,1)}, bf16[256,1024]{1,0:T(8,128)(2,1)}, u32[]{:S(2)}, u32[]{:S(2)}) collective-permute-start(bf16[256,1024]{1,0:T(8,128)(2,1)} %collective-permute-done.31.refs_6_.refs_18_), channel_id=1, source_target_pairs={{0,1},{1,0},{2,3},{3,2},{4,5},{5,4},{6,7},{7,6},{8,9},{9,8},{10,11... | collective-permute-start | bytes 1572872 | tf_op jit(solution)/shard_map/ppermute | solution.py:458
  88.4 41.4 %collective-permute-start.29 = (bf16[256,1024]{1,0:T(8,128)(2,1)}, bf16[256,1024]{1,0:T(8,128)(2,1)}, u32[]{:S(2)}, u32[]{:S(2)}) collective-permute-start(bf16[256,1024]{1,0:T(8,128)(2,1)} %collective-permute-done.28.refs_2_.refs_18_), channel_id=1, source_target_pairs={{0,1},{1,0},{2,3},{3,2},{4,5},{5,4},{6,7},{7,6},{8,9},{9,8},{10,11... | collective-permute-start | bytes 1572872 | tf_op jit(solution)/shard_map/ppermute | solution.py:458
  127.4 26.4 %collective-permute-start.19 = (bf16[256,1024]{1,0:T(8,128)(2,1)}, bf16[256,1024]{1,0:T(8,128)(2,1)S(1)}, u32[]{:S(2)}, u32[]{:S(2)}) collective-permute-start(bf16[256,1024]{1,0:T(8,128)(2,1)} %get-tuple-element.124.refs_4_.refs_8_), channel_id=1, source_target_pairs={{0,2},{1,3},{2,0},{3,1},{4,6},{5,7},{6,4},{7,5},{8,10},{9,11},{10,... | collective-permute-start | bytes 1572872 | tf_op jit(solution)/shard_map/ppermute | solution.py:458
  127.8 26.2 %collective-permute-start.18 = (bf16[256,1024]{1,0:T(8,128)(2,1)}, bf16[256,1024]{1,0:T(8,128)(2,1)S(1)}, u32[]{:S(2)}, u32[]{:S(2)}) collective-permute-start(bf16[256,1024]{1,0:T(8,128)(2,1)} %get-tuple-element.124.refs_4_.refs_8_), channel_id=1, source_target_pairs={{0,1},{1,0},{2,3},{3,2},{4,5},{5,4},{6,7},{7,6},{8,9},{9,8},{10,11... | collective-permute-start | bytes 1572872 | tf_op jit(solution)/shard_map/ppermute | solution.py:458
  128.0 26.3 %collective-permute-start.16 = (bf16[256,1024]{1,0:T(8,128)(2,1)}, bf16[256,1024]{1,0:T(8,128)(2,1)S(1)}, u32[]{:S(2)}, u32[]{:S(2)}) collective-permute-start(bf16[256,1024]{1,0:T(8,128)(2,1)} %get-tuple-element.125.refs_0_.refs_8_), channel_id=1, source_target_pairs={{0,2},{1,3},{2,0},{3,1},{4,6},{5,7},{6,4},{7,5},{8,10},{9,11},{10,... | collective-permute-start | bytes 1572872 | tf_op jit(solution)/shard_map/ppermute | solution.py:458
  129.7 26.3 %collective-permute-start.26 = (bf16[256,1024]{1,0:T(8,128)(2,1)}, bf16[256,1024]{1,0:T(8,128)(2,1)S(1)}, u32[]{:S(2)}, u32[]{:S(2)}) collective-permute-start(bf16[256,1024]{1,0:T(8,128)(2,1)} %collective-permute-done.25.refs_6_.refs_14_), channel_id=1, source_target_pairs={{0,1},{1,0},{2,3},{3,2},{4,5},{5,4},{6,7},{7,6},{8,9},{9,8},{10,11... | collective-permute-start | bytes 1572872 | tf_op jit(solution)/shard_map/ppermute | solution.py:458
  129.8 26.3 %collective-permute-start.23 = (bf16[256,1024]{1,0:T(8,128)(2,1)}, bf16[256,1024]{1,0:T(8,128)(2,1)S(1)}, u32[]{:S(2)}, u32[]{:S(2)}) collective-permute-start(bf16[256,1024]{1,0:T(8,128)(2,1)} %collective-permute-done.22.refs_2_.refs_14_), channel_id=1, source_target_pairs={{0,1},{1,0},{2,3},{3,2},{4,5},{5,4},{6,7},{7,6},{8,9},{9,8},{10,11... | collective-permute-start | bytes 1572872 | tf_op jit(solution)/shard_map/ppermute | solution.py:458
  153.8 25.5 %collective-permute-start.15 = (bf16[256,1024]{1,0:T(8,128)(2,1)S(1)}, bf16[256,1024]{1,0:T(8,128)(2,1)S(1)}, u32[]{:S(2)}, u32[]{:S(2)}) collective-permute-start(bf16[256,1024]{1,0:T(8,128)(2,1)S(1)} %copy-done.29), channel_id=1, source_target_pairs={{0,1},{1,0},{2,3},{3,2},{4,5},{5,4},{6,7},{7,6},{8,9},{9,8},{10,11... | collective-permute-start | bytes 1572872 | tf_op jit(solution)/shard_map/ppermute | solution.py:458
  153.9 25.4 %collective-permute-start.13 = (bf16[256,1024]{1,0:T(8,128)(2,1)S(1)}, bf16[256,1024]{1,0:T(8,128)(2,1)S(1)}, u32[]{:S(2)}, u32[]{:S(2)}) collective-permute-start(bf16[256,1024]{1,0:T(8,128)(2,1)S(1)} %copy-done.26), channel_id=1, source_target_pairs={{0,2},{1,3},{2,0},{3,1},{4,6},{5,7},{6,4},{7,5},{8,10},{9,11},{10,... | collective-permute-start | bytes 1572872 | tf_op jit(solution)/shard_map/ppermute | solution.py:458
  154.4 25.4 %collective-permute-start.10 = (bf16[256,1024]{1,0:T(8,128)(2,1)S(1)}, bf16[256,1024]{1,0:T(8,128)(2,1)S(1)}, u32[]{:S(2)}, u32[]{:S(2)}) collective-permute-start(bf16[256,1024]{1,0:T(8,128)(2,1)S(1)} %copy-done.30), channel_id=1, source_target_pairs={{0,2},{1,3},{2,0},{3,1},{4,6},{5,7},{6,4},{7,5},{8,10},{9,11},{10,... | collective-permute-start | bytes 1572872 | tf_op jit(solution)/shard_map/ppermute | solution.py:458
  156.0 23.8 %collective-permute-start.20 = (bf16[256,1024]{1,0:T(8,128)(2,1)S(1)}, bf16[256,1024]{1,0:T(8,128)(2,1)S(1)}, u32[]{:S(2)}, u32[]{:S(2)}) collective-permute-start(bf16[256,1024]{1,0:T(8,128)(2,1)S(1)} %collective-permute-done.19.refs_6_.refs_10_), channel_id=1, source_target_pairs={{0,1},{1,0},{2,3},{3,2},{4,5},{5,4},{6,7},{7,6},{8,9},{9,8},{10,11... | collective-permute-start | bytes 1572872 | tf_op jit(solution)/shard_map/ppermute | solution.py:458
  156.1 24.2 %collective-permute-start.17 = (bf16[256,1024]{1,0:T(8,128)(2,1)S(1)}, bf16[256,1024]{1,0:T(8,128)(2,1)S(1)}, u32[]{:S(2)}, u32[]{:S(2)}) collective-permute-start(bf16[256,1024]{1,0:T(8,128)(2,1)S(1)} %collective-permute-done.16.refs_2_.refs_10_), channel_id=1, source_target_pairs={{0,1},{1,0},{2,3},{3,2},{4,5},{5,4},{6,7},{7,6},{8,9},{9,8},{10,11... | collective-permute-start | bytes 1572872 | tf_op jit(solution)/shard_map/ppermute | solution.py:458
  179.3 22.9 %collective-permute-start.12 = (bf16[256,1024]{1,0:T(8,128)(2,1)S(1)}, bf16[256,1024]{1,0:T(8,128)(2,1)S(1)}, u32[]{:S(2)}, u32[]{:S(2)}) collective-permute-start(bf16[256,1024]{1,0:T(8,128)(2,1)S(1)} %copy-done.26), channel_id=1, source_target_pairs={{0,1},{1,0},{2,3},{3,2},{4,5},{5,4},{6,7},{7,6},{8,9},{9,8},{10,11... | collective-permute-start | bytes 1572872 | tf_op jit(solution)/shard_map/ppermute | solution.py:458
  179.4 22.9 %collective-permute-start.9 = (bf16[256,1024]{1,0:T(8,128)(2,1)S(1)}, bf16[256,1024]{1,0:T(8,128)(2,1)S(1)}, u32[]{:S(2)}, u32[]{:S(2)}) collective-permute-start(bf16[256,1024]{1,0:T(8,128)(2,1)S(1)} %copy-done.30), channel_id=1, source_target_pairs={{0,1},{1,0},{2,3},{3,2},{4,5},{5,4},{6,7},{7,6},{8,9},{9,8},{10,11... | collective-permute-start | bytes 1572872 | tf_op jit(solution)/shard_map/ppermute | solution.py:458
  179.8 22.4 %collective-permute-start.14 = (bf16[256,1024]{1,0:T(8,128)(2,1)S(1)}, bf16[256,1024]{1,0:T(8,128)(2,1)S(1)}, u32[]{:S(2)}, u32[]{:S(2)}) collective-permute-start(bf16[256,1024]{1,0:T(8,128)(2,1)S(1)} %collective-permute-done.13.refs_6_), channel_id=1, source_target_pairs={{0,1},{1,0},{2,3},{3,2},{4,5},{5,4},{6,7},{7,6},{8,9},{9,8},{10,11... | collective-permute-start | bytes 1572872 | tf_op jit(solution)/shard_map/ppermute | solution.py:458
  179.9 22.4 %collective-permute-start.11 = (bf16[256,1024]{1,0:T(8,128)(2,1)S(1)}, bf16[256,1024]{1,0:T(8,128)(2,1)S(1)}, u32[]{:S(2)}, u32[]{:S(2)}) collective-permute-start(bf16[256,1024]{1,0:T(8,128)(2,1)S(1)} %collective-permute-done.10.refs_2_.refs_6_), channel_id=1, source_target_pairs={{0,1},{1,0},{2,3},{3,2},{4,5},{5,4},{6,7},{7,6},{8,9},{9,8},{10,11... | collective-permute-start | bytes 1572872 | tf_op jit(solution)/shard_map/ppermute | solution.py:458
  302.7 61.6 %collective-permute-start.73 = (bf16[2,256,1024]{2,1,0:T(8,128)(2,1)}, bf16[2,256,1024]{2,1,0:T(8,128)(2,1)}, u32[]{:S(2)}, u32[]{:S(2)}) collective-permute-start(bf16[2,256,1024]{2,1,0:T(8,128)(2,1)} %copy-done.39), channel_id=1, source_target_pairs={{0,1},{1,0},{2,3},{3,2},{4,5},{5,4},{6,7},{7,6},{8,9},{9,8},{10,11... | collective-permute-start | bytes 3145736 | tf_op jit(solution)/shard_map/ppermute | solution.py:458
  302.8 63.7 %collective-permute-start.105 = (bf16[2,256,1024]{2,1,0:T(8,128)(2,1)}, bf16[2,256,1024]{2,1,0:T(8,128)(2,1)}, u32[]{:S(2)}, u32[]{:S(2)}) collective-permute-start(bf16[2,256,1024]{2,1,0:T(8,128)(2,1)} %copy-done.38), channel_id=1, source_target_pairs={{0,1},{1,0},{2,3},{3,2},{4,5},{5,4},{6,7},{7,6},{8,9},{9,8},{10,11... | collective-permute-start | bytes 3145736 | tf_op jit(solution)/shard_map/ppermute | solution.py:458
  303.3 65.1 %collective-permute-start.65 = (bf16[2,256,1024]{2,1,0:T(8,128)(2,1)}, bf16[2,256,1024]{2,1,0:T(8,128)(2,1)}, u32[]{:S(2)}, u32[]{:S(2)}) collective-permute-start(bf16[2,256,1024]{2,1,0:T(8,128)(2,1)} %copy-done.44), channel_id=1, source_target_pairs={{0,1},{1,0},{2,3},{3,2},{4,5},{5,4},{6,7},{7,6},{8,9},{9,8},{10,11... | collective-permute-start | bytes 3145736 | tf_op jit(solution)/shard_map/ppermute | solution.py:458
  306.9 28.1 %collective-permute-start.115 = (f32[16,1024]{1,0:T(8,128)}, f32[16,1024]{1,0:T(8,128)}, u32[]{:S(2)}, u32[]{:S(2)}) collective-permute-start(f32[16,1024]{1,0:T(8,128)} %add.368), channel_id=1, source_target_pairs={{0,4},{4,0},{8,12},{12,8},{16,20},{20,16},{24,28},{28,24},{1,5},{5... | collective-permute-start | bytes 196616 | tf_op jit(solution)/shard_map/ppermute | solution.py:458
  335.9 20.9 %collective-permute-start.116 = (f32[16,1024]{1,0:T(8,128)S(1)}, f32[16,1024]{1,0:T(8,128)S(1)}, u32[]{:S(2)}, u32[]{:S(2)}) collective-permute-start(f32[16,1024]{1,0:T(8,128)S(1)} %add.369), channel_id=1, source_target_pairs={{0,8},{4,12},{8,0},{12,4},{16,24},{20,28},{24,16},{28,20},{1,9},{5... | collective-permute-start | bytes 196616 | tf_op jit(solution)/shard_map/ppermute | solution.py:458
  371.3 138.4 %collective-permute-start.33 = (bf16[2,256,3072]{2,1,0:T(8,128)(2,1)S(1)}, bf16[2,256,3072]{2,1,0:T(8,128)(2,1)S(1)}, u32[]{:S(2)}, u32[]{:S(2)}) collective-permute-start(bf16[2,256,3072]{2,1,0:T(8,128)(2,1)S(1)} %copy-done.36), channel_id=1, source_target_pairs={{0,1},{1,0},{2,3},{3,2},{4,5},{5,4},{6,7},{7,6},{8,9},{9,8},{10,11... | collective-permute-start | bytes 9437192 | tf_op jit(solution)/shard_map/ppermute | solution.py:458
  373.5 36.1 %collective-permute-start.106 = (bf16[1,256,1024]{2,1,0:T(8,128)(2,1)S(1)}, bf16[1,256,1024]{2,1,0:T(8,128)(2,1)S(1)}, u32[]{:S(2)}, u32[]{:S(2)}) collective-permute-start(bf16[1,256,1024]{2,1,0:T(8,128)(2,1)S(1)} %slice.237), channel_id=1, source_target_pairs={{0,2},{1,3},{2,0},{3,1},{4,6},{5,7},{6,4},{7,5},{8,10},{9,11},{10,... | collective-permute-start | bytes 1572872 | tf_op jit(solution)/shard_map/ppermute | solution.py:458
  374.5 24.1 %collective-permute-start.66 = (bf16[2,128,1024]{2,1,0:T(8,128)(2,1)S(1)}, bf16[2,128,1024]{2,1,0:T(8,128)(2,1)S(1)}, u32[]{:S(2)}, u32[]{:S(2)}) collective-permute-start(bf16[2,128,1024]{2,1,0:T(8,128)(2,1)S(1)} %constant_dynamic-slice_fusion.17), channel_id=1, source_target_pairs={{0,4},{4,0},{8,12},{12,8},{16,20},{20,16},{24,28},{28,24},{1,5},{5... | collective-permute-start | bytes 1572872 | tf_op jit(solution)/shard_map/ppermute | solution.py:458
  376.5 34.9 %collective-permute-start.98 = (bf16[1,256,1024]{2,1,0:T(8,128)(2,1)S(1)}, bf16[1,256,1024]{2,1,0:T(8,128)(2,1)S(1)}, u32[]{:S(2)}, u32[]{:S(2)}) collective-permute-start(bf16[1,256,1024]{2,1,0:T(8,128)(2,1)S(1)} %slice.235), channel_id=1, source_target_pairs={{0,2},{1,3},{2,0},{3,1},{4,6},{5,7},{6,4},{7,5},{8,10},{9,11},{10,... | collective-permute-start | bytes 1572872 | tf_op jit(solution)/shard_map/ppermute | solution.py:458
  387.4 21.5 %collective-permute-start.58 = (bf16[2,128,1024]{2,1,0:T(8,128)(2,1)S(1)}, bf16[2,128,1024]{2,1,0:T(8,128)(2,1)S(1)}, u32[]{:S(2)}, u32[]{:S(2)}) collective-permute-start(bf16[2,128,1024]{2,1,0:T(8,128)(2,1)S(1)} %constant_dynamic-slice_fusion.20), channel_id=1, source_target_pairs={{0,4},{4,0},{8,12},{12,8},{16,20},{20,16},{24,28},{28,24},{1,5},{5... | collective-permute-start | bytes 1572872 | tf_op jit(solution)/shard_map/ppermute | solution.py:458
  408.9 14.9 %collective-permute-start.42 = (bf16[2,128,1024]{2,1,0:T(8,128)(2,1)S(1)}, bf16[2,128,1024]{2,1,0:T(8,128)(2,1)S(1)}, u32[]{:S(2)}, u32[]{:S(2)}) collective-permute-start(bf16[2,128,1024]{2,1,0:T(8,128)(2,1)S(1)} %constant_dynamic-slice_fusion.26), channel_id=1, source_target_pairs={{0,4},{4,0},{8,12},{12,8},{16,20},{20,16},{24,28},{28,24},{1,5},{5... | collective-permute-start | bytes 1572872 | tf_op jit(solution)/shard_map/ppermute | solution.py:458
  409.7 25.3 %collective-permute-start.50 = (bf16[2,128,1024]{2,1,0:T(8,128)(2,1)S(1)}, bf16[2,128,1024]{2,1,0:T(8,128)(2,1)S(1)}, u32[]{:S(2)}, u32[]{:S(2)}) collective-permute-start(bf16[2,128,1024]{2,1,0:T(8,128)(2,1)S(1)} %constant_dynamic-slice_fusion.23), channel_id=1, source_target_pairs={{0,4},{4,0},{8,12},{12,8},{16,20},{20,16},{24,28},{28,24},{1,5},{5... | collective-permute-start | bytes 1572872 | tf_op jit(solution)/shard_map/ppermute | solution.py:458
  411.4 24.2 %collective-permute-start.82 = (bf16[1,256,1024]{2,1,0:T(8,128)(2,1)S(1)}, bf16[1,256,1024]{2,1,0:T(8,128)(2,1)S(1)}, u32[]{:S(2)}, u32[]{:S(2)}) collective-permute-start(bf16[1,256,1024]{2,1,0:T(8,128)(2,1)S(1)} %slice.231), channel_id=1, source_target_pairs={{0,2},{1,3},{2,0},{3,1},{4,6},{5,7},{6,4},{7,5},{8,10},{9,11},{10,... | collective-permute-start | bytes 1572872 | tf_op jit(solution)/shard_map/ppermute | solution.py:458
  412.2 28.9 %collective-permute-start.75 = (bf16[2,64,1024]{2,1,0:T(8,128)(2,1)S(1)}, bf16[2,64,1024]{2,1,0:T(8,128)(2,1)S(1)}, u32[]{:S(2)}, u32[]{:S(2)}) collective-permute-start(bf16[2,64,1024]{2,1,0:T(8,128)(2,1)S(1)} %constant_dynamic-slice_fusion.13), channel_id=1, source_target_pairs={{0,8},{4,12},{8,0},{12,4},{16,24},{20,28},{24,16},{28,20},{1,9},{5... | collective-permute-start | bytes 786440 | tf_op jit(solution)/shard_map/ppermute | solution.py:458
  423.8 16.9 %collective-permute-start.107 = (bf16[1,128,1024]{2,1,0:T(8,128)(2,1)S(1)}, bf16[1,128,1024]{2,1,0:T(8,128)(2,1)S(1)}, u32[]{:S(2)}, u32[]{:S(2)}) collective-permute-start(bf16[1,128,1024]{2,1,0:T(8,128)(2,1)S(1)} %constant_dynamic-slice_fusion.2), channel_id=1, source_target_pairs={{0,4},{4,0},{8,12},{12,8},{16,20},{20,16},{24,28},{28,24},{1,5},{5... | collective-permute-start | bytes 786440 | tf_op jit(solution)/shard_map/ppermute | solution.py:458
  446.2 20.5 %collective-permute-start.51 = (bf16[2,64,1024]{2,1,0:T(8,128)(2,1)S(1)}, bf16[2,64,1024]{2,1,0:T(8,128)(2,1)S(1)}, u32[]{:S(2)}, u32[]{:S(2)}) collective-permute-start(bf16[2,64,1024]{2,1,0:T(8,128)(2,1)S(1)} %constant_dynamic-slice_fusion.22), channel_id=1, source_target_pairs={{0,8},{4,12},{8,0},{12,4},{16,24},{20,28},{24,16},{28,20},{1,9},{5... | collective-permute-start | bytes 786440 | tf_op jit(solution)/shard_map/ppermute | solution.py:458
  449.9 16.9 %collective-permute-start.83 = (bf16[1,128,1024]{2,1,0:T(8,128)(2,1)S(1)}, bf16[1,128,1024]{2,1,0:T(8,128)(2,1)S(1)}, u32[]{:S(2)}, u32[]{:S(2)}) collective-permute-start(bf16[1,128,1024]{2,1,0:T(8,128)(2,1)S(1)} %constant_dynamic-slice_fusion.11), channel_id=1, source_target_pairs={{0,4},{4,0},{8,12},{12,8},{16,20},{20,16},{24,28},{28,24},{1,5},{5... | collective-permute-start | bytes 786440 | tf_op jit(solution)/shard_map/ppermute | solution.py:458
  451.9 18.2 %collective-permute-start.76 = (bf16[2,32,1024]{2,1,0:T(8,128)(2,1)S(1)}, bf16[2,32,1024]{2,1,0:T(8,128)(2,1)S(1)}, u32[]{:S(2)}, u32[]{:S(2)}) collective-permute-start(bf16[2,32,1024]{2,1,0:T(8,128)(2,1)S(1)} %constant_dynamic-slice_fusion.12), channel_id=1, source_target_pairs={{0,16},{4,20},{8,24},{12,28},{16,0},{20,4},{24,8},{28,12},{1,17},{... | collective-permute-start | bytes 393224 | tf_op jit(solution)/shard_map/ppermute | solution.py:458
  489.0 23.9 %collective-permute-start.109 = (bf16[1,32,1024]{2,1,0:T(8,128)(2,1)S(1)}, bf16[1,32,1024]{2,1,0:T(8,128)(2,1)S(1)}, u32[]{:S(2)}, u32[]{:S(2)}) collective-permute-start(bf16[1,32,1024]{2,1,0:T(8,128)(2,1)S(1)} %constant_dynamic-slice_fusion), channel_id=1, source_target_pairs={{0,16},{4,20},{8,24},{12,28},{16,0},{20,4},{24,8},{28,12},{1,17},{... | collective-permute-start | bytes 196616 | tf_op jit(solution)/shard_map/ppermute | solution.py:458
  491.6 22.4 %collective-permute-start.101 = (bf16[1,32,1024]{2,1,0:T(8,128)(2,1)S(1)}, bf16[1,32,1024]{2,1,0:T(8,128)(2,1)S(1)}, u32[]{:S(2)}, u32[]{:S(2)}) collective-permute-start(bf16[1,32,1024]{2,1,0:T(8,128)(2,1)S(1)} %constant_dynamic-slice_fusion.3), channel_id=1, source_target_pairs={{0,16},{4,20},{8,24},{12,28},{16,0},{20,4},{24,8},{28,12},{1,17},{... | collective-permute-start | bytes 196616 | tf_op jit(solution)/shard_map/ppermute | solution.py:458
  494.7 20.4 %collective-permute-start.93 = (bf16[1,32,1024]{2,1,0:T(8,128)(2,1)S(1)}, bf16[1,32,1024]{2,1,0:T(8,128)(2,1)S(1)}, u32[]{:S(2)}, u32[]{:S(2)}) collective-permute-start(bf16[1,32,1024]{2,1,0:T(8,128)(2,1)S(1)} %constant_dynamic-slice_fusion.6), channel_id=1, source_target_pairs={{0,16},{4,20},{8,24},{12,28},{16,0},{20,4},{24,8},{28,12},{1,17},{... | collective-permute-start | bytes 196616 | tf_op jit(solution)/shard_map/ppermute | solution.py:458
  512.9 20.5 %collective-permute-start.34 = (bf16[1,256,3072]{2,1,0:T(8,128)(2,1)S(1)}, bf16[1,256,3072]{2,1,0:T(8,128)(2,1)S(1)}, u32[]{:S(2)}, u32[]{:S(2)}) collective-permute-start(bf16[1,256,3072]{2,1,0:T(8,128)(2,1)S(1)} %slice.219), channel_id=1, source_target_pairs={{0,2},{1,3},{2,0},{3,1},{4,6},{5,7},{6,4},{7,5},{8,10},{9,11},{10,... | collective-permute-start | bytes 4718600 | tf_op jit(solution)/shard_map/ppermute | solution.py:458
  535.3 20.5 %collective-permute-start.35 = (bf16[1,128,3072]{2,1,0:T(8,128)(2,1)S(1)}, bf16[1,128,3072]{2,1,0:T(8,128)(2,1)S(1)}, u32[]{:S(2)}, u32[]{:S(2)}) collective-permute-start(bf16[1,128,3072]{2,1,0:T(8,128)(2,1)S(1)} %constant_dynamic-slice_fusion.29), channel_id=1, source_target_pairs={{0,4},{4,0},{8,12},{12,8},{16,20},{20,16},{24,28},{28,24},{1,5},{5... | collective-permute-start | bytes 2359304 | tf_op jit(solution)/shard_map/ppermute | solution.py:458
  538.3 18.4 %collective-permute-start.95 = (bf16[64,1024]{1,0:T(8,128)(2,1)S(1)}, bf16[64,1024]{1,0:T(8,128)(2,1)S(1)}, u32[]{:S(2)}, u32[]{:S(2)}) collective-permute-start(bf16[64,1024]{1,0:T(8,128)(2,1)S(1)} %maximum_select_fusion.27), channel_id=1, source_target_pairs={{0,8},{4,12},{8,0},{12,4},{16,24},{20,28},{24,16},{28,20},{1,9},{5... | collective-permute-start | bytes 393224 | tf_op jit(solution)/shard_map/ppermute | solution.py:458
  539.9 17.7 %collective-permute-start.47 = (bf16[64,1024]{1,0:T(8,128)(2,1)S(1)}, bf16[64,1024]{1,0:T(8,128)(2,1)S(1)}, u32[]{:S(2)}, u32[]{:S(2)}) collective-permute-start(bf16[64,1024]{1,0:T(8,128)(2,1)S(1)} %maximum_select_fusion.21), channel_id=1, source_target_pairs={{0,8},{4,12},{8,0},{12,4},{16,24},{20,28},{24,16},{28,20},{1,9},{5... | collective-permute-start | bytes 393224 | tf_op jit(solution)/shard_map/ppermute | solution.py:458
  542.7 16.6 %collective-permute-start.55 = (bf16[64,1024]{1,0:T(8,128)(2,1)S(1)}, bf16[64,1024]{1,0:T(8,128)(2,1)S(1)}, u32[]{:S(2)}, u32[]{:S(2)}) collective-permute-start(bf16[64,1024]{1,0:T(8,128)(2,1)S(1)} %maximum_select_fusion.22), channel_id=1, source_target_pairs={{0,8},{4,12},{8,0},{12,4},{16,24},{20,28},{24,16},{28,20},{1,9},{5... | collective-permute-start | bytes 393224 | tf_op jit(solution)/shard_map/ppermute | solution.py:458
  555.9 37.8 %collective-permute-start.80 = (bf16[128,1024]{1,0:T(8,128)(2,1)S(1)}, bf16[128,1024]{1,0:T(8,128)(2,1)S(1)}, u32[]{:S(2)}, u32[]{:S(2)}) collective-permute-start(bf16[128,1024]{1,0:T(8,128)(2,1)S(1)} %maximum_select_fusion.16), channel_id=1, source_target_pairs={{0,4},{4,0},{8,12},{12,8},{16,20},{20,16},{24,28},{28,24},{1,5},{5... | collective-permute-start | bytes 786440 | tf_op jit(solution)/shard_map/ppermute | solution.py:458
  557.6 55.5 %collective-permute-start.112 = (bf16[128,1024]{1,0:T(8,128)(2,1)S(1)}, bf16[128,1024]{1,0:T(8,128)(2,1)S(1)}, u32[]{:S(2)}, u32[]{:S(2)}) collective-permute-start(bf16[128,1024]{1,0:T(8,128)(2,1)S(1)} %maximum_select_fusion.20), channel_id=1, source_target_pairs={{0,4},{4,0},{8,12},{12,8},{16,20},{20,16},{24,28},{28,24},{1,5},{5... | collective-permute-start | bytes 786440 | tf_op jit(solution)/shard_map/ppermute | solution.py:458
  559.2 34.2 %collective-permute-start.72 = (bf16[128,1024]{1,0:T(8,128)(2,1)S(1)}, bf16[128,1024]{1,0:T(8,128)(2,1)S(1)}, u32[]{:S(2)}, u32[]{:S(2)}) collective-permute-start(bf16[128,1024]{1,0:T(8,128)(2,1)S(1)} %maximum_select_fusion.15), channel_id=1, source_target_pairs={{0,4},{4,0},{8,12},{12,8},{16,20},{20,16},{24,28},{28,24},{1,5},{5... | collective-permute-start | bytes 786440 | tf_op jit(solution)/shard_map/ppermute | solution.py:458
  559.9 24.3 %collective-permute-start.64 = (bf16[128,1024]{1,0:T(8,128)(2,1)S(1)}, bf16[128,1024]{1,0:T(8,128)(2,1)S(1)}, u32[]{:S(2)}, u32[]{:S(2)}) collective-permute-start(bf16[128,1024]{1,0:T(8,128)(2,1)S(1)} %maximum_select_fusion.14), channel_id=1, source_target_pairs={{0,4},{4,0},{8,12},{12,8},{16,20},{20,16},{24,28},{28,24},{1,5},{5... | collective-permute-start | bytes 786440 | tf_op jit(solution)/shard_map/ppermute | solution.py:458
  566.1 18.0 %collective-permute-start.56 = (bf16[128,1024]{1,0:T(8,128)(2,1)S(1)}, bf16[128,1024]{1,0:T(8,128)(2,1)S(1)}, u32[]{:S(2)}, u32[]{:S(2)}) collective-permute-start(bf16[128,1024]{1,0:T(8,128)(2,1)S(1)} %maximum_select_fusion.13), channel_id=1, source_target_pairs={{0,4},{4,0},{8,12},{12,8},{16,20},{20,16},{24,28},{28,24},{1,5},{5... | collective-permute-start | bytes 786440 | tf_op jit(solution)/shard_map/ppermute | solution.py:458
  584.3 28.7 %collective-permute-start.104 = (bf16[128,1024]{1,0:T(8,128)(2,1)S(1)}, bf16[128,1024]{1,0:T(8,128)(2,1)S(1)}, u32[]{:S(2)}, u32[]{:S(2)}) collective-permute-start(bf16[128,1024]{1,0:T(8,128)(2,1)S(1)} %maximum_select_fusion.19), channel_id=1, source_target_pairs={{0,4},{4,0},{8,12},{12,8},{16,20},{20,16},{24,28},{28,24},{1,5},{5... | collective-permute-start | bytes 786440 | tf_op jit(solution)/shard_map/ppermute | solution.py:458
  592.8 20.0 %collective-permute-start.96 = (bf16[128,1024]{1,0:T(8,128)(2,1)S(1)}, bf16[128,1024]{1,0:T(8,128)(2,1)S(1)}, u32[]{:S(2)}, u32[]{:S(2)}) collective-permute-start(bf16[128,1024]{1,0:T(8,128)(2,1)S(1)} %maximum_select_fusion.18), channel_id=1, source_target_pairs={{0,4},{4,0},{8,12},{12,8},{16,20},{20,16},{24,28},{28,24},{1,5},{5... | collective-permute-start | bytes 786440 | tf_op jit(solution)/shard_map/ppermute | solution.py:458
  593.7 43.3 %collective-permute-start.48 = (bf16[128,1024]{1,0:T(8,128)(2,1)S(1)}, bf16[128,1024]{1,0:T(8,128)(2,1)S(1)}, u32[]{:S(2)}, u32[]{:S(2)}) collective-permute-start(bf16[128,1024]{1,0:T(8,128)(2,1)S(1)} %maximum_select_fusion.12), channel_id=1, source_target_pairs={{0,4},{4,0},{8,12},{12,8},{16,20},{20,16},{24,28},{28,24},{1,5},{5... | collective-permute-start | bytes 786440 | tf_op jit(solution)/shard_map/ppermute | solution.py:458
  618.9 18.2 %collective-permute-start.40 = (bf16[128,3072]{1,0:T(8,128)(2,1)S(1)}, bf16[128,3072]{1,0:T(8,128)(2,1)}, u32[]{:S(2)}, u32[]{:S(2)}) collective-permute-start(bf16[128,3072]{1,0:T(8,128)(2,1)S(1)} %maximum_select_fusion.1), channel_id=1, source_target_pairs={{0,4},{4,0},{8,12},{12,8},{16,20},{20,16},{24,28},{28,24},{1,5},{5... | collective-permute-start | bytes 2359304 | tf_op jit(solution)/shard_map/ppermute | solution.py:458
  (153 other events, 1704.4 us)

commit v2 on v1

v2 whole, which is shorter than its diff:
```python
import jax
import jax.numpy as jnp
from jax import lax
from jax.experimental import pallas as pl
from jax.experimental.pallas import tpu as pltpu
from jax.sharding import PartitionSpec as P

D = 1024
HEADS = 16
HEAD_DIM = 64
FF = 4096
BUF = 64
STEP = 10
BLOCKS = 4
BLOCK = D // BLOCKS
PARTS = 4
PART = FF // PARTS
GROUP = 4
GROUP_W = GROUP * HEAD_DIM

EPS_NORM = 1e-06
MASKED = -1000000000.0
BETA_ONE = 0.9
BETA_TWO = 0.999
EPS_ADAM = 1e-08

BF16 = jnp.bfloat16
F32 = jnp.float32
MIB = 1 << 20


def normalize(values):
    average = jnp.mean(values, axis=-1, keepdims=True)
    centred = values - average
    inverse = lax.rsqrt(jnp.mean(centred * centred, axis=-1, keepdims=True) + EPS_NORM)
    return (centred * inverse, inverse)


def norm_back(upstream, normed, inverse):
    first_term = jnp.mean(upstream, axis=-1, keepdims=True)
    second_term = normed * jnp.mean(upstream * normed, axis=-1, keepdims=True)
    return inverse * (upstream - first_term - second_term)


def dot(left, right):
    return jnp.dot(left, right, preferred_element_type=F32)


def dot_nt(left, right):
    return lax.dot_general(left, right, (((1,), (1,)), ((), ())), preferred_element_type=F32)


def dot_tn(left, right):
    return lax.dot_general(left, right, (((0,), (0,)), ((), ())), preferred_element_type=F32)


def gelu_pair(values):
    size = jnp.abs(values)
    denominator = 1.0 + size * (0.3275911 * 0.7071067811865476)
    ratio = pl.reciprocal(denominator, approx=True)
    ratio = ratio * (2.0 - denominator * ratio)
    bell = jnp.exp(values * values * (-0.5))
    poly = 0.5 * 1.061405429 * ratio - 0.5 * 1.453152027
    poly = poly * ratio + 0.5 * 1.421413741
    poly = poly * ratio - 0.5 * 0.284496736
    poly = poly * ratio + 0.5 * 0.254829592
    tail = poly * ratio * bell
    below = jnp.where(values >= 0, 1.0 - tail, tail)
    return (values * below, below + values * bell * 0.3989422804014327)


def whole(array):
    rank = len(array.shape)
    return pl.BlockSpec(array.shape, lambda *_: (0,) * rank, pipeline_mode=pl.Buffered(1))


def params(limit):
    return pltpu.CompilerParams(vmem_limit_bytes=limit * MIB)


def cost(flops, nbytes):
    return pl.CostEstimate(flops=int(flops), bytes_accessed=int(nbytes), transcendentals=0)


def call(body, *, scalars, ins, in_specs, outs, out_specs, grid, name, limit, work, scratch=(), after=(), aliases=None):
    first = len(scalars) + len(ins)
    ins = [
        pltpu.with_memory_space_constraint(a, pltpu.HBM)
        if a.size * a.dtype.itemsize >= MIB // 4
        else a
        for a in ins
    ]

    def with_after(*refs):
        body(*refs[:first], *refs[first + len(after) :])

    return pl.pallas_call(
        with_after,
        grid_spec=pltpu.PrefetchScalarGridSpec(
            num_scalar_prefetch=len(scalars),
            grid=grid,
            in_specs=[*in_specs, *[pl.BlockSpec(memory_space=pl.ANY)] * len(after)],
            out_specs=out_specs,
            scratch_shapes=list(scratch),
        ),
        out_shape=outs,
        input_output_aliases=aliases or {},
        compiler_params=params(limit),
        cost_estimate=cost(*work),
        name=name,
    )(*scalars, *ins, *after)


def like(shape, dtype):
    return pltpu.HBM(shape, dtype)


def place(order_ref, target, pieces):
    for j, piece in enumerate(pieces):
        at = pl.multiple_of(order_ref[j] * BLOCK, BLOCK)
        target[pl.ds(at, BLOCK), :] = piece[...]


ANY = pl.BlockSpec(memory_space=pl.ANY)


class Piece:
    def __init__(self, array, row, column):
        self.array, self.row, self.column = array, row, column

    def spec(self, width):
        return pl.BlockSpec(
            (BLOCK, width), lambda *_: (self.row, self.column), pipeline_mode=pl.Buffered(1)
        )

    def view(self, ref, width):
        return ref.at[
            self.row * BLOCK : (self.row + 1) * BLOCK,
            self.column * width : (self.column + 1) * width,
        ]


def arrays(pieces):
    return [piece.array for piece in pieces]


def heads_apart(values, scale=None):
    lane = lax.broadcasted_iota(jnp.int32, values.shape, 1) // HEAD_DIM
    if scale is not None:
        values = values * jnp.asarray(scale, values.dtype)
    zero = jnp.zeros_like(values)
    return jnp.concatenate([jnp.where(lane == h, values, zero) for h in range(GROUP)], axis=0)


def heads_together(values, slots):
    lane = lax.broadcasted_iota(jnp.int32, (slots, GROUP_W), 1) // HEAD_DIM
    out = values[:slots]
    for h in range(1, GROUP):
        out = jnp.where(lane == h, values[h * slots : (h + 1) * slots], out)
    return out


def probs_of(keys, queries_apart, shift):
    scores = dot_nt(keys, queries_apart) + shift
    scores = jnp.exp(scores - jnp.max(scores, axis=0, keepdims=True))
    return scores * (1.0 / jnp.sum(scores, axis=0, keepdims=True))


def key_shift(kept, slots):
    at = lax.broadcasted_iota(jnp.int32, (slots, 1), 0)
    return jnp.where(at < BUF + kept, 0.0, MASKED).astype(F32)


def row_spec(slots, width):
    return pl.BlockSpec((slots, width), lambda i, *_: (i, 0))


def qkv_forward(order, x, wqkv, vec, after, width=512):
    images, slots, _ = x.shape
    rows = images * slots

    def body(order_ref, x_ref, *refs):
        w_refs, (vec_ref, bias_ref, h1_ref, qkv_ref, w_s) = refs[:BLOCKS], refs[BLOCKS:]

        @pl.when(pl.program_id(0) == 0)
        def _():
            for n in range(images):
                normed, _ = normalize(x_ref[n].astype(F32))
                hidden = normed * vec_ref[0:1, :] + vec_ref[1:2, :]
                h1_ref[n * slots : (n + 1) * slots, :] = hidden.astype(BF16)

        place(order_ref, w_s, w_refs)
        qkv_ref[...] = (dot(h1_ref[...], w_s[...]) + bias_ref[...]).astype(BF16)

    bias = jnp.concatenate([vec[2:3], jnp.zeros_like(vec[2:3]), vec[3:4]], axis=1)
    return call(
        body,
        scalars=[order],
        ins=[x, *arrays(wqkv), vec, bias],
        in_specs=[whole(x)]
        + [pl.BlockSpec((BLOCK, width), lambda i, *_, row=w.row: (row, i)) for w in wqkv]
        + [whole(vec), pl.BlockSpec((1, width), lambda i, *_: (0, i))],
        outs=[like((rows, D), BF16), like((rows, 3 * D), BF16)],
        out_specs=[
            pl.BlockSpec((rows, D), lambda i, *_: (0, 0)),
            pl.BlockSpec((rows, width), lambda i, *_: (0, i)),
        ],
        scratch=[pltpu.VMEM((D, width), BF16)],
        grid=(3 * D // width,),
        name="qkv_forward",
        limit=30,
        work=(10 * rows * D * D, 18 * MIB),
        after=after,
    )


def attn_mix(kept, qkv, images, after):
    rows = qkv.shape[0]
    slots = rows // images

    def body(kept_ref, qkv_ref, mixed_ref):
        shift = key_shift(kept_ref[pl.program_id(0)], slots)
        for g in range(HEADS // GROUP):
            at = g * GROUP_W
            q, k, v = (qkv_ref[:, n * D + at : n * D + at + GROUP_W] for n in range(3))
            probs = probs_of(k, heads_apart(q, HEAD_DIM**-0.5), shift).astype(BF16)
            mixed_ref[:, at : at + GROUP_W] = heads_together(dot_tn(probs, v), slots).astype(BF16)

    return call(
        body,
        scalars=[kept],
        ins=[qkv],
        in_specs=[row_spec(slots, 3 * D)],
        outs=[like((rows, D), BF16)],
        out_specs=[row_spec(slots, D)],
        grid=(images,),
        name="attn_mix",
        limit=30,
        work=(14 * rows * D * D, 8 * MIB),
        after=after,
    )[0]


def out_project(order, x, mixed, wo, vec, after):
    images, slots, _ = x.shape
    rows = images * slots

    def body(order_ref, x_ref, mixed_ref, *refs):
        wo_refs, (vec_ref, middle_ref, h2_ref, wo_s) = refs[:BLOCKS], refs[BLOCKS:]

        @pl.when(pl.program_id(0) == 0)
        def _():
            place(order_ref, wo_s, wo_refs)

        branch = dot(mixed_ref[...], wo_s[...]) + vec_ref[4:5, :]
        for n in range(2):
            span = slice(n * slots, (n + 1) * slots)
            middle = x_ref[n].astype(F32) + branch[span]
            middle_ref[span, :] = middle
            normed, _ = normalize(middle)
            h2_ref[span, :] = (normed * vec_ref[5:6, :] + vec_ref[6:7, :]).astype(BF16)

    return call(
        body,
        scalars=[order],
        ins=[x, mixed, *arrays(wo), vec],
        in_specs=[pl.BlockSpec((2, slots, D), lambda i, *_: (i, 0, 0)), row_spec(2 * slots, D)]
        + [w.spec(D) for w in wo]
        + [whole(vec)],
        outs=[like((rows, D), F32), like((rows, D), BF16)],
        out_specs=[row_spec(2 * slots, D)] * 2,
        scratch=[pltpu.VMEM((D, D), BF16)],
        grid=(images // 2,),
        name="out_project",
        limit=30,
        work=(6 * rows * D * D, 12 * MIB),
        after=after,
    )


def mlp_part(order, h2, dm, wup, wdn, bu, after, width=512):
    rows = h2.shape[0]
    weights = [*wup, *wdn]

    def body(order_ref, h2_hbm, dm_hbm, *refs):
        weight_refs, (bu_ref, *outs, gbu_ref) = refs[: 2 * BLOCKS], refs[2 * BLOCKS : -10]
        h2_ref, dm_ref, up_s, dn_s, act_ref, dpre_ref, send, keep, in_sems, out_sems = refs[-10:]
        flying = []

        def put(n, source, index):
            copy = pltpu.make_async_copy(
                source.at[index], outs[n].at[index], out_sems.at[len(flying)]
            )
            copy.start()
            flying.append(copy)

        def fetch(n, source, target, first):
            copies = [pltpu.make_async_copy(source, target, in_sems.at[n])]
            for j in range(BLOCKS):
                at = pl.multiple_of(order_ref[j] * BLOCK, BLOCK)
                copies.append(
                    pltpu.make_async_copy(
                        weights[first + j].view(weight_refs[first + j], PART),
                        (dn_s if first else up_s).at[pl.ds(at, BLOCK), :],
                        in_sems.at[n + 1 + j],
                    )
                )
            for copy in copies:
                copy.start()
            return copies

        def arrive(copies):
            for copy in copies:
                copy.wait()

        ups = fetch(0, h2_hbm, h2_ref, 0)
        dns = fetch(1 + BLOCKS, dm_hbm, dm_ref, BLOCKS)

        def front(n, span):
            if n == 0:
                arrive(ups)
            pre = dot(h2_ref[...], up_s[:, span]) + bu_ref[:, span]
            if n == 0:
                arrive(dns)
            return (pre, dot(dm_ref[...], dn_s[:, span]))

        def middle(span, pre, dact):
            act, slope = gelu_pair(pre)
            act = act.astype(BF16)
            dpre = (dact * slope).astype(BF16)
            act_ref[:, span] = act
            dpre_ref[:, span] = dpre
            gbu_ref[:, span] = jnp.sum(dpre.astype(F32), axis=0, keepdims=True)
            return (act, dpre)

        def back(span, act, dpre):
            for first, left_ref, right in ((0, dm_ref, act), (PART, h2_ref, dpre)):
                there = slice(first + span.start, first + span.stop)
                for j in range(BLOCKS):
                    at = pl.multiple_of(order_ref[j] * BLOCK, BLOCK)
                    grad = dot_tn(left_ref[:, pl.ds(at, BLOCK)], right).astype(BF16)
                    (send if j % 2 else keep)[j // 2, :, there] = grad

        def out(span):
            put(0, act_ref, (slice(None), span))
            put(1, dpre_ref, (slice(None), span))
            for first in (0, PART):
                there = slice(first + span.start, first + span.stop)
                put(2, send, (slice(None), slice(None), there))
                put(3, keep, (slice(None), slice(None), there))

        spans = [slice(at, at + width) for at in range(0, PART, width)]
        fresh = front(0, spans[0])
        held = None
        for n, span in enumerate(spans):
            later = front(n + 1, spans[n + 1]) if n + 1 < len(spans) else None
            now = middle(span, *fresh)
            if held is not None:
                back(spans[n - 1], *held)
                out(spans[n - 1])
            held, fresh = now, later
        back(spans[-1], *held)
        out(spans[-1])
        for copy in flying:
            copy.wait()

    one = pl.BlockSpec((1, PART), lambda i, *_: (0, 0))
    return call(
        body,
        scalars=[order],
        ins=[h2, dm, *arrays(weights), bu],
        in_specs=[ANY] * (2 + len(weights)) + [whole(bu)],
        outs=[like((rows, PART), BF16)] * 2
        + [like((2, BLOCK, 2 * PART), BF16)] * 2
        + [like((1, PART), F32)],
        out_specs=[ANY] * 4 + [one],
        scratch=[pltpu.VMEM((rows, D), BF16)] * 2
        + [pltpu.VMEM((D, PART), BF16)] * 2
        + [pltpu.VMEM((rows, PART), BF16)] * 2
        + [pltpu.VMEM((2, BLOCK, 2 * PART), BF16)] * 2
        + [
            pltpu.SemaphoreType.DMA((2 + 2 * BLOCKS,)),
            pltpu.SemaphoreType.DMA((PART // width * 6,)),
        ],
        grid=(1,),
        name="mlp_part",
        limit=40,
        work=(12 * rows * D * PART, 12 * MIB),
        after=after,
    )


def streamed(order_ref, sides, side_refs, weights, weight_refs, side_s, weight_s, sems, use):
    def copies(p):
        slot = p % 2
        yield pltpu.make_async_copy(side_refs[p], side_s.at[slot], sems.at[slot, BLOCKS])
        for j in range(BLOCKS):
            at = pl.multiple_of(order_ref[j] * BLOCK, BLOCK)
            piece = weights[p][j]
            yield pltpu.make_async_copy(
                piece.view(weight_refs[p * BLOCKS + j], PART),
                weight_s.at[slot, pl.ds(at, BLOCK), :],
                sems.at[slot, j],
            )

    for copy in copies(0):
        copy.start()
    for p in range(PARTS):
        if p + 1 < PARTS:
            for copy in copies(p + 1):
                copy.start()
        for copy in copies(p):
            copy.wait()
        use(p, side_s[p % 2], weight_s[p % 2])


def stream_scratch(rows):
    return [
        pltpu.VMEM((2, rows, PART), BF16),
        pltpu.VMEM((2, D, PART), BF16),
        pltpu.SemaphoreType.DMA((2, BLOCKS + 1)),
        pltpu.VMEM((rows, D), F32),
        pltpu.VMEM((rows, D), F32),
        pltpu.SemaphoreType.DMA((1,)),
    ]


def mlp_back(order, dpres, wups, middle, gy, vec, mixed, after):
    rows = middle.shape[0]
    flat = [w for part in wups for w in part]

    def body(order_ref, *refs):
        dpre_refs, refs = refs[:PARTS], refs[PARTS:]
        up_refs, refs = refs[: PARTS * BLOCKS], refs[PARTS * BLOCKS :]
        middle_ref, gy_ref, vec_ref, mixed_ref, dmid_ref, da_ref, sums_ref, send, keep = refs[:9]
        side_s, weight_s, sems, acc, middle_s, middle_sem = refs[9:]

        def use(p, side, weight):
            if p == 0:
                pltpu.make_async_copy(middle_ref, middle_s, middle_sem.at[0]).start()
                acc[...] = dot_nt(side, weight)
            else:
                acc[...] += dot_nt(side, weight)

        streamed(order_ref, dpres, dpre_refs, wups, up_refs, side_s, weight_s, sems, use)
        pltpu.make_async_copy(middle_ref, middle_s, middle_sem.at[0]).wait()
        gain, shift, bias = (jnp.zeros((1, D), F32) for _ in range(3))
        step = rows // 6
        for r in range(0, rows, step):
            span = slice(r, r + step)
            dh2 = acc[span, :]
            normed, inverse = normalize(middle_s[span, :])
            gain += jnp.sum(dh2 * normed, axis=0, keepdims=True)
            shift += jnp.sum(dh2, axis=0, keepdims=True)
            dmid = norm_back(dh2 * vec_ref[5:6, :], normed, inverse) + gy_ref[span, :].astype(F32)
            dmid_ref[span, :] = dmid
            da = dmid.astype(BF16)
            da_ref[span, :] = da
            bias += jnp.sum(da.astype(F32), axis=0, keepdims=True)
        sums_ref[...] = jnp.concatenate([gain, shift, bias, jnp.zeros((5, D), F32)], axis=0)
        for j in range(BLOCKS):
            at = pl.multiple_of(order_ref[j] * BLOCK, BLOCK)
            grad = dot_tn(mixed_ref[:, pl.ds(at, BLOCK)], da_ref[...]).astype(BF16)
            (send if j % 2 else keep)[j // 2] = grad

    return call(
        body,
        scalars=[order],
        ins=[*dpres, *arrays(flat), middle, gy, vec, mixed],
        in_specs=[ANY] * (PARTS + len(flat) + 1) + [whole(gy), whole(vec), whole(mixed)],
        outs=[like((rows, D), F32), like((rows, D), BF16), like((8, D), F32)]
        + [like((2, BLOCK, D), BF16)] * 2,
        out_specs=[
            pl.BlockSpec((rows, D), lambda i, *_: (0, 0)),
            pl.BlockSpec((rows, D), lambda i, *_: (0, 0)),
            pl.BlockSpec((8, D), lambda i, *_: (0, 0)),
            pl.BlockSpec((2, BLOCK, D), lambda i, *_: (0, 0, 0)),
            pl.BlockSpec((2, BLOCK, D), lambda i, *_: (0, 0, 0)),
        ],
        scratch=stream_scratch(rows),
        grid=(1,),
        name="mlp_back",
        limit=40,
        work=(3 * rows * D * FF, 30 * MIB),
        after=after,
    )


def mlp_out(order, acts, wdns, middle, valid, vec, after):
    rows = middle.shape[0]
    flat = [w for part in wdns for w in part]

    def body(order_ref, *refs):
        act_refs, refs = refs[:PARTS], refs[PARTS:]
        dn_refs, refs = refs[: PARTS * BLOCKS], refs[PARTS * BLOCKS :]
        middle_ref, valid_ref, vec_ref, out_ref = refs[:4]
        side_s, weight_s, sems, acc, middle_s, middle_sem = refs[4:]

        def use(p, side, weight):
            if p == 0:
                pltpu.make_async_copy(middle_ref, middle_s, middle_sem.at[0]).start()
                acc[...] = dot_nt(side, weight)
            elif p + 1 < PARTS:
                acc[...] += dot_nt(side, weight)
            else:
                pltpu.make_async_copy(middle_ref, middle_s, middle_sem.at[0]).wait()
                total = acc[...] + dot_nt(side, weight) + middle_s[...] + vec_ref[7:8, :]
                out_ref[...] = (total * valid_ref[...]).astype(BF16)

        streamed(order_ref, acts, act_refs, wdns, dn_refs, side_s, weight_s, sems, use)

    return call(
        body,
        scalars=[order],
        ins=[*acts, *arrays(flat), middle, valid, vec],
        in_specs=[ANY] * (PARTS + len(flat) + 1) + [whole(valid), whole(vec)],
        outs=[like((rows, D), BF16)],
        out_specs=[pl.BlockSpec((rows, D), lambda i, *_: (0, 0))],
        scratch=stream_scratch(rows),
        grid=(1,),
        name="mlp_out",
        limit=40,
        work=(3 * rows * D * FF, 24 * MIB),
        after=after,
    )[0]


def attn_back(order, kept, da, wo, qkv, slots, first, count, before, after):
    rows = da.shape[0]

    def body(order_ref, kept_ref, da_ref, *refs):
        wo_refs, refs = refs[:BLOCKS], refs[BLOCKS:]
        qkv_ref, dqkv_ref, sums_ref, wo_s = refs[0], *refs[-3:]
        image = pl.program_id(0)

        @pl.when(image == 0)
        def _():
            place(order_ref, wo_s, wo_refs)
            sums_ref[...] = jnp.zeros_like(sums_ref)

        shift = key_shift(kept_ref[first + image], slots)
        da = da_ref[...]
        scale = HEAD_DIM**-0.5
        for g in range(HEADS // GROUP):
            at = g * GROUP_W
            spans = [slice(n * D + at, n * D + at + GROUP_W) for n in range(3)]
            q, k, v = (qkv_ref[:, span] for span in spans)
            dmix = dot_nt(da, wo_s[at : at + GROUP_W, :]).astype(BF16)
            apart = heads_apart(q, scale)
            probs = probs_of(k, apart, shift)
            dmix_apart = heads_apart(dmix)
            dv = dot(probs.astype(BF16), dmix_apart).astype(BF16)
            dprob = dot_nt(v, dmix_apart)
            product = probs * dprob
            dsc = (product - probs * jnp.sum(product, axis=0, keepdims=True)).astype(BF16)
            dk = dot(dsc, apart).astype(BF16)
            dq = (heads_together(dot_tn(dsc, k), slots) * scale).astype(BF16)
            for n, grad in enumerate((dq, dk, dv)):
                dqkv_ref[:, spans[n]] = grad
                if n != 1:
                    sums_ref[n : n + 1, at : at + GROUP_W] += jnp.sum(
                        grad.astype(F32), axis=0, keepdims=True
                    )

    row = lambda width: pl.BlockSpec((slots, width), lambda i, *_: (first + i, 0))
    extra = [] if before is None else [before]
    return call(
        body,
        scalars=[order, kept],
        ins=[da, *arrays(wo), qkv, *extra],
        in_specs=[row(D)]
        + [w.spec(D) for w in wo]
        + [row(3 * D)]
        + [pl.BlockSpec(memory_space=pl.ANY)] * len(extra),
        outs=[like((rows, 3 * D), BF16), like((8, D), F32)],
        out_specs=[row(3 * D), pl.BlockSpec((8, D), lambda i, *_: (0, 0))],
        scratch=[pltpu.VMEM((D, D), BF16)],
        grid=(count,),
        aliases={4 + BLOCKS: 0} if extra else None,
        name="attn_back",
        limit=30,
        work=(12 * rows * D * D, 18 * MIB),
        after=after,
    )


def input_back(order, dqkv, wqkv, x, dmid, vec, after):
    images, slots, _ = x.shape
    rows = images * slots

    def body(order_ref, dqkv_ref, *refs):
        wq_refs = refs[:BLOCKS]
        x_ref, dmid_ref, vec_ref, out_ref, sums_ref, acc = refs[BLOCKS:]

        @pl.when(pl.program_id(0) == 0)
        def _():
            sums_ref[...] = jnp.zeros_like(sums_ref)

        grad = dqkv_ref[...]
        for j in range(BLOCKS):
            at = pl.multiple_of(order_ref[j] * BLOCK, BLOCK)
            acc[:, pl.ds(at, BLOCK)] = dot_nt(grad, wq_refs[j][...])
        for n in range(2):
            dh1 = acc[n * slots : (n + 1) * slots, :]
            normed, inverse = normalize(x_ref[n].astype(F32))
            sums_ref[0:1, :] += jnp.sum(dh1 * normed, axis=0, keepdims=True)
            sums_ref[1:2, :] += jnp.sum(dh1, axis=0, keepdims=True)
            total = norm_back(dh1 * vec_ref[0:1, :], normed, inverse)
            out_ref[n] = (total + dmid_ref[n * slots : (n + 1) * slots, :]).astype(BF16)

    image = pl.BlockSpec((2, slots, D), lambda i, *_: (i, 0, 0))
    return call(
        body,
        scalars=[order],
        ins=[dqkv, *arrays(wqkv), x, dmid, vec],
        in_specs=[row_spec(2 * slots, 3 * D)]
        + [w.spec(3 * D) for w in wqkv]
        + [image, row_spec(2 * slots, D), whole(vec)],
        outs=[like((images, slots, D), BF16), like((8, D), F32)],
        out_specs=[image, pl.BlockSpec((8, D), lambda i, *_: (0, 0))],
        scratch=[pltpu.VMEM((2 * slots, D), F32)],
        grid=(images // 2,),
        name="input_back",
        limit=30,
        work=(8 * rows * D * D, 24 * MIB),
        after=after,
    )


def weight_grad(order, left, right, first, after, columns=D, width=512):
    rows = right.shape[0]
    at_block = first // width

    def body(order_ref, left_ref, right_ref, send, keep):
        for j in range(BLOCKS):
            at = pl.multiple_of(order_ref[j] * BLOCK, BLOCK)
            grad = dot_tn(left_ref[:, pl.ds(at, BLOCK)], right_ref[...]).astype(BF16)
            (send if j % 2 else keep)[j // 2] = grad

    grads = pl.BlockSpec((2, BLOCK, width), lambda i, *_: (0, 0, i))
    return call(
        body,
        scalars=[order],
        ins=[left, right],
        in_specs=[whole(left), pl.BlockSpec((rows, width), lambda i, *_: (0, at_block + i))],
        outs=[like((2, BLOCK, columns), BF16)] * 2,
        out_specs=[grads] * 2,
        grid=(columns // width,),
        name="weight_grad",
        limit=30,
        work=(3 * rows * D * columns, 12 * MIB),
        after=after,
    )


def adam_terms(weight, first_mom, second_mom, gradient, rate, decay):
    first_new = BETA_ONE * first_mom + (1.0 - BETA_ONE) * gradient
    second_new = BETA_TWO * second_mom + (1.0 - BETA_TWO) * gradient * gradient
    first_hat = first_new * (1.0 / (1.0 - BETA_ONE**STEP))
    second_hat = second_new * (1.0 / (1.0 - BETA_TWO**STEP))
    weight_new = weight - rate * (first_hat / (jnp.sqrt(second_hat) + EPS_ADAM) + decay * weight)
    return (gradient, first_new, second_new, weight_new, weight_new.astype(BF16))


def adam_part(total, first, columns, weight, first_mom, second_mom, count, rate, decay, before, after, width=512):
    rows = total.shape[0]
    steps = D // width

    def body(columns_ref, g_ref, w_ref, m_ref, v_ref, *refs):
        gradient = g_ref[...].astype(F32) * (1.0 / count)
        outs = adam_terms(w_ref[...], m_ref[...], v_ref[...], gradient, rate, decay)
        for ref, value in zip(refs[-6:], outs):
            ref[...] = value
        refs[-1][...] = jnp.zeros_like(refs[-1])

    there = pl.BlockSpec((rows, width), lambda i, n, where: (0, where[i] * steps + n))
    shape = weight.shape
    *outs, mark = call(
        body,
        scalars=[jnp.array(columns, jnp.int32)],
        ins=[total, weight, first_mom, second_mom, *before],
        in_specs=[pl.BlockSpec((rows, width), lambda i, n, where: (0, (first + i) * steps + n))]
        + [there] * 3
        + [ANY] * len(before),
        outs=[jax.ShapeDtypeStruct(shape, F32)] * 4
        + [jax.ShapeDtypeStruct(shape, BF16), jax.ShapeDtypeStruct((8, 128), F32)],
        out_specs=[there] * 5 + [pl.BlockSpec((8, 128), lambda i, n, where: (0, 0))],
        grid=(len(columns), steps),
        aliases={5 + n: n for n in range(len(before))},
        name="adam_part",
        limit=30,
        work=(3 * MIB * 1024 * len(columns), 10 * MIB),
        after=after,
    )
    return (outs, mark)


def swap(values, axis, bit):
    size = lax.axis_size(axis)
    return lax.ppermute(values, axis, [(i, i ^ bit) for i in range(size)])


def bits_of(size):
    return [1 << n for n in range(size.bit_length() - 1)]


def beside(bit):
    return "x" if bit == 1 else f"z{bit}"


def added(terms):
    return sum(t.astype(F32) for t in terms).astype(BF16)


class Links:
    def __init__(self):
        self.shards = lax.axis_size("shard")
        self.replicas = lax.axis_size("replica")
        self.direct = self.shards == BLOCKS and self.replicas >= 4
        self.direct = self.direct and self.replicas & (self.replicas - 1) == 0
        index = jnp.arange(BLOCKS, dtype=jnp.int32)
        self.order = index ^ lax.axis_index("shard") if self.direct else index
        self.replica = lax.axis_index("replica")

    def bit(self, bit):
        return (self.replica & bit) != 0

    def place(self, bit):
        return self.bit(bit).astype(jnp.int32)

    def both(self, bit, mine, other, axis):
        return jnp.where(
            self.bit(bit),
            jnp.concatenate([other, mine], axis=axis),
            jnp.concatenate([mine, other], axis=axis),
        )


    def halving(self, terms, bits):
        for bit in bits:
            half = terms[0].shape[1] // 2
            up = self.place(bit)
            piece = lambda at: [lax.dynamic_slice_in_dim(t, at * half, half, 1) for t in terms]
            (got,) = yield [(beside(bit), "replica", bit, added(piece(1 - up)))]
            terms = piece(up) + [got]
        return terms

    def part_steps(self, send, keep, y_first):
        (got,) = yield [("core", "shard", 1, send)]
        terms = [keep, got]
        if y_first:
            (got,) = yield [("y/", "shard", 2, added([t[1] for t in terms]))]
            terms = [t[:1] for t in terms] + [got[None]]
        terms = yield from self.halving(terms, bits_of(self.replicas)[:1])
        return added(terms)

    def chunk_steps(self, parts):
        while not all(part.done for part in parts):
            yield []
        bits = bits_of(self.replicas)
        terms = [jnp.concatenate([part.value for part in parts], axis=2)]
        terms = yield from self.halving(terms, bits[1:])
        if terms[0].shape[0] == 2:
            (got,) = yield [("y", "shard", 2, added([t[1] for t in terms]))]
            terms = [t[0] for t in terms] + [got]
        now = added(terms)
        now = now.reshape(-1, now.shape[-1])
        for bit in reversed(bits):
            (got,) = yield [(beside(bit), "replica", bit, now)]
            now = self.both(bit, now, got, 0)
        return now

    def total_steps(self, values):
        for axis, size in (("shard", self.shards), ("replica", self.replicas)):
            for bit in bits_of(size):
                (got,) = yield [("small", axis, bit, values)]
                values = values + got
        return values

    def small_steps(self, own):
        (got,) = yield [("small", "shard", 1, own)]
        pair = jnp.stack([own, got])
        (got,) = yield [("small", "shard", 2, pair)]
        return jnp.concatenate([pair, got])[self.order]

    def near_steps(self, own):
        (got,) = yield [("core", "shard", 1, own)]
        return got

    def far_steps(self, own):
        (far,) = yield [("y", "shard", 2, own)]
        (behind,) = yield [("core", "shard", 1, far)]
        return (far, behind)

    def shared_steps(self, sent, whole_block):
        (got,) = yield [("y" if whole_block else "y/", "shard", 2, sent)]
        width = got.shape[1] // 2
        mine = [got[:, :width], got[:, width:]]
        other = yield [(beside(1), "replica", 1, mine[0]), (beside(2), "replica", 2, mine[1])]
        if whole_block:
            far = [self.both(bit, m, o, 1) for bit, m, o in zip((1, 2), mine, other)]
            far = [jnp.concatenate(far, axis=1)]
        else:
            far = [
                jnp.concatenate(
                    [
                        jnp.where(self.bit(bit) == (n == 1), m, o)
                        for bit, m, o in zip((1, 2), mine, other)
                    ],
                    axis=1,
                )
                for n in range(2)
            ]
        behind = yield [("core", "shard", 1, f) for f in far]
        return list(zip(far, behind))


LATENCY = 2.0
PACE = {"core": 2.0, "y": 22.5, "x": 22.5, "z2": 22.5, "small": 1.0}
MOST_FLYING = 5


class Flow:
    def __init__(self, steps):
        self.steps, self.value, self.done = steps, None, False
        self.flying, self.parts, self.ready = [], [], 0.0
        self.asked = next(steps)

    def give(self, arrays):
        try:
            self.asked = self.steps.send(arrays)
        except StopIteration as end:
            self.asked, self.value, self.done = [], end.value, True


class Pipeline:
    def __init__(self, token):
        self.now, self.free, self.flows, self.token = 0.0, {}, [], token

    def add(self, steps, urgent=False):
        flow = Flow(steps)
        self.flows.insert(0 if urgent else len(self.flows), flow)
        return flow

    def tie(self, arrays):
        if not arrays:
            return []
        *arrays, self.token = lax.optimization_barrier((*arrays, self.token))
        return arrays

    def turn(self, window=None, slack=1.0, ahead=6.0):
        landed = [f for f in self.flows if f.flying and f.ready <= self.now + slack]
        arrived = [array for flow in landed for array in flow.flying]
        tied = self.tie(arrived)
        for flow in landed:
            got, tied = tied[: len(flow.flying)], tied[len(flow.flying) :]
            flow.flying = []
            if flow.asked[0][0].endswith("/"):
                flow.parts += got
                if flow.asked[0][3].shape[0]:
                    continue
                got, flow.parts = [jnp.concatenate(flow.parts, axis=0)], []
            flow.give(got)
            if flow.done and isinstance(flow.value, jax.Array):
                (flow.value,) = self.tie([flow.value])
        for flow in self.flows:
            if not flow.done and not flow.flying and not flow.asked:
                flow.give([])
        self.flows = [flow for flow in self.flows if not flow.done]
        issued = []
        for flow in self.flows:
            if flow.flying or not flow.asked:
                continue
            count = sum(len(f.flying) for f in self.flows) + len(flow.asked)
            links = [link.strip("/") for link, *_ in flow.asked]
            until = self.now + ahead if window is None else self.now + window - 8.0
            if count > MOST_FLYING or any(self.free.get(k, 0.0) > until for k in links):
                continue
            for n, (link, axis, bit, values) in enumerate(flow.asked):
                if link.endswith("/"):
                    link = link.strip("/")
                    rows = values.shape[0]
                    pace = PACE[link] * values.size * values.dtype.itemsize / MIB / rows
                    busy = max(0.0, self.free.get(link, 0.0) - self.now)
                    room = int(((window or 1000) - LATENCY - busy) / pace + 8) // 16 * 16
                    if rows - room > 16 and window is not None:
                        rows = max(room, 32)
                    flow.asked[n] = (link + "/", axis, bit, values[rows:])
                    values = values[:rows]
                issued.append((flow, len(flow.flying), axis, bit, values))
                flow.flying.append(values)
                size = values.size * values.dtype.itemsize / MIB
                start = max(self.now, self.free.get(link, 0.0))
                self.free[link] = start + size * PACE.get(link, 45.0)
                flow.ready = max(flow.ready, self.free[link] + LATENCY)
        started = {id(flow) for flow, *_ in issued}
        pending = [
            flow for flow in self.flows if not flow.flying and flow.asked and id(flow) not in started
        ]
        pending = [(flow, n) for flow in pending for n in range(len(flow.asked))]
        operands = [values for *_, values in issued] + [f.asked[n][3] for f, n in pending]
        operands = self.tie(operands)
        for (flow, n, axis, bit, _), values in zip(issued, operands):
            flow.flying[n] = swap(values, axis, bit)
        for (flow, n), values in zip(pending, operands[len(issued) :]):
            flow.asked[n] = (*flow.asked[n][:3], values)
        return arrived + [self.token]

    def spend(self, length, token):
        self.now += length
        self.token = token

    def wait(self):
        times = [flow.ready for flow in self.flows if flow.flying]
        return max(0.0, min(times) - self.now) if times else 0.0

    def skip(self, wait=0.0):
        times = [flow.ready for flow in self.flows if flow.flying]
        self.now = max(self.now, min(times) + wait) if times else self.now + 1.0

    def reach(self, flow, link):
        self.turn()
        while flow.asked[0][0] != link:
            self.skip()
            if flow.flying and flow.ready <= self.now + 1.0:
                return
            self.turn()

    def finish(self, *flows, window=None, wait=0.0):
        after = self.turn(window)
        while not all(flow.done for flow in flows):
            self.skip(wait)
            after = self.turn(window)
        return after


def on_device(
    tokens,
    out_grad,
    kept_count,
    attn_w,
    mlp_w,
    vectors,
    attn_m,
    mlp_m,
    small_m,
    attn_v,
    mlp_v,
    small_v,
):
    images, slots, _ = tokens.shape
    rows = images * slots
    links = Links()
    order = links.order
    owned = vectors.shape[0]
    image_total = images * links.replicas * links.shards

    attn_low, mlp_low, wo_low = (a.astype(BF16) for a in (attn_w, mlp_w, attn_w[:, 3 * D :]))
    small_low = jnp.pad(vectors.astype(BF16).T, ((0, 4), (0, 0)))
    at = jnp.arange(slots, dtype=jnp.int32)
    valid = (at[None, :] < (BUF + kept_count)[:, None]).reshape(rows, 1)
    gy = jnp.where(valid, out_grad.reshape(rows, D), jnp.zeros((), BF16))
    pipe = Pipeline(order)
    if links.direct:

        def half(array, first, width, bit):
            return lax.dynamic_slice_in_dim(array, first + links.place(bit) * width, width, 1)

        def halves(array, first, second, width):
            sent = [half(array, first, width, 1), half(array, second, width, 2)]
            return jnp.concatenate(sent, axis=1).astype(BF16)

        pair = 3 * D // 2
        qkv_flow = pipe.add(links.shared_steps(halves(attn_w, 0, pair, pair // 2), True))
        vec_flow = pipe.add(links.small_steps(small_low))
        near_flow = pipe.add(links.near_steps(attn_low))
        sends = [halves(mlp_w, n, FF + n, PART) for n in range(0, FF, 2 * PART)]
        pipe.turn()
        sends[0], sends[1], mlp_low, wo_low, gy = pipe.tie([*sends, mlp_low, wo_low, gy])
        mlp_flows = [pipe.add(links.shared_steps(sends[0], False))]
        wo_flow = pipe.add(links.far_steps(wo_low))
        mlp_flows.append(pipe.add(links.shared_steps(sends[1], False)))
        after = pipe.finish(qkv_flow, vec_flow, near_flow, window=12, wait=3.0)
        attn_near, ((attn_far, behind),) = near_flow.value, qkv_flow.value
        wqkv = [Piece(array, 0, 0) for array in (attn_low, attn_near, attn_far, behind)]
        small_full = vec_flow.value.transpose(1, 0, 2).reshape(16, D)
    else:
        gather = lambda array, axis: lax.all_gather(array, "shard", axis=axis, tiled=True)
        attn_full, mlp_full = gather(attn_low, 0), gather(mlp_low, 0)
        small_full = gather(small_low, 1)
        wqkv = [Piece(attn_full, j, 0) for j in range(BLOCKS)]
        wo = [Piece(attn_full, j, 3) for j in range(BLOCKS)]
        wups = [[Piece(mlp_full, j, p) for j in range(BLOCKS)] for p in range(PARTS)]
        wdns = [[Piece(mlp_full, j, 4 + p) for j in range(BLOCKS)] for p in range(PARTS)]
        after = []
    vec = small_full.astype(F32)

    totals = []

    def summed(send, keep, urgent=False):
        if links.direct:
            return pipe.add(links.part_steps(send, keep, True), urgent)
        return (send, keep)

    def chunk(name, *parts):
        if links.direct:
            totals.append((name, pipe.add(links.chunk_steps(parts), name[0] == "attn")))
            return
        stacked = [jnp.stack([k[0], s[0], k[1], s[1]]).reshape(D, -1) for s, k in parts]
        part = lax.psum_scatter(
            jnp.concatenate(stacked, axis=1), "shard", scatter_dimension=0, tiled=True
        )
        totals.append((name, lax.psum(part, "replica")))

    h1, qkv = qkv_forward(order, tokens, wqkv, vec, after)
    pipe.spend(17, h1)
    if links.direct:
        mlp_near_flow = pipe.add(links.near_steps(mlp_low))
    mixed = attn_mix(kept_count, qkv, images, pipe.turn(17))
    pipe.spend(17, mixed)
    if links.direct:
        after = pipe.finish(wo_flow, window=10)
        wo_far, behind = wo_flow.value
        wo = [Piece(attn_low, 0, 3), Piece(attn_near, 0, 3), Piece(wo_far, 0, 0), Piece(behind, 0, 0)]
    middle, h2 = out_project(order, tokens, mixed, wo, vec, after)
    pipe.spend(10, h2)

    acts, dpres, gbus = [], [], []
    if links.direct:
        wups, wdns = [], []
    for p in range(PARTS):
        if links.direct:
            flow = mlp_flows[p // 2]
            after = pipe.finish(flow, mlp_near_flow, window=17)
            far, behind = flow.value[p % 2]
            near = [(mlp_low, p, 4 + p), (mlp_near_flow.value, p, 4 + p)]
            four = [*near, (far, 0, 1), (behind, 0, 1)]
            wups.append([Piece(array, 0, up) for array, up, _ in four])
            wdns.append([Piece(array, 0, down) for array, _, down in four])
        act, dpre, send, keep, gbu = mlp_part(
            order, h2, gy, wups[p], wdns[p], vec[8 + p : 9 + p], after
        )
        acts.append(act)
        dpres.append(dpre)
        gbus.append(gbu)
        pipe.spend(17, gbu)
        part = summed(send, keep)
        if p % 2:
            chunk(("mlp", 3 + p, p - 1, 4 + p, p), before, part)
        before = part
        if p == 0 and links.direct:
            pipe.reach(part, "y/")
    dmid, da, two_sums, send, keep = mlp_back(
        order, dpres, wups, middle, gy, vec, mixed, pipe.turn(26)
    )
    pipe.spend(26, two_sums)
    out_part = summed(send, keep)

    split = images // 2
    dqkv, sums_a = attn_back(order, kept_count, da, wo, qkv, slots, 0, split, None, pipe.turn(19))
    pipe.spend(19, sums_a)
    dqkv, sums_b = attn_back(
        order, kept_count, da, wo, qkv, slots, split, images - split, dqkv, pipe.turn(19)
    )
    pipe.spend(19, sums_b)
    qkv_sums = sums_a + sums_b
    send, keep = weight_grad(order, h1, dqkv, D, pipe.turn(9), 2 * D)
    pipe.spend(9, send)
    chunk(("attn", 1, 2), summed(send, keep, True))
    send, keep = weight_grad(order, h1, dqkv, 0, pipe.turn(9), D)
    pipe.spend(9, send)
    chunk(("attn", 0, 3), summed(send, keep, True), out_part)
    in_grad, one_sums = input_back(order, dqkv, wqkv, tokens, dmid, vec, pipe.turn(19))
    pipe.spend(19, one_sums)

    g_down = jnp.sum(gy, axis=0, dtype=F32, keepdims=True)
    small = jnp.concatenate(
        [
            one_sums[0:2],
            qkv_sums[0:1],
            qkv_sums[2:3],
            two_sums[2:3],
            two_sums[0:2],
            g_down,
            *gbus,
            jnp.zeros((4, D), F32),
        ],
        axis=0,
    )
    if links.direct:
        totals.append(("small", pipe.add(links.total_steps(small))))
    else:
        totals.append(("small", lax.psum(small, ("replica", "shard"))))
    result = mlp_out(order, acts, wdns, middle, valid.astype(F32), vec, pipe.turn(17))
    pipe.spend(17, result)
    result = result.reshape(images, slots, D)

    outs = {"attn": [], "mlp": []}
    state = {
        "attn": (attn_w, attn_m, attn_v, image_total, 0.1, 0.05),
        "mlp": (mlp_w, mlp_m, mlp_v, image_total, 0.05, 0.05),
    }
    small_out, pieces = None, []
    while totals or pieces:
        after = pipe.turn()
        through = lambda total: not isinstance(total, Flow) or total.done
        for name, total in [entry for entry in totals if through(entry[1])]:
            total = total.value if isinstance(total, Flow) else total
            if name == "small":
                total = lax.dynamic_slice_in_dim(
                    total, lax.axis_index("shard") * owned, owned, 1
                )
                gradient = total[:12].T / image_total
                small_out = adam_terms(vectors, small_m, small_v, gradient, 1.0, 0.0)
                continue
            pieces += [(name[0], total, n, column) for n, column in enumerate(name[1:])]
        totals = [entry for entry in totals if not through(entry[1])]
        wait = pipe.wait() if totals else 1000.0
        kind, total, first, _ = pieces[0] if pieces else (None,) * 4
        columns = [c for k, t, _, c in pieces if t is total][: int((wait + 1.0) / 4.0)]
        if columns:
            outs[kind], mark = adam_part(total, first, columns, *state[kind], outs[kind], after)
            pipe.spend(4.0 * len(columns), mark)
            pieces = pieces[len(columns) :]
        elif totals:
            pipe.skip(1.5)
    attn_out, mlp_out_ = outs["attn"], outs["mlp"]
    return (result, in_grad, *attn_out, *mlp_out_, *small_out)


def solution(mesh):
    tokens = P(("replica", "shard"), None, None)
    owned = P("shard", None)
    in_specs = (tokens, tokens, P(("replica", "shard")), *[owned] * 9)
    out_specs = (tokens, tokens, *[owned] * 15)
    return jax.shard_map(
        on_device, mesh=mesh, in_specs=in_specs, out_specs=out_specs, check_vma=False
    )
```

time: 655 us -> 501 us (0.76)
  waiting for transfers between devices: 221 us -> 93.8 us
  Pallas kernels: 188 us -> 238 us
  local copies, waits for them, and re-layouts: 80.9 us -> 45 us
  starting transfers between devices: 99.8 us -> 68.9 us
  other arithmetic: 58.5 us -> 43.5 us
    ppermute x118 -> x75, waiting for transfers between devices: 221 us -> 93.8 us  [swap(): return lax.ppermute(values, axis, [(i, i ^ bit) for i in range(size)])]
    pallas_call x11 -> x21, Pallas kernels: 188 us -> 238 us  [call(): pl.pallas_call(with_after, grid_spec=pltpu.PrefetchScalarGridSpec(num_sca...]
    unnamed x199 -> x188, local copies, waits for them, and re-layouts: 53.6 us -> 12.7 us
    ppermute x118 -> x75, starting transfers between devices: 99.8 us -> 68.9 us  [swap(): return lax.ppermute(values, axis, [(i, i ^ bit) for i in range(size)])]
    convert_element_type x44 -> x29, other arithmetic: 43.4 us -> 24.1 us  [the longest x25 14.4 us: added(): return sum((t.astype(F32) for t in terms)).astype(BF16)]
    slice x13 -> x33, local copies, waits for them, and re-layouts: 3.3 us -> 21.8 us  [the longest x14 9.41 us: part_steps(): terms = [t[:1] for t in terms] + [got[None]]]
    pallas_call x3 -> x0, local copies, waits for them, and re-layouts: 10.3 us -> none  [attn_forward(): pl.pallas_call(body, grid_spec=pltpu.PrefetchScalarGridSpec(num_scalar_pr...]
    pad x4 -> x0, local copies, waits for them, and re-layouts: 9.14 us -> none  [transposed(): return jnp.pad(values.T, ((0, 0), (0, -rows % 256)))]
  transfers between devices with their start and end apart: 118 -> 75, of which waited for: 41 -> 28; matrix products, arithmetic and copies ran while one was open for 11% -> 8% of each run, Pallas kernels for 16% -> 46%
where the time goes in v2:
time: 501 us; the launch traced here: 492 us
  Pallas kernels  238 us (48%)
  waiting for transfers between devices  93.8 us (19%)
  starting transfers between devices  68.9 us (14%)
  local copies, waits for them, and re-layouts  45 us (9%)
  other arithmetic  43.5 us (9%)
    pallas_call x21, Pallas kernels, call(): pl.pallas_call(with_after, grid_spec=pltpu.PrefetchScalarGridSpec(num_sca...  238 us
    ppermute x75, waiting for transfers between devices, swap(): return lax.ppermute(values, axis, [(i, i ^ bit) for i in range(size)])  93.8 us
    ppermute x75, starting transfers between devices, swap(): return lax.ppermute(values, axis, [(i, i ^ bit) for i in range(size)])  68.9 us
    convert_element_type x25, other arithmetic, added(): return sum((t.astype(F32) for t in terms)).astype(BF16)  14.4 us
    unnamed x188, local copies, waits for them, and re-layouts  12.7 us
  transfers between devices with their start and end apart: 75, of which 28 were waited for; matrix products, arithmetic and copies ran while one was open for 8% of the time, Pallas kernels for 46%

profile of v2, /device:TPU:0, one launch (start us, length us, event | category | flops | bytes accessed | tf_op | source)
XLA Modules:
  0.0 492.4 jit_solution(11997423868139957938)
XLA Ops:
  0.7 2.5 convert_element_type.471.refs_2_.refs_3_
  3.2 2.2 dynamic-slice_convert_fusion.5
  6.9 3.0 collective-permute-start.2
  10.6 2.5 dynamic-slice_convert_fusion.1
  15.0 1.7 bitcast_select_fusion.refs_2_.refs_22_
  17.6 6.0 %convert_element_type.473.refs_3_.refs_7_.refs_5_.refs_9_.refs_13_.refs_17_ = bf16[256,8192]{1,0:T(8,128)(2,1)} convert(f32[256,8192]{1,0:T(8,128)} %refs_2_.12) | non-fusion elementwise | flops 2097152 | bytes 12582912 | tf_op jit(solution)/shard_map/convert_element_type | solution.py:958
  23.7 4.4 collective-permute-done.3
  29.9 1.8 collective-permute-start.6
  34.8 6.9 %collective-permute-done.4 = bf16[256,768]{1,0:T(8,128)(2,1)S(1)} collective-permute-done((bf16[256,768]{1,0:T(8,128)(2,1)S(1)}, bf16[256,768]{1,0:T(8,128)(2,1)S(1)}, u32[]{:S(2)}, u32[]{:S(2)}) %collective-permute-start.4) | collective-permute-done | bytes 393248 | tf_op jit(solution)/shard_map/ppermute | solution.py:700
  45.1 1.9 collective-permute-done.7.refs_5_.refs_8_
  48.2 13.2 %qkv_forward.1 = (bf16[960,1024]{1,0:T(8,128)(2,1)}, bf16[960,3072]{1,0:T(8,128)(2,1)}) custom-call(s32[4]{0:T(128)S(1)} %iota_xor_fusion.refs_0_.refs_9_, bf16[6,160,1024]{2,1,0:T(8,128)(2,1)} %refs_6_.1, bf16[256,4096]{1,0:T(8,128)(2,1)} %copy-done.51, bf16[256,4096]{1,0:T(8,128)(2,1)} %collective-permute-done.1.refs_3_.refs_4_, ...), custom_call_target="tpu_custom_call" | custom-call | flops 10066329600 | bytes 18874368 | tf_op jit(solution)/shard_map/qkv_forward/pallas_call | solution.py:97
  62.3 6.3 %collective-permute-done.9.refs_3_.refs_5_ = bf16[256,1024]{1,0:T(8,128)(2,1)S(1)} collective-permute-done((bf16[256,1024]{1,0:T(8,128)(2,1)S(1)}, bf16[256,1024]{1,0:T(8,128)(2,1)S(1)}, u32[]{:S(2)}, u32[]{:S(2)}) %collective-permute-start.9) | collective-permute-done | bytes 524320 | tf_op jit(solution)/shard_map/ppermute | solution.py:700
  72.0 13.2 %attn_mix.1.refs_2_.refs_12_.refs_24_ = bf16[960,1024]{1,0:T(8,128)(2,1)} custom-call(s32[6]{0:T(128)S(1)} %copy-done.30, bf16[960,3072]{1,0:T(8,128)(2,1)} %get-tuple-element.428.refs_1_.refs_7_, bf16[112,2048]{1,0:T(8,128)(2,1)S(1)} %collective-permute-done.8.refs_2_, bf16[256,1024]{1,0:T(8,128)(2,1)S(1)} %collective-permute-done.9.refs_3_.refs_5_, ...), custom_call_target="tpu_custom_call" | custom-call | flops 14092861440 | bytes 8388608 | tf_op jit(solution)/shard_map/attn_mix/pallas_call | solution.py:97
  85.3 3.2 collective-permute-done.10.refs_8_
  92.3 8.2 %out_project.1 = (f32[960,1024]{1,0:T(8,128)}, bf16[960,1024]{1,0:T(8,128)(2,1)}) custom-call(s32[4]{0:T(128)S(1)} %iota_xor_fusion.refs_0_.refs_9_, bf16[6,160,1024]{2,1,0:T(8,128)(2,1)} %refs_6_.1, bf16[960,1024]{1,0:T(8,128)(2,1)} %attn_mix.1.refs_2_.refs_12_.refs_24_, bf16[256,4096]{1,0:T(8,128)(2,1)} %copy-done.51, ...), custom_call_target="tpu_custom_call" | custom-call | flops 6039797760 | bytes 12582912 | tf_op jit(solution)/shard_map/out_project/pallas_call | solution.py:97
  108.1 15.1 %mlp_part.4 = (bf16[960,1024]{1,0:T(8,128)(2,1)}, bf16[960,1024]{1,0:T(8,128)(2,1)}, bf16[2,256,2048]{2,1,0:T(8,128)(2,1)}, bf16[2,256,2048]{2,1,0:T(8,128)(2,1)}, f32[1,1024]{1,0:T(1,128)}) custom-call(s32[4]{0:T(128)S(1)} %iota_xor_fusion.refs_0_.refs_9_, bf16[960,1024]{1,0:T(8,128)(2,1)} %get-tuple-element.466.refs_1_.refs_14_, ...), custom_call_target="tpu_custom_call" | custom-call | flops 12079595520 | bytes 12582912 | tf_op jit(solution)/shard_map/mlp_part/pallas_call | solution.py:97
  123.6 2.1 copy-done.84
  126.4 5.0 %collective-permute-done.22.refs_6_.refs_10_.refs_16_ = bf16[256,2048]{1,0:T(8,128)(2,1)S(1)} collective-permute-done((bf16[256,2048]{1,0:T(8,128)(2,1)S(1)}, bf16[256,2048]{1,0:T(8,128)(2,1)S(1)}, u32[]{:S(2)}, u32[]{:S(2)}) %collective-permute-start.22) | collective-permute-done | bytes 1048608 | tf_op jit(solution)/shard_map/ppermute | solution.py:700
  134.5 15.5 %mlp_part.5 = (bf16[960,1024]{1,0:T(8,128)(2,1)}, bf16[960,1024]{1,0:T(8,128)(2,1)}, bf16[2,256,2048]{2,1,0:T(8,128)(2,1)}, bf16[2,256,2048]{2,1,0:T(8,128)(2,1)}, f32[1,1024]{1,0:T(1,128)}) custom-call(s32[4]{0:T(128)S(1)} %iota_xor_fusion.refs_0_.refs_9_, bf16[960,1024]{1,0:T(8,128)(2,1)} %get-tuple-element.466.refs_1_.refs_14_, ...), custom_call_target="tpu_custom_call" | custom-call | flops 12079595520 | bytes 12582912 | tf_op jit(solution)/shard_map/mlp_part/pallas_call | solution.py:97
  150.1 1.6 collective-permute-done.24.refs_12_
  154.8 15.3 %mlp_part.6 = (bf16[960,1024]{1,0:T(8,128)(2,1)}, bf16[960,1024]{1,0:T(8,128)(2,1)}, bf16[2,256,2048]{2,1,0:T(8,128)(2,1)}, bf16[2,256,2048]{2,1,0:T(8,128)(2,1)}, f32[1,1024]{1,0:T(1,128)}) custom-call(s32[4]{0:T(128)S(1)} %iota_xor_fusion.refs_0_.refs_9_, bf16[960,1024]{1,0:T(8,128)(2,1)} %get-tuple-element.466.refs_1_.refs_14_, ...), custom_call_target="tpu_custom_call" | custom-call | flops 12079595520 | bytes 12582912 | tf_op jit(solution)/shard_map/mlp_part/pallas_call | solution.py:97
  178.0 15.6 %mlp_part.7 = (bf16[960,1024]{1,0:T(8,128)(2,1)}, bf16[960,1024]{1,0:T(8,128)(2,1)}, bf16[2,256,2048]{2,1,0:T(8,128)(2,1)}, bf16[2,256,2048]{2,1,0:T(8,128)(2,1)}, f32[1,1024]{1,0:T(1,128)}) custom-call(s32[4]{0:T(128)S(1)} %iota_xor_fusion.refs_0_.refs_9_, bf16[960,1024]{1,0:T(8,128)(2,1)} %get-tuple-element.466.refs_1_.refs_14_, ...), custom_call_target="tpu_custom_call" | custom-call | flops 12079595520 | bytes 12582912 | tf_op jit(solution)/shard_map/mlp_part/pallas_call | solution.py:97
  193.7 1.9 slice_bitcast_fusion.6
  205.3 20.9 %mlp_back.1 = (f32[960,1024]{1,0:T(8,128)}, bf16[960,1024]{1,0:T(8,128)(2,1)}, f32[8,1024]{1,0:T(8,128)}, bf16[2,256,1024]{2,1,0:T(8,128)(2,1)}, bf16[2,256,1024]{2,1,0:T(8,128)(2,1)}) custom-call(s32[4]{0:T(128)S(1)} %iota_xor_fusion.refs_0_.refs_9_, bf16[960,1024]{1,0:T(8,128)(2,1)} %get-tuple-element.506.refs_1_, ...), custom_call_target="tpu_custom_call" | custom-call | flops 12079595520 | bytes 31457280 | tf_op jit(solution)/shard_map/mlp_back/pallas_call | solution.py:97
  227.5 2.8 collective-permute-done.30.refs_8_
  230.3 1.6 add_convert_fusion.1
  236.2 14.5 %attn_back.2 = (bf16[960,3072]{1,0:T(8,128)(2,1)}, f32[8,1024]{1,0:T(8,128)}) custom-call(s32[4]{0:T(128)S(1)} %iota_xor_fusion.refs_0_.refs_9_, s32[6]{0:T(128)S(1)} %copy-done.30, bf16[960,1024]{1,0:T(8,128)(2,1)} %get-tuple-element.521.refs_2_, bf16[256,4096]{1,0:T(8,128)(2,1)} %copy-done.51, bf16[256,4096]{1,0:T(8,128)(2,1)} %collective-permute-done.1.refs_3_.refs_4_, ...), custom_call_target="tpu_custom_call" | custom-call | flops 12079595520 | bytes 18874368 | tf_op jit(solution)/shard_map/attn_back/pallas_call | solution.py:97
  252.1 1.8 collective-permute-done.34.refs_10_
  254.9 1.6 collective-permute-start.37
  258.5 14.6 %attn_back.3 = (bf16[960,3072]{1,0:T(8,128)(2,1)}, f32[8,1024]{1,0:T(8,128)}) custom-call(s32[4]{0:T(128)S(1)} %iota_xor_fusion.refs_0_.refs_9_, s32[6]{0:T(128)S(1)} %copy-done.30, bf16[960,1024]{1,0:T(8,128)(2,1)} %get-tuple-element.521.refs_2_, bf16[256,4096]{1,0:T(8,128)(2,1)} %copy-done.51, ...), custom_call_target="tpu_custom_call", output_to_operand_aliasing={{0}: (8, {})} | custom-call | flops 12079595520 | bytes 18874368 | tf_op jit(solution)/shard_map/attn_back/pallas_call | solution.py:97
  277.5 8.6 %weight_grad.2 = (bf16[2,256,2048]{2,1,0:T(8,128)(2,1)}, bf16[2,256,2048]{2,1,0:T(8,128)(2,1)}) custom-call(s32[4]{0:T(128)S(1)} %iota_xor_fusion.refs_0_.refs_9_, bf16[960,1024]{1,0:T(8,128)(2,1)} %get-tuple-element.436.refs_4_.refs_1_, bf16[960,3072]{1,0:T(8,128)(2,1)} %get-tuple-element.549.refs_2_.refs_1_, ...), custom_call_target="tpu_custom_call" | custom-call | flops 6039797760 | bytes 12582912 | tf_op jit(solution)/shard_map/weight_grad/pallas_call | solution.py:97
  287.2 2.0 convert_reduce_fusion
  293.0 2.6 collective-permute-start.42
  296.6 5.9 %weight_grad.3 = (bf16[2,256,1024]{2,1,0:T(8,128)(2,1)}, bf16[2,256,1024]{2,1,0:T(8,128)(2,1)}) custom-call(s32[4]{0:T(128)S(1)} %iota_xor_fusion.refs_0_.refs_9_, bf16[960,1024]{1,0:T(8,128)(2,1)} %get-tuple-element.436.refs_4_.refs_1_, bf16[960,3072]{1,0:T(8,128)(2,1)} %get-tuple-element.549.refs_2_.refs_1_, bf16[160,1024]{1,0:T(8,128)(2,1)S(1)} %copy-done.13, ...), custom_call_target="tpu_custom_call" | custom-call | flops 3019898880 | bytes 12582912 | tf_op jit(solution)/shard_map/weight_grad/pallas_call | solution.py:97
  302.4 1.9 slice.321
  304.3 3.5 collective-permute-done.42.refs_10_
  312.2 2.3 fusion.23
  316.3 3.1 collective-permute-start.47
  320.5 15.0 %input_back.1 = (bf16[6,160,1024]{2,1,0:T(8,128)(2,1)}, f32[8,1024]{1,0:T(8,128)}) custom-call(s32[4]{0:T(128)S(1)} %iota_xor_fusion.refs_0_.refs_9_, bf16[960,3072]{1,0:T(8,128)(2,1)} %get-tuple-element.549.refs_2_.refs_1_, bf16[256,4096]{1,0:T(8,128)(2,1)} %copy-done.51, bf16[256,4096]{1,0:T(8,128)(2,1)} %collective-permute-done.1.refs_3_.refs_4_, ...), custom_call_target="tpu_custom_call" | custom-call | flops 8053063680 | bytes 25165824 | tf_op jit(solution)/shard_map/input_back/pallas_call | solution.py:97
  343.7 1.9 collective-permute-start.52
  345.5 13.6 %mlp_out.1.refs_7_ = bf16[960,1024]{1,0:T(8,128)(2,1)} custom-call(s32[4]{0:T(128)S(1)} %iota_xor_fusion.refs_0_.refs_9_, bf16[960,1024]{1,0:T(8,128)(2,1)} %get-tuple-element.467.refs_1_, bf16[960,1024]{1,0:T(8,128)(2,1)} %get-tuple-element.485.refs_2_, bf16[960,1024]{1,0:T(8,128)(2,1)} %get-tuple-element.492.refs_3_, ...), custom_call_target="tpu_custom_call" | custom-call | flops 12079595520 | bytes 25165824 | tf_op jit(solution)/shard_map/mlp_out/pallas_call | solution.py:97
  360.0 2.2 collective-permute-done.51
  367.2 1.6 collective-permute-done.56
  371.4 2.0 collective-permute-done.57
  374.3 1.8 collective-permute-start.60
  376.0 9.3 %collective-permute-done.60 = f32[16,1024]{1,0:T(8,128)S(1)} collective-permute-done((f32[16,1024]{1,0:T(8,128)S(1)}, f32[16,1024]{1,0:T(8,128)S(1)}, u32[]{:S(2)}, u32[]{:S(2)}) %collective-permute-start.60) | collective-permute-done | bytes 65568 | tf_op jit(solution)/shard_map/ppermute | solution.py:700
  385.5 5.1 %collective-permute-done.61 = f32[16,1024]{1,0:T(8,128)S(1)} collective-permute-done((f32[16,1024]{1,0:T(8,128)S(1)}, f32[16,1024]{1,0:T(8,128)S(1)}, u32[]{:S(2)}, u32[]{:S(2)}) %collective-permute-start.61) | collective-permute-done | bytes 65568 | tf_op jit(solution)/shard_map/ppermute | solution.py:700
  392.0 2.1 collective-permute-start.66
  394.1 3.6 collective-permute-done.62
  399.3 9.8 %collective-permute-done.66 = bf16[64,4096]{1,0:T(8,128)(2,1)S(1)} collective-permute-done((bf16[64,4096]{1,0:T(8,128)(2,1)S(1)}, bf16[64,4096]{1,0:T(8,128)(2,1)S(1)}, u32[]{:S(2)}, u32[]{:S(2)}) %collective-permute-start.66) | collective-permute-done | bytes 524320 | tf_op jit(solution)/shard_map/ppermute | solution.py:700
  409.3 7.7 %collective-permute-done.65.refs_6_ = bf16[128,4096]{1,0:T(8,128)(2,1)S(1)} collective-permute-done((bf16[128,4096]{1,0:T(8,128)(2,1)S(1)}, bf16[128,4096]{1,0:T(8,128)(2,1)S(1)}, u32[]{:S(2)}, u32[]{:S(2)}) %collective-permute-start.65) | collective-permute-done | bytes 1048608 | tf_op jit(solution)/shard_map/ppermute | solution.py:700
  417.0 1.9 maximum_select_fusion.refs_1_
  419.3 2.2 collective-permute-start.67
  421.5 8.3 %adam_part.7 = (f32[256,8192]{1,0:T(8,128)}, f32[256,8192]{1,0:T(8,128)}, f32[256,8192]{1,0:T(8,128)}, f32[256,8192]{1,0:T(8,128)}, bf16[256,8192]{1,0:T(8,128)(2,1)}, /*index=5*/f32[8,128]{1,0:T(8,128)S(1)}) custom-call(s32[2]{0:T(128)S(1)} %copy-done.27, bf16[256,4096]{1,0:T(8,128)(2,1)} %maximum_select_fusion.refs_1_, f32[256,8192]{1,0:T(8,128)} %refs_2_.12, ...), custom_call_target="tpu_custom_call" | custom-call | flops 6442450944 | bytes 10485760 | tf_op jit(solution)/shard_map/adam_part/pallas_call | solution.py:97
  431.5 8.3 %adam_part.8 = (f32[256,8192]{1,0:T(8,128)}, f32[256,8192]{1,0:T(8,128)}, f32[256,8192]{1,0:T(8,128)}, f32[256,8192]{1,0:T(8,128)}, bf16[256,8192]{1,0:T(8,128)(2,1)}, /*index=5*/f32[8,128]{1,0:T(8,128)S(1)}) custom-call(s32[2]{0:T(128)S(1)} %copy-done.25, ...), custom_call_target="tpu_custom_call", output_to_operand_aliasing={{0}: (5, {}), {1}: (6, {}), {2}: (7, {}), {3}: (8, {}), {4}... | custom-call | flops 6442450944 | bytes 10485760 | tf_op jit(solution)/shard_map/adam_part/pallas_call | solution.py:97
  439.9 2.7 collective-permute-start.69
  444.8 4.1 adam_part.9
  449.6 2.4 collective-permute-start.71
  452.0 4.2 adam_part.10
  458.1 5.3 %collective-permute-done.72.refs_10_ = bf16[64,2048]{1,0:T(8,128)(2,1)S(1)} collective-permute-done((bf16[64,2048]{1,0:T(8,128)(2,1)S(1)}, bf16[64,2048]{1,0:T(8,128)(2,1)S(1)}, u32[]{:S(2)}, u32[]{:S(2)}) %collective-permute-start.72) | collective-permute-done | bytes 262176 | tf_op jit(solution)/shard_map/ppermute | solution.py:700
  463.5 1.8 maximum_select_fusion.1.refs_1_
  466.5 11.8 %adam_part.11 = (f32[256,8192]{1,0:T(8,128)}, f32[256,8192]{1,0:T(8,128)}, f32[256,8192]{1,0:T(8,128)}, f32[256,8192]{1,0:T(8,128)}, bf16[256,8192]{1,0:T(8,128)(2,1)}, /*index=5*/f32[8,128]{1,0:T(8,128)S(1)}) custom-call(s32[3]{0:T(128)S(1)} %copy-done.24, ...), custom_call_target="tpu_custom_call", output_to_operand_aliasing={{0}: (5, {}), {1}: (6, {}), {2}: (7, {}), {3}: (8, {}), {4}... | custom-call | flops 9663676416 | bytes 10485760 | tf_op jit(solution)/shard_map/adam_part/pallas_call | solution.py:97
  479.6 4.2 adam_part.12
  483.7 8.3 %adam_part.13 = (f32[256,4096]{1,0:T(8,128)}, f32[256,4096]{1,0:T(8,128)}, f32[256,4096]{1,0:T(8,128)}, f32[256,4096]{1,0:T(8,128)}, bf16[256,4096]{1,0:T(8,128)(2,1)}, /*index=5*/f32[8,128]{1,0:T(8,128)}) custom-call(s32[2]{0:T(128)S(1)} %copy-done.26, ...), custom_call_target="tpu_custom_call", output_to_operand_aliasing={{0}: (5, {}), {1}: (6, {}), {2}: (7, {}), {3}: (8, {}), {4}... | custom-call | flops 6442450944 | bytes 10485760 | tf_op jit(solution)/shard_map/adam_part/pallas_call | solution.py:97
  (432 shorter events, 111.1 us)
Async XLA Ops:
  6.4 17.2 %collective-permute-start.1 = (bf16[256,4096]{1,0:T(8,128)(2,1)S(1)}, bf16[256,4096]{1,0:T(8,128)(2,1)}, u32[]{:S(2)}, u32[]{:S(2)}) collective-permute-start(bf16[256,4096]{1,0:T(8,128)(2,1)S(1)} %convert_element_type.471.refs_2_.refs_3_), channel_id=1, source_target_pairs={{0,1},{1,0},{2,3},{3,2},{4,5},{5,4},{6,7},{7,6},{8,9},{9,8},{10,11... | collective-permute-start | bytes 6291464 | tf_op jit(solution)/shard_map/ppermute | solution.py:700
  6.8 16.7 %collective-permute-start = (bf16[16,256]{1,0:T(8,128)(2,1)S(1)}, bf16[16,256]{1,0:T(8,128)(2,1)S(1)}, u32[]{:S(2)}, u32[]{:S(2)}) collective-permute-start(bf16[16,256]{1,0:T(8,128)(2,1)S(1)} %get-tuple-element.380), channel_id=1, source_target_pairs={{0,1},{1,0},{2,3},{3,2},{4,5},{5,4},{6,7},{7,6},{8,9},{9,8},{10,11... | collective-permute-start | bytes 24584 | tf_op jit(solution)/shard_map/ppermute | solution.py:700
  6.9 21.9 %collective-permute-start.2 = (bf16[256,1536]{1,0:T(8,128)(2,1)}, bf16[256,1536]{1,0:T(8,128)(2,1)}, u32[]{:S(2)}, u32[]{:S(2)}) collective-permute-start(bf16[256,1536]{1,0:T(8,128)(2,1)} %pad_maximum_fusion.7), channel_id=1, source_target_pairs={{0,2},{1,3},{2,0},{3,1},{4,6},{5,7},{6,4},{7,5},{8,10},{9,11},{10,... | collective-permute-start | bytes 2359304 | tf_op jit(solution)/shard_map/ppermute | solution.py:700
  29.9 13.0 %collective-permute-start.6 = (bf16[112,2048]{1,0:T(8,128)(2,1)S(1)}, bf16[112,2048]{1,0:T(8,128)(2,1)S(1)}, u32[]{:S(2)}, u32[]{:S(2)}) collective-permute-start(bf16[112,2048]{1,0:T(8,128)(2,1)S(1)} %get-tuple-element.413), channel_id=1, source_target_pairs={{0,2},{1,3},{2,0},{3,1},{4,6},{5,7},{6,4},{7,5},{8,10},{9,11},{10,... | collective-permute-start | bytes 1376264 | tf_op jit(solution)/shard_map/ppermute | solution.py:700
  31.7 10.0 %collective-permute-start.4 = (bf16[256,768]{1,0:T(8,128)(2,1)S(1)}, bf16[256,768]{1,0:T(8,128)(2,1)S(1)}, u32[]{:S(2)}, u32[]{:S(2)}) collective-permute-start(bf16[256,768]{1,0:T(8,128)(2,1)S(1)} %get-tuple-element.411), channel_id=1, source_target_pairs={{0,4},{4,0},{8,12},{12,8},{16,20},{20,16},{24,28},{28,24},{1,5},{5... | collective-permute-start | bytes 1179656 | tf_op jit(solution)/shard_map/ppermute | solution.py:700
  33.2 9.7 %collective-permute-start.5 = (bf16[256,768]{1,0:T(8,128)(2,1)S(1)}, bf16[256,768]{1,0:T(8,128)(2,1)S(1)}, u32[]{:S(2)}, u32[]{:S(2)}) collective-permute-start(bf16[256,768]{1,0:T(8,128)(2,1)S(1)} %get-tuple-element.412), channel_id=1, source_target_pairs={{0,8},{4,12},{8,0},{12,4},{16,24},{20,28},{24,16},{28,20},{1,9},{5... | collective-permute-start | bytes 1179656 | tf_op jit(solution)/shard_map/ppermute | solution.py:700
  44.5 17.7 %collective-permute-start.8 = (bf16[112,2048]{1,0:T(8,128)(2,1)S(1)}, bf16[112,2048]{1,0:T(8,128)(2,1)S(1)}, u32[]{:S(2)}, u32[]{:S(2)}) collective-permute-start(bf16[112,2048]{1,0:T(8,128)(2,1)S(1)} %get-tuple-element.429), channel_id=1, source_target_pairs={{0,2},{1,3},{2,0},{3,1},{4,6},{5,7},{6,4},{7,5},{8,10},{9,11},{10,... | collective-permute-start | bytes 1376264 | tf_op jit(solution)/shard_map/ppermute | solution.py:700
  47.0 21.6 %collective-permute-start.9 = (bf16[256,1024]{1,0:T(8,128)(2,1)S(1)}, bf16[256,1024]{1,0:T(8,128)(2,1)S(1)}, u32[]{:S(2)}, u32[]{:S(2)}) collective-permute-start(bf16[256,1024]{1,0:T(8,128)(2,1)S(1)} %copy-done.76), channel_id=1, source_target_pairs={{0,2},{1,3},{2,0},{3,1},{4,6},{5,7},{6,4},{7,5},{8,10},{9,11},{10,... | collective-permute-start | bytes 1572872 | tf_op jit(solution)/shard_map/ppermute | solution.py:700
  68.6 19.9 %collective-permute-start.13 = (bf16[256,8192]{1,0:T(8,128)(2,1)}, bf16[256,8192]{1,0:T(8,128)(2,1)}, u32[]{:S(2)}, u32[]{:S(2)}) collective-permute-start(bf16[256,8192]{1,0:T(8,128)(2,1)} %convert_element_type.473.refs_3_.refs_7_.refs_5_.refs_9_.refs_13_.refs_17_), channel_id=1, source_target_pairs={{0,1},{1,0},{2,3},{3,2},{4,5},{5,4},{6,7},{7,6},{8,9},{9,8},{10,11... | collective-permute-start | bytes 12582920 | tf_op jit(solution)/shard_map/ppermute | solution.py:700
  69.9 18.7 %collective-permute-start.12 = (bf16[144,2048]{1,0:T(8,128)(2,1)}, bf16[144,2048]{1,0:T(8,128)(2,1)S(1)}, u32[]{:S(2)}, u32[]{:S(2)}) collective-permute-start(bf16[144,2048]{1,0:T(8,128)(2,1)} %slice.254), channel_id=1, source_target_pairs={{0,2},{1,3},{2,0},{3,1},{4,6},{5,7},{6,4},{7,5},{8,10},{9,11},{10,... | collective-permute-start | bytes 1769480 | tf_op jit(solution)/shard_map/ppermute | solution.py:700
  70.4 18.1 %collective-permute-start.11 = (bf16[256,1024]{1,0:T(8,128)(2,1)S(1)}, bf16[256,1024]{1,0:T(8,128)(2,1)S(1)}, u32[]{:S(2)}, u32[]{:S(2)}) collective-permute-start(bf16[256,1024]{1,0:T(8,128)(2,1)S(1)} %collective-permute-done.9.refs_3_.refs_5_), channel_id=1, source_target_pairs={{0,1},{1,0},{2,3},{3,2},{4,5},{5,4},{6,7},{7,6},{8,9},{9,8},{10,11... | collective-permute-start | bytes 1572872 | tf_op jit(solution)/shard_map/ppermute | solution.py:700
  70.5 18.0 %collective-permute-start.10 = (bf16[32,2048]{1,0:T(8,128)(2,1)}, bf16[32,2048]{1,0:T(8,128)(2,1)S(1)}, u32[]{:S(2)}, u32[]{:S(2)}) collective-permute-start(bf16[32,2048]{1,0:T(8,128)(2,1)} %slice.253), channel_id=1, source_target_pairs={{0,2},{1,3},{2,0},{3,1},{4,6},{5,7},{6,4},{7,5},{8,10},{9,11},{10,... | collective-permute-start | bytes 393224 | tf_op jit(solution)/shard_map/ppermute | solution.py:700
  88.7 12.0 %collective-permute-start.16 = (bf16[112,2048]{1,0:T(8,128)(2,1)S(1)}, bf16[112,2048]{1,0:T(8,128)(2,1)S(1)}, u32[]{:S(2)}, u32[]{:S(2)}) collective-permute-start(bf16[112,2048]{1,0:T(8,128)(2,1)S(1)} %slice.257), channel_id=1, source_target_pairs={{0,2},{1,3},{2,0},{3,1},{4,6},{5,7},{6,4},{7,5},{8,10},{9,11},{10,... | collective-permute-start | bytes 1376264 | tf_op jit(solution)/shard_map/ppermute | solution.py:700
  89.2 13.1 %collective-permute-start.14 = (bf16[256,1024]{1,0:T(8,128)(2,1)S(1)}, bf16[256,1024]{1,0:T(8,128)(2,1)S(1)}, u32[]{:S(2)}, u32[]{:S(2)}) collective-permute-start(bf16[256,1024]{1,0:T(8,128)(2,1)S(1)} %get-tuple-element.452), channel_id=1, source_target_pairs={{0,4},{4,0},{8,12},{12,8},{16,20},{20,16},{24,28},{28,24},{1,5},{5... | collective-permute-start | bytes 1572872 | tf_op jit(solution)/shard_map/ppermute | solution.py:700
  90.7 12.8 %collective-permute-start.15 = (bf16[256,1024]{1,0:T(8,128)(2,1)S(1)}, bf16[256,1024]{1,0:T(8,128)(2,1)S(1)}, u32[]{:S(2)}, u32[]{:S(2)}) collective-permute-start(bf16[256,1024]{1,0:T(8,128)(2,1)S(1)} %get-tuple-element.453), channel_id=1, source_target_pairs={{0,8},{4,12},{8,0},{12,4},{16,24},{20,28},{24,16},{28,20},{1,9},{5... | collective-permute-start | bytes 1572872 | tf_op jit(solution)/shard_map/ppermute | solution.py:700
  104.4 18.8 %collective-permute-start.19 = (bf16[256,1024]{1,0:T(8,128)(2,1)S(1)}, bf16[256,1024]{1,0:T(8,128)(2,1)S(1)}, u32[]{:S(2)}, u32[]{:S(2)}) collective-permute-start(bf16[256,1024]{1,0:T(8,128)(2,1)S(1)} %get-tuple-element.469), channel_id=1, source_target_pairs={{0,4},{4,0},{8,12},{12,8},{16,20},{20,16},{24,28},{28,24},{1,5},{5... | collective-permute-start | bytes 1572872 | tf_op jit(solution)/shard_map/ppermute | solution.py:700
  105.0 18.2 %collective-permute-start.20 = (bf16[256,1024]{1,0:T(8,128)(2,1)S(1)}, bf16[256,1024]{1,0:T(8,128)(2,1)S(1)}, u32[]{:S(2)}, u32[]{:S(2)}) collective-permute-start(bf16[256,1024]{1,0:T(8,128)(2,1)S(1)} %get-tuple-element.470), channel_id=1, source_target_pairs={{0,8},{4,12},{8,0},{12,4},{16,24},{20,28},{24,16},{28,20},{1,9},{5... | collective-permute-start | bytes 1572872 | tf_op jit(solution)/shard_map/ppermute | solution.py:700
  125.7 7.2 %collective-permute-start.21 = (bf16[2,256,2048]{2,1,0:T(8,128)(2,1)S(1)}, bf16[2,256,2048]{2,1,0:T(8,128)(2,1)S(1)}, u32[]{:S(2)}, u32[]{:S(2)}) collective-permute-start(bf16[2,256,2048]{2,1,0:T(8,128)(2,1)S(1)} %copy-done.84), channel_id=1, source_target_pairs={{0,1},{1,0},{2,3},{3,2},{4,5},{5,4},{6,7},{7,6},{8,9},{9,8},{10,11... | collective-permute-start | bytes 6291464 | tf_op jit(solution)/shard_map/ppermute | solution.py:700
  133.4 18.3 %collective-permute-start.24 = (bf16[176,2048]{1,0:T(8,128)(2,1)S(1)}, bf16[176,2048]{1,0:T(8,128)(2,1)S(1)}, u32[]{:S(2)}, u32[]{:S(2)}) collective-permute-start(bf16[176,2048]{1,0:T(8,128)(2,1)S(1)} %slice_bitcast_fusion.3), channel_id=1, source_target_pairs={{0,2},{1,3},{2,0},{3,1},{4,6},{5,7},{6,4},{7,5},{8,10},{9,11},{10,... | collective-permute-start | bytes 2162696 | tf_op jit(solution)/shard_map/ppermute | solution.py:700
  151.7 18.5 %collective-permute-start.26 = (bf16[2,256,2048]{2,1,0:T(8,128)(2,1)}, bf16[2,256,2048]{2,1,0:T(8,128)(2,1)S(1)}, u32[]{:S(2)}, u32[]{:S(2)}) collective-permute-start(bf16[2,256,2048]{2,1,0:T(8,128)(2,1)} %get-tuple-element.495), channel_id=1, source_target_pairs={{0,1},{1,0},{2,3},{3,2},{4,5},{5,4},{6,7},{7,6},{8,9},{9,8},{10,11... | collective-permute-start | bytes 6291464 | tf_op jit(solution)/shard_map/ppermute | solution.py:700
  153.7 16.5 %collective-permute-start.25 = (bf16[80,2048]{1,0:T(8,128)(2,1)S(1)}, bf16[80,2048]{1,0:T(8,128)(2,1)S(1)}, u32[]{:S(2)}, u32[]{:S(2)}) collective-permute-start(bf16[80,2048]{1,0:T(8,128)(2,1)S(1)} %slice_bitcast_fusion.7), channel_id=1, source_target_pairs={{0,2},{1,3},{2,0},{3,1},{4,6},{5,7},{6,4},{7,5},{8,10},{9,11},{10,... | collective-permute-start | bytes 983048 | tf_op jit(solution)/shard_map/ppermute | solution.py:700
  173.2 22.3 %collective-permute-start.29 = (bf16[2,256,2048]{2,1,0:T(8,128)(2,1)}, bf16[2,256,2048]{2,1,0:T(8,128)(2,1)S(1)}, u32[]{:S(2)}, u32[]{:S(2)}) collective-permute-start(bf16[2,256,2048]{2,1,0:T(8,128)(2,1)} %get-tuple-element.512), channel_id=1, source_target_pairs={{0,1},{1,0},{2,3},{3,2},{4,5},{5,4},{6,7},{7,6},{8,9},{9,8},{10,11... | collective-permute-start | bytes 6291464 | tf_op jit(solution)/shard_map/ppermute | solution.py:700
  173.5 22.1 %collective-permute-start.28 = (bf16[176,2048]{1,0:T(8,128)(2,1)}, bf16[176,2048]{1,0:T(8,128)(2,1)S(1)}, u32[]{:S(2)}, u32[]{:S(2)}) collective-permute-start(bf16[176,2048]{1,0:T(8,128)(2,1)} %slice_bitcast_fusion.2), channel_id=1, source_target_pairs={{0,2},{1,3},{2,0},{3,1},{4,6},{5,7},{6,4},{7,5},{8,10},{9,11},{10,... | collective-permute-start | bytes 2162696 | tf_op jit(solution)/shard_map/ppermute | solution.py:700
  174.5 21.0 %collective-permute-start.27 = (bf16[1,128,2048]{2,1,0:T(8,128)(2,1)}, bf16[1,128,2048]{2,1,0:T(8,128)(2,1)S(1)}, u32[]{:S(2)}, u32[]{:S(2)}) collective-permute-start(bf16[1,128,2048]{2,1,0:T(8,128)(2,1)} %fusion.14), channel_id=1, source_target_pairs={{0,4},{4,0},{8,12},{12,8},{16,20},{20,16},{24,28},{28,24},{1,5},{5... | collective-permute-start | bytes 1572872 | tf_op jit(solution)/shard_map/ppermute | solution.py:700
  199.0 31.2 %collective-permute-start.32 = (bf16[2,256,2048]{2,1,0:T(8,128)(2,1)}, bf16[2,256,2048]{2,1,0:T(8,128)(2,1)}, u32[]{:S(2)}, u32[]{:S(2)}) collective-permute-start(bf16[2,256,2048]{2,1,0:T(8,128)(2,1)} %get-tuple-element.524), channel_id=1, source_target_pairs={{0,1},{1,0},{2,3},{3,2},{4,5},{5,4},{6,7},{7,6},{8,9},{9,8},{10,11... | collective-permute-start | bytes 6291464 | tf_op jit(solution)/shard_map/ppermute | solution.py:700
  203.3 27.0 %collective-permute-start.31 = (bf16[192,2048]{1,0:T(8,128)(2,1)S(1)}, bf16[192,2048]{1,0:T(8,128)(2,1)S(1)}, u32[]{:S(2)}, u32[]{:S(2)}) collective-permute-start(bf16[192,2048]{1,0:T(8,128)(2,1)S(1)} %copy-done.74), channel_id=1, source_target_pairs={{0,2},{1,3},{2,0},{3,1},{4,6},{5,7},{6,4},{7,5},{8,10},{9,11},{10,... | collective-permute-start | bytes 2359304 | tf_op jit(solution)/shard_map/ppermute | solution.py:700
  204.4 25.9 %collective-permute-start.30 = (bf16[80,2048]{1,0:T(8,128)(2,1)S(1)}, bf16[80,2048]{1,0:T(8,128)(2,1)S(1)}, u32[]{:S(2)}, u32[]{:S(2)}) collective-permute-start(bf16[80,2048]{1,0:T(8,128)(2,1)S(1)} %copy-done.77), channel_id=1, source_target_pairs={{0,2},{1,3},{2,0},{3,1},{4,6},{5,7},{6,4},{7,5},{8,10},{9,11},{10,... | collective-permute-start | bytes 983048 | tf_op jit(solution)/shard_map/ppermute | solution.py:700
  233.1 20.7 %collective-permute-start.36 = (bf16[2,256,1024]{2,1,0:T(8,128)(2,1)S(1)}, bf16[2,256,1024]{2,1,0:T(8,128)(2,1)S(1)}, u32[]{:S(2)}, u32[]{:S(2)}) collective-permute-start(bf16[2,256,1024]{2,1,0:T(8,128)(2,1)S(1)} %copy-done.86), channel_id=1, source_target_pairs={{0,1},{1,0},{2,3},{3,2},{4,5},{5,4},{6,7},{7,6},{8,9},{9,8},{10,11... | collective-permute-start | bytes 3145736 | tf_op jit(solution)/shard_map/ppermute | solution.py:700
  233.1 20.7 %collective-permute-start.33 = (bf16[1,128,2048]{2,1,0:T(8,128)(2,1)S(1)}, bf16[1,128,2048]{2,1,0:T(8,128)(2,1)S(1)}, u32[]{:S(2)}, u32[]{:S(2)}) collective-permute-start(bf16[1,128,2048]{2,1,0:T(8,128)(2,1)S(1)} %fusion.11), channel_id=1, source_target_pairs={{0,4},{4,0},{8,12},{12,8},{16,20},{20,16},{24,28},{28,24},{1,5},{5... | collective-permute-start | bytes 1572872 | tf_op jit(solution)/shard_map/ppermute | solution.py:700
  234.2 19.7 %collective-permute-start.35 = (bf16[128,2048]{1,0:T(8,128)(2,1)S(1)}, bf16[128,2048]{1,0:T(8,128)(2,1)S(1)}, u32[]{:S(2)}, u32[]{:S(2)}) collective-permute-start(bf16[128,2048]{1,0:T(8,128)(2,1)S(1)} %get-tuple-element.536), channel_id=1, source_target_pairs={{0,2},{1,3},{2,0},{3,1},{4,6},{5,7},{6,4},{7,5},{8,10},{9,11},{10,... | collective-permute-start | bytes 1572872 | tf_op jit(solution)/shard_map/ppermute | solution.py:700
  235.1 18.7 %collective-permute-start.34 = (bf16[64,2048]{1,0:T(8,128)(2,1)S(1)}, bf16[64,2048]{1,0:T(8,128)(2,1)S(1)}, u32[]{:S(2)}, u32[]{:S(2)}) collective-permute-start(bf16[64,2048]{1,0:T(8,128)(2,1)S(1)} %slice_bitcast_fusion.9), channel_id=1, source_target_pairs={{0,2},{1,3},{2,0},{3,1},{4,6},{5,7},{6,4},{7,5},{8,10},{9,11},{10,... | collective-permute-start | bytes 786440 | tf_op jit(solution)/shard_map/ppermute | solution.py:700
  254.9 18.4 %collective-permute-start.37 = (bf16[1,64,4096]{2,1,0:T(8,128)(2,1)S(1)}, bf16[1,64,4096]{2,1,0:T(8,128)(2,1)S(1)}, u32[]{:S(2)}, u32[]{:S(2)}) collective-permute-start(bf16[1,64,4096]{2,1,0:T(8,128)(2,1)S(1)} %constant_dynamic-slice_fusion.3), channel_id=1, source_target_pairs={{0,8},{4,12},{8,0},{12,4},{16,24},{20,28},{24,16},{28,20},{1,9},{5... | collective-permute-start | bytes 1572872 | tf_op jit(solution)/shard_map/ppermute | solution.py:700
  256.5 16.8 %collective-permute-start.38 = (bf16[1,128,2048]{2,1,0:T(8,128)(2,1)S(1)}, bf16[1,128,2048]{2,1,0:T(8,128)(2,1)S(1)}, u32[]{:S(2)}, u32[]{:S(2)}) collective-permute-start(bf16[1,128,2048]{2,1,0:T(8,128)(2,1)S(1)} %fusion.8), channel_id=1, source_target_pairs={{0,4},{4,0},{8,12},{12,8},{16,20},{20,16},{24,28},{28,24},{1,5},{5... | collective-permute-start | bytes 1572872 | tf_op jit(solution)/shard_map/ppermute | solution.py:700
  257.4 15.9 %collective-permute-start.39 = (bf16[128,2048]{1,0:T(8,128)(2,1)S(1)}, bf16[128,2048]{1,0:T(8,128)(2,1)S(1)}, u32[]{:S(2)}, u32[]{:S(2)}) collective-permute-start(bf16[128,2048]{1,0:T(8,128)(2,1)S(1)} %get-tuple-element.552), channel_id=1, source_target_pairs={{0,2},{1,3},{2,0},{3,1},{4,6},{5,7},{6,4},{7,5},{8,10},{9,11},{10,... | collective-permute-start | bytes 1572872 | tf_op jit(solution)/shard_map/ppermute | solution.py:700
  276.5 9.6 %collective-permute-start.40 = (bf16[160,1024]{1,0:T(8,128)(2,1)S(1)}, bf16[160,1024]{1,0:T(8,128)(2,1)S(1)}, u32[]{:S(2)}, u32[]{:S(2)}) collective-permute-start(bf16[160,1024]{1,0:T(8,128)(2,1)S(1)} %slice.302), channel_id=1, source_target_pairs={{0,2},{1,3},{2,0},{3,1},{4,6},{5,7},{6,4},{7,5},{8,10},{9,11},{10,... | collective-permute-start | bytes 983048 | tf_op jit(solution)/shard_map/ppermute | solution.py:700
  286.8 21.0 %collective-permute-start.41 = (bf16[2,256,2048]{2,1,0:T(8,128)(2,1)}, bf16[2,256,2048]{2,1,0:T(8,128)(2,1)S(1)}, u32[]{:S(2)}, u32[]{:S(2)}) collective-permute-start(bf16[2,256,2048]{2,1,0:T(8,128)(2,1)} %get-tuple-element.568.refs_4_), channel_id=1, source_target_pairs={{0,1},{1,0},{2,3},{3,2},{4,5},{5,4},{6,7},{7,6},{8,9},{9,8},{10,11... | collective-permute-start | bytes 6291464 | tf_op jit(solution)/shard_map/ppermute | solution.py:700
  291.9 15.9 %collective-permute-start.43 = (bf16[1,128,2048]{2,1,0:T(8,128)(2,1)S(1)}, bf16[1,128,2048]{2,1,0:T(8,128)(2,1)S(1)}, u32[]{:S(2)}, u32[]{:S(2)}) collective-permute-start(bf16[1,128,2048]{2,1,0:T(8,128)(2,1)S(1)} %copy-done.75), channel_id=1, source_target_pairs={{0,4},{4,0},{8,12},{12,8},{16,20},{20,16},{24,28},{28,24},{1,5},{5... | collective-permute-start | bytes 1572872 | tf_op jit(solution)/shard_map/ppermute | solution.py:700
  293.0 14.8 %collective-permute-start.42 = (bf16[1,32,4096]{2,1,0:T(8,128)(2,1)S(1)}, bf16[1,32,4096]{2,1,0:T(8,128)(2,1)S(1)}, u32[]{:S(2)}, u32[]{:S(2)}) collective-permute-start(bf16[1,32,4096]{2,1,0:T(8,128)(2,1)S(1)} %copy-done.78), channel_id=1, source_target_pairs={{0,16},{4,20},{8,24},{12,28},{16,0},{20,4},{24,8},{28,12},{1,17},{... | collective-permute-start | bytes 786440 | tf_op jit(solution)/shard_map/ppermute | solution.py:700
  295.7 12.2 %collective-permute-start.44 = (bf16[96,1024]{1,0:T(8,128)(2,1)S(1)}, bf16[96,1024]{1,0:T(8,128)(2,1)S(1)}, u32[]{:S(2)}, u32[]{:S(2)}) collective-permute-start(bf16[96,1024]{1,0:T(8,128)(2,1)S(1)} %slice.303), channel_id=1, source_target_pairs={{0,2},{1,3},{2,0},{3,1},{4,6},{5,7},{6,4},{7,5},{8,10},{9,11},{10,... | collective-permute-start | bytes 589832 | tf_op jit(solution)/shard_map/ppermute | solution.py:700
  315.4 23.5 %collective-permute-start.45 = (bf16[2,256,1024]{2,1,0:T(8,128)(2,1)}, bf16[2,256,1024]{2,1,0:T(8,128)(2,1)S(1)}, u32[]{:S(2)}, u32[]{:S(2)}) collective-permute-start(bf16[2,256,1024]{2,1,0:T(8,128)(2,1)} %get-tuple-element.588.refs_13_), channel_id=1, source_target_pairs={{0,1},{1,0},{2,3},{3,2},{4,5},{5,4},{6,7},{7,6},{8,9},{9,8},{10,11... | collective-permute-start | bytes 3145736 | tf_op jit(solution)/shard_map/ppermute | solution.py:700
  315.4 23.4 %collective-permute-start.46 = (bf16[192,2048]{1,0:T(8,128)(2,1)}, bf16[192,2048]{1,0:T(8,128)(2,1)S(1)}, u32[]{:S(2)}, u32[]{:S(2)}) collective-permute-start(bf16[192,2048]{1,0:T(8,128)(2,1)} %slice_bitcast_fusion), channel_id=1, source_target_pairs={{0,2},{1,3},{2,0},{3,1},{4,6},{5,7},{6,4},{7,5},{8,10},{9,11},{10,... | collective-permute-start | bytes 2359304 | tf_op jit(solution)/shard_map/ppermute | solution.py:700
  316.3 22.6 %collective-permute-start.48 = (bf16[1,64,4096]{2,1,0:T(8,128)(2,1)}, bf16[1,64,4096]{2,1,0:T(8,128)(2,1)S(1)}, u32[]{:S(2)}, u32[]{:S(2)}) collective-permute-start(bf16[1,64,4096]{2,1,0:T(8,128)(2,1)} %constant_dynamic-slice_fusion.1), channel_id=1, source_target_pairs={{0,8},{4,12},{8,0},{12,4},{16,24},{20,28},{24,16},{28,20},{1,9},{5... | collective-permute-start | bytes 1572872 | tf_op jit(solution)/shard_map/ppermute | solution.py:700
  316.3 22.5 %collective-permute-start.47 = (bf16[32,4096]{1,0:T(8,128)(2,1)}, bf16[32,4096]{1,0:T(8,128)(2,1)S(1)}, u32[]{:S(2)}, u32[]{:S(2)}) collective-permute-start(bf16[32,4096]{1,0:T(8,128)(2,1)} %fusion.23), channel_id=1, source_target_pairs={{0,16},{4,20},{8,24},{12,28},{16,0},{20,4},{24,8},{28,12},{1,17},{... | collective-permute-start | bytes 786440 | tf_op jit(solution)/shard_map/ppermute | solution.py:700
  319.4 19.4 %collective-permute-start.49 = (bf16[1,128,1024]{2,1,0:T(8,128)(2,1)}, bf16[1,128,1024]{2,1,0:T(8,128)(2,1)S(1)}, u32[]{:S(2)}, u32[]{:S(2)}) collective-permute-start(bf16[1,128,1024]{2,1,0:T(8,128)(2,1)} %fusion.22), channel_id=1, source_target_pairs={{0,4},{4,0},{8,12},{12,8},{16,20},{20,16},{24,28},{28,24},{1,5},{5... | collective-permute-start | bytes 786440 | tf_op jit(solution)/shard_map/ppermute | solution.py:700
  342.6 17.4 %collective-permute-start.50 = (bf16[256,1024]{1,0:T(8,128)(2,1)S(1)}, bf16[256,1024]{1,0:T(8,128)(2,1)S(1)}, u32[]{:S(2)}, u32[]{:S(2)}) collective-permute-start(bf16[256,1024]{1,0:T(8,128)(2,1)S(1)} %fusion.16), channel_id=1, source_target_pairs={{0,2},{1,3},{2,0},{3,1},{4,6},{5,7},{6,4},{7,5},{8,10},{9,11},{10,... | collective-permute-start | bytes 1572872 | tf_op jit(solution)/shard_map/ppermute | solution.py:700
  343.7 18.5 %collective-permute-start.51 = (bf16[64,4096]{1,0:T(8,128)(2,1)S(1)}, bf16[64,4096]{1,0:T(8,128)(2,1)S(1)}, u32[]{:S(2)}, u32[]{:S(2)}) collective-permute-start(bf16[64,4096]{1,0:T(8,128)(2,1)S(1)} %maximum_select_fusion.8), channel_id=1, source_target_pairs={{0,8},{4,12},{8,0},{12,4},{16,24},{20,28},{24,16},{28,20},{1,9},{5... | collective-permute-start | bytes 1572872 | tf_op jit(solution)/shard_map/ppermute | solution.py:700
  343.7 16.3 %collective-permute-start.52 = (bf16[1,32,4096]{2,1,0:T(8,128)(2,1)S(1)}, bf16[1,32,4096]{2,1,0:T(8,128)(2,1)S(1)}, u32[]{:S(2)}, u32[]{:S(2)}) collective-permute-start(bf16[1,32,4096]{2,1,0:T(8,128)(2,1)S(1)} %add_convert_fusion.8), channel_id=1, source_target_pairs={{0,16},{4,20},{8,24},{12,28},{16,0},{20,4},{24,8},{28,12},{1,17},{... | collective-permute-start | bytes 786440 | tf_op jit(solution)/shard_map/ppermute | solution.py:700
  345.5 13.7 %collective-permute-start.53 = (f32[16,1024]{1,0:T(8,128)S(1)}, f32[16,1024]{1,0:T(8,128)S(1)}, u32[]{:S(2)}, u32[]{:S(2)}) collective-permute-start(f32[16,1024]{1,0:T(8,128)S(1)} %concatenate.179), channel_id=1, source_target_pairs={{0,1},{1,0},{2,3},{3,2},{4,5},{5,4},{6,7},{7,6},{8,9},{9,8},{10,11... | collective-permute-start | bytes 196616 | tf_op jit(solution)/shard_map/ppermute | solution.py:700
  365.0 8.4 %collective-permute-start.54 = (bf16[1,128,1024]{2,1,0:T(8,128)(2,1)S(1)}, bf16[1,128,1024]{2,1,0:T(8,128)(2,1)S(1)}, u32[]{:S(2)}, u32[]{:S(2)}) collective-permute-start(bf16[1,128,1024]{2,1,0:T(8,128)(2,1)S(1)} %fusion.19), channel_id=1, source_target_pairs={{0,4},{4,0},{8,12},{12,8},{16,20},{20,16},{24,28},{28,24},{1,5},{5... | collective-permute-start | bytes 786440 | tf_op jit(solution)/shard_map/ppermute | solution.py:700
  365.9 7.5 %collective-permute-start.55 = (bf16[64,2048]{1,0:T(8,128)(2,1)S(1)}, bf16[64,2048]{1,0:T(8,128)(2,1)S(1)}, u32[]{:S(2)}, u32[]{:S(2)}) collective-permute-start(bf16[64,2048]{1,0:T(8,128)(2,1)S(1)} %slice_bitcast_fusion.8), channel_id=1, source_target_pairs={{0,2},{1,3},{2,0},{3,1},{4,6},{5,7},{6,4},{7,5},{8,10},{9,11},{10,... | collective-permute-start | bytes 786440 | tf_op jit(solution)/shard_map/ppermute | solution.py:700
  370.0 15.5 %collective-permute-start.59 = (bf16[32,4096]{1,0:T(8,128)(2,1)S(1)}, bf16[32,4096]{1,0:T(8,128)(2,1)S(1)}, u32[]{:S(2)}, u32[]{:S(2)}) collective-permute-start(bf16[32,4096]{1,0:T(8,128)(2,1)S(1)} %fusion.24), channel_id=1, source_target_pairs={{0,16},{4,20},{8,24},{12,28},{16,0},{20,4},{24,8},{28,12},{1,17},{... | collective-permute-start | bytes 786440 | tf_op jit(solution)/shard_map/ppermute | solution.py:700
  373.9 16.7 %collective-permute-start.58 = (bf16[1,64,2048]{2,1,0:T(8,128)(2,1)S(1)}, bf16[1,64,2048]{2,1,0:T(8,128)(2,1)S(1)}, u32[]{:S(2)}, u32[]{:S(2)}) collective-permute-start(bf16[1,64,2048]{2,1,0:T(8,128)(2,1)S(1)} %constant_dynamic-slice_fusion.4), channel_id=1, source_target_pairs={{0,8},{4,12},{8,0},{12,4},{16,24},{20,28},{24,16},{28,20},{1,9},{5... | collective-permute-start | bytes 786440 | tf_op jit(solution)/shard_map/ppermute | solution.py:700
  374.3 11.1 %collective-permute-start.60 = (f32[16,1024]{1,0:T(8,128)S(1)}, f32[16,1024]{1,0:T(8,128)S(1)}, u32[]{:S(2)}, u32[]{:S(2)}) collective-permute-start(f32[16,1024]{1,0:T(8,128)S(1)} %add.399), channel_id=1, source_target_pairs={{0,8},{4,12},{8,0},{12,4},{16,24},{20,28},{24,16},{28,20},{1,9},{5... | collective-permute-start | bytes 196616 | tf_op jit(solution)/shard_map/ppermute | solution.py:700
  390.9 26.2 %collective-permute-start.65 = (bf16[128,4096]{1,0:T(8,128)(2,1)S(1)}, bf16[128,4096]{1,0:T(8,128)(2,1)S(1)}, u32[]{:S(2)}, u32[]{:S(2)}) collective-permute-start(bf16[128,4096]{1,0:T(8,128)(2,1)S(1)} %maximum_select_fusion.2), channel_id=1, source_target_pairs={{0,4},{4,0},{8,12},{12,8},{16,20},{20,16},{24,28},{28,24},{1,5},{5... | collective-permute-start | bytes 3145736 | tf_op jit(solution)/shard_map/ppermute | solution.py:700
  392.0 17.0 %collective-permute-start.66 = (bf16[64,4096]{1,0:T(8,128)(2,1)S(1)}, bf16[64,4096]{1,0:T(8,128)(2,1)S(1)}, u32[]{:S(2)}, u32[]{:S(2)}) collective-permute-start(bf16[64,4096]{1,0:T(8,128)(2,1)S(1)} %maximum_select_fusion.9), channel_id=1, source_target_pairs={{0,8},{4,12},{8,0},{12,4},{16,24},{20,28},{24,16},{28,20},{1,9},{5... | collective-permute-start | bytes 1572872 | tf_op jit(solution)/shard_map/ppermute | solution.py:700
  397.8 11.5 %collective-permute-start.64 = (bf16[32,2048]{1,0:T(8,128)(2,1)S(1)}, bf16[32,2048]{1,0:T(8,128)(2,1)S(1)}, u32[]{:S(2)}, u32[]{:S(2)}) collective-permute-start(bf16[32,2048]{1,0:T(8,128)(2,1)S(1)} %fusion.25), channel_id=1, source_target_pairs={{0,16},{4,20},{8,24},{12,28},{16,0},{20,4},{24,8},{28,12},{1,17},{... | collective-permute-start | bytes 393224 | tf_op jit(solution)/shard_map/ppermute | solution.py:700
  398.2 31.7 %collective-permute-start.63 = (bf16[1,128,2048]{2,1,0:T(8,128)(2,1)S(1)}, bf16[1,128,2048]{2,1,0:T(8,128)(2,1)S(1)}, u32[]{:S(2)}, u32[]{:S(2)}) collective-permute-start(bf16[1,128,2048]{2,1,0:T(8,128)(2,1)S(1)} %fusion), channel_id=1, source_target_pairs={{0,4},{4,0},{8,12},{12,8},{16,20},{20,16},{24,28},{28,24},{1,5},{5... | collective-permute-start | bytes 1572872 | tf_op jit(solution)/shard_map/ppermute | solution.py:700
  419.3 10.5 %collective-permute-start.67 = (bf16[64,2048]{1,0:T(8,128)(2,1)S(1)}, bf16[64,2048]{1,0:T(8,128)(2,1)S(1)}, u32[]{:S(2)}, u32[]{:S(2)}) collective-permute-start(bf16[64,2048]{1,0:T(8,128)(2,1)S(1)} %maximum_select_fusion.12), channel_id=1, source_target_pairs={{0,8},{4,12},{8,0},{12,4},{16,24},{20,28},{24,16},{28,20},{1,9},{5... | collective-permute-start | bytes 786440 | tf_op jit(solution)/shard_map/ppermute | solution.py:700
  430.3 9.4 %collective-permute-start.68 = (bf16[1,64,2048]{2,1,0:T(8,128)(2,1)S(1)}, bf16[1,64,2048]{2,1,0:T(8,128)(2,1)S(1)}, u32[]{:S(2)}, u32[]{:S(2)}) collective-permute-start(bf16[1,64,2048]{2,1,0:T(8,128)(2,1)S(1)} %constant_dynamic-slice_fusion), channel_id=1, source_target_pairs={{0,8},{4,12},{8,0},{12,4},{16,24},{20,28},{24,16},{28,20},{1,9},{5... | collective-permute-start | bytes 786440 | tf_op jit(solution)/shard_map/ppermute | solution.py:700
  430.4 13.1 %collective-permute-start.70 = (bf16[128,2048]{1,0:T(8,128)(2,1)S(1)}, bf16[128,2048]{1,0:T(8,128)(2,1)S(1)}, u32[]{:S(2)}, u32[]{:S(2)}) collective-permute-start(bf16[128,2048]{1,0:T(8,128)(2,1)S(1)} %maximum_select_fusion.10), channel_id=1, source_target_pairs={{0,4},{4,0},{8,12},{12,8},{16,20},{20,16},{24,28},{28,24},{1,5},{5... | collective-permute-start | bytes 1572872 | tf_op jit(solution)/shard_map/ppermute | solution.py:700
  439.9 9.7 %collective-permute-start.69 = (bf16[1,32,2048]{2,1,0:T(8,128)(2,1)S(1)}, bf16[1,32,2048]{2,1,0:T(8,128)(2,1)S(1)}, u32[]{:S(2)}, u32[]{:S(2)}) collective-permute-start(bf16[1,32,2048]{2,1,0:T(8,128)(2,1)S(1)} %add_convert_fusion.12), channel_id=1, source_target_pairs={{0,16},{4,20},{8,24},{12,28},{16,0},{20,4},{24,8},{28,12},{1,17},{... | collective-permute-start | bytes 393224 | tf_op jit(solution)/shard_map/ppermute | solution.py:700
  442.6 20.9 %collective-permute-start.73 = (bf16[128,4096]{1,0:T(8,128)(2,1)S(1)}, bf16[128,4096]{1,0:T(8,128)(2,1)S(1)}, u32[]{:S(2)}, u32[]{:S(2)}) collective-permute-start(bf16[128,4096]{1,0:T(8,128)(2,1)S(1)} %maximum_select_fusion.3), channel_id=1, source_target_pairs={{0,4},{4,0},{8,12},{12,8},{16,20},{20,16},{24,28},{28,24},{1,5},{5... | collective-permute-start | bytes 3145736 | tf_op jit(solution)/shard_map/ppermute | solution.py:700
  449.6 7.4 %collective-permute-start.71 = (bf16[32,2048]{1,0:T(8,128)(2,1)S(1)}, bf16[32,2048]{1,0:T(8,128)(2,1)S(1)}, u32[]{:S(2)}, u32[]{:S(2)}) collective-permute-start(bf16[32,2048]{1,0:T(8,128)(2,1)S(1)} %fusion.26), channel_id=1, source_target_pairs={{0,16},{4,20},{8,24},{12,28},{16,0},{20,4},{24,8},{28,12},{1,17},{... | collective-permute-start | bytes 393224 | tf_op jit(solution)/shard_map/ppermute | solution.py:700
  465.4 12.9 %collective-permute-start.74 = (bf16[128,2048]{1,0:T(8,128)(2,1)S(1)}, bf16[128,2048]{1,0:T(8,128)(2,1)S(1)}, u32[]{:S(2)}, u32[]{:S(2)}) collective-permute-start(bf16[128,2048]{1,0:T(8,128)(2,1)S(1)} %maximum_select_fusion.11), channel_id=1, source_target_pairs={{0,4},{4,0},{8,12},{12,8},{16,20},{20,16},{24,28},{28,24},{1,5},{5... | collective-permute-start | bytes 1572872 | tf_op jit(solution)/shard_map/ppermute | solution.py:700
  (99 other events, 775.8 us)

commit v3 on v2

--- a/solution.py
+++ b/solution.py
@@ -175,20 +175,11 @@
     return pl.BlockSpec((slots, width), lambda i, *_: (i, 0))
 
 
-def qkv_forward(order, x, wqkv, vec, after, width=512):
-    images, slots, _ = x.shape
-    rows = images * slots
-
-    def body(order_ref, x_ref, *refs):
-        w_refs, (vec_ref, bias_ref, h1_ref, qkv_ref, w_s) = refs[:BLOCKS], refs[BLOCKS:]
-
-        @pl.when(pl.program_id(0) == 0)
-        def _():
-            for n in range(images):
-                normed, _ = normalize(x_ref[n].astype(F32))
-                hidden = normed * vec_ref[0:1, :] + vec_ref[1:2, :]
-                h1_ref[n * slots : (n + 1) * slots, :] = hidden.astype(BF16)
-
+def qkv_forward(order, h1, wqkv, vec, after, width=512):
+    rows = h1.shape[0]
+
+    def body(order_ref, h1_ref, *refs):
+        w_refs, (bias_ref, qkv_ref, w_s) = refs[:BLOCKS], refs[BLOCKS:]
         place(order_ref, w_s, w_refs)
         qkv_ref[...] = (dot(h1_ref[...], w_s[...]) + bias_ref[...]).astype(BF16)
 
@@ -196,22 +187,19 @@
     return call(
         body,
         scalars=[order],
-        ins=[x, *arrays(wqkv), vec, bias],
-        in_specs=[whole(x)]
+        ins=[h1, *arrays(wqkv), bias],
+        in_specs=[whole(h1)]
         + [pl.BlockSpec((BLOCK, width), lambda i, *_, row=w.row: (row, i)) for w in wqkv]
-        + [whole(vec), pl.BlockSpec((1, width), lambda i, *_: (0, i))],
-        outs=[like((rows, D), BF16), like((rows, 3 * D), BF16)],
-        out_specs=[
-            pl.BlockSpec((rows, D), lambda i, *_: (0, 0)),
-            pl.BlockSpec((rows, width), lambda i, *_: (0, i)),
-        ],
+        + [pl.BlockSpec((1, width), lambda i, *_: (0, i))],
+        outs=[like((rows, 3 * D), BF16)],
+        out_specs=[pl.BlockSpec((rows, width), lambda i, *_: (0, i))],
         scratch=[pltpu.VMEM((D, width), BF16)],
         grid=(3 * D // width,),
         name="qkv_forward",
         limit=30,
         work=(10 * rows * D * D, 18 * MIB),
         after=after,
-    )
+    )[0]
 
 
 def attn_mix(kept, qkv, images, after):
@@ -432,8 +420,8 @@
     def body(order_ref, *refs):
         dpre_refs, refs = refs[:PARTS], refs[PARTS:]
         up_refs, refs = refs[: PARTS * BLOCKS], refs[PARTS * BLOCKS :]
-        middle_ref, gy_ref, vec_ref, mixed_ref, dmid_ref, da_ref, sums_ref, send, keep = refs[:9]
-        side_s, weight_s, sems, acc, middle_s, middle_sem = refs[9:]
+        middle_ref, gy_ref, vec_ref, mixed_ref, da_ref, sums_ref, send, keep = refs[:8]
+        side_s, weight_s, sems, acc, middle_s, middle_sem = refs[8:]
 
         def use(p, side, weight):
             if p == 0:
@@ -444,7 +432,7 @@
 
         streamed(order_ref, dpres, dpre_refs, wups, up_refs, side_s, weight_s, sems, use)
         pltpu.make_async_copy(middle_ref, middle_s, middle_sem.at[0]).wait()
-        gain, shift, bias = (jnp.zeros((1, D), F32) for _ in range(3))
+        gain, shift, bias, down = (jnp.zeros((1, D), F32) for _ in range(4))
         step = rows // 6
         for r in range(0, rows, step):
             span = slice(r, r + step)
@@ -453,11 +441,11 @@
             gain += jnp.sum(dh2 * normed, axis=0, keepdims=True)
             shift += jnp.sum(dh2, axis=0, keepdims=True)
             dmid = norm_back(dh2 * vec_ref[5:6, :], normed, inverse) + gy_ref[span, :].astype(F32)
-            dmid_ref[span, :] = dmid
             da = dmid.astype(BF16)
             da_ref[span, :] = da
             bias += jnp.sum(da.astype(F32), axis=0, keepdims=True)
-        sums_ref[...] = jnp.concatenate([gain, shift, bias, jnp.zeros((5, D), F32)], axis=0)
+            down += jnp.sum(gy_ref[span, :].astype(F32), axis=0, keepdims=True)
+        sums_ref[...] = jnp.concatenate([gain, shift, bias, down, jnp.zeros((4, D), F32)], axis=0)
         for j in range(BLOCKS):
             at = pl.multiple_of(order_ref[j] * BLOCK, BLOCK)
             grad = dot_tn(mixed_ref[:, pl.ds(at, BLOCK)], da_ref[...]).astype(BF16)
@@ -468,10 +456,9 @@
         scalars=[order],
         ins=[*dpres, *arrays(flat), middle, gy, vec, mixed],
         in_specs=[ANY] * (PARTS + len(flat) + 1) + [whole(gy), whole(vec), whole(mixed)],
-        outs=[like((rows, D), F32), like((rows, D), BF16), like((8, D), F32)]
+        outs=[like((rows, D), BF16), like((8, D), F32)]
         + [like((2, BLOCK, D), BF16)] * 2,
         out_specs=[
-            pl.BlockSpec((rows, D), lambda i, *_: (0, 0)),
             pl.BlockSpec((rows, D), lambda i, *_: (0, 0)),
             pl.BlockSpec((8, D), lambda i, *_: (0, 0)),
             pl.BlockSpec((2, BLOCK, D), lambda i, *_: (0, 0, 0)),
@@ -584,13 +571,13 @@
     )
 
 
-def input_back(order, dqkv, wqkv, x, dmid, vec, after):
+def input_back(order, dqkv, wqkv, x, da, vec, after):
     images, slots, _ = x.shape
     rows = images * slots
 
     def body(order_ref, dqkv_ref, *refs):
         wq_refs = refs[:BLOCKS]
-        x_ref, dmid_ref, vec_ref, out_ref, sums_ref, acc = refs[BLOCKS:]
+        x_ref, da_ref, vec_ref, out_ref, sums_ref, acc = refs[BLOCKS:]
 
         @pl.when(pl.program_id(0) == 0)
         def _():
@@ -606,13 +593,13 @@
             sums_ref[0:1, :] += jnp.sum(dh1 * normed, axis=0, keepdims=True)
             sums_ref[1:2, :] += jnp.sum(dh1, axis=0, keepdims=True)
             total = norm_back(dh1 * vec_ref[0:1, :], normed, inverse)
-            out_ref[n] = (total + dmid_ref[n * slots : (n + 1) * slots, :]).astype(BF16)
+            out_ref[n] = (total + da_ref[n * slots : (n + 1) * slots, :].astype(F32)).astype(BF16)
 
     image = pl.BlockSpec((2, slots, D), lambda i, *_: (i, 0, 0))
     return call(
         body,
         scalars=[order],
-        ins=[dqkv, *arrays(wqkv), x, dmid, vec],
+        ins=[dqkv, *arrays(wqkv), x, da, vec],
         in_specs=[row_spec(2 * slots, 3 * D)]
         + [w.spec(3 * D) for w in wqkv]
         + [image, row_spec(2 * slots, D), whole(vec)],
@@ -627,9 +614,9 @@
     )
 
 
-def weight_grad(order, left, right, first, after, columns=D, width=512):
+def kv_grad(order, left, right, after, width=512):
     rows = right.shape[0]
-    at_block = first // width
+    steps = D // width
 
     def body(order_ref, left_ref, right_ref, send, keep):
         for j in range(BLOCKS):
@@ -642,13 +629,43 @@
         body,
         scalars=[order],
         ins=[left, right],
-        in_specs=[whole(left), pl.BlockSpec((rows, width), lambda i, *_: (0, at_block + i))],
+        in_specs=[whole(left), pl.BlockSpec((rows, width), lambda i, *_: (0, steps + i))],
+        outs=[like((2, BLOCK, 2 * D), BF16)] * 2,
+        out_specs=[grads] * 2,
+        grid=(2 * steps,),
+        name="kv_grad",
+        limit=30,
+        work=(8 * rows * D * D, 16 * MIB),
+        after=after,
+    )
+
+
+def query_grad(order, left, right, small, after):
+    rows = right.shape[0]
+    columns = D + 128
+
+    def body(order_ref, left_ref, right_ref, small_ref, send, keep):
+        for j in range(BLOCKS):
+            at = pl.multiple_of(order_ref[j] * BLOCK, BLOCK)
+            target = send if j % 2 else keep
+            grad = dot_tn(left_ref[:, pl.ds(at, BLOCK)], right_ref[...]).astype(BF16)
+            target[j // 2, :, :D] = grad
+            some = small_ref[:, pl.ds(at, BLOCK)]
+            some = jnp.concatenate([some, jnp.zeros((112, BLOCK), F32)], axis=0)
+            target[j // 2, :, D:] = some.T.astype(BF16)
+
+    out = pl.BlockSpec((2, BLOCK, columns), lambda i, *_: (0, 0, 0))
+    return call(
+        body,
+        scalars=[order],
+        ins=[left, right, small],
+        in_specs=[whole(left), pl.BlockSpec((rows, D), lambda i, *_: (0, 0)), whole(small)],
         outs=[like((2, BLOCK, columns), BF16)] * 2,
-        out_specs=[grads] * 2,
-        grid=(columns // width,),
-        name="weight_grad",
+        out_specs=[out] * 2,
+        grid=(1,),
+        name="query_grad",
         limit=30,
-        work=(3 * rows * D * columns, 12 * MIB),
+        work=(6 * rows * D * D, 10 * MIB),
         after=after,
     )
 
@@ -662,31 +679,37 @@
     return (gradient, first_new, second_new, weight_new, weight_new.astype(BF16))
 
 
-def adam_part(total, first, columns, weight, first_mom, second_mom, count, rate, decay, before, after, width=512):
-    rows = total.shape[0]
+def adam_part(halves, second, first, columns, weight, first_mom, second_mom, count, rate, decay, before, after):
+    half = halves[0].shape[0]
+    rows = 2 * half
+    width = D if len(columns) > 1 else D // 2
     steps = D // width
 
-    def body(columns_ref, g_ref, w_ref, m_ref, v_ref, *refs):
-        gradient = g_ref[...].astype(F32) * (1.0 / count)
-        outs = adam_terms(w_ref[...], m_ref[...], v_ref[...], gradient, rate, decay)
-        for ref, value in zip(refs[-6:], outs):
-            ref[...] = value
+    def body(columns_ref, second_ref, a_ref, b_ref, w_ref, m_ref, v_ref, *refs):
+        lower = second_ref[0] == 1
+        a, b = (ref[...].astype(F32) * (1.0 / count) for ref in (a_ref, b_ref))
+        for n, gradient in enumerate((jnp.where(lower, b, a), jnp.where(lower, a, b))):
+            span = slice(n * half, (n + 1) * half)
+            terms = (w_ref[span, :], m_ref[span, :], v_ref[span, :])
+            outs = adam_terms(*terms, gradient, rate, decay)
+            for ref, value in zip(refs[-6:], outs):
+                ref[span, :] = value
         refs[-1][...] = jnp.zeros_like(refs[-1])
 
-    there = pl.BlockSpec((rows, width), lambda i, n, where: (0, where[i] * steps + n))
+    there = pl.BlockSpec((rows, width), lambda i, n, where, _: (0, where[i] * steps + n))
     shape = weight.shape
     *outs, mark = call(
         body,
-        scalars=[jnp.array(columns, jnp.int32)],
-        ins=[total, weight, first_mom, second_mom, *before],
-        in_specs=[pl.BlockSpec((rows, width), lambda i, n, where: (0, (first + i) * steps + n))]
+        scalars=[jnp.array(columns, jnp.int32), second],
+        ins=[*halves, weight, first_mom, second_mom, *before],
+        in_specs=[pl.BlockSpec((half, width), lambda i, n, *_: (0, (first + i) * steps + n))] * 2
         + [there] * 3
         + [ANY] * len(before),
         outs=[jax.ShapeDtypeStruct(shape, F32)] * 4
         + [jax.ShapeDtypeStruct(shape, BF16), jax.ShapeDtypeStruct((8, 128), F32)],
-        out_specs=[there] * 5 + [pl.BlockSpec((8, 128), lambda i, n, where: (0, 0))],
+        out_specs=[there] * 5 + [pl.BlockSpec((8, 128), lambda i, n, *_: (0, 0))],
         grid=(len(columns), steps),
-        aliases={5 + n: n for n in range(len(before))},
+        aliases={7 + n: n for n in range(len(before))},
         name="adam_part",
         limit=30,
         work=(3 * MIB * 1024 * len(columns), 10 * MIB),
@@ -740,17 +763,17 @@
         for bit in bits:
             half = terms[0].shape[1] // 2
             up = self.place(bit)
-            piece = lambda at: [lax.dynamic_slice_in_dim(t, at * half, half, 1) for t in terms]
+            size = (1, half, terms[0].shape[2])
+            piece = lambda at: [lax.dynamic_slice(t, (0, at * half, 0), size) for t in terms]
             (got,) = yield [(beside(bit), "replica", bit, added(piece(1 - up)))]
             terms = piece(up) + [got]
         return terms
 
-    def part_steps(self, send, keep, y_first):
+    def part_steps(self, send, keep):
         (got,) = yield [("core", "shard", 1, send)]
         terms = [keep, got]
-        if y_first:
-            (got,) = yield [("y/", "shard", 2, added([t[1] for t in terms]))]
-            terms = [t[:1] for t in terms] + [got[None]]
+        (got,) = yield [("y/", "shard", 2, added([t[1] for t in terms]))]
+        terms += [got[None]]
         terms = yield from self.halving(terms, bits_of(self.replicas)[:1])
         return added(terms)
 
@@ -760,22 +783,13 @@
         bits = bits_of(self.replicas)
         terms = [jnp.concatenate([part.value for part in parts], axis=2)]
         terms = yield from self.halving(terms, bits[1:])
-        if terms[0].shape[0] == 2:
-            (got,) = yield [("y", "shard", 2, added([t[1] for t in terms]))]
-            terms = [t[0] for t in terms] + [got]
-        now = added(terms)
-        now = now.reshape(-1, now.shape[-1])
-        for bit in reversed(bits):
+        now = added(terms)[0]
+        for bit in reversed(bits[1:]):
             (got,) = yield [(beside(bit), "replica", bit, now)]
             now = self.both(bit, now, got, 0)
-        return now
-
-    def total_steps(self, values):
-        for axis, size in (("shard", self.shards), ("replica", self.replicas)):
-            for bit in bits_of(size):
-                (got,) = yield [("small", axis, bit, values)]
-                values = values + got
-        return values
+        link = beside(1) + ("/" if now.shape[1] > 3 * D else "")
+        (got,) = yield [(link, "replica", 1, now)]
+        return (now, got)
 
     def small_steps(self, own):
         (got,) = yield [("small", "shard", 1, own)]
@@ -788,7 +802,7 @@
         return got
 
     def far_steps(self, own):
-        (far,) = yield [("y", "shard", 2, own)]
+        (far,) = yield [("y/", "shard", 2, own)]
         (behind,) = yield [("core", "shard", 1, far)]
         return (far, behind)
 
@@ -821,25 +835,25 @@
 
 
 class Flow:
-    def __init__(self, steps):
-        self.steps, self.value, self.done = steps, None, False
+    def __init__(self, steps, rank):
+        self.steps, self.rank, self.value, self.done = steps, rank, None, False
         self.flying, self.parts, self.ready = [], [], 0.0
-        self.asked = next(steps)
+        self.asked, self.sent = next(steps), 0
 
     def give(self, arrays):
         try:
-            self.asked = self.steps.send(arrays)
+            self.asked, self.sent = self.steps.send(arrays), 0
         except StopIteration as end:
             self.asked, self.value, self.done = [], end.value, True
 
 
 class Pipeline:
     def __init__(self, token):
-        self.now, self.free, self.flows, self.token = 0.0, {}, [], token
-
-    def add(self, steps, urgent=False):
-        flow = Flow(steps)
-        self.flows.insert(0 if urgent else len(self.flows), flow)
+        self.now, self.free, self.flows, self.token, self.landed = 0.0, {}, [], token, []
+
+    def add(self, steps, rank=1):
+        flow = Flow(steps, rank)
+        self.flows = sorted([*self.flows, flow], key=lambda flow: flow.rank)
         return flow
 
     def tie(self, arrays):
@@ -848,16 +862,17 @@
         *arrays, self.token = lax.optimization_barrier((*arrays, self.token))
         return arrays
 
-    def turn(self, window=None, slack=1.0, ahead=6.0):
+    def land(self, slack=2.0):
         landed = [f for f in self.flows if f.flying and f.ready <= self.now + slack]
         arrived = [array for flow in landed for array in flow.flying]
+        self.landed += arrived
         tied = self.tie(arrived)
         for flow in landed:
             got, tied = tied[: len(flow.flying)], tied[len(flow.flying) :]
             flow.flying = []
             if flow.asked[0][0].endswith("/"):
                 flow.parts += got
-                if flow.asked[0][3].shape[0]:
+                if flow.sent < flow.asked[0][3].shape[0]:
                     continue
                 got, flow.parts = [jnp.concatenate(flow.parts, axis=0)], []
             flow.give(got)
@@ -867,36 +882,39 @@
             if not flow.done and not flow.flying and not flow.asked:
                 flow.give([])
         self.flows = [flow for flow in self.flows if not flow.done]
+
+    def start(self, window=None, ahead=6.0, only=None):
         issued = []
+        until = self.now + (ahead if window is None else window - 5.0)
         for flow in self.flows:
-            if flow.flying or not flow.asked:
+            if flow.flying or not flow.asked or (only is not None and flow is not only):
                 continue
             count = sum(len(f.flying) for f in self.flows) + len(flow.asked)
             links = [link.strip("/") for link, *_ in flow.asked]
-            until = self.now + ahead if window is None else self.now + window - 8.0
             if count > MOST_FLYING or any(self.free.get(k, 0.0) > until for k in links):
+                continue
+            if window is not None and not all(self.fits(window, *asked) for asked in flow.asked):
                 continue
             for n, (link, axis, bit, values) in enumerate(flow.asked):
                 if link.endswith("/"):
-                    link = link.strip("/")
-                    rows = values.shape[0]
+                    link, rows = link.strip("/"), values.shape[0]
+                    left = rows - flow.sent
                     pace = PACE[link] * values.size * values.dtype.itemsize / MIB / rows
                     busy = max(0.0, self.free.get(link, 0.0) - self.now)
                     room = int(((window or 1000) - LATENCY - busy) / pace + 8) // 16 * 16
-                    if rows - room > 16 and window is not None:
-                        rows = max(room, 32)
-                    flow.asked[n] = (link + "/", axis, bit, values[rows:])
-                    values = values[:rows]
+                    if left - room > 16 and window is not None:
+                        left = room
+                    if left < 32:
+                        continue
+                    values = values[flow.sent : flow.sent + left]
+                    flow.sent += left
                 issued.append((flow, len(flow.flying), axis, bit, values))
                 flow.flying.append(values)
                 size = values.size * values.dtype.itemsize / MIB
                 start = max(self.now, self.free.get(link, 0.0))
                 self.free[link] = start + size * PACE.get(link, 45.0)
                 flow.ready = max(flow.ready, self.free[link] + LATENCY)
-        started = {id(flow) for flow, *_ in issued}
-        pending = [
-            flow for flow in self.flows if not flow.flying and flow.asked and id(flow) not in started
-        ]
+        pending = [flow for flow in self.flows if not flow.flying and flow.asked]
         pending = [(flow, n) for flow in pending for n in range(len(flow.asked))]
         operands = [values for *_, values in issued] + [f.asked[n][3] for f, n in pending]
         operands = self.tie(operands)
@@ -904,7 +922,19 @@
             flow.flying[n] = swap(values, axis, bit)
         for (flow, n), values in zip(pending, operands[len(issued) :]):
             flow.asked[n] = (*flow.asked[n][:3], values)
-        return arrived + [self.token]
+        after, self.landed = self.landed + [self.token], []
+        return after
+
+    def fits(self, window, link, axis, bit, values):
+        if link.endswith("/"):
+            return True
+        busy = max(0.0, self.free.get(link, 0.0) - self.now)
+        length = values.size * values.dtype.itemsize / MIB * PACE.get(link, 45.0)
+        return busy + length + LATENCY <= window + 1.5
+
+    def turn(self, window=None):
+        self.land()
+        return self.start(window)
 
     def spend(self, length, token):
         self.now += length
@@ -912,26 +942,25 @@
 
     def wait(self):
         times = [flow.ready for flow in self.flows if flow.flying]
-        return max(0.0, min(times) - self.now) if times else 0.0
+        return max(0.0, min(times) - self.now) if times else 1.0
 
     def skip(self, wait=0.0):
-        times = [flow.ready for flow in self.flows if flow.flying]
-        self.now = max(self.now, min(times) + wait) if times else self.now + 1.0
-
-    def reach(self, flow, link):
-        self.turn()
+        self.now += self.wait() + wait
+
+    def reach(self, flow, link, gap=None, wait=0.0, alone=False):
+        self.land()
         while flow.asked[0][0] != link:
-            self.skip()
-            if flow.flying and flow.ready <= self.now + 1.0:
-                return
-            self.turn()
-
-    def finish(self, *flows, window=None, wait=0.0):
-        after = self.turn(window)
+            self.start(gap, only=flow if alone else None)
+            self.now = max(self.now, flow.ready) if alone else self.now + self.wait() + wait
+            self.land()
+
+    def finish(self, *flows, window=None, gap=None, wait=0.0):
+        self.land()
         while not all(flow.done for flow in flows):
+            self.start(gap)
             self.skip(wait)
-            after = self.turn(window)
-        return after
+            self.land()
+        return self.start(window)
 
 
 def on_device(
@@ -955,12 +984,17 @@
     owned = vectors.shape[0]
     image_total = images * links.replicas * links.shards
 
-    attn_low, mlp_low, wo_low = (a.astype(BF16) for a in (attn_w, mlp_w, attn_w[:, 3 * D :]))
     small_low = jnp.pad(vectors.astype(BF16).T, ((0, 4), (0, 0)))
     at = jnp.arange(slots, dtype=jnp.int32)
     valid = (at[None, :] < (BUF + kept_count)[:, None]).reshape(rows, 1)
     gy = jnp.where(valid, out_grad.reshape(rows, D), jnp.zeros((), BF16))
     pipe = Pipeline(order)
+
+    def first_norm(small_full):
+        normed, _ = normalize(tokens.reshape(rows, D).astype(F32))
+        vec = small_full.astype(F32)
+        return (normed * vec[0:1] + vec[1:2]).astype(BF16)
+
     if links.direct:
 
         def half(array, first, width, bit):
@@ -971,20 +1005,30 @@
             return jnp.concatenate(sent, axis=1).astype(BF16)
 
         pair = 3 * D // 2
-        qkv_flow = pipe.add(links.shared_steps(halves(attn_w, 0, pair, pair // 2), True))
-        vec_flow = pipe.add(links.small_steps(small_low))
-        near_flow = pipe.add(links.near_steps(attn_low))
-        sends = [halves(mlp_w, n, FF + n, PART) for n in range(0, FF, 2 * PART)]
+        qkv_flow = pipe.add(links.shared_steps(halves(attn_w, 0, pair, pair // 2), True), 0)
+        vec_flow = pipe.add(links.small_steps(small_low), 0)
+        pipe.turn()
+        attn_after, mlp_after = pipe.tie([attn_w, mlp_w])
+        attn_low, mlp_low = attn_after.astype(BF16), mlp_after.astype(BF16)
+        wo_low = attn_after[:, 3 * D :].astype(BF16)
+        sends = [halves(mlp_after, n, FF + n, PART) for n in range(0, FF, 2 * PART)]
         pipe.turn()
         sends[0], sends[1], mlp_low, wo_low, gy = pipe.tie([*sends, mlp_low, wo_low, gy])
-        mlp_flows = [pipe.add(links.shared_steps(sends[0], False))]
-        wo_flow = pipe.add(links.far_steps(wo_low))
-        mlp_flows.append(pipe.add(links.shared_steps(sends[1], False)))
-        after = pipe.finish(qkv_flow, vec_flow, near_flow, window=12, wait=3.0)
+        mlp_flows = [pipe.add(links.shared_steps(sends[0], False), 0)]
+        wo_flow = pipe.add(links.far_steps(wo_low), 0)
+        mlp_flows.append(pipe.add(links.shared_steps(sends[1], False), 0))
+        pipe.reach(qkv_flow, beside(1), gap=5)
+        near_flow = pipe.add(links.near_steps(attn_low), 0)
+        small_full = vec_flow.value.transpose(1, 0, 2).reshape(16, D)
+        pipe.start(12)
+        (h1,) = pipe.tie([first_norm(small_full)])
+        pipe.now = max(flow.ready for flow in pipe.flows if flow.flying)
+        pipe.land()
+        after = pipe.finish(qkv_flow, vec_flow, near_flow, window=13, gap=14)
         attn_near, ((attn_far, behind),) = near_flow.value, qkv_flow.value
         wqkv = [Piece(array, 0, 0) for array in (attn_low, attn_near, attn_far, behind)]
-        small_full = vec_flow.value.transpose(1, 0, 2).reshape(16, D)
     else:
+        attn_low, mlp_low = attn_w.astype(BF16), mlp_w.astype(BF16)
         gather = lambda array, axis: lax.all_gather(array, "shard", axis=axis, tiled=True)
         attn_full, mlp_full = gather(attn_low, 0), gather(mlp_low, 0)
         small_full = gather(small_low, 1)
@@ -993,33 +1037,35 @@
         wups = [[Piece(mlp_full, j, p) for j in range(BLOCKS)] for p in range(PARTS)]
         wdns = [[Piece(mlp_full, j, 4 + p) for j in range(BLOCKS)] for p in range(PARTS)]
         after = []
+        h1 = first_norm(small_full)
     vec = small_full.astype(F32)
 
     totals = []
 
     def summed(send, keep, urgent=False):
         if links.direct:
-            return pipe.add(links.part_steps(send, keep, True), urgent)
+            return pipe.add(links.part_steps(send, keep), 1 if urgent else 2)
         return (send, keep)
 
     def chunk(name, *parts):
         if links.direct:
-            totals.append((name, pipe.add(links.chunk_steps(parts), name[0] == "attn")))
+            totals.append((name, pipe.add(links.chunk_steps(parts), 1 if name[0] == "attn" else 2)))
             return
         stacked = [jnp.stack([k[0], s[0], k[1], s[1]]).reshape(D, -1) for s, k in parts]
         part = lax.psum_scatter(
             jnp.concatenate(stacked, axis=1), "shard", scatter_dimension=0, tiled=True
         )
-        totals.append((name, lax.psum(part, "replica")))
-
-    h1, qkv = qkv_forward(order, tokens, wqkv, vec, after)
-    pipe.spend(17, h1)
+        part = lax.psum(part, "replica")
+        totals.append((name, (part[: part.shape[0] // 2], part[part.shape[0] // 2 :])))
+
+    qkv = qkv_forward(order, h1, wqkv, vec, after)
+    pipe.spend(15, qkv)
     if links.direct:
-        mlp_near_flow = pipe.add(links.near_steps(mlp_low))
+        mlp_near_flow = pipe.add(links.near_steps(mlp_low), 0)
     mixed = attn_mix(kept_count, qkv, images, pipe.turn(17))
     pipe.spend(17, mixed)
     if links.direct:
-        after = pipe.finish(wo_flow, window=10)
+        after = pipe.finish(wo_flow, window=10, gap=16)
         wo_far, behind = wo_flow.value
         wo = [Piece(attn_low, 0, 3), Piece(attn_near, 0, 3), Piece(wo_far, 0, 0), Piece(behind, 0, 0)]
     middle, h2 = out_project(order, tokens, mixed, wo, vec, after)
@@ -1045,12 +1091,14 @@
         gbus.append(gbu)
         pipe.spend(17, gbu)
         part = summed(send, keep)
-        if p % 2:
+        if p == PARTS - 1:
             chunk(("mlp", 3 + p, p - 1, 4 + p, p), before, part)
+        elif p < PARTS - 2:
+            chunk(("mlp", 4 + p, p), part)
         before = part
         if p == 0 and links.direct:
-            pipe.reach(part, "y/")
-    dmid, da, two_sums, send, keep = mlp_back(
+            pipe.reach(part, "y/", alone=True)
+    da, two_sums, send, keep = mlp_back(
         order, dpres, wups, middle, gy, vec, mixed, pipe.turn(26)
     )
     pipe.spend(26, two_sums)
@@ -1064,16 +1112,15 @@
     )
     pipe.spend(19, sums_b)
     qkv_sums = sums_a + sums_b
-    send, keep = weight_grad(order, h1, dqkv, D, pipe.turn(9), 2 * D)
-    pipe.spend(9, send)
-    chunk(("attn", 1, 2), summed(send, keep, True))
-    send, keep = weight_grad(order, h1, dqkv, 0, pipe.turn(9), D)
-    pipe.spend(9, send)
-    chunk(("attn", 0, 3), summed(send, keep, True), out_part)
-    in_grad, one_sums = input_back(order, dqkv, wqkv, tokens, dmid, vec, pipe.turn(19))
+    send, keep = kv_grad(order, h1, dqkv, pipe.turn(14))
+    pipe.spend(14, send)
+    kv_part = summed(send, keep, True)
+    chunk(("attn", 1, 2), kv_part)
+    if links.direct:
+        pipe.reach(kv_part, "y/", alone=True)
+    in_grad, one_sums = input_back(order, dqkv, wqkv, tokens, da, vec, pipe.turn(19))
     pipe.spend(19, one_sums)
 
-    g_down = jnp.sum(gy, axis=0, dtype=F32, keepdims=True)
     small = jnp.concatenate(
         [
             one_sums[0:2],
@@ -1081,16 +1128,15 @@
             qkv_sums[2:3],
             two_sums[2:3],
             two_sums[0:2],
-            g_down,
+            two_sums[3:4],
             *gbus,
             jnp.zeros((4, D), F32),
         ],
         axis=0,
     )
-    if links.direct:
-        totals.append(("small", pipe.add(links.total_steps(small))))
-    else:
-        totals.append(("small", lax.psum(small, ("replica", "shard"))))
+    send, keep = query_grad(order, h1, dqkv, small, pipe.turn(10))
+    pipe.spend(10, send)
+    chunk(("attn", 3, 0), out_part, summed(send, keep, True))
     result = mlp_out(order, acts, wdns, middle, valid.astype(F32), vec, pipe.turn(17))
     pipe.spend(17, result)
     result = result.reshape(images, slots, D)
@@ -1101,26 +1147,28 @@
         "mlp": (mlp_w, mlp_m, mlp_v, image_total, 0.05, 0.05),
     }
     small_out, pieces = None, []
+    second = (links.place(1) if links.direct else jnp.zeros((), jnp.int32)).reshape(1)
     while totals or pieces:
         after = pipe.turn()
         through = lambda total: not isinstance(total, Flow) or total.done
         for name, total in [entry for entry in totals if through(entry[1])]:
             total = total.value if isinstance(total, Flow) else total
-            if name == "small":
-                total = lax.dynamic_slice_in_dim(
-                    total, lax.axis_index("shard") * owned, owned, 1
+            if total[0].shape[1] % D:
+                some = [half[:, 2 * D : 2 * D + 12] for half in total]
+                gradient = jnp.where(
+                    second[0] == 1, jnp.concatenate(some[::-1]), jnp.concatenate(some)
                 )
-                gradient = total[:12].T / image_total
+                gradient = gradient.astype(F32) / image_total
                 small_out = adam_terms(vectors, small_m, small_v, gradient, 1.0, 0.0)
-                continue
             pieces += [(name[0], total, n, column) for n, column in enumerate(name[1:])]
         totals = [entry for entry in totals if not through(entry[1])]
         wait = pipe.wait() if totals else 1000.0
         kind, total, first, _ = pieces[0] if pieces else (None,) * 4
-        columns = [c for k, t, _, c in pieces if t is total][: int((wait + 1.0) / 4.0)]
+        fit = 1 if totals else 4
+        columns = [c for k, t, _, c in pieces if t is total][:fit]
         if columns:
-            outs[kind], mark = adam_part(total, first, columns, *state[kind], outs[kind], after)
-            pipe.spend(4.0 * len(columns), mark)
+            outs[kind], mark = adam_part(total, second, first, columns, *state[kind], outs[kind], after)
+            pipe.spend(1.0 + 3.2 * len(columns), mark)
             pieces = pieces[len(columns) :]
         elif totals:
             pipe.skip(1.5)

time: 501 us -> 470 us (0.938)
  waiting for transfers between devices: 93.8 us -> 68.2 us
    ppermute x75, waiting for transfers between devices: 93.8 us -> 68.2 us  [swap(): return lax.ppermute(values, axis, [(i, i ^ bit) for i in range(size)])]
    slice x31 -> x22, local copies, waits for them, and re-layouts: 21.2 us -> 12.4 us  [the longest x16 12.3 us: start(): values = values[flow.sent:flow.sent + left]]
    unnamed x188 -> x155, local copies, waits for them, and re-layouts: 12.7 us -> 18 us
    select_n x14 -> x12, other arithmetic: 8.92 us -> 3.9 us  [both(): jnp.where(self.bit(bit), jnp.concatenate([other, mine], axis=axis), jnp.c...]
    convert_element_type x25 -> x26, other arithmetic: 14.4 us -> 17.5 us  [added(): return sum((t.astype(F32) for t in terms)).astype(BF16)]
    pallas_call x21 -> x25, Pallas kernels: 238 us -> 238 us  [call(): pl.pallas_call(with_after, grid_spec=pltpu.PrefetchScalarGridSpec(num_sca...]
  transfers between devices with their start and end apart: 75 -> 75, of which waited for: 28 -> 21; matrix products, arithmetic and copies ran while one was open for 8% -> 7% of each run, Pallas kernels for 46% -> 49%
where the time goes in v3:
time: 470 us; the launch traced here: 461 us
  Pallas kernels  238 us (51%)
  starting transfers between devices  70.8 us (15%)
  waiting for transfers between devices  68.2 us (15%)
  local copies, waits for them, and re-layouts  41.6 us (9%)
  other arithmetic  40.1 us (9%)
    pallas_call x25, Pallas kernels, call(): pl.pallas_call(with_after, grid_spec=pltpu.PrefetchScalarGridSpec(num_sca...  238 us
    ppermute x75, starting transfers between devices, swap(): return lax.ppermute(values, axis, [(i, i ^ bit) for i in range(size)])  70.8 us
    ppermute x75, waiting for transfers between devices, swap(): return lax.ppermute(values, axis, [(i, i ^ bit) for i in range(size)])  68.2 us
    unnamed x155, local copies, waits for them, and re-layouts  18 us
    convert_element_type x26, other arithmetic, added(): return sum((t.astype(F32) for t in terms)).astype(BF16)  17.5 us
    slice x16, local copies, waits for them, and re-layouts, start(): values = values[flow.sent:flow.sent + left]  12.3 us
  transfers between devices with their start and end apart: 75, of which 21 were waited for; matrix products, arithmetic and copies ran while one was open for 7% of the time, Pallas kernels for 49%

profile of v3, /device:TPU:0, one launch (start us, length us, event | category | flops | bytes accessed | tf_op | source)
XLA Modules:
  0.0 461.3 jit_solution(14699787605266877973)
XLA Ops:
  4.3 2.5 collective-permute-start.2
  6.8 2.5 dynamic-slice_convert_fusion.1
  11.6 1.6 bitcast_select_fusion.refs_2_.refs_22_
  13.2 6.1 %convert_element_type.511.refs_3_.refs_7_.refs_5_.refs_9_.refs_13_.refs_17_ = bf16[256,8192]{1,0:T(8,128)(2,1)} convert(f32[256,8192]{1,0:T(8,128)} %refs_4_.18) | non-fusion elementwise | flops 2097152 | bytes 12582912 | tf_op jit(solution)/shard_map/convert_element_type | solution.py:1012
  21.1 4.4 collective-permute-done.1
  26.1 1.8 slice.227
  27.9 1.9 fusion.41
  31.1 1.8 collective-permute-start.5
  37.1 2.0 fusion.3.refs_1_
  39.1 5.2 %collective-permute-done.3 = bf16[256,768]{1,0:T(8,128)(2,1)S(1)} collective-permute-done((bf16[256,768]{1,0:T(8,128)(2,1)}, bf16[256,768]{1,0:T(8,128)(2,1)S(1)}, u32[]{:S(2)}, u32[]{:S(2)}) %collective-permute-start.3) | collective-permute-done | bytes 393248 | tf_op jit(solution)/shard_map/ppermute | solution.py:723
  47.7 1.7 collective-permute-done.7.refs_5_.refs_7_
  50.6 11.7 %qkv_forward.1.refs_1_.refs_4_.refs_7_ = bf16[960,3072]{1,0:T(8,128)(2,1)} custom-call(s32[4]{0:T(128)S(1)} %iota_xor_fusion.refs_0_.refs_8_, bf16[960,1024]{1,0:T(8,128)(2,1)} %fusion.3.refs_1_, bf16[256,4096]{1,0:T(8,128)(2,1)} %copy-done.42, bf16[256,4096]{1,0:T(8,128)(2,1)} %collective-permute-done.6.refs_3_.refs_4_, bf16[256,3072]{1,0:T(8,128)(2,1)} %copy-done.57, ...), custom_call_target="tpu_custom_call" | custom-call | flops 10066329600 | bytes 18874368 | tf_op jit(solution)/shard_map/qkv_forward/pallas_call | solution.py:97
  63.1 2.9 collective-permute-done.9.refs_3_
  71.5 13.2 %attn_mix.1.refs_2_.refs_11_.refs_24_ = bf16[960,1024]{1,0:T(8,128)(2,1)} custom-call(s32[6]{0:T(128)S(1)} %copy-done.27, bf16[960,3072]{1,0:T(8,128)(2,1)} %qkv_forward.1.refs_1_.refs_4_.refs_7_, bf16[144,2048]{1,0:T(8,128)(2,1)S(1)} %collective-permute-done.8.refs_2_, bf16[80,1024]{1,0:T(8,128)(2,1)S(1)} %collective-permute-done.9.refs_3_, ...), custom_call_target="tpu_custom_call" | custom-call | flops 14092861440 | bytes 8388608 | tf_op jit(solution)/shard_map/attn_mix/pallas_call | solution.py:97
  84.8 2.2 collective-permute-done.13
  89.6 2.8 collective-permute-done.17.refs_6_.refs_10_
  93.2 8.1 %out_project.1 = (f32[960,1024]{1,0:T(8,128)}, bf16[960,1024]{1,0:T(8,128)(2,1)}) custom-call(s32[4]{0:T(128)S(1)} %iota_xor_fusion.refs_0_.refs_8_, bf16[6,160,1024]{2,1,0:T(8,128)(2,1)} %refs_6_.12, bf16[960,1024]{1,0:T(8,128)(2,1)} %attn_mix.1.refs_2_.refs_11_.refs_24_, bf16[256,4096]{1,0:T(8,128)(2,1)} %copy-done.42, ...), custom_call_target="tpu_custom_call" | custom-call | flops 6039797760 | bytes 12582912 | tf_op jit(solution)/shard_map/out_project/pallas_call | solution.py:97
  101.4 5.2 %collective-permute-done.18.refs_12_ = bf16[176,2048]{1,0:T(8,128)(2,1)S(1)} collective-permute-done((bf16[176,2048]{1,0:T(8,128)(2,1)S(1)}, bf16[176,2048]{1,0:T(8,128)(2,1)S(1)}, u32[]{:S(2)}, u32[]{:S(2)}) %collective-permute-start.18) | collective-permute-done | bytes 720928 | tf_op jit(solution)/shard_map/ppermute | solution.py:723
  108.6 15.1 %mlp_part.4 = (bf16[960,1024]{1,0:T(8,128)(2,1)}, bf16[960,1024]{1,0:T(8,128)(2,1)}, bf16[2,256,2048]{2,1,0:T(8,128)(2,1)}, bf16[2,256,2048]{2,1,0:T(8,128)(2,1)}, f32[1,1024]{1,0:T(1,128)}) custom-call(s32[4]{0:T(128)S(1)} %iota_xor_fusion.refs_0_.refs_8_, bf16[960,1024]{1,0:T(8,128)(2,1)} %get-tuple-element.475.refs_1_.refs_13_, ...), custom_call_target="tpu_custom_call" | custom-call | flops 12079595520 | bytes 12582912 | tf_op jit(solution)/shard_map/mlp_part/pallas_call | solution.py:97
  124.1 2.1 copy-done.68
  126.3 4.2 collective-permute-done.21.refs_12_
  132.2 15.5 %mlp_part.5 = (bf16[960,1024]{1,0:T(8,128)(2,1)}, bf16[960,1024]{1,0:T(8,128)(2,1)}, bf16[2,256,2048]{2,1,0:T(8,128)(2,1)}, bf16[2,256,2048]{2,1,0:T(8,128)(2,1)}, f32[1,1024]{1,0:T(1,128)}) custom-call(s32[4]{0:T(128)S(1)} %iota_xor_fusion.refs_0_.refs_8_, bf16[960,1024]{1,0:T(8,128)(2,1)} %get-tuple-element.475.refs_1_.refs_13_, ...), custom_call_target="tpu_custom_call" | custom-call | flops 12079595520 | bytes 12582912 | tf_op jit(solution)/shard_map/mlp_part/pallas_call | solution.py:97
  154.0 15.3 %mlp_part.6 = (bf16[960,1024]{1,0:T(8,128)(2,1)}, bf16[960,1024]{1,0:T(8,128)(2,1)}, bf16[2,256,2048]{2,1,0:T(8,128)(2,1)}, bf16[2,256,2048]{2,1,0:T(8,128)(2,1)}, f32[1,1024]{1,0:T(1,128)}) custom-call(s32[4]{0:T(128)S(1)} %iota_xor_fusion.refs_0_.refs_8_, bf16[960,1024]{1,0:T(8,128)(2,1)} %get-tuple-element.475.refs_1_.refs_13_, ...), custom_call_target="tpu_custom_call" | custom-call | flops 12079595520 | bytes 12582912 | tf_op jit(solution)/shard_map/mlp_part/pallas_call | solution.py:97
  171.2 2.6 fusion.18
  178.7 15.4 %mlp_part.7 = (bf16[960,1024]{1,0:T(8,128)(2,1)}, bf16[960,1024]{1,0:T(8,128)(2,1)}, bf16[2,256,2048]{2,1,0:T(8,128)(2,1)}, bf16[2,256,2048]{2,1,0:T(8,128)(2,1)}, f32[1,1024]{1,0:T(1,128)}) custom-call(s32[4]{0:T(128)S(1)} %iota_xor_fusion.refs_0_.refs_8_, bf16[960,1024]{1,0:T(8,128)(2,1)} %get-tuple-element.475.refs_1_.refs_13_, ...), custom_call_target="tpu_custom_call" | custom-call | flops 12079595520 | bytes 12582912 | tf_op jit(solution)/shard_map/mlp_part/pallas_call | solution.py:97
  194.1 1.7 slice_bitcast_fusion.6
  199.8 1.6 collective-permute-start.32
  203.4 20.8 %mlp_back.1 = (bf16[960,1024]{1,0:T(8,128)(2,1)}, f32[8,1024]{1,0:T(8,128)}, bf16[2,256,1024]{2,1,0:T(8,128)(2,1)}, bf16[2,256,1024]{2,1,0:T(8,128)(2,1)}) custom-call(s32[4]{0:T(128)S(1)} %iota_xor_fusion.refs_0_.refs_8_, bf16[960,1024]{1,0:T(8,128)(2,1)} %get-tuple-element.516.refs_1_, bf16[960,1024]{1,0:T(8,128)(2,1)} %get-tuple-element.517.refs_2_, ...), custom_call_target="tpu_custom_call" | custom-call | flops 12079595520 | bytes 31457280 | tf_op jit(solution)/shard_map/mlp_back/pallas_call | solution.py:97
  225.3 1.7 collective-permute-done.31.refs_9_
  227.0 1.8 add_convert_fusion.1
  234.3 2.6 collective-permute-start.34
  236.9 14.5 %attn_back.2 = (bf16[960,3072]{1,0:T(8,128)(2,1)}, f32[8,1024]{1,0:T(8,128)}) custom-call(s32[4]{0:T(128)S(1)} %iota_xor_fusion.refs_0_.refs_8_, s32[6]{0:T(128)S(1)} %copy-done.27, bf16[960,1024]{1,0:T(8,128)(2,1)} %get-tuple-element.532.refs_2_.refs_7_, bf16[256,4096]{1,0:T(8,128)(2,1)} %copy-done.42, ...), custom_call_target="tpu_custom_call" | custom-call | flops 12079595520 | bytes 18874368 | tf_op jit(solution)/shard_map/attn_back/pallas_call | solution.py:97
  254.5 1.6 collective-permute-start.42
  258.1 1.7 collective-permute-start.39
  259.8 14.7 %attn_back.3 = (bf16[960,3072]{1,0:T(8,128)(2,1)}, f32[8,1024]{1,0:T(8,128)}) custom-call(s32[4]{0:T(128)S(1)} %iota_xor_fusion.refs_0_.refs_8_, s32[6]{0:T(128)S(1)} %copy-done.27, bf16[960,1024]{1,0:T(8,128)(2,1)} %get-tuple-element.532.refs_2_.refs_7_, bf16[256,4096]{1,0:T(8,128)(2,1)} %copy-done.42, ...), custom_call_target="tpu_custom_call", output_to_operand_aliasing={{0}: (8, {})} | custom-call | flops 12079595520 | bytes 18874368 | tf_op jit(solution)/shard_map/attn_back/pallas_call | solution.py:97
  280.3 8.6 %kv_grad.1 = (bf16[2,256,2048]{2,1,0:T(8,128)(2,1)}, bf16[2,256,2048]{2,1,0:T(8,128)(2,1)}) custom-call(s32[4]{0:T(128)S(1)} %iota_xor_fusion.refs_0_.refs_8_, bf16[960,1024]{1,0:T(8,128)(2,1)} %fusion.3.refs_1_, bf16[960,3072]{1,0:T(8,128)(2,1)} %get-tuple-element.563.refs_2_.refs_1_, bf16[32,2048]{1,0:T(8,128)(2,1)S(1)} %collective-permute-done.39.refs_3_, ...), custom_call_target="tpu_custom_call" | custom-call | flops 8053063680 | bytes 16777216 | tf_op jit(solution)/shard_map/kv_grad/pallas_call | solution.py:97
  295.1 3.9 collective-permute-done.48.refs_9_
  299.1 1.6 add_convert_fusion
  306.6 1.6 collective-permute-start.51
  308.2 14.9 %input_back.1 = (bf16[6,160,1024]{2,1,0:T(8,128)(2,1)}, f32[8,1024]{1,0:T(8,128)}) custom-call(s32[4]{0:T(128)S(1)} %iota_xor_fusion.refs_0_.refs_8_, bf16[960,3072]{1,0:T(8,128)(2,1)} %get-tuple-element.563.refs_2_.refs_1_, bf16[256,4096]{1,0:T(8,128)(2,1)} %copy-done.42, bf16[256,4096]{1,0:T(8,128)(2,1)} %collective-permute-done.6.refs_3_.refs_4_, ...), custom_call_target="tpu_custom_call" | custom-call | flops 8053063680 | bytes 25165824 | tf_op jit(solution)/shard_map/input_back/pallas_call | solution.py:97
  329.8 6.4 %query_grad.1 = (bf16[2,256,1152]{2,1,0:T(8,128)(2,1)}, bf16[2,256,1152]{2,1,0:T(8,128)(2,1)}) custom-call(s32[4]{0:T(128)S(1)} %iota_xor_fusion.refs_0_.refs_8_, bf16[960,1024]{1,0:T(8,128)(2,1)} %fusion.3.refs_1_, bf16[960,3072]{1,0:T(8,128)(2,1)} %get-tuple-element.563.refs_2_.refs_1_, f32[16,1024]{1,0:T(8,128)S(1)} %concatenate.177.refs_3_, ...), custom_call_target="tpu_custom_call" | custom-call | flops 6039797760 | bytes 10485760 | tf_op jit(solution)/shard_map/query_grad/pallas_call | solution.py:97
  342.0 13.6 %mlp_out.1.refs_10_ = bf16[960,1024]{1,0:T(8,128)(2,1)} custom-call(s32[4]{0:T(128)S(1)} %iota_xor_fusion.refs_0_.refs_8_, bf16[960,1024]{1,0:T(8,128)(2,1)} %get-tuple-element.476.refs_1_, bf16[960,1024]{1,0:T(8,128)(2,1)} %get-tuple-element.493.refs_2_, bf16[960,1024]{1,0:T(8,128)(2,1)} %get-tuple-element.502.refs_3_, ...), custom_call_target="tpu_custom_call" | custom-call | flops 12079595520 | bytes 25165824 | tf_op jit(solution)/shard_map/mlp_out/pallas_call | solution.py:97
  357.5 1.6 collective-permute-start.59
  361.0 1.6 collective-permute-start.63
  362.6 4.5 adam_part.11
  367.1 4.2 adam_part.12
  372.8 6.0 %collective-permute-done.63.refs_14_ = bf16[32,4096]{1,0:T(8,128)(2,1)S(1)} collective-permute-done((bf16[32,4096]{1,0:T(8,128)(2,1)S(1)}, bf16[32,4096]{1,0:T(8,128)(2,1)S(1)}, u32[]{:S(2)}, u32[]{:S(2)}) %collective-permute-start.63) | collective-permute-done | bytes 262176 | tf_op jit(solution)/shard_map/ppermute | solution.py:723
  379.6 4.2 adam_part.13
  384.5 2.4 collective-permute-start.65
  386.9 4.2 adam_part.14
  391.5 9.7 %collective-permute-done.65 = bf16[64,4096]{1,0:T(8,128)(2,1)S(1)} collective-permute-done((bf16[64,4096]{1,0:T(8,128)(2,1)S(1)}, bf16[64,4096]{1,0:T(8,128)(2,1)S(1)}, u32[]{:S(2)}, u32[]{:S(2)}) %collective-permute-start.65) | collective-permute-done | bytes 524320 | tf_op jit(solution)/shard_map/ppermute | solution.py:723
  404.0 3.0 collective-permute-done.68
  410.7 5.3 %collective-permute-done.69 = bf16[1,32,2176]{2,1,0:T(8,128)(2,1)S(1)} collective-permute-done((bf16[1,32,2176]{2,1,0:T(8,128)(2,1)S(1)}, bf16[1,32,2176]{2,1,0:T(8,128)(2,1)S(1)}, u32[]{:S(2)}, u32[]{:S(2)}) %collective-permute-start.69) | collective-permute-done | bytes 139296 | tf_op jit(solution)/shard_map/ppermute | solution.py:723
  416.1 1.6 collective-permute-start.70
  417.8 5.3 %collective-permute-done.71.refs_12_ = bf16[32,2176]{1,0:T(8,128)(2,1)S(1)} collective-permute-done((bf16[32,2176]{1,0:T(8,128)(2,1)S(1)}, bf16[32,2176]{1,0:T(8,128)(2,1)S(1)}, u32[]{:S(2)}, u32[]{:S(2)}) %collective-permute-start.71) | collective-permute-done | bytes 139296 | tf_op jit(solution)/shard_map/ppermute | solution.py:723
  423.5 1.7 collective-permute-start.73
  425.3 4.2 adam_part.15
  429.5 4.2 adam_part.16
  433.9 1.6 collective-permute-start.74
  435.6 4.3 adam_part.17
  439.8 4.2 adam_part.18
  444.1 4.2 adam_part.19
  449.2 4.2 adam_part.20
  453.4 7.4 %adam_part.21 = (f32[256,4096]{1,0:T(8,128)}, f32[256,4096]{1,0:T(8,128)}, f32[256,4096]{1,0:T(8,128)}, f32[256,4096]{1,0:T(8,128)}, bf16[256,4096]{1,0:T(8,128)(2,1)}, /*index=5*/f32[8,128]{1,0:T(8,128)}) custom-call(s32[2]{0:T(128)S(1)} %copy-done.26, ...), custom_call_target="tpu_custom_call", output_to_operand_aliasing={{0}: (7, {}), {1}: (8, {}), {2}: (9, {}), {3}: (10, {}), {4... | custom-call | flops 6442450944 | bytes 10485760 | tf_op jit(solution)/shard_map/adam_part/pallas_call | solution.py:97
  (396 shorter events, 107.2 us)
Async XLA Ops:
  3.8 17.2 %collective-permute-start = (bf16[16,256]{1,0:T(8,128)(2,1)S(1)}, bf16[16,256]{1,0:T(8,128)(2,1)S(1)}, u32[]{:S(2)}, u32[]{:S(2)}) collective-permute-start(bf16[16,256]{1,0:T(8,128)(2,1)S(1)} %get-tuple-element.388), channel_id=1, source_target_pairs={{0,1},{1,0},{2,3},{3,2},{4,5},{5,4},{6,7},{7,6},{8,9},{9,8},{10,11... | collective-permute-start | bytes 24584 | tf_op jit(solution)/shard_map/ppermute | solution.py:723
  4.3 23.7 %collective-permute-start.2 = (bf16[256,1536]{1,0:T(8,128)(2,1)}, bf16[256,1536]{1,0:T(8,128)(2,1)}, u32[]{:S(2)}, u32[]{:S(2)}) collective-permute-start(bf16[256,1536]{1,0:T(8,128)(2,1)} %pad_maximum_fusion.7), channel_id=1, source_target_pairs={{0,2},{1,3},{2,0},{3,1},{4,6},{5,7},{6,4},{7,5},{8,10},{9,11},{10,... | collective-permute-start | bytes 2359304 | tf_op jit(solution)/shard_map/ppermute | solution.py:723
  29.8 15.5 %collective-permute-start.6 = (bf16[256,4096]{1,0:T(8,128)(2,1)}, bf16[256,4096]{1,0:T(8,128)(2,1)}, u32[]{:S(2)}, u32[]{:S(2)}) collective-permute-start(bf16[256,4096]{1,0:T(8,128)(2,1)} %copy-done.42), channel_id=1, source_target_pairs={{0,1},{1,0},{2,3},{3,2},{4,5},{5,4},{6,7},{7,6},{8,9},{9,8},{10,11... | collective-permute-start | bytes 6291464 | tf_op jit(solution)/shard_map/ppermute | solution.py:723
  31.1 14.2 %collective-permute-start.5 = (bf16[112,2048]{1,0:T(8,128)(2,1)}, bf16[112,2048]{1,0:T(8,128)(2,1)S(1)}, u32[]{:S(2)}, u32[]{:S(2)}) collective-permute-start(bf16[112,2048]{1,0:T(8,128)(2,1)} %slice.227), channel_id=1, source_target_pairs={{0,2},{1,3},{2,0},{3,1},{4,6},{5,7},{6,4},{7,5},{8,10},{9,11},{10,... | collective-permute-start | bytes 1376264 | tf_op jit(solution)/shard_map/ppermute | solution.py:723
  32.9 11.5 %collective-permute-start.3 = (bf16[256,768]{1,0:T(8,128)(2,1)}, bf16[256,768]{1,0:T(8,128)(2,1)S(1)}, u32[]{:S(2)}, u32[]{:S(2)}) collective-permute-start(bf16[256,768]{1,0:T(8,128)(2,1)} %get-tuple-element.421), channel_id=1, source_target_pairs={{0,4},{4,0},{8,12},{12,8},{16,20},{20,16},{24,28},{28,24},{1,5},{5... | collective-permute-start | bytes 1179656 | tf_op jit(solution)/shard_map/ppermute | solution.py:723
  34.4 11.0 %collective-permute-start.4 = (bf16[256,768]{1,0:T(8,128)(2,1)S(1)}, bf16[256,768]{1,0:T(8,128)(2,1)S(1)}, u32[]{:S(2)}, u32[]{:S(2)}) collective-permute-start(bf16[256,768]{1,0:T(8,128)(2,1)S(1)} %get-tuple-element.422), channel_id=1, source_target_pairs={{0,8},{4,12},{8,0},{12,4},{16,24},{20,28},{24,16},{28,20},{1,9},{5... | collective-permute-start | bytes 1179656 | tf_op jit(solution)/shard_map/ppermute | solution.py:723
  47.0 16.2 %collective-permute-start.8 = (bf16[144,2048]{1,0:T(8,128)(2,1)S(1)}, bf16[144,2048]{1,0:T(8,128)(2,1)S(1)}, u32[]{:S(2)}, u32[]{:S(2)}) collective-permute-start(bf16[144,2048]{1,0:T(8,128)(2,1)S(1)} %slice.228), channel_id=1, source_target_pairs={{0,2},{1,3},{2,0},{3,1},{4,6},{5,7},{6,4},{7,5},{8,10},{9,11},{10,... | collective-permute-start | bytes 1769480 | tf_op jit(solution)/shard_map/ppermute | solution.py:723
  49.4 16.6 %collective-permute-start.9 = (bf16[80,1024]{1,0:T(8,128)(2,1)S(1)}, bf16[80,1024]{1,0:T(8,128)(2,1)S(1)}, u32[]{:S(2)}, u32[]{:S(2)}) collective-permute-start(bf16[80,1024]{1,0:T(8,128)(2,1)S(1)} %slice.233), channel_id=1, source_target_pairs={{0,2},{1,3},{2,0},{3,1},{4,6},{5,7},{6,4},{7,5},{8,10},{9,11},{10,... | collective-permute-start | bytes 491528 | tf_op jit(solution)/shard_map/ppermute | solution.py:723
  67.2 19.9 %collective-permute-start.14 = (bf16[256,8192]{1,0:T(8,128)(2,1)}, bf16[256,8192]{1,0:T(8,128)(2,1)}, u32[]{:S(2)}, u32[]{:S(2)}) collective-permute-start(bf16[256,8192]{1,0:T(8,128)(2,1)} %convert_element_type.511.refs_3_.refs_7_.refs_5_.refs_9_.refs_13_.refs_17_), channel_id=1, source_target_pairs={{0,1},{1,0},{2,3},{3,2},{4,5},{5,4},{6,7},{7,6},{8,9},{9,8},{10,11... | collective-permute-start | bytes 12582920 | tf_op jit(solution)/shard_map/ppermute | solution.py:723
  67.2 19.8 %collective-permute-start.10 = (bf16[256,1024]{1,0:T(8,128)(2,1)}, bf16[256,1024]{1,0:T(8,128)(2,1)S(1)}, u32[]{:S(2)}, u32[]{:S(2)}) collective-permute-start(bf16[256,1024]{1,0:T(8,128)(2,1)} %get-tuple-element.450), channel_id=1, source_target_pairs={{0,4},{4,0},{8,12},{12,8},{16,20},{20,16},{24,28},{28,24},{1,5},{5... | collective-permute-start | bytes 1572872 | tf_op jit(solution)/shard_map/ppermute | solution.py:723
  67.9 19.1 %collective-permute-start.11 = (bf16[256,1024]{1,0:T(8,128)(2,1)}, bf16[256,1024]{1,0:T(8,128)(2,1)S(1)}, u32[]{:S(2)}, u32[]{:S(2)}) collective-permute-start(bf16[256,1024]{1,0:T(8,128)(2,1)} %get-tuple-element.451), channel_id=1, source_target_pairs={{0,8},{4,12},{8,0},{12,4},{16,24},{20,28},{24,16},{28,20},{1,9},{5... | collective-permute-start | bytes 1572872 | tf_op jit(solution)/shard_map/ppermute | solution.py:723
  69.5 17.5 %collective-permute-start.12 = (bf16[176,1024]{1,0:T(8,128)(2,1)}, bf16[176,1024]{1,0:T(8,128)(2,1)S(1)}, u32[]{:S(2)}, u32[]{:S(2)}) collective-permute-start(bf16[176,1024]{1,0:T(8,128)(2,1)} %slice.236), channel_id=1, source_target_pairs={{0,2},{1,3},{2,0},{3,1},{4,6},{5,7},{6,4},{7,5},{8,10},{9,11},{10,... | collective-permute-start | bytes 1081352 | tf_op jit(solution)/shard_map/ppermute | solution.py:723
  71.0 16.0 %collective-permute-start.13 = (bf16[80,2048]{1,0:T(8,128)(2,1)}, bf16[80,2048]{1,0:T(8,128)(2,1)S(1)}, u32[]{:S(2)}, u32[]{:S(2)}) collective-permute-start(bf16[80,2048]{1,0:T(8,128)(2,1)} %slice.237), channel_id=1, source_target_pairs={{0,2},{1,3},{2,0},{3,1},{4,6},{5,7},{6,4},{7,5},{8,10},{9,11},{10,... | collective-permute-start | bytes 983048 | tf_op jit(solution)/shard_map/ppermute | solution.py:723
  88.1 18.5 %collective-permute-start.18 = (bf16[176,2048]{1,0:T(8,128)(2,1)S(1)}, bf16[176,2048]{1,0:T(8,128)(2,1)S(1)}, u32[]{:S(2)}, u32[]{:S(2)}) collective-permute-start(bf16[176,2048]{1,0:T(8,128)(2,1)S(1)} %slice.238), channel_id=1, source_target_pairs={{0,2},{1,3},{2,0},{3,1},{4,6},{5,7},{6,4},{7,5},{8,10},{9,11},{10,... | collective-permute-start | bytes 2162696 | tf_op jit(solution)/shard_map/ppermute | solution.py:723
  106.7 17.0 %collective-permute-start.19 = (bf16[256,1024]{1,0:T(8,128)(2,1)S(1)}, bf16[256,1024]{1,0:T(8,128)(2,1)S(1)}, u32[]{:S(2)}, u32[]{:S(2)}) collective-permute-start(bf16[256,1024]{1,0:T(8,128)(2,1)S(1)} %get-tuple-element.479), channel_id=1, source_target_pairs={{0,4},{4,0},{8,12},{12,8},{16,20},{20,16},{24,28},{28,24},{1,5},{5... | collective-permute-start | bytes 1572872 | tf_op jit(solution)/shard_map/ppermute | solution.py:723
  108.2 15.6 %collective-permute-start.20 = (bf16[256,1024]{1,0:T(8,128)(2,1)S(1)}, bf16[256,1024]{1,0:T(8,128)(2,1)S(1)}, u32[]{:S(2)}, u32[]{:S(2)}) collective-permute-start(bf16[256,1024]{1,0:T(8,128)(2,1)S(1)} %get-tuple-element.480), channel_id=1, source_target_pairs={{0,8},{4,12},{8,0},{12,4},{16,24},{20,28},{24,16},{28,20},{1,9},{5... | collective-permute-start | bytes 1572872 | tf_op jit(solution)/shard_map/ppermute | solution.py:723
  130.9 19.6 %collective-permute-start.22 = (bf16[256,2048]{1,0:T(8,128)(2,1)S(1)}, bf16[256,2048]{1,0:T(8,128)(2,1)S(1)}, u32[]{:S(2)}, u32[]{:S(2)}) collective-permute-start(bf16[256,2048]{1,0:T(8,128)(2,1)S(1)} %pad_maximum_fusion.5.refs_5_.refs_9_.refs_15_), channel_id=1, source_target_pairs={{0,1},{1,0},{2,3},{3,2},{4,5},{5,4},{6,7},{7,6},{8,9},{9,8},{10,11... | collective-permute-start | bytes 3145736 | tf_op jit(solution)/shard_map/ppermute | solution.py:723
  131.1 19.4 %collective-permute-start.23 = (bf16[256,2048]{1,0:T(8,128)(2,1)S(1)}, bf16[256,2048]{1,0:T(8,128)(2,1)S(1)}, u32[]{:S(2)}, u32[]{:S(2)}) collective-permute-start(bf16[256,2048]{1,0:T(8,128)(2,1)S(1)} %pad_maximum_fusion.6.refs_5_.refs_9_.refs_19_), channel_id=1, source_target_pairs={{0,1},{1,0},{2,3},{3,2},{4,5},{5,4},{6,7},{7,6},{8,9},{9,8},{10,11... | collective-permute-start | bytes 3145736 | tf_op jit(solution)/shard_map/ppermute | solution.py:723
  131.5 18.2 %collective-permute-start.24 = (bf16[176,2048]{1,0:T(8,128)(2,1)S(1)}, bf16[176,2048]{1,0:T(8,128)(2,1)S(1)}, u32[]{:S(2)}, u32[]{:S(2)}) collective-permute-start(bf16[176,2048]{1,0:T(8,128)(2,1)S(1)} %slice_bitcast_fusion.3), channel_id=1, source_target_pairs={{0,2},{1,3},{2,0},{3,1},{4,6},{5,7},{6,4},{7,5},{8,10},{9,11},{10,... | collective-permute-start | bytes 2162696 | tf_op jit(solution)/shard_map/ppermute | solution.py:723
  151.5 17.9 %collective-permute-start.26 = (bf16[2,256,2048]{2,1,0:T(8,128)(2,1)}, bf16[2,256,2048]{2,1,0:T(8,128)(2,1)S(1)}, u32[]{:S(2)}, u32[]{:S(2)}) collective-permute-start(bf16[2,256,2048]{2,1,0:T(8,128)(2,1)} %get-tuple-element.505), channel_id=1, source_target_pairs={{0,1},{1,0},{2,3},{3,2},{4,5},{5,4},{6,7},{7,6},{8,9},{9,8},{10,11... | collective-permute-start | bytes 6291464 | tf_op jit(solution)/shard_map/ppermute | solution.py:723
  151.5 17.9 %collective-permute-start.25 = (bf16[80,2048]{1,0:T(8,128)(2,1)}, bf16[80,2048]{1,0:T(8,128)(2,1)S(1)}, u32[]{:S(2)}, u32[]{:S(2)}) collective-permute-start(bf16[80,2048]{1,0:T(8,128)(2,1)} %slice_bitcast_fusion.7), channel_id=1, source_target_pairs={{0,2},{1,3},{2,0},{3,1},{4,6},{5,7},{6,4},{7,5},{8,10},{9,11},{10,... | collective-permute-start | bytes 983048 | tf_op jit(solution)/shard_map/ppermute | solution.py:723
  173.9 22.0 %collective-permute-start.29 = (bf16[2,256,2048]{2,1,0:T(8,128)(2,1)}, bf16[2,256,2048]{2,1,0:T(8,128)(2,1)S(1)}, u32[]{:S(2)}, u32[]{:S(2)}) collective-permute-start(bf16[2,256,2048]{2,1,0:T(8,128)(2,1)} %get-tuple-element.522), channel_id=1, source_target_pairs={{0,1},{1,0},{2,3},{3,2},{4,5},{5,4},{6,7},{7,6},{8,9},{9,8},{10,11... | collective-permute-start | bytes 6291464 | tf_op jit(solution)/shard_map/ppermute | solution.py:723
  174.2 21.7 %collective-permute-start.28 = (bf16[176,2048]{1,0:T(8,128)(2,1)}, bf16[176,2048]{1,0:T(8,128)(2,1)S(1)}, u32[]{:S(2)}, u32[]{:S(2)}) collective-permute-start(bf16[176,2048]{1,0:T(8,128)(2,1)} %slice_bitcast_fusion.2), channel_id=1, source_target_pairs={{0,2},{1,3},{2,0},{3,1},{4,6},{5,7},{6,4},{7,5},{8,10},{9,11},{10,... | collective-permute-start | bytes 2162696 | tf_op jit(solution)/shard_map/ppermute | solution.py:723
  175.5 20.4 %collective-permute-start.27 = (bf16[1,128,2048]{2,1,0:T(8,128)(2,1)}, bf16[1,128,2048]{2,1,0:T(8,128)(2,1)S(1)}, u32[]{:S(2)}, u32[]{:S(2)}) collective-permute-start(bf16[1,128,2048]{2,1,0:T(8,128)(2,1)} %fusion.18), channel_id=1, source_target_pairs={{0,4},{4,0},{8,12},{12,8},{16,20},{20,16},{24,28},{28,24},{1,5},{5... | collective-permute-start | bytes 1572872 | tf_op jit(solution)/shard_map/ppermute | solution.py:723
  199.8 27.2 %collective-permute-start.33 = (bf16[2,256,2048]{2,1,0:T(8,128)(2,1)}, bf16[2,256,2048]{2,1,0:T(8,128)(2,1)}, u32[]{:S(2)}, u32[]{:S(2)}) collective-permute-start(bf16[2,256,2048]{2,1,0:T(8,128)(2,1)} %get-tuple-element.536), channel_id=1, source_target_pairs={{0,1},{1,0},{2,3},{3,2},{4,5},{5,4},{6,7},{7,6},{8,9},{9,8},{10,11... | collective-permute-start | bytes 6291464 | tf_op jit(solution)/shard_map/ppermute | solution.py:723
  199.8 27.2 %collective-permute-start.32 = (bf16[192,2048]{1,0:T(8,128)(2,1)}, bf16[192,2048]{1,0:T(8,128)(2,1)S(1)}, u32[]{:S(2)}, u32[]{:S(2)}) collective-permute-start(bf16[192,2048]{1,0:T(8,128)(2,1)} %slice_bitcast_fusion.1), channel_id=1, source_target_pairs={{0,2},{1,3},{2,0},{3,1},{4,6},{5,7},{6,4},{7,5},{8,10},{9,11},{10,... | collective-permute-start | bytes 2359304 | tf_op jit(solution)/shard_map/ppermute | solution.py:723
  201.4 25.6 %collective-permute-start.31 = (bf16[80,2048]{1,0:T(8,128)(2,1)}, bf16[80,2048]{1,0:T(8,128)(2,1)S(1)}, u32[]{:S(2)}, u32[]{:S(2)}) collective-permute-start(bf16[80,2048]{1,0:T(8,128)(2,1)} %slice_bitcast_fusion.6), channel_id=1, source_target_pairs={{0,2},{1,3},{2,0},{3,1},{4,6},{5,7},{6,4},{7,5},{8,10},{9,11},{10,... | collective-permute-start | bytes 983048 | tf_op jit(solution)/shard_map/ppermute | solution.py:723
  201.8 23.4 %collective-permute-start.30 = (bf16[1,64,2048]{2,1,0:T(8,128)(2,1)}, bf16[1,64,2048]{2,1,0:T(8,128)(2,1)S(1)}, u32[]{:S(2)}, u32[]{:S(2)}) collective-permute-start(bf16[1,64,2048]{2,1,0:T(8,128)(2,1)} %constant_dynamic-slice_fusion.3), channel_id=1, source_target_pairs={{0,8},{4,12},{8,0},{12,4},{16,24},{20,28},{24,16},{28,20},{1,9},{5... | collective-permute-start | bytes 786440 | tf_op jit(solution)/shard_map/ppermute | solution.py:723
  230.8 21.1 %collective-permute-start.38 = (bf16[2,256,1024]{2,1,0:T(8,128)(2,1)S(1)}, bf16[2,256,1024]{2,1,0:T(8,128)(2,1)S(1)}, u32[]{:S(2)}, u32[]{:S(2)}) collective-permute-start(bf16[2,256,1024]{2,1,0:T(8,128)(2,1)S(1)} %copy-done.70), channel_id=1, source_target_pairs={{0,1},{1,0},{2,3},{3,2},{4,5},{5,4},{6,7},{7,6},{8,9},{9,8},{10,11... | collective-permute-start | bytes 3145736 | tf_op jit(solution)/shard_map/ppermute | solution.py:723
  230.8 21.1 %collective-permute-start.35 = (bf16[1,128,2048]{2,1,0:T(8,128)(2,1)S(1)}, bf16[1,128,2048]{2,1,0:T(8,128)(2,1)S(1)}, u32[]{:S(2)}, u32[]{:S(2)}) collective-permute-start(bf16[1,128,2048]{2,1,0:T(8,128)(2,1)S(1)} %fusion.15), channel_id=1, source_target_pairs={{0,4},{4,0},{8,12},{12,8},{16,20},{20,16},{24,28},{28,24},{1,5},{5... | collective-permute-start | bytes 1572872 | tf_op jit(solution)/shard_map/ppermute | solution.py:723
  232.2 19.6 %collective-permute-start.37 = (bf16[128,2048]{1,0:T(8,128)(2,1)S(1)}, bf16[128,2048]{1,0:T(8,128)(2,1)S(1)}, u32[]{:S(2)}, u32[]{:S(2)}) collective-permute-start(bf16[128,2048]{1,0:T(8,128)(2,1)S(1)} %get-tuple-element.550), channel_id=1, source_target_pairs={{0,2},{1,3},{2,0},{3,1},{4,6},{5,7},{6,4},{7,5},{8,10},{9,11},{10,... | collective-permute-start | bytes 1572872 | tf_op jit(solution)/shard_map/ppermute | solution.py:723
  233.0 18.9 %collective-permute-start.36 = (bf16[64,2048]{1,0:T(8,128)(2,1)S(1)}, bf16[64,2048]{1,0:T(8,128)(2,1)S(1)}, u32[]{:S(2)}, u32[]{:S(2)}) collective-permute-start(bf16[64,2048]{1,0:T(8,128)(2,1)S(1)} %slice_bitcast_fusion.11), channel_id=1, source_target_pairs={{0,2},{1,3},{2,0},{3,1},{4,6},{5,7},{6,4},{7,5},{8,10},{9,11},{10,... | collective-permute-start | bytes 786440 | tf_op jit(solution)/shard_map/ppermute | solution.py:723
  234.3 17.1 %collective-permute-start.34 = (bf16[1,32,2048]{2,1,0:T(8,128)(2,1)S(1)}, bf16[1,32,2048]{2,1,0:T(8,128)(2,1)S(1)}, u32[]{:S(2)}, u32[]{:S(2)}) collective-permute-start(bf16[1,32,2048]{2,1,0:T(8,128)(2,1)S(1)} %add_convert_fusion.16), channel_id=1, source_target_pairs={{0,16},{4,20},{8,24},{12,28},{16,0},{20,4},{24,8},{28,12},{1,17},{... | collective-permute-start | bytes 393224 | tf_op jit(solution)/shard_map/ppermute | solution.py:723
  253.8 20.7 %collective-permute-start.41 = (bf16[1,128,2048]{2,1,0:T(8,128)(2,1)S(1)}, bf16[1,128,2048]{2,1,0:T(8,128)(2,1)S(1)}, u32[]{:S(2)}, u32[]{:S(2)}) collective-permute-start(bf16[1,128,2048]{2,1,0:T(8,128)(2,1)S(1)} %fusion.12), channel_id=1, source_target_pairs={{0,4},{4,0},{8,12},{12,8},{16,20},{20,16},{24,28},{28,24},{1,5},{5... | collective-permute-start | bytes 1572872 | tf_op jit(solution)/shard_map/ppermute | solution.py:723
  254.5 20.0 %collective-permute-start.42 = (bf16[128,2048]{1,0:T(8,128)(2,1)S(1)}, bf16[128,2048]{1,0:T(8,128)(2,1)S(1)}, u32[]{:S(2)}, u32[]{:S(2)}) collective-permute-start(bf16[128,2048]{1,0:T(8,128)(2,1)S(1)} %get-tuple-element.567), channel_id=1, source_target_pairs={{0,2},{1,3},{2,0},{3,1},{4,6},{5,7},{6,4},{7,5},{8,10},{9,11},{10,... | collective-permute-start | bytes 1572872 | tf_op jit(solution)/shard_map/ppermute | solution.py:723
  256.1 18.4 %collective-permute-start.40 = (bf16[1,64,2048]{2,1,0:T(8,128)(2,1)S(1)}, bf16[1,64,2048]{2,1,0:T(8,128)(2,1)S(1)}, u32[]{:S(2)}, u32[]{:S(2)}) collective-permute-start(bf16[1,64,2048]{2,1,0:T(8,128)(2,1)S(1)} %constant_dynamic-slice_fusion), channel_id=1, source_target_pairs={{0,8},{4,12},{8,0},{12,4},{16,24},{20,28},{24,16},{28,20},{1,9},{5... | collective-permute-start | bytes 786440 | tf_op jit(solution)/shard_map/ppermute | solution.py:723
  257.7 16.8 %collective-permute-start.43 = (bf16[128,1024]{1,0:T(8,128)(2,1)S(1)}, bf16[128,1024]{1,0:T(8,128)(2,1)S(1)}, u32[]{:S(2)}, u32[]{:S(2)}) collective-permute-start(bf16[128,1024]{1,0:T(8,128)(2,1)S(1)} %get-tuple-element.568), channel_id=1, source_target_pairs={{0,2},{1,3},{2,0},{3,1},{4,6},{5,7},{6,4},{7,5},{8,10},{9,11},{10,... | collective-permute-start | bytes 786440 | tf_op jit(solution)/shard_map/ppermute | solution.py:723
  258.1 16.4 %collective-permute-start.39 = (bf16[32,2048]{1,0:T(8,128)(2,1)S(1)}, bf16[32,2048]{1,0:T(8,128)(2,1)S(1)}, u32[]{:S(2)}, u32[]{:S(2)}) collective-permute-start(bf16[32,2048]{1,0:T(8,128)(2,1)S(1)} %fusion.28), channel_id=1, source_target_pairs={{0,16},{4,20},{8,24},{12,28},{16,0},{20,4},{24,8},{28,12},{1,17},{... | collective-permute-start | bytes 393224 | tf_op jit(solution)/shard_map/ppermute | solution.py:723
  276.4 12.6 %collective-permute-start.46 = (bf16[1,128,2048]{2,1,0:T(8,128)(2,1)S(1)}, bf16[1,128,2048]{2,1,0:T(8,128)(2,1)S(1)}, u32[]{:S(2)}, u32[]{:S(2)}) collective-permute-start(bf16[1,128,2048]{2,1,0:T(8,128)(2,1)S(1)} %fusion.11), channel_id=1, source_target_pairs={{0,4},{4,0},{8,12},{12,8},{16,20},{20,16},{24,28},{28,24},{1,5},{5... | collective-permute-start | bytes 1572872 | tf_op jit(solution)/shard_map/ppermute | solution.py:723
  277.8 11.1 %collective-permute-start.44 = (bf16[64,2048]{1,0:T(8,128)(2,1)S(1)}, bf16[64,2048]{1,0:T(8,128)(2,1)S(1)}, u32[]{:S(2)}, u32[]{:S(2)}) collective-permute-start(bf16[64,2048]{1,0:T(8,128)(2,1)S(1)} %maximum_select_fusion.9), channel_id=1, source_target_pairs={{0,8},{4,12},{8,0},{12,4},{16,24},{20,28},{24,16},{28,20},{1,9},{5... | collective-permute-start | bytes 786440 | tf_op jit(solution)/shard_map/ppermute | solution.py:723
  278.3 10.7 %collective-permute-start.47 = (bf16[128,1024]{1,0:T(8,128)(2,1)S(1)}, bf16[128,1024]{1,0:T(8,128)(2,1)S(1)}, u32[]{:S(2)}, u32[]{:S(2)}) collective-permute-start(bf16[128,1024]{1,0:T(8,128)(2,1)S(1)} %get-tuple-element.583), channel_id=1, source_target_pairs={{0,2},{1,3},{2,0},{3,1},{4,6},{5,7},{6,4},{7,5},{8,10},{9,11},{10,... | collective-permute-start | bytes 786440 | tf_op jit(solution)/shard_map/ppermute | solution.py:723
  279.0 9.9 %collective-permute-start.45 = (bf16[1,32,2048]{2,1,0:T(8,128)(2,1)S(1)}, bf16[1,32,2048]{2,1,0:T(8,128)(2,1)S(1)}, u32[]{:S(2)}, u32[]{:S(2)}) collective-permute-start(bf16[1,32,2048]{2,1,0:T(8,128)(2,1)S(1)} %add_convert_fusion.14), channel_id=1, source_target_pairs={{0,16},{4,20},{8,24},{12,28},{16,0},{20,4},{24,8},{28,12},{1,17},{... | collective-permute-start | bytes 393224 | tf_op jit(solution)/shard_map/ppermute | solution.py:723
  301.6 23.2 %collective-permute-start.49 = (bf16[192,2048]{1,0:T(8,128)(2,1)}, bf16[192,2048]{1,0:T(8,128)(2,1)}, u32[]{:S(2)}, u32[]{:S(2)}) collective-permute-start(bf16[192,2048]{1,0:T(8,128)(2,1)} %slice_bitcast_fusion), channel_id=1, source_target_pairs={{0,2},{1,3},{2,0},{3,1},{4,6},{5,7},{6,4},{7,5},{8,10},{9,11},{10,... | collective-permute-start | bytes 2359304 | tf_op jit(solution)/shard_map/ppermute | solution.py:723
  302.9 21.8 %collective-permute-start.50 = (bf16[128,2048]{1,0:T(8,128)(2,1)}, bf16[128,2048]{1,0:T(8,128)(2,1)S(1)}, u32[]{:S(2)}, u32[]{:S(2)}) collective-permute-start(bf16[128,2048]{1,0:T(8,128)(2,1)} %maximum_select_fusion.4.refs_2_), channel_id=1, source_target_pairs={{0,4},{4,0},{8,12},{12,8},{16,20},{20,16},{24,28},{28,24},{1,5},{5... | collective-permute-start | bytes 1572872 | tf_op jit(solution)/shard_map/ppermute | solution.py:723
  303.6 21.2 %collective-permute-start.52 = (bf16[1,64,4096]{2,1,0:T(8,128)(2,1)}, bf16[1,64,4096]{2,1,0:T(8,128)(2,1)}, u32[]{:S(2)}, u32[]{:S(2)}) collective-permute-start(bf16[1,64,4096]{2,1,0:T(8,128)(2,1)} %constant_dynamic-slice_fusion.1), channel_id=1, source_target_pairs={{0,8},{4,12},{8,0},{12,4},{16,24},{20,28},{24,16},{28,20},{1,9},{5... | collective-permute-start | bytes 1572872 | tf_op jit(solution)/shard_map/ppermute | solution.py:723
  305.1 19.6 %collective-permute-start.53 = (bf16[1,128,1024]{2,1,0:T(8,128)(2,1)}, bf16[1,128,1024]{2,1,0:T(8,128)(2,1)}, u32[]{:S(2)}, u32[]{:S(2)}) collective-permute-start(bf16[1,128,1024]{2,1,0:T(8,128)(2,1)} %fusion.25), channel_id=1, source_target_pairs={{0,4},{4,0},{8,12},{12,8},{16,20},{20,16},{24,28},{28,24},{1,5},{5... | collective-permute-start | bytes 786440 | tf_op jit(solution)/shard_map/ppermute | solution.py:723
  306.6 18.2 %collective-permute-start.51 = (bf16[32,2048]{1,0:T(8,128)(2,1)}, bf16[32,2048]{1,0:T(8,128)(2,1)S(1)}, u32[]{:S(2)}, u32[]{:S(2)}) collective-permute-start(bf16[32,2048]{1,0:T(8,128)(2,1)} %fusion.29), channel_id=1, source_target_pairs={{0,16},{4,20},{8,24},{12,28},{16,0},{20,4},{24,8},{28,12},{1,17},{... | collective-permute-start | bytes 393224 | tf_op jit(solution)/shard_map/ppermute | solution.py:723
  328.6 9.0 %collective-permute-start.54 = (bf16[64,2048]{1,0:T(8,128)(2,1)S(1)}, bf16[64,2048]{1,0:T(8,128)(2,1)S(1)}, u32[]{:S(2)}, u32[]{:S(2)}) collective-permute-start(bf16[64,2048]{1,0:T(8,128)(2,1)S(1)} %copy-done.62), channel_id=1, source_target_pairs={{0,2},{1,3},{2,0},{3,1},{4,6},{5,7},{6,4},{7,5},{8,10},{9,11},{10,... | collective-permute-start | bytes 786440 | tf_op jit(solution)/shard_map/ppermute | solution.py:723
  339.1 16.6 %collective-permute-start.57 = (bf16[2,256,1152]{2,1,0:T(8,128)(2,1)S(1)}, bf16[2,256,1152]{2,1,0:T(8,128)(2,1)S(1)}, u32[]{:S(2)}, u32[]{:S(2)}) collective-permute-start(bf16[2,256,1152]{2,1,0:T(8,128)(2,1)S(1)} %copy-done.11), channel_id=1, source_target_pairs={{0,1},{1,0},{2,3},{3,2},{4,5},{5,4},{6,7},{7,6},{8,9},{9,8},{10,11... | collective-permute-start | bytes 3538952 | tf_op jit(solution)/shard_map/ppermute | solution.py:723
  339.1 16.5 %collective-permute-start.56 = (bf16[1,128,2048]{2,1,0:T(8,128)(2,1)S(1)}, bf16[1,128,2048]{2,1,0:T(8,128)(2,1)S(1)}, u32[]{:S(2)}, u32[]{:S(2)}) collective-permute-start(bf16[1,128,2048]{2,1,0:T(8,128)(2,1)S(1)} %fusion.6), channel_id=1, source_target_pairs={{0,4},{4,0},{8,12},{12,8},{16,20},{20,16},{24,28},{28,24},{1,5},{5... | collective-permute-start | bytes 1572872 | tf_op jit(solution)/shard_map/ppermute | solution.py:723
  340.7 15.0 %collective-permute-start.58 = (bf16[1,32,4096]{2,1,0:T(8,128)(2,1)S(1)}, bf16[1,32,4096]{2,1,0:T(8,128)(2,1)S(1)}, u32[]{:S(2)}, u32[]{:S(2)}) collective-permute-start(bf16[1,32,4096]{2,1,0:T(8,128)(2,1)S(1)} %add_convert_fusion.8), channel_id=1, source_target_pairs={{0,16},{4,20},{8,24},{12,28},{16,0},{20,4},{24,8},{28,12},{1,17},{... | collective-permute-start | bytes 786440 | tf_op jit(solution)/shard_map/ppermute | solution.py:723
  357.5 13.8 %collective-permute-start.59 = (bf16[1,64,2048]{2,1,0:T(8,128)(2,1)S(1)}, bf16[1,64,2048]{2,1,0:T(8,128)(2,1)S(1)}, u32[]{:S(2)}, u32[]{:S(2)}) collective-permute-start(bf16[1,64,2048]{2,1,0:T(8,128)(2,1)S(1)} %constant_dynamic-slice_fusion.4), channel_id=1, source_target_pairs={{0,8},{4,12},{8,0},{12,4},{16,24},{20,28},{24,16},{28,20},{1,9},{5... | collective-permute-start | bytes 786440 | tf_op jit(solution)/shard_map/ppermute | solution.py:723
  359.1 19.7 %collective-permute-start.61 = (bf16[256,1152]{1,0:T(8,128)(2,1)S(1)}, bf16[256,1152]{1,0:T(8,128)(2,1)S(1)}, u32[]{:S(2)}, u32[]{:S(2)}) collective-permute-start(bf16[256,1152]{1,0:T(8,128)(2,1)S(1)} %fusion.19), channel_id=1, source_target_pairs={{0,2},{1,3},{2,0},{3,1},{4,6},{5,7},{6,4},{7,5},{8,10},{9,11},{10,... | collective-permute-start | bytes 1769480 | tf_op jit(solution)/shard_map/ppermute | solution.py:723
  359.6 19.2 %collective-permute-start.62 = (bf16[128,2048]{1,0:T(8,128)(2,1)S(1)}, bf16[128,2048]{1,0:T(8,128)(2,1)S(1)}, u32[]{:S(2)}, u32[]{:S(2)}) collective-permute-start(bf16[128,2048]{1,0:T(8,128)(2,1)S(1)} %maximum_select_fusion.5.refs_2_), channel_id=1, source_target_pairs={{0,4},{4,0},{8,12},{12,8},{16,20},{20,16},{24,28},{28,24},{1,5},{5... | collective-permute-start | bytes 1572872 | tf_op jit(solution)/shard_map/ppermute | solution.py:723
  361.0 17.8 %collective-permute-start.63 = (bf16[32,4096]{1,0:T(8,128)(2,1)S(1)}, bf16[32,4096]{1,0:T(8,128)(2,1)S(1)}, u32[]{:S(2)}, u32[]{:S(2)}) collective-permute-start(bf16[32,4096]{1,0:T(8,128)(2,1)S(1)} %fusion.26), channel_id=1, source_target_pairs={{0,16},{4,20},{8,24},{12,28},{16,0},{20,4},{24,8},{28,12},{1,17},{... | collective-permute-start | bytes 786440 | tf_op jit(solution)/shard_map/ppermute | solution.py:723
  371.4 12.4 %collective-permute-start.60 = (bf16[1,32,2048]{2,1,0:T(8,128)(2,1)S(1)}, bf16[1,32,2048]{2,1,0:T(8,128)(2,1)S(1)}, u32[]{:S(2)}, u32[]{:S(2)}) collective-permute-start(bf16[1,32,2048]{2,1,0:T(8,128)(2,1)S(1)} %add_convert_fusion.12), channel_id=1, source_target_pairs={{0,16},{4,20},{8,24},{12,28},{16,0},{20,4},{24,8},{28,12},{1,17},{... | collective-permute-start | bytes 393224 | tf_op jit(solution)/shard_map/ppermute | solution.py:723
  384.5 16.7 %collective-permute-start.65 = (bf16[64,4096]{1,0:T(8,128)(2,1)S(1)}, bf16[64,4096]{1,0:T(8,128)(2,1)S(1)}, u32[]{:S(2)}, u32[]{:S(2)}) collective-permute-start(bf16[64,4096]{1,0:T(8,128)(2,1)S(1)} %maximum_select_fusion.6), channel_id=1, source_target_pairs={{0,8},{4,12},{8,0},{12,4},{16,24},{20,28},{24,16},{28,20},{1,9},{5... | collective-permute-start | bytes 1572872 | tf_op jit(solution)/shard_map/ppermute | solution.py:723
  391.3 15.6 %collective-permute-start.68 = (bf16[1,64,2176]{2,1,0:T(8,128)(2,1)S(1)}, bf16[1,64,2176]{2,1,0:T(8,128)(2,1)S(1)}, u32[]{:S(2)}, u32[]{:S(2)}) collective-permute-start(bf16[1,64,2176]{2,1,0:T(8,128)(2,1)S(1)} %constant_dynamic-slice_fusion.2), channel_id=1, source_target_pairs={{0,8},{4,12},{8,0},{12,4},{16,24},{20,28},{24,16},{28,20},{1,9},{5... | collective-permute-start | bytes 835592 | tf_op jit(solution)/shard_map/ppermute | solution.py:723
  401.4 8.4 %collective-permute-start.67 = (bf16[64,2048]{1,0:T(8,128)(2,1)S(1)}, bf16[64,2048]{1,0:T(8,128)(2,1)S(1)}, u32[]{:S(2)}, u32[]{:S(2)}) collective-permute-start(bf16[64,2048]{1,0:T(8,128)(2,1)S(1)} %maximum_select_fusion.11), channel_id=1, source_target_pairs={{0,8},{4,12},{8,0},{12,4},{16,24},{20,28},{24,16},{28,20},{1,9},{5... | collective-permute-start | bytes 786440 | tf_op jit(solution)/shard_map/ppermute | solution.py:723
  402.5 21.0 %collective-permute-start.72 = (bf16[128,4096]{1,0:T(8,128)(2,1)S(1)}, bf16[128,4096]{1,0:T(8,128)(2,1)S(1)}, u32[]{:S(2)}, u32[]{:S(2)}) collective-permute-start(bf16[128,4096]{1,0:T(8,128)(2,1)S(1)} %maximum_select_fusion.refs_2_), channel_id=1, source_target_pairs={{0,4},{4,0},{8,12},{12,8},{16,20},{20,16},{24,28},{28,24},{1,5},{5... | collective-permute-start | bytes 3145736 | tf_op jit(solution)/shard_map/ppermute | solution.py:723
  407.0 8.9 %collective-permute-start.69 = (bf16[1,32,2176]{2,1,0:T(8,128)(2,1)S(1)}, bf16[1,32,2176]{2,1,0:T(8,128)(2,1)S(1)}, u32[]{:S(2)}, u32[]{:S(2)}) collective-permute-start(bf16[1,32,2176]{2,1,0:T(8,128)(2,1)S(1)} %add_convert_fusion.10), channel_id=1, source_target_pairs={{0,16},{4,20},{8,24},{12,28},{16,0},{20,4},{24,8},{28,12},{1,17},{... | collective-permute-start | bytes 417800 | tf_op jit(solution)/shard_map/ppermute | solution.py:723
  416.1 17.6 %collective-permute-start.70 = (bf16[128,2048]{1,0:T(8,128)(2,1)}, bf16[128,2048]{1,0:T(8,128)(2,1)S(1)}, u32[]{:S(2)}, u32[]{:S(2)}) collective-permute-start(bf16[128,2048]{1,0:T(8,128)(2,1)} %maximum_select_fusion.7.refs_2_), channel_id=1, source_target_pairs={{0,4},{4,0},{8,12},{12,8},{16,20},{20,16},{24,28},{28,24},{1,5},{5... | collective-permute-start | bytes 1572872 | tf_op jit(solution)/shard_map/ppermute | solution.py:723
  423.5 10.2 %collective-permute-start.73 = (bf16[64,2176]{1,0:T(8,128)(2,1)S(1)}, bf16[64,2176]{1,0:T(8,128)(2,1)S(1)}, u32[]{:S(2)}, u32[]{:S(2)}) collective-permute-start(bf16[64,2176]{1,0:T(8,128)(2,1)S(1)} %maximum_select_fusion.8), channel_id=1, source_target_pairs={{0,8},{4,12},{8,0},{12,4},{16,24},{20,28},{24,16},{28,20},{1,9},{5... | collective-permute-start | bytes 835592 | tf_op jit(solution)/shard_map/ppermute | solution.py:723
  433.9 14.5 %collective-permute-start.74 = (bf16[128,2176]{1,0:T(8,128)(2,1)S(1)}, bf16[128,2176]{1,0:T(8,128)(2,1)S(1)}, u32[]{:S(2)}, u32[]{:S(2)}) collective-permute-start(bf16[128,2176]{1,0:T(8,128)(2,1)S(1)} %maximum_select_fusion.3.refs_2_), channel_id=1, source_target_pairs={{0,4},{4,0},{8,12},{12,8},{16,20},{20,16},{24,28},{28,24},{1,5},{5... | collective-permute-start | bytes 1671176 | tf_op jit(solution)/shard_map/ppermute | solution.py:723
  (83 other events, 526.7 us)

commit v4 on v3

--- a/solution.py
+++ b/solution.py
@@ -1058,6 +1058,35 @@
         part = lax.psum(part, "replica")
         totals.append((name, (part[: part.shape[0] // 2], part[part.shape[0] // 2 :])))
 
+    outs = {"attn": [], "mlp": []}
+    state = {
+        "attn": (attn_w, attn_m, attn_v, image_total, 0.1, 0.05),
+        "mlp": (mlp_w, mlp_m, mlp_v, image_total, 0.05, 0.05),
+    }
+    small_outs, pieces = [], []
+    second = (links.place(1) if links.direct else jnp.zeros((), jnp.int32)).reshape(1)
+
+    def collect():
+        through = lambda total: not isinstance(total, Flow) or total.done
+        for name, total in [entry for entry in totals if through(entry[1])]:
+            total = total.value if isinstance(total, Flow) else total
+            if total[0].shape[1] % D:
+                some = [half[:, 2 * D : 2 * D + 12] for half in total]
+                gradient = jnp.where(
+                    second[0] == 1, jnp.concatenate(some[::-1]), jnp.concatenate(some)
+                )
+                gradient = gradient.astype(F32) / image_total
+                small_outs.extend(adam_terms(vectors, small_m, small_v, gradient, 1.0, 0.0))
+            pieces.extend((name[0], total, n, column) for n, column in enumerate(name[1:]))
+        totals[:] = [entry for entry in totals if not through(entry[1])]
+
+    def adam_some(after, fit):
+        kind, total, first, _ = pieces[0]
+        columns = [c for k, t, _, c in pieces if t is total][:fit]
+        outs[kind], mark = adam_part(total, second, first, columns, *state[kind], outs[kind], after)
+        pipe.spend(1.0 + 3.2 * len(columns), mark)
+        del pieces[: len(columns)]
+
     qkv = qkv_forward(order, h1, wqkv, vec, after)
     pipe.spend(15, qkv)
     if links.direct:
@@ -1137,43 +1166,24 @@
     send, keep = query_grad(order, h1, dqkv, small, pipe.turn(10))
     pipe.spend(10, send)
     chunk(("attn", 3, 0), out_part, summed(send, keep, True))
+    if links.direct:
+        after = pipe.turn(5)
+        collect()
+        if pieces:
+            adam_some(after, 1)
     result = mlp_out(order, acts, wdns, middle, valid.astype(F32), vec, pipe.turn(17))
     pipe.spend(17, result)
     result = result.reshape(images, slots, D)
 
-    outs = {"attn": [], "mlp": []}
-    state = {
-        "attn": (attn_w, attn_m, attn_v, image_total, 0.1, 0.05),
-        "mlp": (mlp_w, mlp_m, mlp_v, image_total, 0.05, 0.05),
-    }
-    small_out, pieces = None, []
-    second = (links.place(1) if links.direct else jnp.zeros((), jnp.int32)).reshape(1)
     while totals or pieces:
         after = pipe.turn()
-        through = lambda total: not isinstance(total, Flow) or total.done
-        for name, total in [entry for entry in totals if through(entry[1])]:
-            total = total.value if isinstance(total, Flow) else total
-            if total[0].shape[1] % D:
-                some = [half[:, 2 * D : 2 * D + 12] for half in total]
-                gradient = jnp.where(
-                    second[0] == 1, jnp.concatenate(some[::-1]), jnp.concatenate(some)
-                )
-                gradient = gradient.astype(F32) / image_total
-                small_out = adam_terms(vectors, small_m, small_v, gradient, 1.0, 0.0)
-            pieces += [(name[0], total, n, column) for n, column in enumerate(name[1:])]
-        totals = [entry for entry in totals if not through(entry[1])]
-        wait = pipe.wait() if totals else 1000.0
-        kind, total, first, _ = pieces[0] if pieces else (None,) * 4
-        fit = 1 if totals else 4
-        columns = [c for k, t, _, c in pieces if t is total][:fit]
-        if columns:
-            outs[kind], mark = adam_part(total, second, first, columns, *state[kind], outs[kind], after)
-            pipe.spend(1.0 + 3.2 * len(columns), mark)
-            pieces = pieces[len(columns) :]
+        collect()
+        if pieces:
+            adam_some(after, (2 if len(totals) < 3 else 1) if totals else 4)
         elif totals:
             pipe.skip(1.5)
     attn_out, mlp_out_ = outs["attn"], outs["mlp"]
-    return (result, in_grad, *attn_out, *mlp_out_, *small_out)
+    return (result, in_grad, *attn_out, *mlp_out_, *small_outs)
 
 
 def solution(mesh):

time: 470 us -> 501 us (1.066)
  waiting for transfers between devices: 68.2 us -> 98 us
  starting transfers between devices: 70.8 us -> 65.7 us
    ppermute x75, waiting for transfers between devices: 68.2 us -> 98 us  [swap(): return lax.ppermute(values, axis, [(i, i ^ bit) for i in range(size)])]
    ppermute x75, starting transfers between devices: 70.8 us -> 65.7 us  [swap(): return lax.ppermute(values, axis, [(i, i ^ bit) for i in range(size)])]
    pallas_call x25 -> x22, Pallas kernels: 238 us -> 235 us  [call(): pl.pallas_call(with_after, grid_spec=pltpu.PrefetchScalarGridSpec(num_sca...]
    unnamed x155 -> x189, local copies, waits for them, and re-layouts: 18 us -> 17.5 us
  transfers between devices with their start and end apart: 75 -> 75, of which waited for: 21 -> 26; matrix products, arithmetic and copies ran while one was open for 7% -> 7% of each run, Pallas kernels for 49% -> 45%
where the time goes in v4:
time: 501 us; the launch traced here: 492 us
  Pallas kernels  235 us (47%)
  waiting for transfers between devices  98 us (20%)
  starting transfers between devices  65.7 us (13%)
  local copies, waits for them, and re-layouts  45.7 us (9%)
  other arithmetic  45 us (9%)
    pallas_call x22, Pallas kernels, call(): pl.pallas_call(with_after, grid_spec=pltpu.PrefetchScalarGridSpec(num_sca...  235 us
    ppermute x75, waiting for transfers between devices, swap(): return lax.ppermute(values, axis, [(i, i ^ bit) for i in range(size)])  98 us
    ppermute x75, starting transfers between devices, swap(): return lax.ppermute(values, axis, [(i, i ^ bit) for i in range(size)])  65.7 us
    convert_element_type x26, other arithmetic, added(): return sum((t.astype(F32) for t in terms)).astype(BF16)  21.3 us
    unnamed x189, local copies, waits for them, and re-layouts  17.5 us
    slice x16, local copies, waits for them, and re-layouts, start(): values = values[flow.sent:flow.sent + left]  12.8 us
  transfers between devices with their start and end apart: 75, of which 26 were waited for; matrix products, arithmetic and copies ran while one was open for 7% of the time, Pallas kernels for 45%

profile of v4, /device:TPU:0, one launch (start us, length us, event | category | flops | bytes accessed | tf_op | source)
XLA Modules:
  0.0 492.3 jit_solution(9317340820162983000)
XLA Ops:
  4.3 2.5 collective-permute-start.2
  6.8 2.5 dynamic-slice_convert_fusion.1
  13.3 6.1 %convert_element_type.511.refs_3_.refs_7_.refs_5_.refs_9_.refs_13_.refs_17_ = bf16[256,8192]{1,0:T(8,128)(2,1)} convert(f32[256,8192]{1,0:T(8,128)} %refs_4_.13) | non-fusion elementwise | flops 2097152 | bytes 12582912 | tf_op jit(solution)/shard_map/convert_element_type | solution.py:1012
  21.2 4.4 collective-permute-done.1
  26.1 1.8 slice.227
  28.0 1.9 fusion.41
  37.7 2.0 fusion.3.refs_1_
  39.7 3.5 collective-permute-done.3
  44.9 2.7 collective-permute-done.5
  53.2 11.8 %qkv_forward.1.refs_1_.refs_4_.refs_7_ = bf16[960,3072]{1,0:T(8,128)(2,1)} custom-call(s32[4]{0:T(128)S(1)} %iota_xor_fusion.refs_0_.refs_8_, bf16[960,1024]{1,0:T(8,128)(2,1)} %fusion.3.refs_1_, bf16[256,4096]{1,0:T(8,128)(2,1)} %copy-done.50, bf16[256,4096]{1,0:T(8,128)(2,1)} %collective-permute-done.6.refs_3_.refs_4_, bf16[256,3072]{1,0:T(8,128)(2,1)} %copy-done.68, ...), custom_call_target="tpu_custom_call" | custom-call | flops 10066329600 | bytes 18874368 | tf_op jit(solution)/shard_map/qkv_forward/pallas_call | solution.py:97
  65.7 2.6 collective-permute-done.9.refs_3_
  70.2 1.7 collective-permute-start.12
  72.2 13.2 %attn_mix.1.refs_2_.refs_11_.refs_24_ = bf16[960,1024]{1,0:T(8,128)(2,1)} custom-call(s32[6]{0:T(128)S(1)} %copy-done.34, bf16[960,3072]{1,0:T(8,128)(2,1)} %qkv_forward.1.refs_1_.refs_4_.refs_7_, bf16[144,2048]{1,0:T(8,128)(2,1)S(1)} %collective-permute-done.8.refs_2_, bf16[80,1024]{1,0:T(8,128)(2,1)S(1)} %collective-permute-done.9.refs_3_, ...), custom_call_target="tpu_custom_call" | custom-call | flops 14092861440 | bytes 8388608 | tf_op jit(solution)/shard_map/attn_mix/pallas_call | solution.py:97
  85.4 2.2 collective-permute-done.13
  88.8 1.7 collective-permute-start.18
  90.5 2.5 collective-permute-done.17.refs_6_.refs_10_
  93.9 8.1 %out_project.1 = (f32[960,1024]{1,0:T(8,128)}, bf16[960,1024]{1,0:T(8,128)(2,1)}) custom-call(s32[4]{0:T(128)S(1)} %iota_xor_fusion.refs_0_.refs_8_, bf16[6,160,1024]{2,1,0:T(8,128)(2,1)} %refs_6_.9, bf16[960,1024]{1,0:T(8,128)(2,1)} %attn_mix.1.refs_2_.refs_11_.refs_24_, bf16[256,4096]{1,0:T(8,128)(2,1)} %copy-done.50, ...), custom_call_target="tpu_custom_call" | custom-call | flops 6039797760 | bytes 12582912 | tf_op jit(solution)/shard_map/out_project/pallas_call | solution.py:97
  102.1 5.3 %collective-permute-done.18.refs_12_ = bf16[176,2048]{1,0:T(8,128)(2,1)S(1)} collective-permute-done((bf16[176,2048]{1,0:T(8,128)(2,1)S(1)}, bf16[176,2048]{1,0:T(8,128)(2,1)S(1)}, u32[]{:S(2)}, u32[]{:S(2)}) %collective-permute-start.18) | collective-permute-done | bytes 720928 | tf_op jit(solution)/shard_map/ppermute | solution.py:723
  107.5 1.7 collective-permute-start.19
  110.8 15.1 %mlp_part.4 = (bf16[960,1024]{1,0:T(8,128)(2,1)}, bf16[960,1024]{1,0:T(8,128)(2,1)}, bf16[2,256,2048]{2,1,0:T(8,128)(2,1)}, bf16[2,256,2048]{2,1,0:T(8,128)(2,1)}, f32[1,1024]{1,0:T(1,128)}) custom-call(s32[4]{0:T(128)S(1)} %iota_xor_fusion.refs_0_.refs_8_, bf16[960,1024]{1,0:T(8,128)(2,1)} %get-tuple-element.462.refs_1_.refs_13_, ...), custom_call_target="tpu_custom_call" | custom-call | flops 12079595520 | bytes 12582912 | tf_op jit(solution)/shard_map/mlp_part/pallas_call | solution.py:97
  126.2 2.1 copy-done.84
  128.3 4.2 collective-permute-done.21.refs_12_
  135.1 15.7 %mlp_part.5 = (bf16[960,1024]{1,0:T(8,128)(2,1)}, bf16[960,1024]{1,0:T(8,128)(2,1)}, bf16[2,256,2048]{2,1,0:T(8,128)(2,1)}, bf16[2,256,2048]{2,1,0:T(8,128)(2,1)}, f32[1,1024]{1,0:T(1,128)}) custom-call(s32[4]{0:T(128)S(1)} %iota_xor_fusion.refs_0_.refs_8_, bf16[960,1024]{1,0:T(8,128)(2,1)} %get-tuple-element.462.refs_1_.refs_13_, ...), custom_call_target="tpu_custom_call" | custom-call | flops 12079595520 | bytes 12582912 | tf_op jit(solution)/shard_map/mlp_part/pallas_call | solution.py:97
  157.0 15.3 %mlp_part.6 = (bf16[960,1024]{1,0:T(8,128)(2,1)}, bf16[960,1024]{1,0:T(8,128)(2,1)}, bf16[2,256,2048]{2,1,0:T(8,128)(2,1)}, bf16[2,256,2048]{2,1,0:T(8,128)(2,1)}, f32[1,1024]{1,0:T(1,128)}) custom-call(s32[4]{0:T(128)S(1)} %iota_xor_fusion.refs_0_.refs_8_, bf16[960,1024]{1,0:T(8,128)(2,1)} %get-tuple-element.462.refs_1_.refs_13_, ...), custom_call_target="tpu_custom_call" | custom-call | flops 12079595520 | bytes 12582912 | tf_op jit(solution)/shard_map/mlp_part/pallas_call | solution.py:97
  174.2 2.6 fusion.18
  180.7 15.3 %mlp_part.7 = (bf16[960,1024]{1,0:T(8,128)(2,1)}, bf16[960,1024]{1,0:T(8,128)(2,1)}, bf16[2,256,2048]{2,1,0:T(8,128)(2,1)}, bf16[2,256,2048]{2,1,0:T(8,128)(2,1)}, f32[1,1024]{1,0:T(1,128)}) custom-call(s32[4]{0:T(128)S(1)} %iota_xor_fusion.refs_0_.refs_8_, bf16[960,1024]{1,0:T(8,128)(2,1)} %get-tuple-element.462.refs_1_.refs_13_, ...), custom_call_target="tpu_custom_call" | custom-call | flops 12079595520 | bytes 12582912 | tf_op jit(solution)/shard_map/mlp_part/pallas_call | solution.py:97
  196.1 1.9 slice_bitcast_fusion.6
  202.9 1.8 collective-permute-start.31
  204.9 20.9 %mlp_back.1 = (bf16[960,1024]{1,0:T(8,128)(2,1)}, f32[8,1024]{1,0:T(8,128)}, bf16[2,256,1024]{2,1,0:T(8,128)(2,1)}, bf16[2,256,1024]{2,1,0:T(8,128)(2,1)}) custom-call(s32[4]{0:T(128)S(1)} %iota_xor_fusion.refs_0_.refs_8_, bf16[960,1024]{1,0:T(8,128)(2,1)} %get-tuple-element.503.refs_1_, bf16[960,1024]{1,0:T(8,128)(2,1)} %get-tuple-element.504.refs_2_, ...), custom_call_target="tpu_custom_call" | custom-call | flops 12079595520 | bytes 31457280 | tf_op jit(solution)/shard_map/mlp_back/pallas_call | solution.py:97
  227.1 2.8 collective-permute-done.32.refs_10_
  230.2 1.7 add_convert_fusion.1
  232.1 2.8 collective-permute-start.34
  238.4 14.5 %attn_back.2 = (bf16[960,3072]{1,0:T(8,128)(2,1)}, f32[8,1024]{1,0:T(8,128)}) custom-call(s32[4]{0:T(128)S(1)} %iota_xor_fusion.refs_0_.refs_8_, s32[6]{0:T(128)S(1)} %copy-done.34, bf16[960,1024]{1,0:T(8,128)(2,1)} %get-tuple-element.519.refs_2_.refs_7_, bf16[256,4096]{1,0:T(8,128)(2,1)} %copy-done.50, ...), custom_call_target="tpu_custom_call" | custom-call | flops 12079595520 | bytes 18874368 | tf_op jit(solution)/shard_map/attn_back/pallas_call | solution.py:97
  253.0 1.7 collective-permute-done.37.refs_12_
  261.2 14.6 %attn_back.3 = (bf16[960,3072]{1,0:T(8,128)(2,1)}, f32[8,1024]{1,0:T(8,128)}) custom-call(s32[4]{0:T(128)S(1)} %iota_xor_fusion.refs_0_.refs_8_, s32[6]{0:T(128)S(1)} %copy-done.34, bf16[960,1024]{1,0:T(8,128)(2,1)} %get-tuple-element.519.refs_2_.refs_7_, bf16[256,4096]{1,0:T(8,128)(2,1)} %copy-done.50, ...), custom_call_target="tpu_custom_call", output_to_operand_aliasing={{0}: (8, {})} | custom-call | flops 12079595520 | bytes 18874368 | tf_op jit(solution)/shard_map/attn_back/pallas_call | solution.py:97
  279.5 2.6 collective-permute-start.45
  285.1 8.6 %kv_grad.1 = (bf16[2,256,2048]{2,1,0:T(8,128)(2,1)}, bf16[2,256,2048]{2,1,0:T(8,128)(2,1)}) custom-call(s32[4]{0:T(128)S(1)} %iota_xor_fusion.refs_0_.refs_8_, bf16[960,1024]{1,0:T(8,128)(2,1)} %fusion.3.refs_1_, bf16[960,3072]{1,0:T(8,128)(2,1)} %get-tuple-element.550.refs_2_.refs_1_, bf16[32,2048]{1,0:T(8,128)(2,1)S(1)} %collective-permute-done.39.refs_3_, ...), custom_call_target="tpu_custom_call" | custom-call | flops 8053063680 | bytes 16777216 | tf_op jit(solution)/shard_map/kv_grad/pallas_call | solution.py:97
  301.3 2.3 collective-permute-done.48.refs_9_
  309.9 14.7 %input_back.1 = (bf16[6,160,1024]{2,1,0:T(8,128)(2,1)}, f32[8,1024]{1,0:T(8,128)}) custom-call(s32[4]{0:T(128)S(1)} %iota_xor_fusion.refs_0_.refs_8_, bf16[960,3072]{1,0:T(8,128)(2,1)} %get-tuple-element.550.refs_2_.refs_1_, bf16[256,4096]{1,0:T(8,128)(2,1)} %copy-done.50, bf16[256,4096]{1,0:T(8,128)(2,1)} %collective-permute-done.6.refs_3_.refs_4_, ...), custom_call_target="tpu_custom_call" | custom-call | flops 8053063680 | bytes 25165824 | tf_op jit(solution)/shard_map/input_back/pallas_call | solution.py:97
  330.6 1.9 add_convert_fusion.8
  332.5 2.1 fusion.24
  337.4 6.4 %query_grad.1 = (bf16[2,256,1152]{2,1,0:T(8,128)(2,1)}, bf16[2,256,1152]{2,1,0:T(8,128)(2,1)}) custom-call(s32[4]{0:T(128)S(1)} %copy-done.28, bf16[960,1024]{1,0:T(8,128)(2,1)} %fusion.3.refs_1_, bf16[960,3072]{1,0:T(8,128)(2,1)} %get-tuple-element.550.refs_2_.refs_1_, f32[16,1024]{1,0:T(8,128)S(1)} %concatenate.175.refs_3_, ...), custom_call_target="tpu_custom_call" | custom-call | flops 6039797760 | bytes 10485760 | tf_op jit(solution)/shard_map/query_grad/pallas_call | solution.py:97
  343.9 2.5 fusion.6
  348.1 4.5 adam_part.8
  355.1 2.6 collective-permute-start.59
  357.6 13.6 %mlp_out.1.refs_15_ = bf16[960,1024]{1,0:T(8,128)(2,1)} custom-call(s32[4]{0:T(128)S(1)} %copy-done.28, bf16[960,1024]{1,0:T(8,128)(2,1)} %get-tuple-element.463.refs_1_, bf16[960,1024]{1,0:T(8,128)(2,1)} %get-tuple-element.480.refs_2_, bf16[960,1024]{1,0:T(8,128)(2,1)} %get-tuple-element.489.refs_3_, bf16[960,1024]{1,0:T(8,128)(2,1)} %get-tuple-element.501.refs_4_, ...), custom_call_target="tpu_custom_call" | custom-call | flops 12079595520 | bytes 25165824 | tf_op jit(solution)/shard_map/mlp_out/pallas_call | solution.py:97
  376.5 4.2 adam_part.9
  383.0 2.9 collective-permute-done.61
  387.0 11.7 %collective-permute-done.65 = bf16[32,4096]{1,0:T(8,128)(2,1)S(1)} collective-permute-done((bf16[32,4096]{1,0:T(8,128)(2,1)S(1)}, bf16[32,4096]{1,0:T(8,128)(2,1)S(1)}, u32[]{:S(2)}, u32[]{:S(2)}) %collective-permute-start.65) | collective-permute-done | bytes 262176 | tf_op jit(solution)/shard_map/ppermute | solution.py:723
  398.9 2.6 collective-permute-done.62.refs_12_
  402.5 4.2 adam_part.10
  406.7 4.5 adam_part.11
  411.2 2.0 collective-permute-done.66
  413.2 2.7 collective-permute-done.67
  417.9 6.9 %collective-permute-done.69 = bf16[1,32,2176]{2,1,0:T(8,128)(2,1)S(1)} collective-permute-done((bf16[1,32,2176]{2,1,0:T(8,128)(2,1)S(1)}, bf16[1,32,2176]{2,1,0:T(8,128)(2,1)S(1)}, u32[]{:S(2)}, u32[]{:S(2)}) %collective-permute-start.69) | collective-permute-done | bytes 139296 | tf_op jit(solution)/shard_map/ppermute | solution.py:723
  424.8 2.2 collective-permute-done.68
  429.2 6.3 %collective-permute-done.70 = bf16[32,2176]{1,0:T(8,128)(2,1)S(1)} collective-permute-done((bf16[32,2176]{1,0:T(8,128)(2,1)S(1)}, bf16[32,2176]{1,0:T(8,128)(2,1)S(1)}, u32[]{:S(2)}, u32[]{:S(2)}) %collective-permute-start.70) | collective-permute-done | bytes 139296 | tf_op jit(solution)/shard_map/ppermute | solution.py:723
  435.6 6.9 %collective-permute-done.71.refs_12_ = bf16[64,2176]{1,0:T(8,128)(2,1)S(1)} collective-permute-done((bf16[64,2176]{1,0:T(8,128)(2,1)S(1)}, bf16[64,2176]{1,0:T(8,128)(2,1)S(1)}, u32[]{:S(2)}, u32[]{:S(2)}) %collective-permute-start.71) | collective-permute-done | bytes 278560 | tf_op jit(solution)/shard_map/ppermute | solution.py:723
  443.4 7.4 %adam_part.12 = (f32[256,8192]{1,0:T(8,128)}, f32[256,8192]{1,0:T(8,128)}, f32[256,8192]{1,0:T(8,128)}, f32[256,8192]{1,0:T(8,128)}, bf16[256,8192]{1,0:T(8,128)(2,1)}, /*index=5*/f32[8,128]{1,0:T(8,128)S(1)}) custom-call(s32[2]{0:T(128)S(1)} %copy-done.30, ...), custom_call_target="tpu_custom_call", output_to_operand_aliasing={{0}: (7, {}), {1}: (8, {}), {2}: (9, {}), {3}: (10, {}), {4... | custom-call | flops 6442450944 | bytes 10485760 | tf_op jit(solution)/shard_map/adam_part/pallas_call | solution.py:97
  450.8 1.9 collective-permute-start.73
  453.0 7.4 %adam_part.13 = (f32[256,8192]{1,0:T(8,128)}, f32[256,8192]{1,0:T(8,128)}, f32[256,8192]{1,0:T(8,128)}, f32[256,8192]{1,0:T(8,128)}, bf16[256,8192]{1,0:T(8,128)(2,1)}, /*index=5*/f32[8,128]{1,0:T(8,128)S(1)}) custom-call(s32[2]{0:T(128)S(1)} %copy-done.32, ...), custom_call_target="tpu_custom_call", output_to_operand_aliasing={{0}: (7, {}), {1}: (8, {}), {2}: (9, {}), {3}: (10, {}), {4... | custom-call | flops 6442450944 | bytes 10485760 | tf_op jit(solution)/shard_map/adam_part/pallas_call | solution.py:97
  460.4 14.9 %collective-permute-done.74.refs_3_.refs_7_ = bf16[128,2048]{1,0:T(8,128)(2,1)S(1)} collective-permute-done((bf16[128,2048]{1,0:T(8,128)(2,1)S(1)}, bf16[128,2048]{1,0:T(8,128)(2,1)S(1)}, u32[]{:S(2)}, u32[]{:S(2)}) %collective-permute-start.74) | collective-permute-done | bytes 524320 | tf_op jit(solution)/shard_map/ppermute | solution.py:723
  476.2 7.4 %adam_part.14 = (f32[256,4096]{1,0:T(8,128)}, f32[256,4096]{1,0:T(8,128)}, f32[256,4096]{1,0:T(8,128)}, f32[256,4096]{1,0:T(8,128)}, bf16[256,4096]{1,0:T(8,128)(2,1)}, /*index=5*/f32[8,128]{1,0:T(8,128)S(1)}) custom-call(s32[2]{0:T(128)S(1)} %copy-done.35, s32[1]{0:T(128)} %bitcast.40.refs_1_, bf16[128,2048]{1,0:T(8,128)(2,1)} %maximum_select_fusion.7.refs_2_, ...), custom_call_target="tpu_custom_call" | custom-call | flops 6442450944 | bytes 10485760 | tf_op jit(solution)/shard_map/adam_part/pallas_call | solution.py:97
  484.4 7.4 %adam_part.15 = (f32[256,4096]{1,0:T(8,128)}, f32[256,4096]{1,0:T(8,128)}, f32[256,4096]{1,0:T(8,128)}, f32[256,4096]{1,0:T(8,128)}, bf16[256,4096]{1,0:T(8,128)(2,1)}, /*index=5*/f32[8,128]{1,0:T(8,128)}) custom-call(s32[2]{0:T(128)S(1)} %copy-done.31, ...), custom_call_target="tpu_custom_call", output_to_operand_aliasing={{0}: (7, {}), {1}: (8, {}), {2}: (9, {}), {3}: (10, {}), {4... | custom-call | flops 6442450944 | bytes 10485760 | tf_op jit(solution)/shard_map/adam_part/pallas_call | solution.py:97
  (427 shorter events, 112.7 us)
Async XLA Ops:
  3.8 17.2 %collective-permute-start = (bf16[16,256]{1,0:T(8,128)(2,1)S(1)}, bf16[16,256]{1,0:T(8,128)(2,1)S(1)}, u32[]{:S(2)}, u32[]{:S(2)}) collective-permute-start(bf16[16,256]{1,0:T(8,128)(2,1)S(1)} %get-tuple-element.375), channel_id=1, source_target_pairs={{0,1},{1,0},{2,3},{3,2},{4,5},{5,4},{6,7},{7,6},{8,9},{9,8},{10,11... | collective-permute-start | bytes 24584 | tf_op jit(solution)/shard_map/ppermute | solution.py:723
  4.3 23.7 %collective-permute-start.2 = (bf16[256,1536]{1,0:T(8,128)(2,1)}, bf16[256,1536]{1,0:T(8,128)(2,1)}, u32[]{:S(2)}, u32[]{:S(2)}) collective-permute-start(bf16[256,1536]{1,0:T(8,128)(2,1)} %pad_maximum_fusion.7), channel_id=1, source_target_pairs={{0,2},{1,3},{2,0},{3,1},{4,6},{5,7},{6,4},{7,5},{8,10},{9,11},{10,... | collective-permute-start | bytes 2359304 | tf_op jit(solution)/shard_map/ppermute | solution.py:723
  29.9 17.7 %collective-permute-start.6 = (bf16[256,4096]{1,0:T(8,128)(2,1)}, bf16[256,4096]{1,0:T(8,128)(2,1)}, u32[]{:S(2)}, u32[]{:S(2)}) collective-permute-start(bf16[256,4096]{1,0:T(8,128)(2,1)} %copy-done.50), channel_id=1, source_target_pairs={{0,1},{1,0},{2,3},{3,2},{4,5},{5,4},{6,7},{7,6},{8,9},{9,8},{10,11... | collective-permute-start | bytes 6291464 | tf_op jit(solution)/shard_map/ppermute | solution.py:723
  31.7 11.5 %collective-permute-start.3 = (bf16[256,768]{1,0:T(8,128)(2,1)S(1)}, bf16[256,768]{1,0:T(8,128)(2,1)S(1)}, u32[]{:S(2)}, u32[]{:S(2)}) collective-permute-start(bf16[256,768]{1,0:T(8,128)(2,1)S(1)} %get-tuple-element.408), channel_id=1, source_target_pairs={{0,4},{4,0},{8,12},{12,8},{16,20},{20,16},{24,28},{28,24},{1,5},{5... | collective-permute-start | bytes 1179656 | tf_op jit(solution)/shard_map/ppermute | solution.py:723
  33.4 11.5 %collective-permute-start.4 = (bf16[256,768]{1,0:T(8,128)(2,1)}, bf16[256,768]{1,0:T(8,128)(2,1)S(1)}, u32[]{:S(2)}, u32[]{:S(2)}) collective-permute-start(bf16[256,768]{1,0:T(8,128)(2,1)} %get-tuple-element.409), channel_id=1, source_target_pairs={{0,8},{4,12},{8,0},{12,4},{16,24},{20,28},{24,16},{28,20},{1,9},{5... | collective-permute-start | bytes 1179656 | tf_op jit(solution)/shard_map/ppermute | solution.py:723
  35.0 12.6 %collective-permute-start.5 = (bf16[112,2048]{1,0:T(8,128)(2,1)}, bf16[112,2048]{1,0:T(8,128)(2,1)S(1)}, u32[]{:S(2)}, u32[]{:S(2)}) collective-permute-start(bf16[112,2048]{1,0:T(8,128)(2,1)} %slice.227), channel_id=1, source_target_pairs={{0,2},{1,3},{2,0},{3,1},{4,6},{5,7},{6,4},{7,5},{8,10},{9,11},{10,... | collective-permute-start | bytes 1376264 | tf_op jit(solution)/shard_map/ppermute | solution.py:723
  49.3 16.4 %collective-permute-start.8 = (bf16[144,2048]{1,0:T(8,128)(2,1)S(1)}, bf16[144,2048]{1,0:T(8,128)(2,1)S(1)}, u32[]{:S(2)}, u32[]{:S(2)}) collective-permute-start(bf16[144,2048]{1,0:T(8,128)(2,1)S(1)} %slice.228), channel_id=1, source_target_pairs={{0,2},{1,3},{2,0},{3,1},{4,6},{5,7},{6,4},{7,5},{8,10},{9,11},{10,... | collective-permute-start | bytes 1769480 | tf_op jit(solution)/shard_map/ppermute | solution.py:723
  51.7 16.6 %collective-permute-start.9 = (bf16[80,1024]{1,0:T(8,128)(2,1)S(1)}, bf16[80,1024]{1,0:T(8,128)(2,1)S(1)}, u32[]{:S(2)}, u32[]{:S(2)}) collective-permute-start(bf16[80,1024]{1,0:T(8,128)(2,1)S(1)} %slice.233), channel_id=1, source_target_pairs={{0,2},{1,3},{2,0},{3,1},{4,6},{5,7},{6,4},{7,5},{8,10},{9,11},{10,... | collective-permute-start | bytes 491528 | tf_op jit(solution)/shard_map/ppermute | solution.py:723
  69.2 18.5 %collective-permute-start.14 = (bf16[256,8192]{1,0:T(8,128)(2,1)}, bf16[256,8192]{1,0:T(8,128)(2,1)}, u32[]{:S(2)}, u32[]{:S(2)}) collective-permute-start(bf16[256,8192]{1,0:T(8,128)(2,1)} %convert_element_type.511.refs_3_.refs_7_.refs_5_.refs_9_.refs_13_.refs_17_), channel_id=1, source_target_pairs={{0,1},{1,0},{2,3},{3,2},{4,5},{5,4},{6,7},{7,6},{8,9},{9,8},{10,11... | collective-permute-start | bytes 12582920 | tf_op jit(solution)/shard_map/ppermute | solution.py:723
  69.3 18.4 %collective-permute-start.10 = (bf16[256,1024]{1,0:T(8,128)(2,1)}, bf16[256,1024]{1,0:T(8,128)(2,1)S(1)}, u32[]{:S(2)}, u32[]{:S(2)}) collective-permute-start(bf16[256,1024]{1,0:T(8,128)(2,1)} %get-tuple-element.437), channel_id=1, source_target_pairs={{0,4},{4,0},{8,12},{12,8},{16,20},{20,16},{24,28},{28,24},{1,5},{5... | collective-permute-start | bytes 1572872 | tf_op jit(solution)/shard_map/ppermute | solution.py:723
  69.9 17.8 %collective-permute-start.11 = (bf16[256,1024]{1,0:T(8,128)(2,1)S(1)}, bf16[256,1024]{1,0:T(8,128)(2,1)S(1)}, u32[]{:S(2)}, u32[]{:S(2)}) collective-permute-start(bf16[256,1024]{1,0:T(8,128)(2,1)S(1)} %get-tuple-element.438), channel_id=1, source_target_pairs={{0,8},{4,12},{8,0},{12,4},{16,24},{20,28},{24,16},{28,20},{1,9},{5... | collective-permute-start | bytes 1572872 | tf_op jit(solution)/shard_map/ppermute | solution.py:723
  70.2 17.5 %collective-permute-start.12 = (bf16[176,1024]{1,0:T(8,128)(2,1)}, bf16[176,1024]{1,0:T(8,128)(2,1)S(1)}, u32[]{:S(2)}, u32[]{:S(2)}) collective-permute-start(bf16[176,1024]{1,0:T(8,128)(2,1)} %slice.236), channel_id=1, source_target_pairs={{0,2},{1,3},{2,0},{3,1},{4,6},{5,7},{6,4},{7,5},{8,10},{9,11},{10,... | collective-permute-start | bytes 1081352 | tf_op jit(solution)/shard_map/ppermute | solution.py:723
  71.9 15.8 %collective-permute-start.13 = (bf16[80,2048]{1,0:T(8,128)(2,1)}, bf16[80,2048]{1,0:T(8,128)(2,1)S(1)}, u32[]{:S(2)}, u32[]{:S(2)}) collective-permute-start(bf16[80,2048]{1,0:T(8,128)(2,1)} %slice.237), channel_id=1, source_target_pairs={{0,2},{1,3},{2,0},{3,1},{4,6},{5,7},{6,4},{7,5},{8,10},{9,11},{10,... | collective-permute-start | bytes 983048 | tf_op jit(solution)/shard_map/ppermute | solution.py:723
  88.8 18.5 %collective-permute-start.18 = (bf16[176,2048]{1,0:T(8,128)(2,1)S(1)}, bf16[176,2048]{1,0:T(8,128)(2,1)S(1)}, u32[]{:S(2)}, u32[]{:S(2)}) collective-permute-start(bf16[176,2048]{1,0:T(8,128)(2,1)S(1)} %slice.238), channel_id=1, source_target_pairs={{0,2},{1,3},{2,0},{3,1},{4,6},{5,7},{6,4},{7,5},{8,10},{9,11},{10,... | collective-permute-start | bytes 2162696 | tf_op jit(solution)/shard_map/ppermute | solution.py:723
  107.5 18.4 %collective-permute-start.19 = (bf16[256,1024]{1,0:T(8,128)(2,1)S(1)}, bf16[256,1024]{1,0:T(8,128)(2,1)S(1)}, u32[]{:S(2)}, u32[]{:S(2)}) collective-permute-start(bf16[256,1024]{1,0:T(8,128)(2,1)S(1)} %get-tuple-element.466), channel_id=1, source_target_pairs={{0,4},{4,0},{8,12},{12,8},{16,20},{20,16},{24,28},{28,24},{1,5},{5... | collective-permute-start | bytes 1572872 | tf_op jit(solution)/shard_map/ppermute | solution.py:723
  109.2 16.6 %collective-permute-start.20 = (bf16[256,1024]{1,0:T(8,128)(2,1)S(1)}, bf16[256,1024]{1,0:T(8,128)(2,1)S(1)}, u32[]{:S(2)}, u32[]{:S(2)}) collective-permute-start(bf16[256,1024]{1,0:T(8,128)(2,1)S(1)} %get-tuple-element.467), channel_id=1, source_target_pairs={{0,8},{4,12},{8,0},{12,4},{16,24},{20,28},{24,16},{28,20},{1,9},{5... | collective-permute-start | bytes 1572872 | tf_op jit(solution)/shard_map/ppermute | solution.py:723
  133.0 19.6 %collective-permute-start.22 = (bf16[256,2048]{1,0:T(8,128)(2,1)S(1)}, bf16[256,2048]{1,0:T(8,128)(2,1)S(1)}, u32[]{:S(2)}, u32[]{:S(2)}) collective-permute-start(bf16[256,2048]{1,0:T(8,128)(2,1)S(1)} %pad_maximum_fusion.5.refs_5_.refs_9_.refs_15_), channel_id=1, source_target_pairs={{0,1},{1,0},{2,3},{3,2},{4,5},{5,4},{6,7},{7,6},{8,9},{9,8},{10,11... | collective-permute-start | bytes 3145736 | tf_op jit(solution)/shard_map/ppermute | solution.py:723
  133.2 19.4 %collective-permute-start.23 = (bf16[256,2048]{1,0:T(8,128)(2,1)S(1)}, bf16[256,2048]{1,0:T(8,128)(2,1)S(1)}, u32[]{:S(2)}, u32[]{:S(2)}) collective-permute-start(bf16[256,2048]{1,0:T(8,128)(2,1)S(1)} %pad_maximum_fusion.6.refs_5_.refs_9_.refs_19_), channel_id=1, source_target_pairs={{0,1},{1,0},{2,3},{3,2},{4,5},{5,4},{6,7},{7,6},{8,9},{9,8},{10,11... | collective-permute-start | bytes 3145736 | tf_op jit(solution)/shard_map/ppermute | solution.py:723
  133.6 18.2 %collective-permute-start.24 = (bf16[176,2048]{1,0:T(8,128)(2,1)S(1)}, bf16[176,2048]{1,0:T(8,128)(2,1)S(1)}, u32[]{:S(2)}, u32[]{:S(2)}) collective-permute-start(bf16[176,2048]{1,0:T(8,128)(2,1)S(1)} %slice_bitcast_fusion.3), channel_id=1, source_target_pairs={{0,2},{1,3},{2,0},{3,1},{4,6},{5,7},{6,4},{7,5},{8,10},{9,11},{10,... | collective-permute-start | bytes 2162696 | tf_op jit(solution)/shard_map/ppermute | solution.py:723
  153.6 18.8 %collective-permute-start.26 = (bf16[2,256,2048]{2,1,0:T(8,128)(2,1)}, bf16[2,256,2048]{2,1,0:T(8,128)(2,1)S(1)}, u32[]{:S(2)}, u32[]{:S(2)}) collective-permute-start(bf16[2,256,2048]{2,1,0:T(8,128)(2,1)} %get-tuple-element.492), channel_id=1, source_target_pairs={{0,1},{1,0},{2,3},{3,2},{4,5},{5,4},{6,7},{7,6},{8,9},{9,8},{10,11... | collective-permute-start | bytes 6291464 | tf_op jit(solution)/shard_map/ppermute | solution.py:723
  153.6 18.8 %collective-permute-start.25 = (bf16[80,2048]{1,0:T(8,128)(2,1)}, bf16[80,2048]{1,0:T(8,128)(2,1)S(1)}, u32[]{:S(2)}, u32[]{:S(2)}) collective-permute-start(bf16[80,2048]{1,0:T(8,128)(2,1)} %slice_bitcast_fusion.7), channel_id=1, source_target_pairs={{0,2},{1,3},{2,0},{3,1},{4,6},{5,7},{6,4},{7,5},{8,10},{9,11},{10,... | collective-permute-start | bytes 983048 | tf_op jit(solution)/shard_map/ppermute | solution.py:723
  176.9 21.1 %collective-permute-start.29 = (bf16[2,256,2048]{2,1,0:T(8,128)(2,1)}, bf16[2,256,2048]{2,1,0:T(8,128)(2,1)S(1)}, u32[]{:S(2)}, u32[]{:S(2)}) collective-permute-start(bf16[2,256,2048]{2,1,0:T(8,128)(2,1)} %get-tuple-element.509), channel_id=1, source_target_pairs={{0,1},{1,0},{2,3},{3,2},{4,5},{5,4},{6,7},{7,6},{8,9},{9,8},{10,11... | collective-permute-start | bytes 6291464 | tf_op jit(solution)/shard_map/ppermute | solution.py:723
  177.2 20.8 %collective-permute-start.27 = (bf16[1,128,2048]{2,1,0:T(8,128)(2,1)}, bf16[1,128,2048]{2,1,0:T(8,128)(2,1)S(1)}, u32[]{:S(2)}, u32[]{:S(2)}) collective-permute-start(bf16[1,128,2048]{2,1,0:T(8,128)(2,1)} %fusion.18), channel_id=1, source_target_pairs={{0,4},{4,0},{8,12},{12,8},{16,20},{20,16},{24,28},{28,24},{1,5},{5... | collective-permute-start | bytes 1572872 | tf_op jit(solution)/shard_map/ppermute | solution.py:723
  177.7 20.3 %collective-permute-start.28 = (bf16[176,2048]{1,0:T(8,128)(2,1)}, bf16[176,2048]{1,0:T(8,128)(2,1)S(1)}, u32[]{:S(2)}, u32[]{:S(2)}) collective-permute-start(bf16[176,2048]{1,0:T(8,128)(2,1)} %slice_bitcast_fusion.2), channel_id=1, source_target_pairs={{0,2},{1,3},{2,0},{3,1},{4,6},{5,7},{6,4},{7,5},{8,10},{9,11},{10,... | collective-permute-start | bytes 2162696 | tf_op jit(solution)/shard_map/ppermute | solution.py:723
  202.6 27.2 %collective-permute-start.33 = (bf16[2,256,2048]{2,1,0:T(8,128)(2,1)}, bf16[2,256,2048]{2,1,0:T(8,128)(2,1)}, u32[]{:S(2)}, u32[]{:S(2)}) collective-permute-start(bf16[2,256,2048]{2,1,0:T(8,128)(2,1)} %get-tuple-element.523), channel_id=1, source_target_pairs={{0,1},{1,0},{2,3},{3,2},{4,5},{5,4},{6,7},{7,6},{8,9},{9,8},{10,11... | collective-permute-start | bytes 6291464 | tf_op jit(solution)/shard_map/ppermute | solution.py:723
  202.6 24.4 %collective-permute-start.30 = (bf16[1,64,2048]{2,1,0:T(8,128)(2,1)}, bf16[1,64,2048]{2,1,0:T(8,128)(2,1)S(1)}, u32[]{:S(2)}, u32[]{:S(2)}) collective-permute-start(bf16[1,64,2048]{2,1,0:T(8,128)(2,1)} %constant_dynamic-slice_fusion.4), channel_id=1, source_target_pairs={{0,8},{4,12},{8,0},{12,4},{16,24},{20,28},{24,16},{28,20},{1,9},{5... | collective-permute-start | bytes 786440 | tf_op jit(solution)/shard_map/ppermute | solution.py:723
  202.9 24.1 %collective-permute-start.31 = (bf16[80,2048]{1,0:T(8,128)(2,1)}, bf16[80,2048]{1,0:T(8,128)(2,1)S(1)}, u32[]{:S(2)}, u32[]{:S(2)}) collective-permute-start(bf16[80,2048]{1,0:T(8,128)(2,1)} %slice_bitcast_fusion.6), channel_id=1, source_target_pairs={{0,2},{1,3},{2,0},{3,1},{4,6},{5,7},{6,4},{7,5},{8,10},{9,11},{10,... | collective-permute-start | bytes 983048 | tf_op jit(solution)/shard_map/ppermute | solution.py:723
  204.7 25.2 %collective-permute-start.32 = (bf16[192,2048]{1,0:T(8,128)(2,1)}, bf16[192,2048]{1,0:T(8,128)(2,1)S(1)}, u32[]{:S(2)}, u32[]{:S(2)}) collective-permute-start(bf16[192,2048]{1,0:T(8,128)(2,1)} %slice_bitcast_fusion.1), channel_id=1, source_target_pairs={{0,2},{1,3},{2,0},{3,1},{4,6},{5,7},{6,4},{7,5},{8,10},{9,11},{10,... | collective-permute-start | bytes 2359304 | tf_op jit(solution)/shard_map/ppermute | solution.py:723
  232.1 20.9 %collective-permute-start.34 = (bf16[1,32,2048]{2,1,0:T(8,128)(2,1)S(1)}, bf16[1,32,2048]{2,1,0:T(8,128)(2,1)S(1)}, u32[]{:S(2)}, u32[]{:S(2)}) collective-permute-start(bf16[1,32,2048]{2,1,0:T(8,128)(2,1)S(1)} %add_convert_fusion.16), channel_id=1, source_target_pairs={{0,16},{4,20},{8,24},{12,28},{16,0},{20,4},{24,8},{28,12},{1,17},{... | collective-permute-start | bytes 393224 | tf_op jit(solution)/shard_map/ppermute | solution.py:723
  234.9 18.1 %collective-permute-start.35 = (bf16[1,128,2048]{2,1,0:T(8,128)(2,1)S(1)}, bf16[1,128,2048]{2,1,0:T(8,128)(2,1)S(1)}, u32[]{:S(2)}, u32[]{:S(2)}) collective-permute-start(bf16[1,128,2048]{2,1,0:T(8,128)(2,1)S(1)} %fusion.15), channel_id=1, source_target_pairs={{0,4},{4,0},{8,12},{12,8},{16,20},{20,16},{24,28},{28,24},{1,5},{5... | collective-permute-start | bytes 1572872 | tf_op jit(solution)/shard_map/ppermute | solution.py:723
  236.4 16.6 %collective-permute-start.36 = (bf16[64,2048]{1,0:T(8,128)(2,1)S(1)}, bf16[64,2048]{1,0:T(8,128)(2,1)S(1)}, u32[]{:S(2)}, u32[]{:S(2)}) collective-permute-start(bf16[64,2048]{1,0:T(8,128)(2,1)S(1)} %slice_bitcast_fusion.11), channel_id=1, source_target_pairs={{0,2},{1,3},{2,0},{3,1},{4,6},{5,7},{6,4},{7,5},{8,10},{9,11},{10,... | collective-permute-start | bytes 786440 | tf_op jit(solution)/shard_map/ppermute | solution.py:723
  238.0 16.7 %collective-permute-start.37 = (bf16[128,2048]{1,0:T(8,128)(2,1)S(1)}, bf16[128,2048]{1,0:T(8,128)(2,1)S(1)}, u32[]{:S(2)}, u32[]{:S(2)}) collective-permute-start(bf16[128,2048]{1,0:T(8,128)(2,1)S(1)} %get-tuple-element.537), channel_id=1, source_target_pairs={{0,2},{1,3},{2,0},{3,1},{4,6},{5,7},{6,4},{7,5},{8,10},{9,11},{10,... | collective-permute-start | bytes 1572872 | tf_op jit(solution)/shard_map/ppermute | solution.py:723
  238.4 16.3 %collective-permute-start.38 = (bf16[2,256,1024]{2,1,0:T(8,128)(2,1)S(1)}, bf16[2,256,1024]{2,1,0:T(8,128)(2,1)S(1)}, u32[]{:S(2)}, u32[]{:S(2)}) collective-permute-start(bf16[2,256,1024]{2,1,0:T(8,128)(2,1)S(1)} %copy-done.86), channel_id=1, source_target_pairs={{0,1},{1,0},{2,3},{3,2},{4,5},{5,4},{6,7},{7,6},{8,9},{9,8},{10,11... | collective-permute-start | bytes 3145736 | tf_op jit(solution)/shard_map/ppermute | solution.py:723
  256.6 19.3 %collective-permute-start.39 = (bf16[32,2048]{1,0:T(8,128)(2,1)S(1)}, bf16[32,2048]{1,0:T(8,128)(2,1)S(1)}, u32[]{:S(2)}, u32[]{:S(2)}) collective-permute-start(bf16[32,2048]{1,0:T(8,128)(2,1)S(1)} %fusion.28), channel_id=1, source_target_pairs={{0,16},{4,20},{8,24},{12,28},{16,0},{20,4},{24,8},{28,12},{1,17},{... | collective-permute-start | bytes 393224 | tf_op jit(solution)/shard_map/ppermute | solution.py:723
  257.0 18.9 %collective-permute-start.40 = (bf16[1,64,2048]{2,1,0:T(8,128)(2,1)S(1)}, bf16[1,64,2048]{2,1,0:T(8,128)(2,1)S(1)}, u32[]{:S(2)}, u32[]{:S(2)}) collective-permute-start(bf16[1,64,2048]{2,1,0:T(8,128)(2,1)S(1)} %constant_dynamic-slice_fusion.1), channel_id=1, source_target_pairs={{0,8},{4,12},{8,0},{12,4},{16,24},{20,28},{24,16},{28,20},{1,9},{5... | collective-permute-start | bytes 786440 | tf_op jit(solution)/shard_map/ppermute | solution.py:723
  258.6 18.5 %collective-permute-start.41 = (bf16[1,128,2048]{2,1,0:T(8,128)(2,1)S(1)}, bf16[1,128,2048]{2,1,0:T(8,128)(2,1)S(1)}, u32[]{:S(2)}, u32[]{:S(2)}) collective-permute-start(bf16[1,128,2048]{2,1,0:T(8,128)(2,1)S(1)} %fusion.12), channel_id=1, source_target_pairs={{0,4},{4,0},{8,12},{12,8},{16,20},{20,16},{24,28},{28,24},{1,5},{5... | collective-permute-start | bytes 1572872 | tf_op jit(solution)/shard_map/ppermute | solution.py:723
  259.1 18.0 %collective-permute-start.42 = (bf16[128,2048]{1,0:T(8,128)(2,1)S(1)}, bf16[128,2048]{1,0:T(8,128)(2,1)S(1)}, u32[]{:S(2)}, u32[]{:S(2)}) collective-permute-start(bf16[128,2048]{1,0:T(8,128)(2,1)S(1)} %get-tuple-element.554), channel_id=1, source_target_pairs={{0,2},{1,3},{2,0},{3,1},{4,6},{5,7},{6,4},{7,5},{8,10},{9,11},{10,... | collective-permute-start | bytes 1572872 | tf_op jit(solution)/shard_map/ppermute | solution.py:723
  260.7 16.4 %collective-permute-start.43 = (bf16[128,1024]{1,0:T(8,128)(2,1)S(1)}, bf16[128,1024]{1,0:T(8,128)(2,1)S(1)}, u32[]{:S(2)}, u32[]{:S(2)}) collective-permute-start(bf16[128,1024]{1,0:T(8,128)(2,1)S(1)} %get-tuple-element.555), channel_id=1, source_target_pairs={{0,2},{1,3},{2,0},{3,1},{4,6},{5,7},{6,4},{7,5},{8,10},{9,11},{10,... | collective-permute-start | bytes 786440 | tf_op jit(solution)/shard_map/ppermute | solution.py:723
  279.0 14.9 %collective-permute-start.44 = (bf16[64,2048]{1,0:T(8,128)(2,1)S(1)}, bf16[64,2048]{1,0:T(8,128)(2,1)S(1)}, u32[]{:S(2)}, u32[]{:S(2)}) collective-permute-start(bf16[64,2048]{1,0:T(8,128)(2,1)S(1)} %maximum_select_fusion.9), channel_id=1, source_target_pairs={{0,8},{4,12},{8,0},{12,4},{16,24},{20,28},{24,16},{28,20},{1,9},{5... | collective-permute-start | bytes 786440 | tf_op jit(solution)/shard_map/ppermute | solution.py:723
  279.5 14.3 %collective-permute-start.45 = (bf16[1,32,2048]{2,1,0:T(8,128)(2,1)S(1)}, bf16[1,32,2048]{2,1,0:T(8,128)(2,1)S(1)}, u32[]{:S(2)}, u32[]{:S(2)}) collective-permute-start(bf16[1,32,2048]{2,1,0:T(8,128)(2,1)S(1)} %add_convert_fusion.14), channel_id=1, source_target_pairs={{0,16},{4,20},{8,24},{12,28},{16,0},{20,4},{24,8},{28,12},{1,17},{... | collective-permute-start | bytes 393224 | tf_op jit(solution)/shard_map/ppermute | solution.py:723
  282.0 11.8 %collective-permute-start.46 = (bf16[1,128,2048]{2,1,0:T(8,128)(2,1)S(1)}, bf16[1,128,2048]{2,1,0:T(8,128)(2,1)S(1)}, u32[]{:S(2)}, u32[]{:S(2)}) collective-permute-start(bf16[1,128,2048]{2,1,0:T(8,128)(2,1)S(1)} %fusion.11), channel_id=1, source_target_pairs={{0,4},{4,0},{8,12},{12,8},{16,20},{20,16},{24,28},{28,24},{1,5},{5... | collective-permute-start | bytes 1572872 | tf_op jit(solution)/shard_map/ppermute | solution.py:723
  283.5 10.3 %collective-permute-start.47 = (bf16[128,1024]{1,0:T(8,128)(2,1)S(1)}, bf16[128,1024]{1,0:T(8,128)(2,1)S(1)}, u32[]{:S(2)}, u32[]{:S(2)}) collective-permute-start(bf16[128,1024]{1,0:T(8,128)(2,1)S(1)} %get-tuple-element.569), channel_id=1, source_target_pairs={{0,2},{1,3},{2,0},{3,1},{4,6},{5,7},{6,4},{7,5},{8,10},{9,11},{10,... | collective-permute-start | bytes 786440 | tf_op jit(solution)/shard_map/ppermute | solution.py:723
  305.2 23.7 %collective-permute-start.49 = (bf16[192,2048]{1,0:T(8,128)(2,1)}, bf16[192,2048]{1,0:T(8,128)(2,1)S(1)}, u32[]{:S(2)}, u32[]{:S(2)}) collective-permute-start(bf16[192,2048]{1,0:T(8,128)(2,1)} %slice_bitcast_fusion), channel_id=1, source_target_pairs={{0,2},{1,3},{2,0},{3,1},{4,6},{5,7},{6,4},{7,5},{8,10},{9,11},{10,... | collective-permute-start | bytes 2359304 | tf_op jit(solution)/shard_map/ppermute | solution.py:723
  305.9 23.0 %collective-permute-start.50 = (bf16[128,2048]{1,0:T(8,128)(2,1)}, bf16[128,2048]{1,0:T(8,128)(2,1)S(1)}, u32[]{:S(2)}, u32[]{:S(2)}) collective-permute-start(bf16[128,2048]{1,0:T(8,128)(2,1)} %maximum_select_fusion.4.refs_2_), channel_id=1, source_target_pairs={{0,4},{4,0},{8,12},{12,8},{16,20},{20,16},{24,28},{28,24},{1,5},{5... | collective-permute-start | bytes 1572872 | tf_op jit(solution)/shard_map/ppermute | solution.py:723
  307.4 21.4 %collective-permute-start.51 = (bf16[32,2048]{1,0:T(8,128)(2,1)}, bf16[32,2048]{1,0:T(8,128)(2,1)}, u32[]{:S(2)}, u32[]{:S(2)}) collective-permute-start(bf16[32,2048]{1,0:T(8,128)(2,1)} %fusion.29), channel_id=1, source_target_pairs={{0,16},{4,20},{8,24},{12,28},{16,0},{20,4},{24,8},{28,12},{1,17},{... | collective-permute-start | bytes 393224 | tf_op jit(solution)/shard_map/ppermute | solution.py:723
  307.8 21.1 %collective-permute-start.52 = (bf16[1,64,4096]{2,1,0:T(8,128)(2,1)}, bf16[1,64,4096]{2,1,0:T(8,128)(2,1)}, u32[]{:S(2)}, u32[]{:S(2)}) collective-permute-start(bf16[1,64,4096]{2,1,0:T(8,128)(2,1)} %constant_dynamic-slice_fusion.2), channel_id=1, source_target_pairs={{0,8},{4,12},{8,0},{12,4},{16,24},{20,28},{24,16},{28,20},{1,9},{5... | collective-permute-start | bytes 1572872 | tf_op jit(solution)/shard_map/ppermute | solution.py:723
  309.4 19.5 %collective-permute-start.53 = (bf16[1,128,1024]{2,1,0:T(8,128)(2,1)}, bf16[1,128,1024]{2,1,0:T(8,128)(2,1)}, u32[]{:S(2)}, u32[]{:S(2)}) collective-permute-start(bf16[1,128,1024]{2,1,0:T(8,128)(2,1)} %fusion.25), channel_id=1, source_target_pairs={{0,4},{4,0},{8,12},{12,8},{16,20},{20,16},{24,28},{28,24},{1,5},{5... | collective-permute-start | bytes 786440 | tf_op jit(solution)/shard_map/ppermute | solution.py:723
  334.5 9.4 %collective-permute-start.54 = (bf16[64,2048]{1,0:T(8,128)(2,1)S(1)}, bf16[64,2048]{1,0:T(8,128)(2,1)S(1)}, u32[]{:S(2)}, u32[]{:S(2)}) collective-permute-start(bf16[64,2048]{1,0:T(8,128)(2,1)S(1)} %copy-done.77), channel_id=1, source_target_pairs={{0,2},{1,3},{2,0},{3,1},{4,6},{5,7},{6,4},{7,5},{8,10},{9,11},{10,... | collective-permute-start | bytes 786440 | tf_op jit(solution)/shard_map/ppermute | solution.py:723
  352.8 18.5 %collective-permute-start.57 = (bf16[1,128,2048]{2,1,0:T(8,128)(2,1)S(1)}, bf16[1,128,2048]{2,1,0:T(8,128)(2,1)S(1)}, u32[]{:S(2)}, u32[]{:S(2)}) collective-permute-start(bf16[1,128,2048]{2,1,0:T(8,128)(2,1)S(1)} %copy-done.74), channel_id=1, source_target_pairs={{0,4},{4,0},{8,12},{12,8},{16,20},{20,16},{24,28},{28,24},{1,5},{5... | collective-permute-start | bytes 1572872 | tf_op jit(solution)/shard_map/ppermute | solution.py:723
  353.4 17.8 %collective-permute-start.58 = (bf16[256,1152]{1,0:T(8,128)(2,1)S(1)}, bf16[256,1152]{1,0:T(8,128)(2,1)S(1)}, u32[]{:S(2)}, u32[]{:S(2)}) collective-permute-start(bf16[256,1152]{1,0:T(8,128)(2,1)S(1)} %fusion.19), channel_id=1, source_target_pairs={{0,2},{1,3},{2,0},{3,1},{4,6},{5,7},{6,4},{7,5},{8,10},{9,11},{10,... | collective-permute-start | bytes 1769480 | tf_op jit(solution)/shard_map/ppermute | solution.py:723
  355.1 16.2 %collective-permute-start.59 = (bf16[1,32,4096]{2,1,0:T(8,128)(2,1)S(1)}, bf16[1,32,4096]{2,1,0:T(8,128)(2,1)S(1)}, u32[]{:S(2)}, u32[]{:S(2)}) collective-permute-start(bf16[1,32,4096]{2,1,0:T(8,128)(2,1)S(1)} %copy-done.76), channel_id=1, source_target_pairs={{0,16},{4,20},{8,24},{12,28},{16,0},{20,4},{24,8},{28,12},{1,17},{... | collective-permute-start | bytes 786440 | tf_op jit(solution)/shard_map/ppermute | solution.py:723
  374.3 8.7 %collective-permute-start.60 = (bf16[1,64,2048]{2,1,0:T(8,128)(2,1)S(1)}, bf16[1,64,2048]{2,1,0:T(8,128)(2,1)S(1)}, u32[]{:S(2)}, u32[]{:S(2)}) collective-permute-start(bf16[1,64,2048]{2,1,0:T(8,128)(2,1)S(1)} %constant_dynamic-slice_fusion.3), channel_id=1, source_target_pairs={{0,8},{4,12},{8,0},{12,4},{16,24},{20,28},{24,16},{28,20},{1,9},{5... | collective-permute-start | bytes 786440 | tf_op jit(solution)/shard_map/ppermute | solution.py:723
  376.0 9.9 %collective-permute-start.61 = (bf16[1,128,1152]{2,1,0:T(8,128)(2,1)S(1)}, bf16[1,128,1152]{2,1,0:T(8,128)(2,1)S(1)}, u32[]{:S(2)}, u32[]{:S(2)}) collective-permute-start(bf16[1,128,1152]{2,1,0:T(8,128)(2,1)S(1)} %fusion.20), channel_id=1, source_target_pairs={{0,4},{4,0},{8,12},{12,8},{16,20},{20,16},{24,28},{28,24},{1,5},{5... | collective-permute-start | bytes 884744 | tf_op jit(solution)/shard_map/ppermute | solution.py:723
  380.7 20.7 %collective-permute-start.64 = (bf16[128,2048]{1,0:T(8,128)(2,1)S(1)}, bf16[128,2048]{1,0:T(8,128)(2,1)S(1)}, u32[]{:S(2)}, u32[]{:S(2)}) collective-permute-start(bf16[128,2048]{1,0:T(8,128)(2,1)S(1)} %maximum_select_fusion.5.refs_2_), channel_id=1, source_target_pairs={{0,4},{4,0},{8,12},{12,8},{16,20},{20,16},{24,28},{28,24},{1,5},{5... | collective-permute-start | bytes 1572872 | tf_op jit(solution)/shard_map/ppermute | solution.py:723
  382.3 16.4 %collective-permute-start.65 = (bf16[32,4096]{1,0:T(8,128)(2,1)S(1)}, bf16[32,4096]{1,0:T(8,128)(2,1)S(1)}, u32[]{:S(2)}, u32[]{:S(2)}) collective-permute-start(bf16[32,4096]{1,0:T(8,128)(2,1)S(1)} %fusion.26), channel_id=1, source_target_pairs={{0,16},{4,20},{8,24},{12,28},{16,0},{20,4},{24,8},{28,12},{1,17},{... | collective-permute-start | bytes 786440 | tf_op jit(solution)/shard_map/ppermute | solution.py:723
  386.2 15.2 %collective-permute-start.62 = (bf16[1,32,2048]{2,1,0:T(8,128)(2,1)S(1)}, bf16[1,32,2048]{2,1,0:T(8,128)(2,1)S(1)}, u32[]{:S(2)}, u32[]{:S(2)}) collective-permute-start(bf16[1,32,2048]{2,1,0:T(8,128)(2,1)S(1)} %add_convert_fusion.12), channel_id=1, source_target_pairs={{0,16},{4,20},{8,24},{12,28},{16,0},{20,4},{24,8},{28,12},{1,17},{... | collective-permute-start | bytes 393224 | tf_op jit(solution)/shard_map/ppermute | solution.py:723
  387.0 15.2 %collective-permute-start.63 = (bf16[1,64,2176]{2,1,0:T(8,128)(2,1)S(1)}, bf16[1,64,2176]{2,1,0:T(8,128)(2,1)S(1)}, u32[]{:S(2)}, u32[]{:S(2)}) collective-permute-start(bf16[1,64,2176]{2,1,0:T(8,128)(2,1)S(1)} %constant_dynamic-slice_fusion), channel_id=1, source_target_pairs={{0,8},{4,12},{8,0},{12,4},{16,24},{20,28},{24,16},{28,20},{1,9},{5... | collective-permute-start | bytes 835592 | tf_op jit(solution)/shard_map/ppermute | solution.py:723
  398.8 17.1 %collective-permute-start.67 = (bf16[64,4096]{1,0:T(8,128)(2,1)S(1)}, bf16[64,4096]{1,0:T(8,128)(2,1)S(1)}, u32[]{:S(2)}, u32[]{:S(2)}) collective-permute-start(bf16[64,4096]{1,0:T(8,128)(2,1)S(1)} %maximum_select_fusion.6), channel_id=1, source_target_pairs={{0,8},{4,12},{8,0},{12,4},{16,24},{20,28},{24,16},{28,20},{1,9},{5... | collective-permute-start | bytes 1572872 | tf_op jit(solution)/shard_map/ppermute | solution.py:723
  402.4 10.8 %collective-permute-start.66 = (bf16[32,2048]{1,0:T(8,128)(2,1)S(1)}, bf16[32,2048]{1,0:T(8,128)(2,1)S(1)}, u32[]{:S(2)}, u32[]{:S(2)}) collective-permute-start(bf16[32,2048]{1,0:T(8,128)(2,1)S(1)} %fusion.30), channel_id=1, source_target_pairs={{0,16},{4,20},{8,24},{12,28},{16,0},{20,4},{24,8},{28,12},{1,17},{... | collective-permute-start | bytes 393224 | tf_op jit(solution)/shard_map/ppermute | solution.py:723
  416.2 10.8 %collective-permute-start.68 = (bf16[64,2048]{1,0:T(8,128)(2,1)S(1)}, bf16[64,2048]{1,0:T(8,128)(2,1)S(1)}, u32[]{:S(2)}, u32[]{:S(2)}) collective-permute-start(bf16[64,2048]{1,0:T(8,128)(2,1)S(1)} %maximum_select_fusion.11), channel_id=1, source_target_pairs={{0,8},{4,12},{8,0},{12,4},{16,24},{20,28},{24,16},{28,20},{1,9},{5... | collective-permute-start | bytes 786440 | tf_op jit(solution)/shard_map/ppermute | solution.py:723
  416.3 8.5 %collective-permute-start.69 = (bf16[1,32,2176]{2,1,0:T(8,128)(2,1)S(1)}, bf16[1,32,2176]{2,1,0:T(8,128)(2,1)S(1)}, u32[]{:S(2)}, u32[]{:S(2)}) collective-permute-start(bf16[1,32,2176]{2,1,0:T(8,128)(2,1)S(1)} %add_convert_fusion.10), channel_id=1, source_target_pairs={{0,16},{4,20},{8,24},{12,28},{16,0},{20,4},{24,8},{28,12},{1,17},{... | collective-permute-start | bytes 417800 | tf_op jit(solution)/shard_map/ppermute | solution.py:723
  417.8 24.6 %collective-permute-start.72 = (bf16[128,4096]{1,0:T(8,128)(2,1)S(1)}, bf16[128,4096]{1,0:T(8,128)(2,1)S(1)}, u32[]{:S(2)}, u32[]{:S(2)}) collective-permute-start(bf16[128,4096]{1,0:T(8,128)(2,1)S(1)} %maximum_select_fusion.refs_2_), channel_id=1, source_target_pairs={{0,4},{4,0},{8,12},{12,8},{16,20},{20,16},{24,28},{28,24},{1,5},{5... | collective-permute-start | bytes 3145736 | tf_op jit(solution)/shard_map/ppermute | solution.py:723
  450.8 32.8 %collective-permute-start.73 = (bf16[128,2176]{1,0:T(8,128)(2,1)S(1)}, bf16[128,2176]{1,0:T(8,128)(2,1)S(1)}, u32[]{:S(2)}, u32[]{:S(2)}) collective-permute-start(bf16[128,2176]{1,0:T(8,128)(2,1)S(1)} %maximum_select_fusion.3.refs_2_), channel_id=1, source_target_pairs={{0,4},{4,0},{8,12},{12,8},{16,20},{20,16},{24,28},{28,24},{1,5},{5... | collective-permute-start | bytes 1671176 | tf_op jit(solution)/shard_map/ppermute | solution.py:723
  452.7 22.6 %collective-permute-start.74 = (bf16[128,2048]{1,0:T(8,128)(2,1)S(1)}, bf16[128,2048]{1,0:T(8,128)(2,1)S(1)}, u32[]{:S(2)}, u32[]{:S(2)}) collective-permute-start(bf16[128,2048]{1,0:T(8,128)(2,1)S(1)} %copy-done.75), channel_id=1, source_target_pairs={{0,4},{4,0},{8,12},{12,8},{16,20},{20,16},{24,28},{28,24},{1,5},{5... | collective-permute-start | bytes 1572872 | tf_op jit(solution)/shard_map/ppermute | solution.py:723
  (100 other events, 1043.7 us)

commit v5 on v3

--- a/solution.py
+++ b/solution.py
@@ -1164,7 +1164,7 @@
         totals = [entry for entry in totals if not through(entry[1])]
         wait = pipe.wait() if totals else 1000.0
         kind, total, first, _ = pieces[0] if pieces else (None,) * 4
-        fit = 1 if totals else 4
+        fit = int(wait >= 4.0) if totals else 4
         columns = [c for k, t, _, c in pieces if t is total][:fit]
         if columns:
             outs[kind], mark = adam_part(total, second, first, columns, *state[kind], outs[kind], after)

time: 470 us -> 475 us (1.011)
  waiting for transfers between devices: 68.2 us -> 74.4 us
    ppermute x75, waiting for transfers between devices: 68.2 us -> 74.4 us  [swap(): return lax.ppermute(values, axis, [(i, i ^ bit) for i in range(size)])]
    pallas_call x25 -> x24, Pallas kernels: 238 us -> 237 us  [call(): pl.pallas_call(with_after, grid_spec=pltpu.PrefetchScalarGridSpec(num_sca...]
    unnamed x155 -> x161, local copies, waits for them, and re-layouts: 18 us -> 18.7 us
  transfers between devices with their start and end apart: 75 -> 75, of which waited for: 21 -> 24; matrix products, arithmetic and copies ran while one was open for 7% -> 6% of each run, Pallas kernels for 49% -> 48%
where the time goes in v5:
time: 475 us; the launch traced here: 466 us
  Pallas kernels  237 us (50%)
  waiting for transfers between devices  74.4 us (16%)
  starting transfers between devices  69.6 us (15%)
  local copies, waits for them, and re-layouts  42.3 us (9%)
  other arithmetic  40.4 us (9%)
    pallas_call x24, Pallas kernels, call(): pl.pallas_call(with_after, grid_spec=pltpu.PrefetchScalarGridSpec(num_sca...  237 us
    ppermute x75, waiting for transfers between devices, swap(): return lax.ppermute(values, axis, [(i, i ^ bit) for i in range(size)])  74.4 us
    ppermute x75, starting transfers between devices, swap(): return lax.ppermute(values, axis, [(i, i ^ bit) for i in range(size)])  69.6 us
    unnamed x161, local copies, waits for them, and re-layouts  18.7 us
    convert_element_type x26, other arithmetic, added(): return sum((t.astype(F32) for t in terms)).astype(BF16)  18 us
    slice x16, local copies, waits for them, and re-layouts, start(): values = values[flow.sent:flow.sent + left]  12.3 us
  transfers between devices with their start and end apart: 75, of which 24 were waited for; matrix products, arithmetic and copies ran while one was open for 6% of the time, Pallas kernels for 48%

profile of v5, /device:TPU:0, one launch (start us, length us, event | category | flops | bytes accessed | tf_op | source)
XLA Modules:
  0.0 466.3 jit_solution(12499942698238374055)
XLA Ops:
  4.3 2.5 collective-permute-start.2
  6.8 2.5 dynamic-slice_convert_fusion.1
  11.6 1.6 bitcast_select_fusion.refs_2_.refs_22_
  13.2 6.1 %convert_element_type.511.refs_3_.refs_7_.refs_5_.refs_9_.refs_13_.refs_17_ = bf16[256,8192]{1,0:T(8,128)(2,1)} convert(f32[256,8192]{1,0:T(8,128)} %refs_4_.17) | non-fusion elementwise | flops 2097152 | bytes 12582912 | tf_op jit(solution)/shard_map/convert_element_type | solution.py:1012
  21.1 4.4 collective-permute-done.1
  26.1 1.8 slice.227
  27.9 1.9 fusion.41
  31.1 1.8 collective-permute-start.5
  37.1 2.0 fusion.3.refs_1_
  39.1 5.2 %collective-permute-done.3 = bf16[256,768]{1,0:T(8,128)(2,1)S(1)} collective-permute-done((bf16[256,768]{1,0:T(8,128)(2,1)}, bf16[256,768]{1,0:T(8,128)(2,1)S(1)}, u32[]{:S(2)}, u32[]{:S(2)}) %collective-permute-start.3) | collective-permute-done | bytes 393248 | tf_op jit(solution)/shard_map/ppermute | solution.py:723
  47.7 1.7 collective-permute-done.7.refs_5_.refs_7_
  50.5 11.7 %qkv_forward.1.refs_1_.refs_4_.refs_7_ = bf16[960,3072]{1,0:T(8,128)(2,1)} custom-call(s32[4]{0:T(128)S(1)} %iota_xor_fusion.refs_0_.refs_8_, bf16[960,1024]{1,0:T(8,128)(2,1)} %fusion.3.refs_1_, bf16[256,4096]{1,0:T(8,128)(2,1)} %copy-done.46, bf16[256,4096]{1,0:T(8,128)(2,1)} %collective-permute-done.6.refs_3_.refs_4_, bf16[256,3072]{1,0:T(8,128)(2,1)} %copy-done.61, ...), custom_call_target="tpu_custom_call" | custom-call | flops 10066329600 | bytes 18874368 | tf_op jit(solution)/shard_map/qkv_forward/pallas_call | solution.py:97
  63.2 2.9 collective-permute-done.9.refs_3_
  71.5 13.2 %attn_mix.1.refs_2_.refs_11_.refs_24_ = bf16[960,1024]{1,0:T(8,128)(2,1)} custom-call(s32[6]{0:T(128)S(1)} %copy-done.30, bf16[960,3072]{1,0:T(8,128)(2,1)} %qkv_forward.1.refs_1_.refs_4_.refs_7_, bf16[144,2048]{1,0:T(8,128)(2,1)S(1)} %collective-permute-done.8.refs_2_, bf16[80,1024]{1,0:T(8,128)(2,1)S(1)} %collective-permute-done.9.refs_3_, ...), custom_call_target="tpu_custom_call" | custom-call | flops 14092861440 | bytes 8388608 | tf_op jit(solution)/shard_map/attn_mix/pallas_call | solution.py:97
  84.8 2.2 collective-permute-done.13
  89.6 2.8 collective-permute-done.17.refs_6_.refs_10_
  93.2 8.1 %out_project.1 = (f32[960,1024]{1,0:T(8,128)}, bf16[960,1024]{1,0:T(8,128)(2,1)}) custom-call(s32[4]{0:T(128)S(1)} %iota_xor_fusion.refs_0_.refs_8_, bf16[6,160,1024]{2,1,0:T(8,128)(2,1)} %refs_6_.11, bf16[960,1024]{1,0:T(8,128)(2,1)} %attn_mix.1.refs_2_.refs_11_.refs_24_, bf16[256,4096]{1,0:T(8,128)(2,1)} %copy-done.46, ...), custom_call_target="tpu_custom_call" | custom-call | flops 6039797760 | bytes 12582912 | tf_op jit(solution)/shard_map/out_project/pallas_call | solution.py:97
  101.4 5.2 %collective-permute-done.18.refs_12_ = bf16[176,2048]{1,0:T(8,128)(2,1)S(1)} collective-permute-done((bf16[176,2048]{1,0:T(8,128)(2,1)S(1)}, bf16[176,2048]{1,0:T(8,128)(2,1)S(1)}, u32[]{:S(2)}, u32[]{:S(2)}) %collective-permute-start.18) | collective-permute-done | bytes 720928 | tf_op jit(solution)/shard_map/ppermute | solution.py:723
  108.6 15.1 %mlp_part.4 = (bf16[960,1024]{1,0:T(8,128)(2,1)}, bf16[960,1024]{1,0:T(8,128)(2,1)}, bf16[2,256,2048]{2,1,0:T(8,128)(2,1)}, bf16[2,256,2048]{2,1,0:T(8,128)(2,1)}, f32[1,1024]{1,0:T(1,128)}) custom-call(s32[4]{0:T(128)S(1)} %iota_xor_fusion.refs_0_.refs_8_, bf16[960,1024]{1,0:T(8,128)(2,1)} %get-tuple-element.469.refs_1_.refs_13_, ...), custom_call_target="tpu_custom_call" | custom-call | flops 12079595520 | bytes 12582912 | tf_op jit(solution)/shard_map/mlp_part/pallas_call | solution.py:97
  124.1 2.1 copy-done.71
  126.2 4.2 collective-permute-done.21.refs_12_
  132.2 15.5 %mlp_part.5 = (bf16[960,1024]{1,0:T(8,128)(2,1)}, bf16[960,1024]{1,0:T(8,128)(2,1)}, bf16[2,256,2048]{2,1,0:T(8,128)(2,1)}, bf16[2,256,2048]{2,1,0:T(8,128)(2,1)}, f32[1,1024]{1,0:T(1,128)}) custom-call(s32[4]{0:T(128)S(1)} %iota_xor_fusion.refs_0_.refs_8_, bf16[960,1024]{1,0:T(8,128)(2,1)} %get-tuple-element.469.refs_1_.refs_13_, ...), custom_call_target="tpu_custom_call" | custom-call | flops 12079595520 | bytes 12582912 | tf_op jit(solution)/shard_map/mlp_part/pallas_call | solution.py:97
  154.0 15.3 %mlp_part.6 = (bf16[960,1024]{1,0:T(8,128)(2,1)}, bf16[960,1024]{1,0:T(8,128)(2,1)}, bf16[2,256,2048]{2,1,0:T(8,128)(2,1)}, bf16[2,256,2048]{2,1,0:T(8,128)(2,1)}, f32[1,1024]{1,0:T(1,128)}) custom-call(s32[4]{0:T(128)S(1)} %iota_xor_fusion.refs_0_.refs_8_, bf16[960,1024]{1,0:T(8,128)(2,1)} %get-tuple-element.469.refs_1_.refs_13_, ...), custom_call_target="tpu_custom_call" | custom-call | flops 12079595520 | bytes 12582912 | tf_op jit(solution)/shard_map/mlp_part/pallas_call | solution.py:97
  171.2 2.6 fusion.18
  178.7 15.4 %mlp_part.7 = (bf16[960,1024]{1,0:T(8,128)(2,1)}, bf16[960,1024]{1,0:T(8,128)(2,1)}, bf16[2,256,2048]{2,1,0:T(8,128)(2,1)}, bf16[2,256,2048]{2,1,0:T(8,128)(2,1)}, f32[1,1024]{1,0:T(1,128)}) custom-call(s32[4]{0:T(128)S(1)} %iota_xor_fusion.refs_0_.refs_8_, bf16[960,1024]{1,0:T(8,128)(2,1)} %get-tuple-element.469.refs_1_.refs_13_, ...), custom_call_target="tpu_custom_call" | custom-call | flops 12079595520 | bytes 12582912 | tf_op jit(solution)/shard_map/mlp_part/pallas_call | solution.py:97
  194.1 1.7 slice_bitcast_fusion.6
  199.8 1.6 collective-permute-start.32
  203.4 20.8 %mlp_back.1 = (bf16[960,1024]{1,0:T(8,128)(2,1)}, f32[8,1024]{1,0:T(8,128)}, bf16[2,256,1024]{2,1,0:T(8,128)(2,1)}, bf16[2,256,1024]{2,1,0:T(8,128)(2,1)}) custom-call(s32[4]{0:T(128)S(1)} %iota_xor_fusion.refs_0_.refs_8_, bf16[960,1024]{1,0:T(8,128)(2,1)} %get-tuple-element.510.refs_1_, bf16[960,1024]{1,0:T(8,128)(2,1)} %get-tuple-element.511.refs_2_, ...), custom_call_target="tpu_custom_call" | custom-call | flops 12079595520 | bytes 31457280 | tf_op jit(solution)/shard_map/mlp_back/pallas_call | solution.py:97
  225.3 1.7 collective-permute-done.31.refs_9_
  227.0 1.8 add_convert_fusion.1
  234.3 2.6 collective-permute-start.34
  236.9 14.5 %attn_back.2 = (bf16[960,3072]{1,0:T(8,128)(2,1)}, f32[8,1024]{1,0:T(8,128)}) custom-call(s32[4]{0:T(128)S(1)} %iota_xor_fusion.refs_0_.refs_8_, s32[6]{0:T(128)S(1)} %copy-done.30, bf16[960,1024]{1,0:T(8,128)(2,1)} %get-tuple-element.526.refs_2_.refs_7_, bf16[256,4096]{1,0:T(8,128)(2,1)} %copy-done.46, ...), custom_call_target="tpu_custom_call" | custom-call | flops 12079595520 | bytes 18874368 | tf_op jit(solution)/shard_map/attn_back/pallas_call | solution.py:97
  254.6 1.6 collective-permute-start.42
  258.1 1.7 collective-permute-start.39
  259.8 14.6 %attn_back.3 = (bf16[960,3072]{1,0:T(8,128)(2,1)}, f32[8,1024]{1,0:T(8,128)}) custom-call(s32[4]{0:T(128)S(1)} %iota_xor_fusion.refs_0_.refs_8_, s32[6]{0:T(128)S(1)} %copy-done.30, bf16[960,1024]{1,0:T(8,128)(2,1)} %get-tuple-element.526.refs_2_.refs_7_, bf16[256,4096]{1,0:T(8,128)(2,1)} %copy-done.46, ...), custom_call_target="tpu_custom_call", output_to_operand_aliasing={{0}: (8, {})} | custom-call | flops 12079595520 | bytes 18874368 | tf_op jit(solution)/shard_map/attn_back/pallas_call | solution.py:97
  280.3 8.6 %kv_grad.1 = (bf16[2,256,2048]{2,1,0:T(8,128)(2,1)}, bf16[2,256,2048]{2,1,0:T(8,128)(2,1)}) custom-call(s32[4]{0:T(128)S(1)} %iota_xor_fusion.refs_0_.refs_8_, bf16[960,1024]{1,0:T(8,128)(2,1)} %fusion.3.refs_1_, bf16[960,3072]{1,0:T(8,128)(2,1)} %get-tuple-element.557.refs_2_.refs_1_, bf16[32,2048]{1,0:T(8,128)(2,1)S(1)} %collective-permute-done.39.refs_3_, ...), custom_call_target="tpu_custom_call" | custom-call | flops 8053063680 | bytes 16777216 | tf_op jit(solution)/shard_map/kv_grad/pallas_call | solution.py:97
  295.0 3.9 collective-permute-done.48.refs_9_
  299.0 2.4 add_convert_fusion
  307.2 1.7 collective-permute-start.51
  310.5 14.9 %input_back.1 = (bf16[6,160,1024]{2,1,0:T(8,128)(2,1)}, f32[8,1024]{1,0:T(8,128)}) custom-call(s32[4]{0:T(128)S(1)} %iota_xor_fusion.refs_0_.refs_8_, bf16[960,3072]{1,0:T(8,128)(2,1)} %get-tuple-element.557.refs_2_.refs_1_, bf16[256,4096]{1,0:T(8,128)(2,1)} %copy-done.46, bf16[256,4096]{1,0:T(8,128)(2,1)} %collective-permute-done.6.refs_3_.refs_4_, ...), custom_call_target="tpu_custom_call" | custom-call | flops 8053063680 | bytes 25165824 | tf_op jit(solution)/shard_map/input_back/pallas_call | solution.py:97
  331.9 6.5 %query_grad.1 = (bf16[2,256,1152]{2,1,0:T(8,128)(2,1)}, bf16[2,256,1152]{2,1,0:T(8,128)(2,1)}) custom-call(s32[4]{0:T(128)S(1)} %iota_xor_fusion.refs_0_.refs_8_, bf16[960,1024]{1,0:T(8,128)(2,1)} %fusion.3.refs_1_, bf16[960,3072]{1,0:T(8,128)(2,1)} %get-tuple-element.557.refs_2_.refs_1_, f32[16,1024]{1,0:T(8,128)S(1)} %concatenate.177.refs_3_, ...), custom_call_target="tpu_custom_call" | custom-call | flops 6039797760 | bytes 10485760 | tf_op jit(solution)/shard_map/query_grad/pallas_call | solution.py:97
  343.4 13.6 %mlp_out.1.refs_10_ = bf16[960,1024]{1,0:T(8,128)(2,1)} custom-call(s32[4]{0:T(128)S(1)} %iota_xor_fusion.refs_0_.refs_8_, bf16[960,1024]{1,0:T(8,128)(2,1)} %get-tuple-element.470.refs_1_, bf16[960,1024]{1,0:T(8,128)(2,1)} %get-tuple-element.487.refs_2_, bf16[960,1024]{1,0:T(8,128)(2,1)} %get-tuple-element.496.refs_3_, ...), custom_call_target="tpu_custom_call" | custom-call | flops 12079595520 | bytes 25165824 | tf_op jit(solution)/shard_map/mlp_out/pallas_call | solution.py:97
  358.8 1.6 collective-permute-start.59
  362.1 1.7 collective-permute-start.63
  363.8 4.5 adam_part.10
  368.3 2.1 collective-permute-done.59.refs_12_
  371.9 4.2 adam_part.11
  376.1 4.1 collective-permute-done.63.refs_14_
  381.0 4.2 adam_part.12
  386.0 2.1 collective-permute-start.65
  388.1 4.2 adam_part.13
  392.7 9.6 %collective-permute-done.65 = bf16[64,4096]{1,0:T(8,128)(2,1)S(1)} collective-permute-done((bf16[64,4096]{1,0:T(8,128)(2,1)S(1)}, bf16[64,4096]{1,0:T(8,128)(2,1)S(1)}, u32[]{:S(2)}, u32[]{:S(2)}) %collective-permute-start.65) | collective-permute-done | bytes 524320 | tf_op jit(solution)/shard_map/ppermute | solution.py:723
  405.4 4.0 collective-permute-done.68
  409.9 2.3 collective-permute-done.67
  413.1 6.5 %collective-permute-done.69 = bf16[1,32,2176]{2,1,0:T(8,128)(2,1)S(1)} collective-permute-done((bf16[1,32,2176]{2,1,0:T(8,128)(2,1)S(1)}, bf16[1,32,2176]{2,1,0:T(8,128)(2,1)S(1)}, u32[]{:S(2)}, u32[]{:S(2)}) %collective-permute-start.69) | collective-permute-done | bytes 139296 | tf_op jit(solution)/shard_map/ppermute | solution.py:723
  421.2 5.2 %collective-permute-done.71.refs_12_ = bf16[32,2176]{1,0:T(8,128)(2,1)S(1)} collective-permute-done((bf16[32,2176]{1,0:T(8,128)(2,1)S(1)}, bf16[32,2176]{1,0:T(8,128)(2,1)S(1)}, u32[]{:S(2)}, u32[]{:S(2)}) %collective-permute-start.71) | collective-permute-done | bytes 139296 | tf_op jit(solution)/shard_map/ppermute | solution.py:723
  427.2 1.7 collective-permute-start.73
  428.9 4.2 adam_part.14
  433.1 2.6 collective-permute-done.70.refs_12_.refs_3_
  437.4 4.3 adam_part.15
  441.7 4.2 adam_part.16
  445.9 4.2 adam_part.17
  451.0 7.4 %adam_part.18 = (f32[256,4096]{1,0:T(8,128)}, f32[256,4096]{1,0:T(8,128)}, f32[256,4096]{1,0:T(8,128)}, f32[256,4096]{1,0:T(8,128)}, bf16[256,4096]{1,0:T(8,128)(2,1)}, /*index=5*/f32[8,128]{1,0:T(8,128)S(1)}) custom-call(s32[2]{0:T(128)S(1)} %copy-done.31, s32[1]{0:T(128)} %bitcast.41.refs_1_, bf16[128,2048]{1,0:T(8,128)(2,1)} %maximum_select_fusion.7.refs_2_, ...), custom_call_target="tpu_custom_call" | custom-call | flops 6442450944 | bytes 10485760 | tf_op jit(solution)/shard_map/adam_part/pallas_call | solution.py:97
  458.4 7.4 %adam_part.19 = (f32[256,4096]{1,0:T(8,128)}, f32[256,4096]{1,0:T(8,128)}, f32[256,4096]{1,0:T(8,128)}, f32[256,4096]{1,0:T(8,128)}, bf16[256,4096]{1,0:T(8,128)(2,1)}, /*index=5*/f32[8,128]{1,0:T(8,128)}) custom-call(s32[2]{0:T(128)S(1)} %copy-done.29, ...), custom_call_target="tpu_custom_call", output_to_operand_aliasing={{0}: (7, {}), {1}: (8, {}), {2}: (9, {}), {3}: (10, {}), {4... | custom-call | flops 6442450944 | bytes 10485760 | tf_op jit(solution)/shard_map/adam_part/pallas_call | solution.py:97
  (401 shorter events, 108.8 us)
Async XLA Ops:
  3.8 17.2 %collective-permute-start = (bf16[16,256]{1,0:T(8,128)(2,1)S(1)}, bf16[16,256]{1,0:T(8,128)(2,1)S(1)}, u32[]{:S(2)}, u32[]{:S(2)}) collective-permute-start(bf16[16,256]{1,0:T(8,128)(2,1)S(1)} %get-tuple-element.382), channel_id=1, source_target_pairs={{0,1},{1,0},{2,3},{3,2},{4,5},{5,4},{6,7},{7,6},{8,9},{9,8},{10,11... | collective-permute-start | bytes 24584 | tf_op jit(solution)/shard_map/ppermute | solution.py:723
  4.3 23.7 %collective-permute-start.2 = (bf16[256,1536]{1,0:T(8,128)(2,1)}, bf16[256,1536]{1,0:T(8,128)(2,1)}, u32[]{:S(2)}, u32[]{:S(2)}) collective-permute-start(bf16[256,1536]{1,0:T(8,128)(2,1)} %pad_maximum_fusion.7), channel_id=1, source_target_pairs={{0,2},{1,3},{2,0},{3,1},{4,6},{5,7},{6,4},{7,5},{8,10},{9,11},{10,... | collective-permute-start | bytes 2359304 | tf_op jit(solution)/shard_map/ppermute | solution.py:723
  29.8 15.5 %collective-permute-start.6 = (bf16[256,4096]{1,0:T(8,128)(2,1)}, bf16[256,4096]{1,0:T(8,128)(2,1)}, u32[]{:S(2)}, u32[]{:S(2)}) collective-permute-start(bf16[256,4096]{1,0:T(8,128)(2,1)} %copy-done.46), channel_id=1, source_target_pairs={{0,1},{1,0},{2,3},{3,2},{4,5},{5,4},{6,7},{7,6},{8,9},{9,8},{10,11... | collective-permute-start | bytes 6291464 | tf_op jit(solution)/shard_map/ppermute | solution.py:723
  31.1 14.2 %collective-permute-start.5 = (bf16[112,2048]{1,0:T(8,128)(2,1)}, bf16[112,2048]{1,0:T(8,128)(2,1)S(1)}, u32[]{:S(2)}, u32[]{:S(2)}) collective-permute-start(bf16[112,2048]{1,0:T(8,128)(2,1)} %slice.227), channel_id=1, source_target_pairs={{0,2},{1,3},{2,0},{3,1},{4,6},{5,7},{6,4},{7,5},{8,10},{9,11},{10,... | collective-permute-start | bytes 1376264 | tf_op jit(solution)/shard_map/ppermute | solution.py:723
  32.9 11.5 %collective-permute-start.3 = (bf16[256,768]{1,0:T(8,128)(2,1)}, bf16[256,768]{1,0:T(8,128)(2,1)S(1)}, u32[]{:S(2)}, u32[]{:S(2)}) collective-permute-start(bf16[256,768]{1,0:T(8,128)(2,1)} %get-tuple-element.415), channel_id=1, source_target_pairs={{0,4},{4,0},{8,12},{12,8},{16,20},{20,16},{24,28},{28,24},{1,5},{5... | collective-permute-start | bytes 1179656 | tf_op jit(solution)/shard_map/ppermute | solution.py:723
  34.4 11.0 %collective-permute-start.4 = (bf16[256,768]{1,0:T(8,128)(2,1)S(1)}, bf16[256,768]{1,0:T(8,128)(2,1)S(1)}, u32[]{:S(2)}, u32[]{:S(2)}) collective-permute-start(bf16[256,768]{1,0:T(8,128)(2,1)S(1)} %get-tuple-element.416), channel_id=1, source_target_pairs={{0,8},{4,12},{8,0},{12,4},{16,24},{20,28},{24,16},{28,20},{1,9},{5... | collective-permute-start | bytes 1179656 | tf_op jit(solution)/shard_map/ppermute | solution.py:723
  47.0 16.2 %collective-permute-start.8 = (bf16[144,2048]{1,0:T(8,128)(2,1)S(1)}, bf16[144,2048]{1,0:T(8,128)(2,1)S(1)}, u32[]{:S(2)}, u32[]{:S(2)}) collective-permute-start(bf16[144,2048]{1,0:T(8,128)(2,1)S(1)} %slice.228), channel_id=1, source_target_pairs={{0,2},{1,3},{2,0},{3,1},{4,6},{5,7},{6,4},{7,5},{8,10},{9,11},{10,... | collective-permute-start | bytes 1769480 | tf_op jit(solution)/shard_map/ppermute | solution.py:723
  49.4 16.6 %collective-permute-start.9 = (bf16[80,1024]{1,0:T(8,128)(2,1)S(1)}, bf16[80,1024]{1,0:T(8,128)(2,1)S(1)}, u32[]{:S(2)}, u32[]{:S(2)}) collective-permute-start(bf16[80,1024]{1,0:T(8,128)(2,1)S(1)} %slice.233), channel_id=1, source_target_pairs={{0,2},{1,3},{2,0},{3,1},{4,6},{5,7},{6,4},{7,5},{8,10},{9,11},{10,... | collective-permute-start | bytes 491528 | tf_op jit(solution)/shard_map/ppermute | solution.py:723
  67.2 19.9 %collective-permute-start.14 = (bf16[256,8192]{1,0:T(8,128)(2,1)}, bf16[256,8192]{1,0:T(8,128)(2,1)}, u32[]{:S(2)}, u32[]{:S(2)}) collective-permute-start(bf16[256,8192]{1,0:T(8,128)(2,1)} %convert_element_type.511.refs_3_.refs_7_.refs_5_.refs_9_.refs_13_.refs_17_), channel_id=1, source_target_pairs={{0,1},{1,0},{2,3},{3,2},{4,5},{5,4},{6,7},{7,6},{8,9},{9,8},{10,11... | collective-permute-start | bytes 12582920 | tf_op jit(solution)/shard_map/ppermute | solution.py:723
  67.2 19.8 %collective-permute-start.10 = (bf16[256,1024]{1,0:T(8,128)(2,1)}, bf16[256,1024]{1,0:T(8,128)(2,1)S(1)}, u32[]{:S(2)}, u32[]{:S(2)}) collective-permute-start(bf16[256,1024]{1,0:T(8,128)(2,1)} %get-tuple-element.444), channel_id=1, source_target_pairs={{0,4},{4,0},{8,12},{12,8},{16,20},{20,16},{24,28},{28,24},{1,5},{5... | collective-permute-start | bytes 1572872 | tf_op jit(solution)/shard_map/ppermute | solution.py:723
  67.9 19.1 %collective-permute-start.11 = (bf16[256,1024]{1,0:T(8,128)(2,1)}, bf16[256,1024]{1,0:T(8,128)(2,1)S(1)}, u32[]{:S(2)}, u32[]{:S(2)}) collective-permute-start(bf16[256,1024]{1,0:T(8,128)(2,1)} %get-tuple-element.445), channel_id=1, source_target_pairs={{0,8},{4,12},{8,0},{12,4},{16,24},{20,28},{24,16},{28,20},{1,9},{5... | collective-permute-start | bytes 1572872 | tf_op jit(solution)/shard_map/ppermute | solution.py:723
  69.5 17.5 %collective-permute-start.12 = (bf16[176,1024]{1,0:T(8,128)(2,1)}, bf16[176,1024]{1,0:T(8,128)(2,1)S(1)}, u32[]{:S(2)}, u32[]{:S(2)}) collective-permute-start(bf16[176,1024]{1,0:T(8,128)(2,1)} %slice.236), channel_id=1, source_target_pairs={{0,2},{1,3},{2,0},{3,1},{4,6},{5,7},{6,4},{7,5},{8,10},{9,11},{10,... | collective-permute-start | bytes 1081352 | tf_op jit(solution)/shard_map/ppermute | solution.py:723
  71.0 16.0 %collective-permute-start.13 = (bf16[80,2048]{1,0:T(8,128)(2,1)}, bf16[80,2048]{1,0:T(8,128)(2,1)S(1)}, u32[]{:S(2)}, u32[]{:S(2)}) collective-permute-start(bf16[80,2048]{1,0:T(8,128)(2,1)} %slice.237), channel_id=1, source_target_pairs={{0,2},{1,3},{2,0},{3,1},{4,6},{5,7},{6,4},{7,5},{8,10},{9,11},{10,... | collective-permute-start | bytes 983048 | tf_op jit(solution)/shard_map/ppermute | solution.py:723
  88.1 18.5 %collective-permute-start.18 = (bf16[176,2048]{1,0:T(8,128)(2,1)S(1)}, bf16[176,2048]{1,0:T(8,128)(2,1)S(1)}, u32[]{:S(2)}, u32[]{:S(2)}) collective-permute-start(bf16[176,2048]{1,0:T(8,128)(2,1)S(1)} %slice.238), channel_id=1, source_target_pairs={{0,2},{1,3},{2,0},{3,1},{4,6},{5,7},{6,4},{7,5},{8,10},{9,11},{10,... | collective-permute-start | bytes 2162696 | tf_op jit(solution)/shard_map/ppermute | solution.py:723
  106.7 17.0 %collective-permute-start.19 = (bf16[256,1024]{1,0:T(8,128)(2,1)S(1)}, bf16[256,1024]{1,0:T(8,128)(2,1)S(1)}, u32[]{:S(2)}, u32[]{:S(2)}) collective-permute-start(bf16[256,1024]{1,0:T(8,128)(2,1)S(1)} %get-tuple-element.473), channel_id=1, source_target_pairs={{0,4},{4,0},{8,12},{12,8},{16,20},{20,16},{24,28},{28,24},{1,5},{5... | collective-permute-start | bytes 1572872 | tf_op jit(solution)/shard_map/ppermute | solution.py:723
  108.2 15.6 %collective-permute-start.20 = (bf16[256,1024]{1,0:T(8,128)(2,1)S(1)}, bf16[256,1024]{1,0:T(8,128)(2,1)S(1)}, u32[]{:S(2)}, u32[]{:S(2)}) collective-permute-start(bf16[256,1024]{1,0:T(8,128)(2,1)S(1)} %get-tuple-element.474), channel_id=1, source_target_pairs={{0,8},{4,12},{8,0},{12,4},{16,24},{20,28},{24,16},{28,20},{1,9},{5... | collective-permute-start | bytes 1572872 | tf_op jit(solution)/shard_map/ppermute | solution.py:723
  130.9 19.6 %collective-permute-start.22 = (bf16[256,2048]{1,0:T(8,128)(2,1)S(1)}, bf16[256,2048]{1,0:T(8,128)(2,1)S(1)}, u32[]{:S(2)}, u32[]{:S(2)}) collective-permute-start(bf16[256,2048]{1,0:T(8,128)(2,1)S(1)} %pad_maximum_fusion.5.refs_5_.refs_9_.refs_15_), channel_id=1, source_target_pairs={{0,1},{1,0},{2,3},{3,2},{4,5},{5,4},{6,7},{7,6},{8,9},{9,8},{10,11... | collective-permute-start | bytes 3145736 | tf_op jit(solution)/shard_map/ppermute | solution.py:723
  131.1 19.4 %collective-permute-start.23 = (bf16[256,2048]{1,0:T(8,128)(2,1)S(1)}, bf16[256,2048]{1,0:T(8,128)(2,1)S(1)}, u32[]{:S(2)}, u32[]{:S(2)}) collective-permute-start(bf16[256,2048]{1,0:T(8,128)(2,1)S(1)} %pad_maximum_fusion.6.refs_5_.refs_9_.refs_19_), channel_id=1, source_target_pairs={{0,1},{1,0},{2,3},{3,2},{4,5},{5,4},{6,7},{7,6},{8,9},{9,8},{10,11... | collective-permute-start | bytes 3145736 | tf_op jit(solution)/shard_map/ppermute | solution.py:723
  131.5 18.2 %collective-permute-start.24 = (bf16[176,2048]{1,0:T(8,128)(2,1)S(1)}, bf16[176,2048]{1,0:T(8,128)(2,1)S(1)}, u32[]{:S(2)}, u32[]{:S(2)}) collective-permute-start(bf16[176,2048]{1,0:T(8,128)(2,1)S(1)} %slice_bitcast_fusion.3), channel_id=1, source_target_pairs={{0,2},{1,3},{2,0},{3,1},{4,6},{5,7},{6,4},{7,5},{8,10},{9,11},{10,... | collective-permute-start | bytes 2162696 | tf_op jit(solution)/shard_map/ppermute | solution.py:723
  151.5 17.9 %collective-permute-start.26 = (bf16[2,256,2048]{2,1,0:T(8,128)(2,1)}, bf16[2,256,2048]{2,1,0:T(8,128)(2,1)S(1)}, u32[]{:S(2)}, u32[]{:S(2)}) collective-permute-start(bf16[2,256,2048]{2,1,0:T(8,128)(2,1)} %get-tuple-element.499), channel_id=1, source_target_pairs={{0,1},{1,0},{2,3},{3,2},{4,5},{5,4},{6,7},{7,6},{8,9},{9,8},{10,11... | collective-permute-start | bytes 6291464 | tf_op jit(solution)/shard_map/ppermute | solution.py:723
  151.5 17.9 %collective-permute-start.25 = (bf16[80,2048]{1,0:T(8,128)(2,1)}, bf16[80,2048]{1,0:T(8,128)(2,1)S(1)}, u32[]{:S(2)}, u32[]{:S(2)}) collective-permute-start(bf16[80,2048]{1,0:T(8,128)(2,1)} %slice_bitcast_fusion.7), channel_id=1, source_target_pairs={{0,2},{1,3},{2,0},{3,1},{4,6},{5,7},{6,4},{7,5},{8,10},{9,11},{10,... | collective-permute-start | bytes 983048 | tf_op jit(solution)/shard_map/ppermute | solution.py:723
  173.8 22.0 %collective-permute-start.29 = (bf16[2,256,2048]{2,1,0:T(8,128)(2,1)}, bf16[2,256,2048]{2,1,0:T(8,128)(2,1)S(1)}, u32[]{:S(2)}, u32[]{:S(2)}) collective-permute-start(bf16[2,256,2048]{2,1,0:T(8,128)(2,1)} %get-tuple-element.516), channel_id=1, source_target_pairs={{0,1},{1,0},{2,3},{3,2},{4,5},{5,4},{6,7},{7,6},{8,9},{9,8},{10,11... | collective-permute-start | bytes 6291464 | tf_op jit(solution)/shard_map/ppermute | solution.py:723
  174.1 21.7 %collective-permute-start.28 = (bf16[176,2048]{1,0:T(8,128)(2,1)}, bf16[176,2048]{1,0:T(8,128)(2,1)S(1)}, u32[]{:S(2)}, u32[]{:S(2)}) collective-permute-start(bf16[176,2048]{1,0:T(8,128)(2,1)} %slice_bitcast_fusion.2), channel_id=1, source_target_pairs={{0,2},{1,3},{2,0},{3,1},{4,6},{5,7},{6,4},{7,5},{8,10},{9,11},{10,... | collective-permute-start | bytes 2162696 | tf_op jit(solution)/shard_map/ppermute | solution.py:723
  175.5 20.4 %collective-permute-start.27 = (bf16[1,128,2048]{2,1,0:T(8,128)(2,1)}, bf16[1,128,2048]{2,1,0:T(8,128)(2,1)S(1)}, u32[]{:S(2)}, u32[]{:S(2)}) collective-permute-start(bf16[1,128,2048]{2,1,0:T(8,128)(2,1)} %fusion.18), channel_id=1, source_target_pairs={{0,4},{4,0},{8,12},{12,8},{16,20},{20,16},{24,28},{28,24},{1,5},{5... | collective-permute-start | bytes 1572872 | tf_op jit(solution)/shard_map/ppermute | solution.py:723
  199.8 27.2 %collective-permute-start.33 = (bf16[2,256,2048]{2,1,0:T(8,128)(2,1)}, bf16[2,256,2048]{2,1,0:T(8,128)(2,1)}, u32[]{:S(2)}, u32[]{:S(2)}) collective-permute-start(bf16[2,256,2048]{2,1,0:T(8,128)(2,1)} %get-tuple-element.530), channel_id=1, source_target_pairs={{0,1},{1,0},{2,3},{3,2},{4,5},{5,4},{6,7},{7,6},{8,9},{9,8},{10,11... | collective-permute-start | bytes 6291464 | tf_op jit(solution)/shard_map/ppermute | solution.py:723
  199.8 27.2 %collective-permute-start.32 = (bf16[192,2048]{1,0:T(8,128)(2,1)}, bf16[192,2048]{1,0:T(8,128)(2,1)S(1)}, u32[]{:S(2)}, u32[]{:S(2)}) collective-permute-start(bf16[192,2048]{1,0:T(8,128)(2,1)} %slice_bitcast_fusion.1), channel_id=1, source_target_pairs={{0,2},{1,3},{2,0},{3,1},{4,6},{5,7},{6,4},{7,5},{8,10},{9,11},{10,... | collective-permute-start | bytes 2359304 | tf_op jit(solution)/shard_map/ppermute | solution.py:723
  201.4 25.6 %collective-permute-start.31 = (bf16[80,2048]{1,0:T(8,128)(2,1)}, bf16[80,2048]{1,0:T(8,128)(2,1)S(1)}, u32[]{:S(2)}, u32[]{:S(2)}) collective-permute-start(bf16[80,2048]{1,0:T(8,128)(2,1)} %slice_bitcast_fusion.6), channel_id=1, source_target_pairs={{0,2},{1,3},{2,0},{3,1},{4,6},{5,7},{6,4},{7,5},{8,10},{9,11},{10,... | collective-permute-start | bytes 983048 | tf_op jit(solution)/shard_map/ppermute | solution.py:723
  201.8 23.4 %collective-permute-start.30 = (bf16[1,64,2048]{2,1,0:T(8,128)(2,1)}, bf16[1,64,2048]{2,1,0:T(8,128)(2,1)S(1)}, u32[]{:S(2)}, u32[]{:S(2)}) collective-permute-start(bf16[1,64,2048]{2,1,0:T(8,128)(2,1)} %constant_dynamic-slice_fusion.3), channel_id=1, source_target_pairs={{0,8},{4,12},{8,0},{12,4},{16,24},{20,28},{24,16},{28,20},{1,9},{5... | collective-permute-start | bytes 786440 | tf_op jit(solution)/shard_map/ppermute | solution.py:723
  230.8 21.1 %collective-permute-start.38 = (bf16[2,256,1024]{2,1,0:T(8,128)(2,1)S(1)}, bf16[2,256,1024]{2,1,0:T(8,128)(2,1)S(1)}, u32[]{:S(2)}, u32[]{:S(2)}) collective-permute-start(bf16[2,256,1024]{2,1,0:T(8,128)(2,1)S(1)} %copy-done.73), channel_id=1, source_target_pairs={{0,1},{1,0},{2,3},{3,2},{4,5},{5,4},{6,7},{7,6},{8,9},{9,8},{10,11... | collective-permute-start | bytes 3145736 | tf_op jit(solution)/shard_map/ppermute | solution.py:723
  230.8 21.1 %collective-permute-start.35 = (bf16[1,128,2048]{2,1,0:T(8,128)(2,1)S(1)}, bf16[1,128,2048]{2,1,0:T(8,128)(2,1)S(1)}, u32[]{:S(2)}, u32[]{:S(2)}) collective-permute-start(bf16[1,128,2048]{2,1,0:T(8,128)(2,1)S(1)} %fusion.15), channel_id=1, source_target_pairs={{0,4},{4,0},{8,12},{12,8},{16,20},{20,16},{24,28},{28,24},{1,5},{5... | collective-permute-start | bytes 1572872 | tf_op jit(solution)/shard_map/ppermute | solution.py:723
  232.2 19.6 %collective-permute-start.37 = (bf16[128,2048]{1,0:T(8,128)(2,1)S(1)}, bf16[128,2048]{1,0:T(8,128)(2,1)S(1)}, u32[]{:S(2)}, u32[]{:S(2)}) collective-permute-start(bf16[128,2048]{1,0:T(8,128)(2,1)S(1)} %get-tuple-element.544), channel_id=1, source_target_pairs={{0,2},{1,3},{2,0},{3,1},{4,6},{5,7},{6,4},{7,5},{8,10},{9,11},{10,... | collective-permute-start | bytes 1572872 | tf_op jit(solution)/shard_map/ppermute | solution.py:723
  233.0 18.8 %collective-permute-start.36 = (bf16[64,2048]{1,0:T(8,128)(2,1)S(1)}, bf16[64,2048]{1,0:T(8,128)(2,1)S(1)}, u32[]{:S(2)}, u32[]{:S(2)}) collective-permute-start(bf16[64,2048]{1,0:T(8,128)(2,1)S(1)} %slice_bitcast_fusion.11), channel_id=1, source_target_pairs={{0,2},{1,3},{2,0},{3,1},{4,6},{5,7},{6,4},{7,5},{8,10},{9,11},{10,... | collective-permute-start | bytes 786440 | tf_op jit(solution)/shard_map/ppermute | solution.py:723
  234.3 17.1 %collective-permute-start.34 = (bf16[1,32,2048]{2,1,0:T(8,128)(2,1)S(1)}, bf16[1,32,2048]{2,1,0:T(8,128)(2,1)S(1)}, u32[]{:S(2)}, u32[]{:S(2)}) collective-permute-start(bf16[1,32,2048]{2,1,0:T(8,128)(2,1)S(1)} %add_convert_fusion.16), channel_id=1, source_target_pairs={{0,16},{4,20},{8,24},{12,28},{16,0},{20,4},{24,8},{28,12},{1,17},{... | collective-permute-start | bytes 393224 | tf_op jit(solution)/shard_map/ppermute | solution.py:723
  253.8 20.8 %collective-permute-start.41 = (bf16[1,128,2048]{2,1,0:T(8,128)(2,1)S(1)}, bf16[1,128,2048]{2,1,0:T(8,128)(2,1)S(1)}, u32[]{:S(2)}, u32[]{:S(2)}) collective-permute-start(bf16[1,128,2048]{2,1,0:T(8,128)(2,1)S(1)} %fusion.12), channel_id=1, source_target_pairs={{0,4},{4,0},{8,12},{12,8},{16,20},{20,16},{24,28},{28,24},{1,5},{5... | collective-permute-start | bytes 1572872 | tf_op jit(solution)/shard_map/ppermute | solution.py:723
  254.6 20.0 %collective-permute-start.42 = (bf16[128,2048]{1,0:T(8,128)(2,1)S(1)}, bf16[128,2048]{1,0:T(8,128)(2,1)S(1)}, u32[]{:S(2)}, u32[]{:S(2)}) collective-permute-start(bf16[128,2048]{1,0:T(8,128)(2,1)S(1)} %get-tuple-element.561), channel_id=1, source_target_pairs={{0,2},{1,3},{2,0},{3,1},{4,6},{5,7},{6,4},{7,5},{8,10},{9,11},{10,... | collective-permute-start | bytes 1572872 | tf_op jit(solution)/shard_map/ppermute | solution.py:723
  256.2 18.3 %collective-permute-start.40 = (bf16[1,64,2048]{2,1,0:T(8,128)(2,1)S(1)}, bf16[1,64,2048]{2,1,0:T(8,128)(2,1)S(1)}, u32[]{:S(2)}, u32[]{:S(2)}) collective-permute-start(bf16[1,64,2048]{2,1,0:T(8,128)(2,1)S(1)} %constant_dynamic-slice_fusion), channel_id=1, source_target_pairs={{0,8},{4,12},{8,0},{12,4},{16,24},{20,28},{24,16},{28,20},{1,9},{5... | collective-permute-start | bytes 786440 | tf_op jit(solution)/shard_map/ppermute | solution.py:723
  257.7 16.8 %collective-permute-start.43 = (bf16[128,1024]{1,0:T(8,128)(2,1)S(1)}, bf16[128,1024]{1,0:T(8,128)(2,1)S(1)}, u32[]{:S(2)}, u32[]{:S(2)}) collective-permute-start(bf16[128,1024]{1,0:T(8,128)(2,1)S(1)} %get-tuple-element.562), channel_id=1, source_target_pairs={{0,2},{1,3},{2,0},{3,1},{4,6},{5,7},{6,4},{7,5},{8,10},{9,11},{10,... | collective-permute-start | bytes 786440 | tf_op jit(solution)/shard_map/ppermute | solution.py:723
  258.1 16.4 %collective-permute-start.39 = (bf16[32,2048]{1,0:T(8,128)(2,1)S(1)}, bf16[32,2048]{1,0:T(8,128)(2,1)S(1)}, u32[]{:S(2)}, u32[]{:S(2)}) collective-permute-start(bf16[32,2048]{1,0:T(8,128)(2,1)S(1)} %fusion.28), channel_id=1, source_target_pairs={{0,16},{4,20},{8,24},{12,28},{16,0},{20,4},{24,8},{28,12},{1,17},{... | collective-permute-start | bytes 393224 | tf_op jit(solution)/shard_map/ppermute | solution.py:723
  276.3 12.6 %collective-permute-start.46 = (bf16[1,128,2048]{2,1,0:T(8,128)(2,1)S(1)}, bf16[1,128,2048]{2,1,0:T(8,128)(2,1)S(1)}, u32[]{:S(2)}, u32[]{:S(2)}) collective-permute-start(bf16[1,128,2048]{2,1,0:T(8,128)(2,1)S(1)} %fusion.11), channel_id=1, source_target_pairs={{0,4},{4,0},{8,12},{12,8},{16,20},{20,16},{24,28},{28,24},{1,5},{5... | collective-permute-start | bytes 1572872 | tf_op jit(solution)/shard_map/ppermute | solution.py:723
  277.8 11.2 %collective-permute-start.44 = (bf16[64,2048]{1,0:T(8,128)(2,1)S(1)}, bf16[64,2048]{1,0:T(8,128)(2,1)S(1)}, u32[]{:S(2)}, u32[]{:S(2)}) collective-permute-start(bf16[64,2048]{1,0:T(8,128)(2,1)S(1)} %maximum_select_fusion.9), channel_id=1, source_target_pairs={{0,8},{4,12},{8,0},{12,4},{16,24},{20,28},{24,16},{28,20},{1,9},{5... | collective-permute-start | bytes 786440 | tf_op jit(solution)/shard_map/ppermute | solution.py:723
  278.2 10.7 %collective-permute-start.47 = (bf16[128,1024]{1,0:T(8,128)(2,1)S(1)}, bf16[128,1024]{1,0:T(8,128)(2,1)S(1)}, u32[]{:S(2)}, u32[]{:S(2)}) collective-permute-start(bf16[128,1024]{1,0:T(8,128)(2,1)S(1)} %get-tuple-element.577), channel_id=1, source_target_pairs={{0,2},{1,3},{2,0},{3,1},{4,6},{5,7},{6,4},{7,5},{8,10},{9,11},{10,... | collective-permute-start | bytes 786440 | tf_op jit(solution)/shard_map/ppermute | solution.py:723
  279.0 10.0 %collective-permute-start.45 = (bf16[1,32,2048]{2,1,0:T(8,128)(2,1)S(1)}, bf16[1,32,2048]{2,1,0:T(8,128)(2,1)S(1)}, u32[]{:S(2)}, u32[]{:S(2)}) collective-permute-start(bf16[1,32,2048]{2,1,0:T(8,128)(2,1)S(1)} %add_convert_fusion.14), channel_id=1, source_target_pairs={{0,16},{4,20},{8,24},{12,28},{16,0},{20,4},{24,8},{28,12},{1,17},{... | collective-permute-start | bytes 393224 | tf_op jit(solution)/shard_map/ppermute | solution.py:723
  302.3 24.7 %collective-permute-start.49 = (bf16[192,2048]{1,0:T(8,128)(2,1)}, bf16[192,2048]{1,0:T(8,128)(2,1)S(1)}, u32[]{:S(2)}, u32[]{:S(2)}) collective-permute-start(bf16[192,2048]{1,0:T(8,128)(2,1)} %slice_bitcast_fusion), channel_id=1, source_target_pairs={{0,2},{1,3},{2,0},{3,1},{4,6},{5,7},{6,4},{7,5},{8,10},{9,11},{10,... | collective-permute-start | bytes 2359304 | tf_op jit(solution)/shard_map/ppermute | solution.py:723
  303.6 23.4 %collective-permute-start.50 = (bf16[128,2048]{1,0:T(8,128)(2,1)}, bf16[128,2048]{1,0:T(8,128)(2,1)S(1)}, u32[]{:S(2)}, u32[]{:S(2)}) collective-permute-start(bf16[128,2048]{1,0:T(8,128)(2,1)} %maximum_select_fusion.4.refs_2_), channel_id=1, source_target_pairs={{0,4},{4,0},{8,12},{12,8},{16,20},{20,16},{24,28},{28,24},{1,5},{5... | collective-permute-start | bytes 1572872 | tf_op jit(solution)/shard_map/ppermute | solution.py:723
  304.3 22.7 %collective-permute-start.52 = (bf16[1,64,4096]{2,1,0:T(8,128)(2,1)}, bf16[1,64,4096]{2,1,0:T(8,128)(2,1)S(1)}, u32[]{:S(2)}, u32[]{:S(2)}) collective-permute-start(bf16[1,64,4096]{2,1,0:T(8,128)(2,1)} %constant_dynamic-slice_fusion.1), channel_id=1, source_target_pairs={{0,8},{4,12},{8,0},{12,4},{16,24},{20,28},{24,16},{28,20},{1,9},{5... | collective-permute-start | bytes 1572872 | tf_op jit(solution)/shard_map/ppermute | solution.py:723
  305.8 21.2 %collective-permute-start.53 = (bf16[1,128,1024]{2,1,0:T(8,128)(2,1)}, bf16[1,128,1024]{2,1,0:T(8,128)(2,1)S(1)}, u32[]{:S(2)}, u32[]{:S(2)}) collective-permute-start(bf16[1,128,1024]{2,1,0:T(8,128)(2,1)} %fusion.25), channel_id=1, source_target_pairs={{0,4},{4,0},{8,12},{12,8},{16,20},{20,16},{24,28},{28,24},{1,5},{5... | collective-permute-start | bytes 786440 | tf_op jit(solution)/shard_map/ppermute | solution.py:723
  307.2 19.8 %collective-permute-start.51 = (bf16[32,2048]{1,0:T(8,128)(2,1)}, bf16[32,2048]{1,0:T(8,128)(2,1)S(1)}, u32[]{:S(2)}, u32[]{:S(2)}) collective-permute-start(bf16[32,2048]{1,0:T(8,128)(2,1)} %fusion.29), channel_id=1, source_target_pairs={{0,16},{4,20},{8,24},{12,28},{16,0},{20,4},{24,8},{28,12},{1,17},{... | collective-permute-start | bytes 393224 | tf_op jit(solution)/shard_map/ppermute | solution.py:723
  330.6 7.8 %collective-permute-start.54 = (bf16[64,2048]{1,0:T(8,128)(2,1)}, bf16[64,2048]{1,0:T(8,128)(2,1)S(1)}, u32[]{:S(2)}, u32[]{:S(2)}) collective-permute-start(bf16[64,2048]{1,0:T(8,128)(2,1)} %slice_bitcast_fusion.8), channel_id=1, source_target_pairs={{0,2},{1,3},{2,0},{3,1},{4,6},{5,7},{6,4},{7,5},{8,10},{9,11},{10,... | collective-permute-start | bytes 786440 | tf_op jit(solution)/shard_map/ppermute | solution.py:723
  340.5 16.6 %collective-permute-start.57 = (bf16[2,256,1152]{2,1,0:T(8,128)(2,1)S(1)}, bf16[2,256,1152]{2,1,0:T(8,128)(2,1)S(1)}, u32[]{:S(2)}, u32[]{:S(2)}) collective-permute-start(bf16[2,256,1152]{2,1,0:T(8,128)(2,1)S(1)} %copy-done.12), channel_id=1, source_target_pairs={{0,1},{1,0},{2,3},{3,2},{4,5},{5,4},{6,7},{7,6},{8,9},{9,8},{10,11... | collective-permute-start | bytes 3538952 | tf_op jit(solution)/shard_map/ppermute | solution.py:723
  340.5 16.5 %collective-permute-start.56 = (bf16[1,128,2048]{2,1,0:T(8,128)(2,1)S(1)}, bf16[1,128,2048]{2,1,0:T(8,128)(2,1)S(1)}, u32[]{:S(2)}, u32[]{:S(2)}) collective-permute-start(bf16[1,128,2048]{2,1,0:T(8,128)(2,1)S(1)} %fusion.6), channel_id=1, source_target_pairs={{0,4},{4,0},{8,12},{12,8},{16,20},{20,16},{24,28},{28,24},{1,5},{5... | collective-permute-start | bytes 1572872 | tf_op jit(solution)/shard_map/ppermute | solution.py:723
  342.1 15.0 %collective-permute-start.58 = (bf16[1,32,4096]{2,1,0:T(8,128)(2,1)S(1)}, bf16[1,32,4096]{2,1,0:T(8,128)(2,1)S(1)}, u32[]{:S(2)}, u32[]{:S(2)}) collective-permute-start(bf16[1,32,4096]{2,1,0:T(8,128)(2,1)S(1)} %add_convert_fusion.8), channel_id=1, source_target_pairs={{0,16},{4,20},{8,24},{12,28},{16,0},{20,4},{24,8},{28,12},{1,17},{... | collective-permute-start | bytes 786440 | tf_op jit(solution)/shard_map/ppermute | solution.py:723
  358.8 11.6 %collective-permute-start.59 = (bf16[1,64,2048]{2,1,0:T(8,128)(2,1)S(1)}, bf16[1,64,2048]{2,1,0:T(8,128)(2,1)S(1)}, u32[]{:S(2)}, u32[]{:S(2)}) collective-permute-start(bf16[1,64,2048]{2,1,0:T(8,128)(2,1)S(1)} %constant_dynamic-slice_fusion.4), channel_id=1, source_target_pairs={{0,8},{4,12},{8,0},{12,4},{16,24},{20,28},{24,16},{28,20},{1,9},{5... | collective-permute-start | bytes 786440 | tf_op jit(solution)/shard_map/ppermute | solution.py:723
  360.4 19.8 %collective-permute-start.61 = (bf16[256,1152]{1,0:T(8,128)(2,1)S(1)}, bf16[256,1152]{1,0:T(8,128)(2,1)S(1)}, u32[]{:S(2)}, u32[]{:S(2)}) collective-permute-start(bf16[256,1152]{1,0:T(8,128)(2,1)S(1)} %fusion.19), channel_id=1, source_target_pairs={{0,2},{1,3},{2,0},{3,1},{4,6},{5,7},{6,4},{7,5},{8,10},{9,11},{10,... | collective-permute-start | bytes 1769480 | tf_op jit(solution)/shard_map/ppermute | solution.py:723
  360.8 19.4 %collective-permute-start.62 = (bf16[128,2048]{1,0:T(8,128)(2,1)S(1)}, bf16[128,2048]{1,0:T(8,128)(2,1)S(1)}, u32[]{:S(2)}, u32[]{:S(2)}) collective-permute-start(bf16[128,2048]{1,0:T(8,128)(2,1)S(1)} %maximum_select_fusion.5.refs_2_), channel_id=1, source_target_pairs={{0,4},{4,0},{8,12},{12,8},{16,20},{20,16},{24,28},{28,24},{1,5},{5... | collective-permute-start | bytes 1572872 | tf_op jit(solution)/shard_map/ppermute | solution.py:723
  362.1 18.1 %collective-permute-start.63 = (bf16[32,4096]{1,0:T(8,128)(2,1)S(1)}, bf16[32,4096]{1,0:T(8,128)(2,1)S(1)}, u32[]{:S(2)}, u32[]{:S(2)}) collective-permute-start(bf16[32,4096]{1,0:T(8,128)(2,1)S(1)} %fusion.26), channel_id=1, source_target_pairs={{0,16},{4,20},{8,24},{12,28},{16,0},{20,4},{24,8},{28,12},{1,17},{... | collective-permute-start | bytes 786440 | tf_op jit(solution)/shard_map/ppermute | solution.py:723
  370.4 14.7 %collective-permute-start.60 = (bf16[1,32,2048]{2,1,0:T(8,128)(2,1)S(1)}, bf16[1,32,2048]{2,1,0:T(8,128)(2,1)S(1)}, u32[]{:S(2)}, u32[]{:S(2)}) collective-permute-start(bf16[1,32,2048]{2,1,0:T(8,128)(2,1)S(1)} %add_convert_fusion.12), channel_id=1, source_target_pairs={{0,16},{4,20},{8,24},{12,28},{16,0},{20,4},{24,8},{28,12},{1,17},{... | collective-permute-start | bytes 393224 | tf_op jit(solution)/shard_map/ppermute | solution.py:723
  386.0 16.4 %collective-permute-start.65 = (bf16[64,4096]{1,0:T(8,128)(2,1)S(1)}, bf16[64,4096]{1,0:T(8,128)(2,1)S(1)}, u32[]{:S(2)}, u32[]{:S(2)}) collective-permute-start(bf16[64,4096]{1,0:T(8,128)(2,1)S(1)} %maximum_select_fusion.6), channel_id=1, source_target_pairs={{0,8},{4,12},{8,0},{12,4},{16,24},{20,28},{24,16},{28,20},{1,9},{5... | collective-permute-start | bytes 1572872 | tf_op jit(solution)/shard_map/ppermute | solution.py:723
  392.6 16.9 %collective-permute-start.68 = (bf16[1,64,2176]{2,1,0:T(8,128)(2,1)S(1)}, bf16[1,64,2176]{2,1,0:T(8,128)(2,1)S(1)}, u32[]{:S(2)}, u32[]{:S(2)}) collective-permute-start(bf16[1,64,2176]{2,1,0:T(8,128)(2,1)S(1)} %constant_dynamic-slice_fusion.2), channel_id=1, source_target_pairs={{0,8},{4,12},{8,0},{12,4},{16,24},{20,28},{24,16},{28,20},{1,9},{5... | collective-permute-start | bytes 835592 | tf_op jit(solution)/shard_map/ppermute | solution.py:723
  402.7 9.6 %collective-permute-start.67 = (bf16[64,2048]{1,0:T(8,128)(2,1)S(1)}, bf16[64,2048]{1,0:T(8,128)(2,1)S(1)}, u32[]{:S(2)}, u32[]{:S(2)}) collective-permute-start(bf16[64,2048]{1,0:T(8,128)(2,1)S(1)} %maximum_select_fusion.11), channel_id=1, source_target_pairs={{0,8},{4,12},{8,0},{12,4},{16,24},{20,28},{24,16},{28,20},{1,9},{5... | collective-permute-start | bytes 786440 | tf_op jit(solution)/shard_map/ppermute | solution.py:723
  404.0 23.1 %collective-permute-start.72 = (bf16[128,4096]{1,0:T(8,128)(2,1)S(1)}, bf16[128,4096]{1,0:T(8,128)(2,1)S(1)}, u32[]{:S(2)}, u32[]{:S(2)}) collective-permute-start(bf16[128,4096]{1,0:T(8,128)(2,1)S(1)} %maximum_select_fusion.refs_2_), channel_id=1, source_target_pairs={{0,4},{4,0},{8,12},{12,8},{16,20},{20,16},{24,28},{28,24},{1,5},{5... | collective-permute-start | bytes 3145736 | tf_op jit(solution)/shard_map/ppermute | solution.py:723
  409.5 10.1 %collective-permute-start.69 = (bf16[1,32,2176]{2,1,0:T(8,128)(2,1)S(1)}, bf16[1,32,2176]{2,1,0:T(8,128)(2,1)S(1)}, u32[]{:S(2)}, u32[]{:S(2)}) collective-permute-start(bf16[1,32,2176]{2,1,0:T(8,128)(2,1)S(1)} %add_convert_fusion.10), channel_id=1, source_target_pairs={{0,16},{4,20},{8,24},{12,28},{16,0},{20,4},{24,8},{28,12},{1,17},{... | collective-permute-start | bytes 417800 | tf_op jit(solution)/shard_map/ppermute | solution.py:723
  419.8 16.0 %collective-permute-start.70 = (bf16[128,2048]{1,0:T(8,128)(2,1)}, bf16[128,2048]{1,0:T(8,128)(2,1)S(1)}, u32[]{:S(2)}, u32[]{:S(2)}) collective-permute-start(bf16[128,2048]{1,0:T(8,128)(2,1)} %maximum_select_fusion.7.refs_2_), channel_id=1, source_target_pairs={{0,4},{4,0},{8,12},{12,8},{16,20},{20,16},{24,28},{28,24},{1,5},{5... | collective-permute-start | bytes 1572872 | tf_op jit(solution)/shard_map/ppermute | solution.py:723
  427.2 8.6 %collective-permute-start.73 = (bf16[64,2176]{1,0:T(8,128)(2,1)S(1)}, bf16[64,2176]{1,0:T(8,128)(2,1)S(1)}, u32[]{:S(2)}, u32[]{:S(2)}) collective-permute-start(bf16[64,2176]{1,0:T(8,128)(2,1)S(1)} %maximum_select_fusion.8), channel_id=1, source_target_pairs={{0,8},{4,12},{8,0},{12,4},{16,24},{20,28},{24,16},{28,20},{1,9},{5... | collective-permute-start | bytes 835592 | tf_op jit(solution)/shard_map/ppermute | solution.py:723
  435.9 14.3 %collective-permute-start.74 = (bf16[128,2176]{1,0:T(8,128)(2,1)S(1)}, bf16[128,2176]{1,0:T(8,128)(2,1)S(1)}, u32[]{:S(2)}, u32[]{:S(2)}) collective-permute-start(bf16[128,2176]{1,0:T(8,128)(2,1)S(1)} %maximum_select_fusion.3.refs_2_), channel_id=1, source_target_pairs={{0,4},{4,0},{8,12},{12,8},{16,20},{20,16},{24,28},{28,24},{1,5},{5... | collective-permute-start | bytes 1671176 | tf_op jit(solution)/shard_map/ppermute | solution.py:723
  (86 other events, 548.7 us)
